TPU v7x, 32 devices: a whole 2x2x4 slice. The times are simulated.
32 devices in a mesh: dp: 8 (over z, core), expert: 4 (over y, x).
Axes of the slice: x: 2, y: 2, z: 4, core: 2. Of those that a mesh axis runs over, the one named last changes fastest.
Arguments:
- saved_input: bfloat16 [4096, 2048], P(('dp', 'expert')), parts along dimension 0, may hold values from -6 to 6
- grad_out: bfloat16 [4096, 2048], P(('dp', 'expert')), parts along dimension 0, may hold values from -6 to 6
- routes: int32 [4096, 8], P(('dp', 'expert')), parts along dimension 0, may hold values from 0 to 15, all different within a row
- route_gates: bfloat16 [4096, 8], P(('dp', 'expert')), parts along dimension 0, may hold values from 0.049804688 to 0.5
- gate_proj: bfloat16 [16, 2048, 768], P('expert'), may hold values from -0.125 to 0.125
- up_proj: bfloat16 [16, 2048, 768], P('expert'), may hold values from -0.125 to 0.125
- down_proj: bfloat16 [16, 768, 2048], P('expert'), may hold values from -0.21875 to 0.21875
Outputs:
- grad_in: bfloat16 [4096, 2048], P(('dp', 'expert')), parts along dimension 0
There are 8 independent parts, one for each index of `dp`. A program takes and returns all parts, laid end to end along the dimension named above; an argument that names none is the same for every part. Nothing has to cross between parts.
Inputs may be any that keep to these rules, and one draw needn't show every extreme that they name: `routes`: each token names 8 different experts, and every expert is named by some token.
All inputs are finite; a program needn't handle non-finite values.
Results may differ from a plain program's by a relative error of at most 0.0057.
Values may be sent and summed in bfloat16 or wider, within the bound.
No kernel may reach another device: no remote copies, remote signals or barrier semaphores. Data moves between devices by JAX's collectives and lax.ppermute only.
A program may use at most 128 MiB of HBM per device.

v0:
```python
import jax
import jax.numpy as jnp
from jax import lax
from jax.sharding import PartitionSpec as P

CAP = 56


def pair_ranks(ordered, experts):
    labels = jnp.arange(experts, dtype=jnp.int32)
    matches = (ordered[..., None] == labels).astype(jnp.int32)
    earlier = jnp.cumsum(matches, axis=-2) - matches
    return jnp.sum(earlier * matches, axis=-1)


def expert_rows(input_rows, grad_rows, gate_rows, gate_proj, up_proj, down_proj):
    gate_pre = jnp.einsum(
        "nmed,edf->nmef", input_rows, gate_proj, preferred_element_type=jnp.float32
    )
    up_pre = jnp.einsum("nmed,edf->nmef", input_rows, up_proj, preferred_element_type=jnp.float32)
    back_grad = jnp.einsum(
        "nmed,efd->nmef", grad_rows, down_proj, preferred_element_type=jnp.float32
    )
    scaled = gate_rows.astype(jnp.float32)[..., None] * back_grad
    sigmoid_gate = jax.nn.sigmoid(gate_pre)
    gate_grad = (scaled * up_pre * sigmoid_gate * (1.0 + gate_pre * (1.0 - sigmoid_gate))).astype(
        jnp.bfloat16
    )
    up_grad = (scaled * gate_pre * sigmoid_gate).astype(jnp.bfloat16)
    summed = jnp.einsum("nmef,edf->nmed", gate_grad, gate_proj, preferred_element_type=jnp.float32)
    summed = summed + jnp.einsum(
        "nmef,edf->nmed", up_grad, up_proj, preferred_element_type=jnp.float32
    )
    return summed.astype(jnp.bfloat16)


def body(saved_input, grad_out, routes, route_gates, gate_proj, up_proj, down_proj):
    devices = lax.axis_size("expert")
    local_experts = gate_proj.shape[0]
    experts = devices * local_experts
    tok_rows, features = saved_input.shape
    top_count = routes.shape[1]
    slot_count = experts * CAP
    grid_shape = (devices, CAP, local_experts, features)
    gate_shape = (devices, CAP, local_experts)
    zero_row = jnp.zeros((1, features), jnp.bfloat16)
    pair_index = jnp.arange(top_count * tok_rows, dtype=jnp.int32)
    ordered = jnp.swapaxes(routes, 0, 1).reshape(-1)
    ranking = pair_ranks(ordered, experts)
    kept_pair = ranking < CAP
    owner_dev = ordered // local_experts
    local_slot = ordered % local_experts
    slot_of = jnp.where(
        kept_pair, (owner_dev * CAP + ranking) * local_experts + local_slot, slot_count
    )
    tiled_index = pair_index % tok_rows
    send_input = (
        jnp.zeros((slot_count, features), jnp.bfloat16)
        .at[slot_of]
        .set(saved_input[tiled_index], mode="drop")
    )
    send_grad = (
        jnp.zeros((slot_count, features), jnp.bfloat16)
        .at[slot_of]
        .set(grad_out[tiled_index], mode="drop")
    )
    pair_gates = jnp.swapaxes(route_gates, 0, 1).reshape(-1)
    send_gate = jnp.zeros((slot_count,), jnp.bfloat16).at[slot_of].set(pair_gates, mode="drop")
    send_input = send_input.reshape(grid_shape)
    send_grad = send_grad.reshape(grid_shape)
    send_gate = send_gate.reshape(gate_shape)
    arrived = (
        lax.all_to_all(send_input, "expert", split_axis=0, concat_axis=0, tiled=True),
        lax.all_to_all(send_grad, "expert", split_axis=0, concat_axis=0, tiled=True),
        lax.all_to_all(send_gate, "expert", split_axis=0, concat_axis=0, tiled=True),
    )
    expert_out = expert_rows(arrived[0], arrived[1], arrived[2], gate_proj, up_proj, down_proj)
    returned = lax.all_to_all(expert_out, "expert", split_axis=0, concat_axis=0, tiled=True)
    gathered_back = jnp.concatenate([returned.reshape(slot_count, features), zero_row], 0)
    picked = gathered_back[slot_of].reshape(top_count, tok_rows, features)
    return jnp.sum(picked.astype(jnp.float32), axis=0).astype(jnp.bfloat16)


def solution(mesh):
    in_specs = (
        P(("dp", "expert"), None),
        P(("dp", "expert"), None),
        P(("dp", "expert"), None),
        P(("dp", "expert"), None),
        P("expert", None, None),
        P("expert", None, None),
        P("expert", None, None),
    )
    out_specs = P(("dp", "expert"), None)
    return jax.shard_map(body, mesh=mesh, in_specs=in_specs, out_specs=out_specs, check_vma=False)
```

profile of v0, /device:TPU:0, one launch (start us, length us, event | category | flops | bytes accessed | tf_op | source)
XLA Modules:
  0.0 274.8 jit_solution(1835120570232336824)
XLA Ops:
  0.0 0.0 copy-start
  0.0 0.8 fusion.49
  0.8 4.5 %reduce-window.6 = s32[16,8,128]{2,1,0:T(8,128)S(1)} reduce-window(s32[16,8,128]{2,1,0:T(8,128)S(1)} %fusion.49, s32[]{:T(128)} %constant.51.clone.1), window={size=1x1x128 pad=0_0x0_0x127_0}, to_apply=%region_0.0 | reduce-window | flops 2080768 | bytes 131076 | tf_op jit(solution)/shard_map/reduce-window
  5.3 0.1 slice.14
  5.3 0.1 copy.16
  5.5 0.1 copy.17
  5.6 0.1 broadcast_add_fusion
  5.7 0.7 fusion.48
  6.4 0.7 compare_select_fusion
  7.1 7.7 %scatter_custom_fusion = bf16[896]{0:T(1024)(128)(2,1)S(1)} fusion(s32[1024]{0:T(1024)S(1)} %bitcast.116, bf16[1024]{0:T(1024)(128)(2,1)} %bitcast.119, bf16[]{:T(256)} %constant.50.clone.1), kind=kCustom, calls=%fused_computation.66 | custom fusion | bytes 2304 | tf_op jit(solution)/shard_map/scatter | solution.py:68
  14.9 0.1 reshape.225
  15.0 0.7 copy.18
  15.7 5.4 %all-to-all-start = ((bf16[4,56,4]{1,2,0:T(4,128)(2,1)}), bf16[4,56,4]{1,2,0:T(4,128)(2,1)S(1)}, u32[]{:S(2)}, u32[]{:S(2)}) async-start(bf16[4,56,4]{1,2,0:T(4,128)(2,1)} %copy.18), calls=%async_computation | async-start | bytes 8192 | tf_op jit(solution)/shard_map/all_to_all | solution.py:75
  21.2 0.0 copy-done
  21.2 22.7 %scatter_custom_fusion.2 = bf16[896,2048]{1,0:T(8,128)(2,1)} fusion(s32[1024]{0:T(1024)S(1)} %bitcast.117, bf16[128,2048]{1,0:T(8,128)(2,1)S(1)} %copy-done, s32[1024]{0:T(1024)S(1)} %broadcast_clamp_fusion.1, bf16[]{:T(256)} %constant.50.clone.1), kind=kCustom, calls=%fused_computation.17 | custom fusion | bytes 3670018 | tf_op jit(solution)/shard_map/scatter | solution.py:60
  43.9 6.6 %reshape.227 = bf16[4,56,4,2048]{3,2,1,0:T(4,128)(2,1)} reshape(bf16[896,2048]{1,0:T(8,128)(2,1)} %scatter_custom_fusion.2) | data formatting | bytes 7340032 | tf_op jit(solution)/shard_map/reshape | solution.py:69
  50.4 5.8 %copy.22 = bf16[4,56,4,2048]{3,1,2,0:T(8,128)(2,1)} copy(bf16[4,56,4,2048]{3,2,1,0:T(4,128)(2,1)} %reshape.227) | data formatting | bytes 7340032 | tf_op jit(solution)/shard_map/reshape | solution.py:69
  56.3 0.0 all-to-all-done
  56.3 4.7 %all-to-all-start.2 = ((bf16[4,56,4,2048]{3,1,2,0:T(8,128)(2,1)}), bf16[4,56,4,2048]{3,1,2,0:T(8,128)(2,1)}, u32[]{:S(2)}, u32[]{:S(2)}) async-start(bf16[4,56,4,2048]{3,1,2,0:T(8,128)(2,1)} %copy.22), calls=%async_computation.2 | async-start | bytes 7340032 | tf_op jit(solution)/shard_map/all_to_all | solution.py:73
  61.0 21.9 %scatter_custom_fusion.1 = bf16[896,2048]{1,0:T(8,128)(2,1)} fusion(s32[1024]{0:T(1024)S(1)} %bitcast.118, bf16[128,2048]{1,0:T(8,128)(2,1)} %param.8, s32[1024]{0:T(1024)S(1)} %broadcast_clamp_fusion.1, bf16[]{:T(256)} %constant.50.clone.1), kind=kCustom, calls=%fused_computation.19 | custom fusion | bytes 3670528 | tf_op jit(solution)/shard_map/scatter | solution.py:65
  82.9 6.6 %reshape.226 = bf16[4,56,4,2048]{3,2,1,0:T(4,128)(2,1)} reshape(bf16[896,2048]{1,0:T(8,128)(2,1)} %scatter_custom_fusion.1) | data formatting | bytes 7340032 | tf_op jit(solution)/shard_map/reshape | solution.py:70
  89.5 5.9 %copy.20 = bf16[4,56,4,2048]{3,1,2,0:T(8,128)(2,1)} copy(bf16[4,56,4,2048]{3,2,1,0:T(4,128)(2,1)} %reshape.226) | data formatting | bytes 7340032 | tf_op jit(solution)/shard_map/reshape | solution.py:70
  95.4 7.5 %all-to-all-done.2 = bf16[4,56,4,2048]{3,1,2,0:T(8,128)(2,1)} async-done(((bf16[4,56,4,2048]{3,1,2,0:T(8,128)(2,1)}), bf16[4,56,4,2048]{3,1,2,0:T(8,128)(2,1)}, u32[]{:S(2)}, u32[]{:S(2)}) %all-to-all-start.2) | async-done | bytes 3670048 | tf_op jit(solution)/shard_map/all_to_all | solution.py:73
  102.9 4.9 %all-to-all-start.1 = ((bf16[4,56,4,2048]{3,1,2,0:T(8,128)(2,1)}), bf16[4,56,4,2048]{3,1,2,0:T(8,128)(2,1)}, u32[]{:S(2)}, u32[]{:S(2)}) async-start(bf16[4,56,4,2048]{3,1,2,0:T(8,128)(2,1)} %copy.20), calls=%async_computation.1 | async-start | bytes 7340032 | tf_op jit(solution)/shard_map/all_to_all | solution.py:74
  107.8 8.7 %fusion.2 = f32[4,4,56,768]{3,2,1,0:T(8,128)S(1)} fusion(bf16[4,2048,768]{2,1,0:T(8,128)(2,1)} %param.11, bf16[4,56,4,2048]{3,1,2,0:T(8,128)(2,1)} %all-to-all-done.2), kind=kOutput, calls=%fused_computation.8 | convolution fusion | flops 2818572288 | bytes 19005440 | tf_op jit(solution)/shard_map/nmed,edf->nmef/dot_general | solution.py:17
  116.5 32.4 %all-to-all-done.1 = bf16[4,56,4,2048]{3,1,2,0:T(8,128)(2,1)} async-done(((bf16[4,56,4,2048]{3,1,2,0:T(8,128)(2,1)}), bf16[4,56,4,2048]{3,1,2,0:T(8,128)(2,1)}, u32[]{:S(2)}, u32[]{:S(2)}) %all-to-all-start.1) | async-done | bytes 3670048 | tf_op jit(solution)/shard_map/all_to_all | solution.py:74
  149.0 11.2 %fusion.4 = f32[4,4,56,768]{3,2,1,0:T(8,128)} fusion(bf16[4,768,2048]{2,1,0:T(8,128)(2,1)} %param.13, bf16[4,56,4,2048]{3,1,2,0:T(8,128)(2,1)} %all-to-all-done.1), kind=kOutput, calls=%fused_computation.10 | convolution fusion | flops 2818572288 | bytes 19005440 | tf_op jit(solution)/shard_map/nmed,efd->nmef/dot_general | solution.py:21
  160.2 15.4 %fusion = f32[4,4,56,2048]{3,2,1,0:T(8,128)} fusion(bf16[4,2048,768]{2,1,0:T(8,128)(2,1)} %param.11, f32[4,4,56,768]{3,2,1,0:T(8,128)S(1)} %fusion.2, f32[4,4,56,768]{3,2,1,0:T(8,128)} %fusion.4, bf16[4,2048,768]{2,1,0:T(8,128)(2,1)} %param.12, bf16[4,56,4,2048]{3,1,2,0:T(8,128)(2,1)} %all-to-all-done.2, f32[4,56,4]{1,0,2:T(4,128)S(1)} %copy.19), kind=kOutput, calls=%fused_computation.6 | convolution fusion | flops 5644713984 | bytes 41684480 | tf_op jit(solution)/shard_map/nmef,edf->nmed/dot_general | solution.py:30
  175.6 15.7 %fusion.19 = bf16[4,56,4,2048]{3,1,0,2:T(8,128)(2,1)} fusion(f32[4,4,56,2048]{3,2,1,0:T(8,128)} %fusion, bf16[4,2048,768]{2,1,0:T(8,128)(2,1)} %param.12, f32[4,4,56,768]{3,2,1,0:T(8,128)S(1)} %fusion.2, f32[4,4,56,768]{3,2,1,0:T(8,128)} %fusion.4, f32[4,56,4]{1,0,2:T(4,128)S(1)} %copy.19), kind=kOutput, calls=%fused_computation.24 | convolution fusion | flops 2827059200 | bytes 29101568 | tf_op jit(solution)/shard_map/nmef,edf->nmed/dot_general | solution.py:31
  191.3 4.4 %copy.25 = bf16[4,56,4,2048]{3,1,2,0:T(8,128)(2,1)} copy(bf16[4,56,4,2048]{3,1,0,2:T(8,128)(2,1)} %fusion.19) | data formatting | bytes 7340032 | tf_op jit(solution)/shard_map/convert_element_type | solution.py:34
  195.7 5.0 %all-to-all-start.3 = ((bf16[4,56,4,2048]{3,1,2,0:T(8,128)(2,1)}), bf16[4,56,4,2048]{3,1,2,0:T(8,128)(2,1)}, u32[]{:S(2)}, u32[]{:S(2)}) async-start(bf16[4,56,4,2048]{3,1,2,0:T(8,128)(2,1)} %copy.25), calls=%async_computation.3 | async-start | bytes 7340032 | tf_op jit(solution)/shard_map/all_to_all | solution.py:78
  200.7 41.2 %all-to-all-done.3 = bf16[4,56,4,2048]{3,1,2,0:T(8,128)(2,1)} async-done(((bf16[4,56,4,2048]{3,1,2,0:T(8,128)(2,1)}), bf16[4,56,4,2048]{3,1,2,0:T(8,128)(2,1)}, u32[]{:S(2)}, u32[]{:S(2)}) %all-to-all-start.3) | async-done | bytes 3670048 | tf_op jit(solution)/shard_map/all_to_all | solution.py:78
  241.9 6.7 %copy.26 = bf16[4,56,4,2048]{3,2,1,0:T(4,128)(2,1)} copy(bf16[4,56,4,2048]{3,1,2,0:T(8,128)(2,1)} %all-to-all-done.3) | data formatting | bytes 7340032 | tf_op jit(solution)/shard_map/all_to_all | solution.py:78
  248.6 6.3 %reshape.228 = bf16[896,2048]{1,0:T(8,128)(2,1)} reshape(bf16[4,56,4,2048]{3,2,1,0:T(4,128)(2,1)} %copy.26) | data formatting | bytes 7340032 | tf_op jit(solution)/shard_map/reshape | solution.py:79
  254.9 4.4 %concatenate.3 = bf16[897,2048]{1,0:T(8,128)(2,1)} pad(bf16[896,2048]{1,0:T(8,128)(2,1)} %reshape.228, bf16[]{:T(256)} %constant.50.clone.1), padding=0_1x0_0 | pad | bytes 7344130 | tf_op jit(solution)/shard_map/concatenate | solution.py:79
  259.3 0.0 copy-start.1
  259.3 11.4 %gather_fusion = bf16[1024,2048]{1,0:T(8,128)(2,1)} fusion(bf16[897,2048]{1,0:T(8,128)(2,1)} %concatenate.3, s32[1024]{0:T(1024)S(1)} %broadcast_clamp_fusion), kind=kCustom, calls=%fused_computation.2 | custom fusion | bytes 8392704 | tf_op jit(solution)/shard_map/gather | solution.py:80
  270.7 3.8 %reduce_sum.25 = bf16[128,2048]{1,0:T(8,128)(2,1)} reduce(bf16[8,128,2048]{2,1,0:T(8,128)(2,1)} %bitcast.107, bf16[]{:T(256)} %constant.50.clone.1), dimensions={0}, to_apply=%region_6.7 | reduce | flops 1835008 | bytes 4718594 | tf_op jit(solution)/shard_map/reduce_sum | solution.py:81
  274.5 0.0 copy-done.1
  (7 shorter events, 0.1 us)
Async XLA Ops:
  0.0 21.2 %copy-start = (bf16[128,2048]{1,0:T(8,128)(2,1)S(1)}, bf16[128,2048]{1,0:T(8,128)(2,1)}, u32[]{:S(2)}) copy-start(bf16[128,2048]{1,0:T(8,128)(2,1)} %param.7) | copy-start | bytes 1572868
  15.7 40.6 %all-to-all-start = ((bf16[4,56,4]{1,2,0:T(4,128)(2,1)}), bf16[4,56,4]{1,2,0:T(4,128)(2,1)S(1)}, u32[]{:S(2)}, u32[]{:S(2)}) async-start(bf16[4,56,4]{1,2,0:T(4,128)(2,1)} %copy.18), calls=%async_computation | async-start | bytes 8192 | tf_op jit(solution)/shard_map/all_to_all | solution.py:75
  56.3 46.6 %all-to-all-start.2 = ((bf16[4,56,4,2048]{3,1,2,0:T(8,128)(2,1)}), bf16[4,56,4,2048]{3,1,2,0:T(8,128)(2,1)}, u32[]{:S(2)}, u32[]{:S(2)}) async-start(bf16[4,56,4,2048]{3,1,2,0:T(8,128)(2,1)} %copy.22), calls=%async_computation.2 | async-start | bytes 7340032 | tf_op jit(solution)/shard_map/all_to_all | solution.py:73
  102.9 46.1 %all-to-all-start.1 = ((bf16[4,56,4,2048]{3,1,2,0:T(8,128)(2,1)}), bf16[4,56,4,2048]{3,1,2,0:T(8,128)(2,1)}, u32[]{:S(2)}, u32[]{:S(2)}) async-start(bf16[4,56,4,2048]{3,1,2,0:T(8,128)(2,1)} %copy.20), calls=%async_computation.1 | async-start | bytes 7340032 | tf_op jit(solution)/shard_map/all_to_all | solution.py:74
  195.7 46.2 %all-to-all-start.3 = ((bf16[4,56,4,2048]{3,1,2,0:T(8,128)(2,1)}), bf16[4,56,4,2048]{3,1,2,0:T(8,128)(2,1)}, u32[]{:S(2)}, u32[]{:S(2)}) async-start(bf16[4,56,4,2048]{3,1,2,0:T(8,128)(2,1)} %copy.25), calls=%async_computation.3 | async-start | bytes 7340032 | tf_op jit(solution)/shard_map/all_to_all | solution.py:78
  259.3 15.3 %copy-start.1 = (bf16[128,2048]{1,0:T(8,128)(2,1)S(1)}, bf16[128,2048]{1,0:T(8,128)(2,1)}, u32[]{:S(2)}) copy-start(bf16[128,2048]{1,0:T(8,128)(2,1)} %param.7) | copy-start | bytes 1572868
where the time goes:
time: 280 us; the launch traced here: 275 us
  local copies, waits for them, and re-layouts  112 us (40%)
  waiting for transfers between devices  81.2 us (29%)
  matrix products  51 us (18%)
  starting transfers between devices  20 us (7%)
  other arithmetic  10.7 us (4%)
    all_to_all x1, waiting for transfers between devices, body(): lax.all_to_all(expert_out, 'expert', split_axis=0, concat_axis=0, tiled=T...  41.2 us
    all_to_all x1, waiting for transfers between devices, body(): lax.all_to_all(send_grad, 'expert', split_axis=0, concat_axis=0, tiled=True)  32.4 us
    scatter x1, local copies, waits for them, and re-layouts, body(): send_input = jnp.zeros((slot_count, features), jnp.bfloat16).at[slot_of]....  22.7 us
    scatter x1, local copies, waits for them, and re-layouts, body(): send_grad = jnp.zeros((slot_count, features), jnp.bfloat16).at[slot_of].s...  21.9 us
    dot_general x1, matrix products, expert_rows(): jnp.einsum('nmef,edf->nmed', up_grad, up_proj, preferred_element_type=jnp...  15.7 us
    dot_general x1, matrix products, expert_rows(): jnp.einsum('nmef,edf->nmed', gate_grad, gate_proj, preferred_element_type...  15.4 us
    reshape x2, local copies, waits for them, and re-layouts, body(): send_grad = send_grad.reshape(grid_shape)  12.4 us
    reshape x2, local copies, waits for them, and re-layouts, body(): send_input = send_input.reshape(grid_shape)  12.4 us
  transfers between devices with their start and end apart: 4, of which 3 were waited for; matrix products, arithmetic and copies ran while one was open for 28% of the time, Pallas kernels for 0%

commit v1 on v0

v1 whole, which is shorter than its diff:
```python
import functools

import jax
import jax.numpy as jnp
from jax import lax
from jax.experimental import pallas as pl
from jax.experimental.pallas import tpu as pltpu
from jax.sharding import PartitionSpec as P

CAP = 56
SLOT = 64
UNUSED = 200.0
MIB = 1 << 20
CHUNKS = 4

NT = (((1,), (1,)), ((), ()))
TN = (((0,), (0,)), ((), ()))


def dot(a, b, dims=(((1,), (0,)), ((), ()))):
    return lax.dot_general(a, b, dims, preferred_element_type=jnp.float32)


def params(limit):
    return pltpu.CompilerParams(vmem_limit_bytes=limit * MIB)


def whole(shape):
    return pl.BlockSpec(shape, lambda *_: (0,) * len(shape))


def rank_kernel(experts, routes_ref, gates_ref, out_ref):
    tokens, top = routes_ref.shape
    chosen = routes_ref[...].astype(jnp.float32).T
    gates = gates_ref[...].astype(jnp.float32).T
    label = lax.broadcasted_iota(jnp.int32, (experts, tokens), 0).astype(jnp.float32)
    hits = [(chosen[k : k + 1, :] == label).astype(jnp.float32) for k in range(top)]
    before = lax.broadcasted_iota(jnp.int32, (tokens, tokens), 0)
    after = lax.broadcasted_iota(jnp.int32, (tokens, tokens), 1)
    earlier = (before < after).astype(jnp.bfloat16)
    base = jnp.zeros((experts, 1), jnp.float32)
    rank = jnp.zeros((experts, tokens), jnp.float32)
    taken = jnp.zeros((experts, tokens), jnp.float32)
    gate = jnp.zeros((experts, tokens), jnp.float32)
    for k in range(top):
        inside = dot(hits[k].astype(jnp.bfloat16), earlier)
        rank += hits[k] * (inside + base)
        taken += hits[k]
        gate += hits[k] * gates[k : k + 1, :]
        base += jnp.sum(hits[k], axis=1, keepdims=True)
    rank = jnp.where((taken > 0.5) & (rank < CAP), rank, UNUSED)
    out_ref[:experts, :] = rank.astype(jnp.bfloat16)
    out_ref[experts:, :] = gate.astype(jnp.bfloat16)


def rank_table(routes, gates, experts):
    tokens = routes.shape[0]
    return pl.pallas_call(
        functools.partial(rank_kernel, experts),
        out_shape=jax.ShapeDtypeStruct((2 * experts, tokens), jnp.bfloat16),
    )(routes, gates)


def pre_kernel(axis, n, local, me_of, table_ref, x_ref, wg_ref, wu_ref, a_ref, b_ref, pick_ref, xs, gcol):
    experts = n * local
    tokens = x_ref.shape[1]

    @pl.when((pl.program_id(0) == 0) & (pl.program_id(1) == 0))
    def _():
        me = lax.axis_index(axis)
        row = lax.broadcasted_iota(jnp.int32, (2 * experts, tokens), 0)
        slot = lax.broadcasted_iota(jnp.int32, (SLOT, tokens), 0).astype(jnp.float32)
        for g in range(n):
            table = table_ref[g].astype(jnp.float32)
            picks = []
            for j in range(local):
                e = me * local + j
                rank = jnp.sum(jnp.where(row == e, table, 0.0), axis=0, keepdims=True)
                gate = jnp.sum(jnp.where(row == e + experts, table, 0.0), axis=0, keepdims=True)
                pick = (slot == rank).astype(jnp.float32)
                gcol[j, g * SLOT : (g + 1) * SLOT, :] = jnp.sum(pick * gate, axis=1, keepdims=True)
                picks.append(pick.astype(jnp.bfloat16))
            pick = jnp.concatenate(picks, axis=0)
            pick_ref[g] = pick
            rows = dot(pick, x_ref[g]).astype(jnp.bfloat16)
            for j in range(local):
                xs[j, g * SLOT : (g + 1) * SLOT, :] = rows[j * SLOT : (j + 1) * SLOT, :]

    e = pl.program_id(0)
    gate_pre = dot(xs[e], wg_ref[0])
    up_pre = dot(xs[e], wu_ref[0])
    sig = jax.nn.sigmoid(gate_pre)
    weighted = gcol[e] * sig
    a_ref[0] = weighted * up_pre * (1.0 + gate_pre * (1.0 - sig))
    b_ref[0] = weighted * gate_pre


def pre(axis, n, table, x_all, wg, wu):
    local, features, hidden = wg.shape
    tokens = x_all.shape[1]
    rows = n * SLOT
    cols = hidden // 2
    weight = pl.BlockSpec((1, features, cols), lambda e, f: (e, 0, f))
    result = pl.BlockSpec((1, rows, cols), lambda e, f: (e, 0, f))
    return pl.pallas_call(
        functools.partial(pre_kernel, axis, n, local, None),
        grid=(local, hidden // cols),
        in_specs=[whole(table.shape), whole(x_all.shape), weight, weight],
        out_specs=[result, result, whole((n, local * SLOT, tokens))],
        out_shape=[
            jax.ShapeDtypeStruct((local, rows, hidden), jnp.float32),
            jax.ShapeDtypeStruct((local, rows, hidden), jnp.float32),
            jax.ShapeDtypeStruct((n, local * SLOT, tokens), jnp.bfloat16),
        ],
        scratch_shapes=[
            pltpu.VMEM((local, rows, features), jnp.bfloat16),
            pltpu.VMEM((local, rows, 1), jnp.float32),
        ],
        compiler_params=params(48),
        cost_estimate=pl.CostEstimate(
            flops=4 * local * rows * features * hidden,
            bytes_accessed=4 * local * features * hidden + 8 * local * rows * hidden,
            transcendentals=local * rows * hidden,
        ),
    )(table, x_all, wg, wu)


def back_kernel(n, local, pick_ref, g_ref, wd_ref, a_ref, b_ref, hg_ref, hu_ref, gs):
    @pl.when((pl.program_id(0) == 0) & (pl.program_id(1) == 0))
    def _():
        for g in range(n):
            rows = dot(pick_ref[g], g_ref[g]).astype(jnp.bfloat16)
            for j in range(local):
                gs[j, g * SLOT : (g + 1) * SLOT, :] = rows[j * SLOT : (j + 1) * SLOT, :]

    back = dot(gs[pl.program_id(0)], wd_ref[0], NT)
    hg_ref[0] = (back * a_ref[0]).astype(jnp.bfloat16)
    hu_ref[0] = (back * b_ref[0]).astype(jnp.bfloat16)


def back(n, pick, g_all, wd, a, b):
    local, hidden, features = wd.shape
    rows = n * SLOT
    cols = hidden // 2
    block = pl.BlockSpec((1, rows, cols), lambda e, f: (e, 0, f))
    shape = jax.ShapeDtypeStruct((local, rows, hidden), jnp.bfloat16)
    return pl.pallas_call(
        functools.partial(back_kernel, n, local),
        grid=(local, hidden // cols),
        in_specs=[
            whole(pick.shape),
            whole(g_all.shape),
            pl.BlockSpec((1, cols, features), lambda e, f: (e, f, 0)),
            block,
            block,
        ],
        out_specs=[block, block],
        out_shape=[shape, shape],
        scratch_shapes=[pltpu.VMEM((local, rows, features), jnp.bfloat16)],
        compiler_params=params(40),
        cost_estimate=pl.CostEstimate(
            flops=2 * local * rows * features * hidden,
            bytes_accessed=2 * local * features * hidden + 12 * local * rows * hidden,
            transcendentals=0,
        ),
    )(pick, g_all, wd, a, b)


def out_kernel(axis, n, local, orders, pick_ref, hg_ref, hu_ref, wg_ref, wu_ref, *rest):
    outs, rows_ref = rest[:-1], rest[-1]
    e = pl.program_id(0)
    rows = (dot(hg_ref[0], wg_ref[0], NT) + dot(hu_ref[0], wu_ref[0], NT)).astype(jnp.bfloat16)
    for g in range(n):
        rows_ref[g, e] = rows[g * SLOT : (g + 1) * SLOT, :]

    @pl.when(e == local - 1)
    def _():
        me = lax.axis_index(axis)
        for out_ref, order in zip(outs, orders):
            for i, k in enumerate(order):
                g = lax.bitwise_xor(me, k)
                part = rows_ref[g].reshape(local * SLOT, -1)
                out_ref[i] = dot(pick_ref[g], part, TN).astype(out_ref.dtype)


def partial_sums(axis, n, orders, chunk, pick, hg, hu, wg, wu):
    local, features, hidden = wg.shape
    tokens = pick.shape[2]
    rows = n * SLOT
    cols = features // CHUNKS
    act = pl.BlockSpec((1, rows, hidden), lambda e: (e, 0, 0))
    weight = pl.BlockSpec((1, cols, hidden), lambda e: (e, chunk, 0))
    shapes = [(len(order), tokens, cols) for order in orders]
    types = [jnp.float32] + [jnp.bfloat16] * (len(orders) - 1)
    return pl.pallas_call(
        functools.partial(out_kernel, axis, n, local, orders),
        grid=(local,),
        in_specs=[whole(pick.shape), act, act, weight, weight],
        out_specs=[whole(s) for s in shapes],
        out_shape=[jax.ShapeDtypeStruct(s, t) for s, t in zip(shapes, types)],
        scratch_shapes=[pltpu.VMEM((n, local, SLOT, cols), jnp.bfloat16)],
        compiler_params=params(32),
        cost_estimate=pl.CostEstimate(
            flops=4 * local * rows * cols * hidden,
            bytes_accessed=4 * local * (cols + rows) * hidden,
            transcendentals=0,
        ),
    )(pick, hg, hu, wg, wu)


def sum_kernel(*refs):
    parts, out_ref = refs[:-1], refs[-1]
    each = len(parts) // CHUNKS
    cols = out_ref.shape[1] // CHUNKS
    for c in range(CHUNKS):
        own, *others = parts[c * each : (c + 1) * each]
        total = own[0]
        for other in others:
            total += other[0].astype(jnp.float32)
        out_ref[:, c * cols : (c + 1) * cols] = total.astype(jnp.bfloat16)


def body(axis, saved_input, grad_out, routes, route_gates, gate_proj, up_proj, down_proj):
    n = lax.axis_size(axis)
    local = gate_proj.shape[0]
    experts = n * local
    tokens, features = saved_input.shape

    def swap(array, k):
        return lax.ppermute(array, axis, [(i, i ^ k) for i in range(n)])

    table = lax.all_gather(rank_table(routes, route_gates, experts), axis)
    x_all = lax.all_gather(saved_input, axis)
    g_all = lax.all_gather(grad_out, axis)
    a, b, pick = pre(axis, n, table, x_all, gate_proj, up_proj)
    hg, hu = back(n, pick, g_all, down_proj, a, b)
    parts = []
    for chunk in range(CHUNKS):
        if n == 4:
            near, far = (1, 2) if chunk % 2 == 0 else (2, 1)
            orders = ((0,), (near, 3), (far,))
            own, two, one = partial_sums(axis, n, orders, chunk, pick, hg, hu, gate_proj, up_proj)
            two = swap(two, near)
            relay = (two[1:2].astype(jnp.float32) + one.astype(jnp.float32)).astype(jnp.bfloat16)
            parts += [own, two[:1], swap(relay, far)]
        else:
            orders = tuple((k,) for k in range(n))
            own, *others = partial_sums(axis, n, orders, chunk, pick, hg, hu, gate_proj, up_proj)
            parts += [own] + [swap(other, k + 1) for k, other in enumerate(others)]
    return pl.pallas_call(
        sum_kernel,
        out_shape=jax.ShapeDtypeStruct((tokens, features), jnp.bfloat16),
        compiler_params=params(48),
    )(*parts)


def solution(mesh):
    tokens = P(("dp", "expert"), None)
    weights = P("expert", None, None)
    return jax.shard_map(
        functools.partial(body, "expert"),
        mesh=mesh,
        in_specs=(tokens, tokens, tokens, tokens, weights, weights, weights),
        out_specs=tokens,
        check_vma=False,
    )
```

time: 280 us -> 148 us (0.53); the launches traced: 275 us -> 147 us
  local copies, waits for them, and re-layouts: 112 us -> 12.5 us
  matrix products: 51 us -> 0 us
  Pallas kernels: 0 us -> 48.9 us
  waiting for transfers between devices: 81.2 us -> 54.2 us
  between operations: 0.36 us -> 13.5 us
  starting transfers between devices: 20 us -> 8.45 us
  other arithmetic: 10.7 us -> 0.13 us
  blocking collectives: 0 us -> 9.77 us
    all_to_all x4 -> x0, waiting for transfers between devices: 81.2 us -> none  [the longest x1 41.2 us: body(): lax.all_to_all(expert_out, 'expert', split_axis=0, concat_axis=0, tiled=T...]
    scatter x3 -> x0, local copies, waits for them, and re-layouts: 52.3 us -> none  [the longest x1 22.7 us: body(): send_input = jnp.zeros((slot_count, features), jnp.bfloat16).at[slot_of]....]
    dot_general x4 -> x0, matrix products: 51 us -> none  [the longest x1 15.7 us: expert_rows(): jnp.einsum('nmef,edf->nmed', up_grad, up_proj, preferred_element_type=jnp...]
    pallas_call x0 -> x8, Pallas kernels: none -> 48.9 us  [the longest x4 18 us: partial_sums(): pl.pallas_call(functools.partial(out_kernel, axis, n, local, orders), gri...]
    all_gather x0 -> x2, waiting for transfers between devices: none -> 43.5 us  [the longest x1 25 us: body(): x_all = lax.all_gather(saved_input, axis)]
    reshape x7 -> x0, local copies, waits for them, and re-layouts: 32 us -> none  [the longest x2 12.4 us: body(): send_grad = send_grad.reshape(grid_shape)]
    all_to_all x4 -> x0, starting transfers between devices: 20 us -> none  [the longest x1 5.38 us: body(): lax.all_to_all(send_gate, 'expert', split_axis=0, concat_axis=0, tiled=True)]
    unnamed x4 -> x10, local copies, waits for them, and re-layouts: 0.01 us -> 12.4 us
  transfers between devices with their start and end apart: 4 -> 10, of which waited for: 3 -> 7; matrix products, arithmetic and copies ran while one was open for 28% -> 2% of each run, Pallas kernels for 0% -> 19%
where the time goes in v1:
time: 148 us; the launch traced here: 147 us
  waiting for transfers between devices  54.2 us (37%)
  Pallas kernels  48.9 us (33%)
  between operations  13.5 us (9%)
  local copies, waits for them, and re-layouts  12.5 us (8%)
  blocking collectives  9.77 us (7%)
  starting transfers between devices  8.45 us (6%)
    all_gather x1, waiting for transfers between devices, body(): x_all = lax.all_gather(saved_input, axis)  25 us
    all_gather x1, waiting for transfers between devices, body(): g_all = lax.all_gather(grad_out, axis)  18.5 us
    pallas_call x4, Pallas kernels, partial_sums(): pl.pallas_call(functools.partial(out_kernel, axis, n, local, orders), gri...  18 us
    pallas_call x1, Pallas kernels, pre(): pl.pallas_call(functools.partial(pre_kernel, axis, n, local, None), grid=...  17.1 us
    unnamed x10, local copies, waits for them, and re-layouts  12.4 us
    pallas_call x1, Pallas kernels, back(): pl.pallas_call(functools.partial(back_kernel, n, local), grid=(local, hid...  11.2 us
    all_gather x1, blocking collectives, body(): table = lax.all_gather(rank_table(routes, route_gates, experts), axis)  9.77 us
    ppermute x8, waiting for transfers between devices, swap(): return lax.ppermute(array, axis, [(i, i ^ k) for i in range(n)])  9.29 us
  transfers between devices with their start and end apart: 10, of which 7 were waited for; matrix products, arithmetic and copies ran while one was open for 2% of the time, Pallas kernels for 19%

profile of v1, /device:TPU:0, one launch (start us, length us, event | category | flops | bytes accessed | tf_op | source)
XLA Modules:
  0.0 147.5 jit_solution(13307749470102207793)
XLA Ops:
  6.5 0.0 all-gather.6.cloned.1.call-start
  6.5 0.7 all-gather.6.cloned.1.call-update
  7.3 0.0 all-gather.8.cloned.1.call-start
  7.3 0.7 all-gather.8.cloned.1.call-update
  8.0 1.4 copy.9.gates_ref
  9.4 1.4 copy.8.routes_ref
  10.8 1.7 %shard_map.73 = bf16[32,128]{1,0:T(8,128)(2,1)} custom-call(s32[128,8]{1,0:T(8,128)} %copy.8.routes_ref, bf16[128,8]{1,0:T(8,128)(2,1)} %copy.9.gates_ref), custom_call_target="tpu_custom_call" | custom-call | tf_op jit(solution)/shard_map/pallas_call | solution.py:58
  12.5 9.8 %all-gather = bf16[128,128]{1,0:T(8,128)(2,1)S(1)} all-gather(bf16[32,128]{1,0:T(8,128)(2,1)} %shard_map.73), channel_id=2, replica_groups=mesh['dp'=8,'expert'=4] {'expert'}, dimensions={0}, use_global_device_ids=true | all-gather | bytes 40960 | tf_op jit(solution)/shard_map/all_gather | solution.py:232
  22.2 25.0 %all-gather.6.cloned.1.call-done = bf16[512,2048]{1,0:T(8,128)(2,1)} async-done(((bf16[128,2048]{1,0:T(8,128)(2,1)}), bf16[512,2048]{1,0:T(8,128)(2,1)}) %all-gather.6.cloned.1.call-update) | async-done | bytes 2097168 | tf_op jit(solution)/shard_map/all_gather | solution.py:233
  47.3 0.0 copy-start.3
  47.3 1.6 %copy-done.3 = bf16[512,2048]{1,0:T(8,128)(2,1)S(1)} copy-done((bf16[512,2048]{1,0:T(8,128)(2,1)S(1)}, bf16[512,2048]{1,0:T(8,128)(2,1)}, u32[]{:S(2)}) %copy-start.3) | copy-done | bytes 2097176
  48.9 17.1 %shard_map.74 = (f32[4,256,768]{2,1,0:T(8,128)S(1)}, f32[4,256,768]{2,1,0:T(8,128)}, bf16[4,256,128]{2,1,0:T(8,128)(2,1)S(1)}) custom-call(bf16[4,32,128]{2,1,0:T(8,128)(2,1)S(1)} %bitcast.5, bf16[4,128,2048]{2,1,0:T(8,128)(2,1)S(1)} %bitcast.4, bf16[4,2048,768]{2,1,0:T(8,128)(2,1)} %wg_ref.9, bf16[4,2048,768]{2,1,0:T(8,128)(2,1)} %wu_ref.9), custom_call_target="tpu_custom_call" | custom-call | flops 6442450944 | bytes 31457280 | tf_op jit(solution)/shard_map/pallas_call | solution.py:105
  65.9 18.5 %all-gather.8.cloned.1.call-done = bf16[512,2048]{1,0:T(8,128)(2,1)} async-done(((bf16[128,2048]{1,0:T(8,128)(2,1)}), bf16[512,2048]{1,0:T(8,128)(2,1)}) %all-gather.8.cloned.1.call-update) | async-done | bytes 2097168 | tf_op jit(solution)/shard_map/all_gather | solution.py:234
  84.4 0.0 copy-start.1
  84.4 1.9 %copy-done.1 = f32[4,256,768]{2,1,0:T(8,128)S(1)} copy-done((f32[4,256,768]{2,1,0:T(8,128)S(1)}, f32[4,256,768]{2,1,0:T(8,128)}, u32[]{:S(2)}) %copy-start.1) | copy-done | bytes 3145752
  86.3 0.0 copy-start.2
  86.3 1.6 %copy-done.2 = bf16[512,2048]{1,0:T(8,128)(2,1)S(1)} copy-done((bf16[512,2048]{1,0:T(8,128)(2,1)S(1)}, bf16[512,2048]{1,0:T(8,128)(2,1)}, u32[]{:S(2)}) %copy-start.2) | copy-done | bytes 2097176
  87.9 11.2 %shard_map.75 = (bf16[4,256,768]{2,1,0:T(8,128)(2,1)S(1)}, bf16[4,256,768]{2,1,0:T(8,128)(2,1)S(1)}) custom-call(bf16[4,256,128]{2,1,0:T(8,128)(2,1)S(1)} %get-tuple-element.22.pick_ref, bf16[4,128,2048]{2,1,0:T(8,128)(2,1)S(1)} %bitcast.3, bf16[4,768,2048]{2,1,0:T(8,128)(2,1)} %wd_ref.1, f32[4,256,768]{2,1,0:T(8,128)S(1)} %get-tuple-element.23.a_ref, ...), custom_call_target="tpu_custom_call" | custom-call | flops 3221225472 | bytes 22020096 | tf_op jit(solution)/shard_map/pallas_call | solution.py:147
  99.1 0.0 copy-start
  99.1 4.6 %copy-done = bf16[4,2048,768]{2,1,0:T(8,128)(2,1)S(1)} copy-done((bf16[4,2048,768]{2,1,0:T(8,128)(2,1)S(1)}, bf16[4,2048,768]{2,1,0:T(8,128)(2,1)}, u32[]{:S(2)}) %copy-start) | copy-done | bytes 12582936
  103.7 4.5 %shard_map.79 = (f32[1,128,512]{2,1,0:T(8,128)S(1)}, bf16[2,128,512]{2,1,0:T(8,128)(2,1)S(1)}, bf16[1,128,512]{2,1,0:T(8,128)(2,1)S(1)}) custom-call(bf16[4,256,128]{2,1,0:T(8,128)(2,1)S(1)} %get-tuple-element.22.pick_ref, bf16[4,256,768]{2,1,0:T(8,128)(2,1)S(1)} %get-tuple-element.25.hg_ref, bf16[4,256,768]{2,1,0:T(8,128)(2,1)S(1)} %get-tuple-element.26.hu_ref, ...), custom_call_target="tpu_custom_call" | custom-call | flops 1610612736 | bytes 9437184 | tf_op jit(solution)/shard_map/pallas_call | solution.py:195
  108.2 4.5 %shard_map.78 = (f32[1,128,512]{2,1,0:T(8,128)S(1)}, bf16[2,128,512]{2,1,0:T(8,128)(2,1)S(1)}, bf16[1,128,512]{2,1,0:T(8,128)(2,1)S(1)}) custom-call(bf16[4,256,128]{2,1,0:T(8,128)(2,1)S(1)} %get-tuple-element.22.pick_ref, bf16[4,256,768]{2,1,0:T(8,128)(2,1)S(1)} %get-tuple-element.25.hg_ref, bf16[4,256,768]{2,1,0:T(8,128)(2,1)S(1)} %get-tuple-element.26.hu_ref, ...), custom_call_target="tpu_custom_call" | custom-call | flops 1610612736 | bytes 9437184 | tf_op jit(solution)/shard_map/pallas_call | solution.py:195
  112.7 1.5 %collective-permute-start.6 = (bf16[2,128,512]{2,1,0:T(8,128)(2,1)S(1)}, bf16[2,128,512]{2,1,0:T(8,128)(2,1)S(1)}, u32[]{:S(2)}, u32[]{:S(2)}) collective-permute-start(bf16[2,128,512]{2,1,0:T(8,128)(2,1)S(1)} %get-tuple-element.37), channel_id=1, source_target_pairs={{0,2},{1,3},{2,0},{3,1},{4,6},{5,7},{6,4},{7,5},{8,10},{9,11},{10,... | collective-permute-start | bytes 786440 | tf_op jit(solution)/shard_map/ppermute | solution.py:230
  114.3 0.6 collective-permute-start.4
  114.8 4.5 %shard_map.77 = (f32[1,128,512]{2,1,0:T(8,128)S(1)}, bf16[2,128,512]{2,1,0:T(8,128)(2,1)S(1)}, bf16[1,128,512]{2,1,0:T(8,128)(2,1)S(1)}) custom-call(bf16[4,256,128]{2,1,0:T(8,128)(2,1)S(1)} %get-tuple-element.22.pick_ref, bf16[4,256,768]{2,1,0:T(8,128)(2,1)S(1)} %get-tuple-element.25.hg_ref, bf16[4,256,768]{2,1,0:T(8,128)(2,1)S(1)} %get-tuple-element.26.hu_ref, ...), custom_call_target="tpu_custom_call" | custom-call | flops 1610612736 | bytes 9437184 | tf_op jit(solution)/shard_map/pallas_call | solution.py:195
  119.3 4.5 %shard_map.76 = (f32[1,128,512]{2,1,0:T(8,128)S(1)}, bf16[2,128,512]{2,1,0:T(8,128)(2,1)S(1)}, bf16[1,128,512]{2,1,0:T(8,128)(2,1)S(1)}) custom-call(bf16[4,256,128]{2,1,0:T(8,128)(2,1)S(1)} %get-tuple-element.22.pick_ref, bf16[4,256,768]{2,1,0:T(8,128)(2,1)S(1)} %get-tuple-element.25.hg_ref, bf16[4,256,768]{2,1,0:T(8,128)(2,1)S(1)} %get-tuple-element.26.hu_ref, ...), custom_call_target="tpu_custom_call" | custom-call | flops 1610612736 | bytes 9437184 | tf_op jit(solution)/shard_map/pallas_call | solution.py:195
  123.9 1.5 %collective-permute-start.2 = (bf16[2,128,512]{2,1,0:T(8,128)(2,1)S(1)}, bf16[2,128,512]{2,1,0:T(8,128)(2,1)S(1)}, u32[]{:S(2)}, u32[]{:S(2)}) collective-permute-start(bf16[2,128,512]{2,1,0:T(8,128)(2,1)S(1)} %get-tuple-element.31), channel_id=1, source_target_pairs={{0,2},{1,3},{2,0},{3,1},{4,6},{5,7},{6,4},{7,5},{8,10},{9,11},{10,... | collective-permute-start | bytes 786440 | tf_op jit(solution)/shard_map/ppermute | solution.py:230
  125.4 0.6 collective-permute-start
  125.9 0.0 collective-permute-done.6
  126.0 1.5 %collective-permute-start.7 = (bf16[1,128,512]{2,1,0:T(8,128)(2,1)S(1)}, bf16[1,128,512]{2,1,0:T(8,128)(2,1)S(1)}, u32[]{:S(2)}, u32[]{:S(2)}) collective-permute-start(bf16[1,128,512]{2,1,0:T(8,128)(2,1)S(1)} %add_convert_fusion), channel_id=1, source_target_pairs={{0,1},{1,0},{2,3},{3,2},{4,5},{5,4},{6,7},{7,6},{8,9},{9,8},{10,11... | collective-permute-start | bytes 393224 | tf_op jit(solution)/shard_map/ppermute | solution.py:230
  127.5 0.0 collective-permute-done.4
  127.5 0.6 collective-permute-start.5
  128.2 4.6 %collective-permute-done.2 = bf16[2,128,512]{2,1,0:T(8,128)(2,1)S(1)} collective-permute-done((bf16[2,128,512]{2,1,0:T(8,128)(2,1)S(1)}, bf16[2,128,512]{2,1,0:T(8,128)(2,1)S(1)}, u32[]{:S(2)}, u32[]{:S(2)}) %collective-permute-start.2) | collective-permute-done | bytes 262176 | tf_op jit(solution)/shard_map/ppermute | solution.py:230
  132.8 1.5 %collective-permute-start.3 = (bf16[1,128,512]{2,1,0:T(8,128)(2,1)S(1)}, bf16[1,128,512]{2,1,0:T(8,128)(2,1)S(1)}, u32[]{:S(2)}, u32[]{:S(2)}) collective-permute-start(bf16[1,128,512]{2,1,0:T(8,128)(2,1)S(1)} %add_convert_fusion.2), channel_id=1, source_target_pairs={{0,1},{1,0},{2,3},{3,2},{4,5},{5,4},{6,7},{7,6},{8,9},{9,8},{10,11... | collective-permute-start | bytes 393224 | tf_op jit(solution)/shard_map/ppermute | solution.py:230
  134.4 0.3 collective-permute-done
  134.7 0.6 collective-permute-start.1
  135.3 1.5 %collective-permute-done.7.refs_11_ = bf16[1,128,512]{2,1,0:T(8,128)(2,1)S(1)} collective-permute-done((bf16[1,128,512]{2,1,0:T(8,128)(2,1)S(1)}, bf16[1,128,512]{2,1,0:T(8,128)(2,1)S(1)}, u32[]{:S(2)}, u32[]{:S(2)}) %collective-permute-start.7) | collective-permute-done | bytes 131104 | tf_op jit(solution)/shard_map/ppermute | solution.py:230
  136.8 0.0 collective-permute-done.5.refs_8_
  136.8 1.4 collective-permute-done.3.refs_5_
  138.2 1.5 %collective-permute-done.1.refs_2_ = bf16[1,128,512]{2,1,0:T(8,128)(2,1)S(1)} collective-permute-done((bf16[1,128,512]{2,1,0:T(8,128)(2,1)S(1)}, bf16[1,128,512]{2,1,0:T(8,128)(2,1)S(1)}, u32[]{:S(2)}, u32[]{:S(2)}) %collective-permute-start.1) | collective-permute-done | bytes 131104 | tf_op jit(solution)/shard_map/ppermute | solution.py:230
  139.7 0.9 shard_map.80
  (8 shorter events, 0.2 us)
Async XLA Ops:
  6.5 40.7 %all-gather.6.cloned.1.call-start = ((), (), s32[]{:S(2)}) async-start(), calls=%async_computation | async-start | bytes 2621440 | tf_op jit(solution)/shard_map/all_gather | solution.py:233
  7.3 77.2 %all-gather.8.cloned.1.call-start = ((), (), s32[]{:S(2)}) async-start(), calls=%async_computation.1 | async-start | bytes 2621440 | tf_op jit(solution)/shard_map/all_gather | solution.py:234
  47.3 1.6 %copy-start.3 = (bf16[512,2048]{1,0:T(8,128)(2,1)S(1)}, bf16[512,2048]{1,0:T(8,128)(2,1)}, u32[]{:S(2)}) copy-start(bf16[512,2048]{1,0:T(8,128)(2,1)} %all-gather.6.cloned.1.call-done) | copy-start | bytes 6291460
  84.4 1.9 %copy-start.1 = (f32[4,256,768]{2,1,0:T(8,128)S(1)}, f32[4,256,768]{2,1,0:T(8,128)}, u32[]{:S(2)}) copy-start(f32[4,256,768]{2,1,0:T(8,128)} %get-tuple-element.24.b_ref) | copy-start | bytes 9437188
  86.3 1.6 %copy-start.2 = (bf16[512,2048]{1,0:T(8,128)(2,1)S(1)}, bf16[512,2048]{1,0:T(8,128)(2,1)}, u32[]{:S(2)}) copy-start(bf16[512,2048]{1,0:T(8,128)(2,1)} %all-gather.8.cloned.1.call-done) | copy-start | bytes 6291460
  99.1 4.6 %copy-start = (bf16[4,2048,768]{2,1,0:T(8,128)(2,1)S(1)}, bf16[4,2048,768]{2,1,0:T(8,128)(2,1)}, u32[]{:S(2)}) copy-start(bf16[4,2048,768]{2,1,0:T(8,128)(2,1)} %wg_ref.9) | copy-start | bytes 37748740
  112.7 13.2 %collective-permute-start.6 = (bf16[2,128,512]{2,1,0:T(8,128)(2,1)S(1)}, bf16[2,128,512]{2,1,0:T(8,128)(2,1)S(1)}, u32[]{:S(2)}, u32[]{:S(2)}) collective-permute-start(bf16[2,128,512]{2,1,0:T(8,128)(2,1)S(1)} %get-tuple-element.37), channel_id=1, source_target_pairs={{0,2},{1,3},{2,0},{3,1},{4,6},{5,7},{6,4},{7,5},{8,10},{9,11},{10,... | collective-permute-start | bytes 786440 | tf_op jit(solution)/shard_map/ppermute | solution.py:230
  114.3 13.3 %collective-permute-start.4 = (bf16[2,128,512]{2,1,0:T(8,128)(2,1)S(1)}, bf16[2,128,512]{2,1,0:T(8,128)(2,1)S(1)}, u32[]{:S(2)}, u32[]{:S(2)}) collective-permute-start(bf16[2,128,512]{2,1,0:T(8,128)(2,1)S(1)} %get-tuple-element.34), channel_id=1, source_target_pairs={{0,1},{1,0},{2,3},{3,2},{4,5},{5,4},{6,7},{7,6},{8,9},{9,8},{10,11... | collective-permute-start | bytes 786440 | tf_op jit(solution)/shard_map/ppermute | solution.py:230
  123.9 8.9 %collective-permute-start.2 = (bf16[2,128,512]{2,1,0:T(8,128)(2,1)S(1)}, bf16[2,128,512]{2,1,0:T(8,128)(2,1)S(1)}, u32[]{:S(2)}, u32[]{:S(2)}) collective-permute-start(bf16[2,128,512]{2,1,0:T(8,128)(2,1)S(1)} %get-tuple-element.31), channel_id=1, source_target_pairs={{0,2},{1,3},{2,0},{3,1},{4,6},{5,7},{6,4},{7,5},{8,10},{9,11},{10,... | collective-permute-start | bytes 786440 | tf_op jit(solution)/shard_map/ppermute | solution.py:230
  125.4 9.2 %collective-permute-start = (bf16[2,128,512]{2,1,0:T(8,128)(2,1)S(1)}, bf16[2,128,512]{2,1,0:T(8,128)(2,1)S(1)}, u32[]{:S(2)}, u32[]{:S(2)}) collective-permute-start(bf16[2,128,512]{2,1,0:T(8,128)(2,1)S(1)} %get-tuple-element.28), channel_id=1, source_target_pairs={{0,1},{1,0},{2,3},{3,2},{4,5},{5,4},{6,7},{7,6},{8,9},{9,8},{10,11... | collective-permute-start | bytes 786440 | tf_op jit(solution)/shard_map/ppermute | solution.py:230
  126.0 10.8 %collective-permute-start.7 = (bf16[1,128,512]{2,1,0:T(8,128)(2,1)S(1)}, bf16[1,128,512]{2,1,0:T(8,128)(2,1)S(1)}, u32[]{:S(2)}, u32[]{:S(2)}) collective-permute-start(bf16[1,128,512]{2,1,0:T(8,128)(2,1)S(1)} %add_convert_fusion), channel_id=1, source_target_pairs={{0,1},{1,0},{2,3},{3,2},{4,5},{5,4},{6,7},{7,6},{8,9},{9,8},{10,11... | collective-permute-start | bytes 393224 | tf_op jit(solution)/shard_map/ppermute | solution.py:230
  127.5 9.3 %collective-permute-start.5 = (bf16[1,128,512]{2,1,0:T(8,128)(2,1)S(1)}, bf16[1,128,512]{2,1,0:T(8,128)(2,1)S(1)}, u32[]{:S(2)}, u32[]{:S(2)}) collective-permute-start(bf16[1,128,512]{2,1,0:T(8,128)(2,1)S(1)} %add_convert_fusion.1), channel_id=1, source_target_pairs={{0,2},{1,3},{2,0},{3,1},{4,6},{5,7},{6,4},{7,5},{8,10},{9,11},{10,... | collective-permute-start | bytes 393224 | tf_op jit(solution)/shard_map/ppermute | solution.py:230
  132.8 5.4 %collective-permute-start.3 = (bf16[1,128,512]{2,1,0:T(8,128)(2,1)S(1)}, bf16[1,128,512]{2,1,0:T(8,128)(2,1)S(1)}, u32[]{:S(2)}, u32[]{:S(2)}) collective-permute-start(bf16[1,128,512]{2,1,0:T(8,128)(2,1)S(1)} %add_convert_fusion.2), channel_id=1, source_target_pairs={{0,1},{1,0},{2,3},{3,2},{4,5},{5,4},{6,7},{7,6},{8,9},{9,8},{10,11... | collective-permute-start | bytes 393224 | tf_op jit(solution)/shard_map/ppermute | solution.py:230
  134.7 5.0 %collective-permute-start.1 = (bf16[1,128,512]{2,1,0:T(8,128)(2,1)S(1)}, bf16[1,128,512]{2,1,0:T(8,128)(2,1)S(1)}, u32[]{:S(2)}, u32[]{:S(2)}) collective-permute-start(bf16[1,128,512]{2,1,0:T(8,128)(2,1)S(1)} %add_convert_fusion.3), channel_id=1, source_target_pairs={{0,2},{1,3},{2,0},{3,1},{4,6},{5,7},{6,4},{7,5},{8,10},{9,11},{10,... | collective-permute-start | bytes 393224 | tf_op jit(solution)/shard_map/ppermute | solution.py:230
Sparse Core Ops, SparseCore 0:
  9.2 38.0 all-gather.5
  49.1 35.2 all-gather.7

commit v2 on v1

--- a/solution.py
+++ b/solution.py
@@ -30,9 +30,9 @@
 
 
 def rank_kernel(experts, routes_ref, gates_ref, out_ref):
-    tokens, top = routes_ref.shape
-    chosen = routes_ref[...].astype(jnp.float32).T
-    gates = gates_ref[...].astype(jnp.float32).T
+    top, tokens = routes_ref.shape
+    chosen = routes_ref[...].astype(jnp.float32)
+    gates = gates_ref[...].astype(jnp.float32)
     label = lax.broadcasted_iota(jnp.int32, (experts, tokens), 0).astype(jnp.float32)
     hits = [(chosen[k : k + 1, :] == label).astype(jnp.float32) for k in range(top)]
     before = lax.broadcasted_iota(jnp.int32, (tokens, tokens), 0)
@@ -54,24 +54,35 @@
 
 
 def rank_table(routes, gates, experts):
-    tokens = routes.shape[0]
+    tokens = routes.shape[1]
     return pl.pallas_call(
         functools.partial(rank_kernel, experts),
         out_shape=jax.ShapeDtypeStruct((2 * experts, tokens), jnp.bfloat16),
     )(routes, gates)
 
 
-def pre_kernel(axis, n, local, me_of, table_ref, x_ref, wg_ref, wu_ref, a_ref, b_ref, pick_ref, xs, gcol):
+def gather_rows(pick, refs, first, count, out, group, local):
+    blocks = [refs[first + i][...] for i in range(count)]
+    tokens = blocks[0] if count == 1 else jnp.concatenate(blocks, axis=0)
+    rows = dot(pick, tokens).astype(jnp.bfloat16)
+    for j in range(local):
+        out[j, group * SLOT : (group + 1) * SLOT, :] = rows[j * SLOT : (j + 1) * SLOT, :]
+
+
+def pre_kernel(axis, n, local, counts, *refs):
+    table_refs, token_refs = refs[:n], refs[n : n + sum(counts)]
+    wg_ref, wu_ref, a_ref, b_ref, pick_ref, xs, gcol = refs[n + sum(counts) :]
     experts = n * local
-    tokens = x_ref.shape[1]
+    tokens = table_refs[0].shape[1]
 
     @pl.when((pl.program_id(0) == 0) & (pl.program_id(1) == 0))
     def _():
         me = lax.axis_index(axis)
         row = lax.broadcasted_iota(jnp.int32, (2 * experts, tokens), 0)
         slot = lax.broadcasted_iota(jnp.int32, (SLOT, tokens), 0).astype(jnp.float32)
+        first = 0
         for g in range(n):
-            table = table_ref[g].astype(jnp.float32)
+            table = table_refs[g][...].astype(jnp.float32)
             picks = []
             for j in range(local):
                 e = me * local + j
@@ -82,9 +93,8 @@
                 picks.append(pick.astype(jnp.bfloat16))
             pick = jnp.concatenate(picks, axis=0)
             pick_ref[g] = pick
-            rows = dot(pick, x_ref[g]).astype(jnp.bfloat16)
-            for j in range(local):
-                xs[j, g * SLOT : (g + 1) * SLOT, :] = rows[j * SLOT : (j + 1) * SLOT, :]
+            gather_rows(pick, token_refs, first, counts[g], xs, g, local)
+            first += counts[g]
 
     e = pl.program_id(0)
     gate_pre = dot(xs[e], wg_ref[0])
@@ -95,22 +105,24 @@
     b_ref[0] = weighted * gate_pre
 
 
-def pre(axis, n, table, x_all, wg, wu):
+def pre(axis, n, tables, tokens, wg, wu):
     local, features, hidden = wg.shape
-    tokens = x_all.shape[1]
     rows = n * SLOT
     cols = hidden // 2
+    counts = [len(t) for t in tokens]
+    blocks = [block for t in tokens for block in t]
     weight = pl.BlockSpec((1, features, cols), lambda e, f: (e, 0, f))
     result = pl.BlockSpec((1, rows, cols), lambda e, f: (e, 0, f))
-    return pl.pallas_call(
-        functools.partial(pre_kernel, axis, n, local, None),
+    picks = (n, local * SLOT, tables[0].shape[1])
+    return pl.pallas_call(
+        functools.partial(pre_kernel, axis, n, local, counts),
         grid=(local, hidden // cols),
-        in_specs=[whole(table.shape), whole(x_all.shape), weight, weight],
-        out_specs=[result, result, whole((n, local * SLOT, tokens))],
+        in_specs=[whole(t.shape) for t in [*tables, *blocks]] + [weight, weight],
+        out_specs=[result, result, whole(picks)],
         out_shape=[
             jax.ShapeDtypeStruct((local, rows, hidden), jnp.float32),
             jax.ShapeDtypeStruct((local, rows, hidden), jnp.float32),
-            jax.ShapeDtypeStruct((n, local * SLOT, tokens), jnp.bfloat16),
+            jax.ShapeDtypeStruct(picks, jnp.bfloat16),
         ],
         scratch_shapes=[
             pltpu.VMEM((local, rows, features), jnp.bfloat16),
@@ -122,34 +134,39 @@
             bytes_accessed=4 * local * features * hidden + 8 * local * rows * hidden,
             transcendentals=local * rows * hidden,
         ),
-    )(table, x_all, wg, wu)
-
-
-def back_kernel(n, local, pick_ref, g_ref, wd_ref, a_ref, b_ref, hg_ref, hu_ref, gs):
+    )(*tables, *blocks, wg, wu)
+
+
+def back_kernel(n, local, counts, pick_ref, *refs):
+    token_refs = refs[: sum(counts)]
+    wd_ref, a_ref, b_ref, hg_ref, hu_ref, gs = refs[sum(counts) :]
+
     @pl.when((pl.program_id(0) == 0) & (pl.program_id(1) == 0))
     def _():
+        first = 0
         for g in range(n):
-            rows = dot(pick_ref[g], g_ref[g]).astype(jnp.bfloat16)
-            for j in range(local):
-                gs[j, g * SLOT : (g + 1) * SLOT, :] = rows[j * SLOT : (j + 1) * SLOT, :]
+            gather_rows(pick_ref[g], token_refs, first, counts[g], gs, g, local)
+            first += counts[g]
 
     back = dot(gs[pl.program_id(0)], wd_ref[0], NT)
     hg_ref[0] = (back * a_ref[0]).astype(jnp.bfloat16)
     hu_ref[0] = (back * b_ref[0]).astype(jnp.bfloat16)
 
 
-def back(n, pick, g_all, wd, a, b):
+def back(n, pick, tokens, wd, a, b):
     local, hidden, features = wd.shape
     rows = n * SLOT
     cols = hidden // 2
+    counts = [len(t) for t in tokens]
+    blocks = [block for t in tokens for block in t]
     block = pl.BlockSpec((1, rows, cols), lambda e, f: (e, 0, f))
     shape = jax.ShapeDtypeStruct((local, rows, hidden), jnp.bfloat16)
     return pl.pallas_call(
-        functools.partial(back_kernel, n, local),
+        functools.partial(back_kernel, n, local, counts),
         grid=(local, hidden // cols),
         in_specs=[
             whole(pick.shape),
-            whole(g_all.shape),
+            *[whole(t.shape) for t in blocks],
             pl.BlockSpec((1, cols, features), lambda e, f: (e, f, 0)),
             block,
             block,
@@ -163,10 +180,10 @@
             bytes_accessed=2 * local * features * hidden + 12 * local * rows * hidden,
             transcendentals=0,
         ),
-    )(pick, g_all, wd, a, b)
-
-
-def out_kernel(axis, n, local, orders, pick_ref, hg_ref, hu_ref, wg_ref, wu_ref, *rest):
+    )(pick, *blocks, wd, a, b)
+
+
+def out_kernel(n, local, orders, pick_ref, hg_ref, hu_ref, wg_ref, wu_ref, *rest):
     outs, rows_ref = rest[:-1], rest[-1]
     e = pl.program_id(0)
     rows = (dot(hg_ref[0], wg_ref[0], NT) + dot(hu_ref[0], wu_ref[0], NT)).astype(jnp.bfloat16)
@@ -175,15 +192,13 @@
 
     @pl.when(e == local - 1)
     def _():
-        me = lax.axis_index(axis)
         for out_ref, order in zip(outs, orders):
-            for i, k in enumerate(order):
-                g = lax.bitwise_xor(me, k)
+            for i, g in enumerate(order):
                 part = rows_ref[g].reshape(local * SLOT, -1)
                 out_ref[i] = dot(pick_ref[g], part, TN).astype(out_ref.dtype)
 
 
-def partial_sums(axis, n, orders, chunk, pick, hg, hu, wg, wu):
+def partial_sums(n, orders, chunk, pick, hg, hu, wg, wu):
     local, features, hidden = wg.shape
     tokens = pick.shape[2]
     rows = n * SLOT
@@ -193,7 +208,7 @@
     shapes = [(len(order), tokens, cols) for order in orders]
     types = [jnp.float32] + [jnp.bfloat16] * (len(orders) - 1)
     return pl.pallas_call(
-        functools.partial(out_kernel, axis, n, local, orders),
+        functools.partial(out_kernel, n, local, orders),
         grid=(local,),
         in_specs=[whole(pick.shape), act, act, weight, weight],
         out_specs=[whole(s) for s in shapes],
@@ -229,23 +244,32 @@
     def swap(array, k):
         return lax.ppermute(array, axis, [(i, i ^ k) for i in range(n)])
 
-    table = lax.all_gather(rank_table(routes, route_gates, experts), axis)
-    x_all = lax.all_gather(saved_input, axis)
-    g_all = lax.all_gather(grad_out, axis)
-    a, b, pick = pre(axis, n, table, x_all, gate_proj, up_proj)
-    hg, hu = back(n, pick, g_all, down_proj, a, b)
+    table = rank_table(routes.T, route_gates.T, experts)
+    tables = [table] + [swap(table, k) for k in range(1, n)]
+    if n == 4:
+        half = tokens // 2
+        upper, lower = saved_input[:half], saved_input[half:]
+        near = [[]] + [[swap(upper, k), swap(lower, k)] for k in (1, 2)]
+        relayed = [swap(near[1][0], 2), swap(near[2][1], 1)]
+        x_blocks = [[saved_input], near[1], near[2], relayed]
+        grad_out, *_ = lax.optimization_barrier((grad_out, near[1], near[2]))
+    else:
+        x_blocks = [[saved_input]] + [[swap(saved_input, k)] for k in range(1, n)]
+    g_blocks = [[grad_out]] + [[swap(grad_out, k)] for k in range(1, n)]
+    a, b, pick = pre(axis, n, tables, x_blocks, gate_proj, up_proj)
+    hg, hu = back(n, pick, g_blocks, down_proj, a, b)
     parts = []
     for chunk in range(CHUNKS):
         if n == 4:
-            near, far = (1, 2) if chunk % 2 == 0 else (2, 1)
-            orders = ((0,), (near, 3), (far,))
-            own, two, one = partial_sums(axis, n, orders, chunk, pick, hg, hu, gate_proj, up_proj)
-            two = swap(two, near)
+            first, last = (1, 2) if chunk % 2 == 0 else (2, 1)
+            orders = ((0,), (first, 3), (last,))
+            own, two, one = partial_sums(n, orders, chunk, pick, hg, hu, gate_proj, up_proj)
+            two = swap(two, first)
             relay = (two[1:2].astype(jnp.float32) + one.astype(jnp.float32)).astype(jnp.bfloat16)
-            parts += [own, two[:1], swap(relay, far)]
+            parts += [own, two[:1], swap(relay, last)]
         else:
             orders = tuple((k,) for k in range(n))
-            own, *others = partial_sums(axis, n, orders, chunk, pick, hg, hu, gate_proj, up_proj)
+            own, *others = partial_sums(n, orders, chunk, pick, hg, hu, gate_proj, up_proj)
             parts += [own] + [swap(other, k + 1) for k, other in enumerate(others)]
     return pl.pallas_call(
         sum_kernel,

time: 148 us -> 115 us (0.78)
  waiting for transfers between devices: 54.2 us -> 13.8 us
  starting transfers between devices: 8.45 us -> 24.6 us
  local copies, waits for them, and re-layouts: 12.5 us -> 26 us
  between operations: 13.5 us -> 0.23 us
  blocking collectives: 9.77 us -> 0 us
    all_gather x2 -> x0, waiting for transfers between devices: 43.5 us -> none  [the longest x1 25 us: body(): x_all = lax.all_gather(saved_input, axis)]
    ppermute x8 -> x20, starting transfers between devices: 8.41 us -> 24.6 us  [swap(): return lax.ppermute(array, axis, [(i, i ^ k) for i in range(n)])]
    unnamed x10 -> x62, local copies, waits for them, and re-layouts: 12.4 us -> 24.9 us
    all_gather x1 -> x0, blocking collectives: 9.77 us -> none  [body(): table = lax.all_gather(rank_table(routes, route_gates, experts), axis)]
    ppermute x8 -> x20, waiting for transfers between devices: 9.29 us -> 13.8 us  [swap(): return lax.ppermute(array, axis, [(i, i ^ k) for i in range(n)])]
  transfers between devices with their start and end apart: 10 -> 20, of which waited for: 7 -> 8; matrix products, arithmetic and copies ran while one was open for 2% -> 0% of each run, Pallas kernels for 19% -> 24%
where the time goes in v2:
time: 115 us; the launch traced here: 114 us
  Pallas kernels  48.9 us (43%)
  local copies, waits for them, and re-layouts  26 us (23%)
  starting transfers between devices  24.6 us (21%)
  waiting for transfers between devices  13.8 us (12%)
    unnamed x62, local copies, waits for them, and re-layouts  24.9 us
    ppermute x20, starting transfers between devices, swap(): return lax.ppermute(array, axis, [(i, i ^ k) for i in range(n)])  24.6 us
    pallas_call x4, Pallas kernels, partial_sums(): pl.pallas_call(functools.partial(out_kernel, n, local, orders), grid=(loc...  18 us
    pallas_call x1, Pallas kernels, pre(): pl.pallas_call(functools.partial(pre_kernel, axis, n, local, counts), gri...  17.1 us
    ppermute x20, waiting for transfers between devices, swap(): return lax.ppermute(array, axis, [(i, i ^ k) for i in range(n)])  13.8 us
    pallas_call x1, Pallas kernels, back(): pl.pallas_call(functools.partial(back_kernel, n, local, counts), grid=(lo...  11.3 us
  transfers between devices with their start and end apart: 20, of which 8 were waited for; matrix products, arithmetic and copies ran while one was open for 0% of the time, Pallas kernels for 24%

profile of v2, /device:TPU:0, one launch (start us, length us, event | category | flops | bytes accessed | tf_op | source)
XLA Modules:
  0.0 113.6 jit_solution(17680284759086849668)
XLA Ops:
  0.0 1.1 fusion
  1.1 3.0 %collective-permute-start.6 = (bf16[64,2048]{1,0:T(8,128)(2,1)S(1)}, bf16[64,2048]{1,0:T(8,128)(2,1)S(1)}, u32[]{:S(2)}, u32[]{:S(2)}) collective-permute-start(bf16[64,2048]{1,0:T(8,128)(2,1)S(1)} %get-tuple-element.41), channel_id=1, source_target_pairs={{0,2},{1,3},{2,0},{3,1},{4,6},{5,7},{6,4},{7,5},{8,10},{9,11},{10,... | collective-permute-start | bytes 786440 | tf_op jit(solution)/shard_map/ppermute | solution.py:245
  4.1 1.5 %collective-permute-start.3 = (bf16[64,2048]{1,0:T(8,128)(2,1)S(1)}, bf16[64,2048]{1,0:T(8,128)(2,1)S(1)}, u32[]{:S(2)}, u32[]{:S(2)}) collective-permute-start(bf16[64,2048]{1,0:T(8,128)(2,1)S(1)} %get-tuple-element.42), channel_id=1, source_target_pairs={{0,1},{1,0},{2,3},{3,2},{4,5},{5,4},{6,7},{7,6},{8,9},{9,8},{10,11... | collective-permute-start | bytes 786440 | tf_op jit(solution)/shard_map/ppermute | solution.py:245
  5.6 0.5 collective-permute-start.4
  6.1 0.1 collective-permute-start.5
  6.2 5.0 %collective-permute-done.6.refs_8_ = bf16[64,2048]{1,0:T(8,128)(2,1)S(1)} collective-permute-done((bf16[64,2048]{1,0:T(8,128)(2,1)S(1)}, bf16[64,2048]{1,0:T(8,128)(2,1)S(1)}, u32[]{:S(2)}, u32[]{:S(2)}) %collective-permute-start.6) | collective-permute-done | bytes 262176 | tf_op jit(solution)/shard_map/ppermute | solution.py:245
  11.2 2.0 %collective-permute-start.8 = (bf16[64,2048]{1,0:T(8,128)(2,1)S(1)}, bf16[64,2048]{1,0:T(8,128)(2,1)S(1)}, u32[]{:S(2)}, u32[]{:S(2)}) collective-permute-start(bf16[64,2048]{1,0:T(8,128)(2,1)S(1)} %collective-permute-done.6.refs_8_), channel_id=1, source_target_pairs={{0,1},{1,0},{2,3},{3,2},{4,5},{5,4},{6,7},{7,6},{8,9},{9,8},{10,11... | collective-permute-start | bytes 786440 | tf_op jit(solution)/shard_map/ppermute | solution.py:245
  13.3 0.1 collective-permute-done.3.refs_5_
  13.3 1.5 %collective-permute-start.7 = (bf16[64,2048]{1,0:T(8,128)(2,1)S(1)}, bf16[64,2048]{1,0:T(8,128)(2,1)S(1)}, u32[]{:S(2)}, u32[]{:S(2)}) collective-permute-start(bf16[64,2048]{1,0:T(8,128)(2,1)S(1)} %collective-permute-done.3.refs_5_), channel_id=1, source_target_pairs={{0,2},{1,3},{2,0},{3,1},{4,6},{5,7},{6,4},{7,5},{8,10},{9,11},{10,... | collective-permute-start | bytes 786440 | tf_op jit(solution)/shard_map/ppermute | solution.py:245
  14.8 0.7 copy-done.17
  15.5 1.5 %shard_map.73.refs_0_ = bf16[32,128]{1,0:T(8,128)(2,1)} custom-call(s32[8,128]{1,0:T(8,128)} %bitcast.4, bf16[8,128]{1,0:T(8,128)(2,1)} %bitcast.5), custom_call_target="tpu_custom_call" | custom-call | tf_op jit(solution)/shard_map/pallas_call | solution.py:58
  17.0 1.5 %collective-permute-start.2 = (bf16[32,128]{1,0:T(8,128)(2,1)}, bf16[32,128]{1,0:T(8,128)(2,1)S(1)}, u32[]{:S(2)}, u32[]{:S(2)}) collective-permute-start(bf16[32,128]{1,0:T(8,128)(2,1)} %shard_map.73.refs_0_), channel_id=1, source_target_pairs={{0,3},{1,2},{2,1},{3,0},{4,7},{5,6},{6,5},{7,4},{8,11},{9,10},{10,... | collective-permute-start | bytes 24584 | tf_op jit(solution)/shard_map/ppermute | solution.py:245
  18.5 0.5 collective-permute-done.4.refs_6_
  19.0 0.7 copy-done.19
  19.7 0.0 collective-permute-start.1
  19.7 0.7 copy-done.21
  20.4 2.0 %collective-permute-start = (bf16[32,128]{1,0:T(8,128)(2,1)}, bf16[32,128]{1,0:T(8,128)(2,1)S(1)}, u32[]{:S(2)}, u32[]{:S(2)}) collective-permute-start(bf16[32,128]{1,0:T(8,128)(2,1)} %shard_map.73.refs_0_), channel_id=1, source_target_pairs={{0,1},{1,0},{2,3},{3,2},{4,5},{5,4},{6,7},{7,6},{8,9},{9,8},{10,11... | collective-permute-start | bytes 24584 | tf_op jit(solution)/shard_map/ppermute | solution.py:245
  22.4 0.8 collective-permute-done.2.refs_3_
  23.2 2.6 %collective-permute-start.11 = (bf16[128,2048]{1,0:T(8,128)(2,1)}, bf16[128,2048]{1,0:T(8,128)(2,1)S(1)}, u32[]{:S(2)}, u32[]{:S(2)}) collective-permute-start(bf16[128,2048]{1,0:T(8,128)(2,1)} %refs_0_), channel_id=1, source_target_pairs={{0,3},{1,2},{2,1},{3,0},{4,7},{5,6},{6,5},{7,4},{8,11},{9,10},{10,... | collective-permute-start | bytes 1572872 | tf_op jit(solution)/shard_map/ppermute | solution.py:245
  25.8 0.0 collective-permute-done.1.refs_2_
  25.8 0.5 collective-permute-start.10
  26.3 0.4 collective-permute-start.9
  26.7 0.7 copy-done.23
  27.4 0.7 copy-done.25
  28.1 1.0 copy-done.3
  29.1 0.9 copy-done.18
  30.1 0.9 copy-done.20
  31.0 0.9 copy-done.22
  32.0 0.9 copy-done.24
  32.9 0.9 copy-done.26
  33.9 0.7 copy-done.27
  34.6 17.1 %shard_map.74 = (f32[4,256,768]{2,1,0:T(8,128)S(1)}, f32[4,256,768]{2,1,0:T(8,128)}, bf16[4,256,128]{2,1,0:T(8,128)(2,1)S(1)}) custom-call(bf16[32,128]{1,0:T(8,128)(2,1)S(1)} %copy-done.27, bf16[32,128]{1,0:T(8,128)(2,1)S(1)} %collective-permute-done.refs_1_, bf16[32,128]{1,0:T(8,128)(2,1)S(1)} %collective-permute-done.1.refs_2_, ...), custom_call_target="tpu_custom_call" | custom-call | flops 6442450944 | bytes 31457280 | tf_op jit(solution)/shard_map/pallas_call | solution.py:117
  51.6 1.7 %copy-done = f32[4,256,768]{2,1,0:T(8,128)} copy-done((f32[4,256,768]{2,1,0:T(8,128)}, f32[4,256,768]{2,1,0:T(8,128)S(1)}, u32[]{:S(2)}) %copy-start) | copy-done | bytes 3145752
  53.3 0.8 copy-done.5
  54.1 0.8 copy-done.7
  55.0 0.8 copy-done.9
  55.7 1.9 %copy-done.1 = f32[4,256,768]{2,1,0:T(8,128)S(1)} copy-done((f32[4,256,768]{2,1,0:T(8,128)S(1)}, f32[4,256,768]{2,1,0:T(8,128)}, u32[]{:S(2)}) %copy-start.1) | copy-done | bytes 3145752
  57.6 1.9 %copy-done.2 = f32[4,256,768]{2,1,0:T(8,128)S(1)} copy-done((f32[4,256,768]{2,1,0:T(8,128)S(1)}, f32[4,256,768]{2,1,0:T(8,128)}, u32[]{:S(2)}) %copy-start.2) | copy-done | bytes 3145752
  59.5 1.0 copy-done.4
  60.6 1.0 copy-done.6
  61.6 1.0 copy-done.8
  62.7 1.0 copy-done.10
  63.7 11.3 %shard_map.75 = (bf16[4,256,768]{2,1,0:T(8,128)(2,1)S(1)}, bf16[4,256,768]{2,1,0:T(8,128)(2,1)S(1)}) custom-call(bf16[4,256,128]{2,1,0:T(8,128)(2,1)S(1)} %get-tuple-element.23.pick_ref, bf16[128,2048]{1,0:T(8,128)(2,1)S(1)} %copy-done.4, bf16[128,2048]{1,0:T(8,128)(2,1)S(1)} %copy-done.10, bf16[128,2048]{1,0:T(8,128)(2,1)S(1)} %copy-done.8, ...), custom_call_target="tpu_custom_call" | custom-call | flops 3221225472 | bytes 22020096 | tf_op jit(solution)/shard_map/pallas_call | solution.py:164
  75.1 4.5 %shard_map.79 = (f32[1,128,512]{2,1,0:T(8,128)S(1)}, bf16[2,128,512]{2,1,0:T(8,128)(2,1)S(1)}, bf16[1,128,512]{2,1,0:T(8,128)(2,1)S(1)}) custom-call(bf16[4,256,128]{2,1,0:T(8,128)(2,1)S(1)} %get-tuple-element.23.pick_ref, bf16[4,256,768]{2,1,0:T(8,128)(2,1)S(1)} %get-tuple-element.27.hg_ref, bf16[4,256,768]{2,1,0:T(8,128)(2,1)S(1)} %get-tuple-element.28.hu_ref, ...), custom_call_target="tpu_custom_call" | custom-call | flops 1610612736 | bytes 9437184 | tf_op jit(solution)/shard_map/pallas_call | solution.py:210
  79.6 4.5 %shard_map.78 = (f32[1,128,512]{2,1,0:T(8,128)S(1)}, bf16[2,128,512]{2,1,0:T(8,128)(2,1)S(1)}, bf16[1,128,512]{2,1,0:T(8,128)(2,1)S(1)}) custom-call(bf16[4,256,128]{2,1,0:T(8,128)(2,1)S(1)} %get-tuple-element.23.pick_ref, bf16[4,256,768]{2,1,0:T(8,128)(2,1)S(1)} %get-tuple-element.27.hg_ref, bf16[4,256,768]{2,1,0:T(8,128)(2,1)S(1)} %get-tuple-element.28.hu_ref, ...), custom_call_target="tpu_custom_call" | custom-call | flops 1610612736 | bytes 9437184 | tf_op jit(solution)/shard_map/pallas_call | solution.py:210
  84.1 1.7 %collective-permute-start.18 = (bf16[2,128,512]{2,1,0:T(8,128)(2,1)S(1)}, bf16[2,128,512]{2,1,0:T(8,128)(2,1)S(1)}, u32[]{:S(2)}, u32[]{:S(2)}) collective-permute-start(bf16[2,128,512]{2,1,0:T(8,128)(2,1)S(1)} %get-tuple-element.39), channel_id=1, source_target_pairs={{0,2},{1,3},{2,0},{3,1},{4,6},{5,7},{6,4},{7,5},{8,10},{9,11},{10,... | collective-permute-start | bytes 786440 | tf_op jit(solution)/shard_map/ppermute | solution.py:245
  85.8 1.5 %collective-permute-start.16 = (bf16[2,128,512]{2,1,0:T(8,128)(2,1)S(1)}, bf16[2,128,512]{2,1,0:T(8,128)(2,1)S(1)}, u32[]{:S(2)}, u32[]{:S(2)}) collective-permute-start(bf16[2,128,512]{2,1,0:T(8,128)(2,1)S(1)} %get-tuple-element.36), channel_id=1, source_target_pairs={{0,1},{1,0},{2,3},{3,2},{4,5},{5,4},{6,7},{7,6},{8,9},{9,8},{10,11... | collective-permute-start | bytes 786440 | tf_op jit(solution)/shard_map/ppermute | solution.py:245
  87.3 4.5 %shard_map.77 = (f32[1,128,512]{2,1,0:T(8,128)S(1)}, bf16[2,128,512]{2,1,0:T(8,128)(2,1)S(1)}, bf16[1,128,512]{2,1,0:T(8,128)(2,1)S(1)}) custom-call(bf16[4,256,128]{2,1,0:T(8,128)(2,1)S(1)} %get-tuple-element.23.pick_ref, bf16[4,256,768]{2,1,0:T(8,128)(2,1)S(1)} %get-tuple-element.27.hg_ref, bf16[4,256,768]{2,1,0:T(8,128)(2,1)S(1)} %get-tuple-element.28.hu_ref, ...), custom_call_target="tpu_custom_call" | custom-call | flops 1610612736 | bytes 9437184 | tf_op jit(solution)/shard_map/pallas_call | solution.py:210
  91.8 4.6 %shard_map.76 = (f32[1,128,512]{2,1,0:T(8,128)S(1)}, bf16[2,128,512]{2,1,0:T(8,128)(2,1)S(1)}, bf16[1,128,512]{2,1,0:T(8,128)(2,1)S(1)}) custom-call(bf16[4,256,128]{2,1,0:T(8,128)(2,1)S(1)} %get-tuple-element.23.pick_ref, bf16[4,256,768]{2,1,0:T(8,128)(2,1)S(1)} %get-tuple-element.27.hg_ref, bf16[4,256,768]{2,1,0:T(8,128)(2,1)S(1)} %get-tuple-element.28.hu_ref, ...), custom_call_target="tpu_custom_call" | custom-call | flops 1610612736 | bytes 9437184 | tf_op jit(solution)/shard_map/pallas_call | solution.py:210
  96.4 0.0 copy-start.15
  96.4 0.6 collective-permute-start.14
  97.0 0.4 collective-permute-start.12
  97.4 1.7 %collective-permute-start.19 = (bf16[1,128,512]{2,1,0:T(8,128)(2,1)S(1)}, bf16[1,128,512]{2,1,0:T(8,128)(2,1)S(1)}, u32[]{:S(2)}, u32[]{:S(2)}) collective-permute-start(bf16[1,128,512]{2,1,0:T(8,128)(2,1)S(1)} %add_convert_fusion), channel_id=1, source_target_pairs={{0,1},{1,0},{2,3},{3,2},{4,5},{5,4},{6,7},{7,6},{8,9},{9,8},{10,11... | collective-permute-start | bytes 393224 | tf_op jit(solution)/shard_map/ppermute | solution.py:245
  99.2 1.6 %collective-permute-start.17 = (bf16[1,128,512]{2,1,0:T(8,128)(2,1)S(1)}, bf16[1,128,512]{2,1,0:T(8,128)(2,1)S(1)}, u32[]{:S(2)}, u32[]{:S(2)}) collective-permute-start(bf16[1,128,512]{2,1,0:T(8,128)(2,1)S(1)} %add_convert_fusion.1), channel_id=1, source_target_pairs={{0,2},{1,3},{2,0},{3,1},{4,6},{5,7},{6,4},{7,5},{8,10},{9,11},{10,... | collective-permute-start | bytes 393224 | tf_op jit(solution)/shard_map/ppermute | solution.py:245
  100.8 3.5 %collective-permute-done.14 = bf16[2,128,512]{2,1,0:T(8,128)(2,1)S(1)} collective-permute-done((bf16[2,128,512]{2,1,0:T(8,128)(2,1)S(1)}, bf16[2,128,512]{2,1,0:T(8,128)(2,1)S(1)}, u32[]{:S(2)}, u32[]{:S(2)}) %collective-permute-start.14) | collective-permute-done | bytes 262176 | tf_op jit(solution)/shard_map/ppermute | solution.py:245
  104.3 0.1 collective-permute-start.15
  104.4 0.4 collective-permute-done.12
  104.8 1.4 %collective-permute-start.13 = (bf16[1,128,512]{2,1,0:T(8,128)(2,1)S(1)}, bf16[1,128,512]{2,1,0:T(8,128)(2,1)S(1)}, u32[]{:S(2)}, u32[]{:S(2)}) collective-permute-start(bf16[1,128,512]{2,1,0:T(8,128)(2,1)S(1)} %add_convert_fusion.3), channel_id=1, source_target_pairs={{0,2},{1,3},{2,0},{3,1},{4,6},{5,7},{6,4},{7,5},{8,10},{9,11},{10,... | collective-permute-start | bytes 393224 | tf_op jit(solution)/shard_map/ppermute | solution.py:245
  106.3 3.0 %collective-permute-done.15.refs_5_ = bf16[1,128,512]{2,1,0:T(8,128)(2,1)S(1)} collective-permute-done((bf16[1,128,512]{2,1,0:T(8,128)(2,1)S(1)}, bf16[1,128,512]{2,1,0:T(8,128)(2,1)S(1)}, u32[]{:S(2)}, u32[]{:S(2)}) %collective-permute-start.15) | collective-permute-done | bytes 131104 | tf_op jit(solution)/shard_map/ppermute | solution.py:245
  109.3 0.5 collective-permute-done.13.refs_2_
  109.8 0.9 copy-done.12
  110.8 0.9 copy-done.14
  111.7 0.9 copy-done.16
  112.7 0.9 shard_map.80
  (56 shorter events, 0.3 us)
Async XLA Ops:
  1.1 10.2 %collective-permute-start.6 = (bf16[64,2048]{1,0:T(8,128)(2,1)S(1)}, bf16[64,2048]{1,0:T(8,128)(2,1)S(1)}, u32[]{:S(2)}, u32[]{:S(2)}) collective-permute-start(bf16[64,2048]{1,0:T(8,128)(2,1)S(1)} %get-tuple-element.41), channel_id=1, source_target_pairs={{0,2},{1,3},{2,0},{3,1},{4,6},{5,7},{6,4},{7,5},{8,10},{9,11},{10,... | collective-permute-start | bytes 786440 | tf_op jit(solution)/shard_map/ppermute | solution.py:245
  4.1 9.2 %collective-permute-start.3 = (bf16[64,2048]{1,0:T(8,128)(2,1)S(1)}, bf16[64,2048]{1,0:T(8,128)(2,1)S(1)}, u32[]{:S(2)}, u32[]{:S(2)}) collective-permute-start(bf16[64,2048]{1,0:T(8,128)(2,1)S(1)} %get-tuple-element.42), channel_id=1, source_target_pairs={{0,1},{1,0},{2,3},{3,2},{4,5},{5,4},{6,7},{7,6},{8,9},{9,8},{10,11... | collective-permute-start | bytes 786440 | tf_op jit(solution)/shard_map/ppermute | solution.py:245
  5.6 13.4 %collective-permute-start.4 = (bf16[64,2048]{1,0:T(8,128)(2,1)S(1)}, bf16[64,2048]{1,0:T(8,128)(2,1)S(1)}, u32[]{:S(2)}, u32[]{:S(2)}) collective-permute-start(bf16[64,2048]{1,0:T(8,128)(2,1)S(1)} %get-tuple-element.41), channel_id=1, source_target_pairs={{0,1},{1,0},{2,3},{3,2},{4,5},{5,4},{6,7},{7,6},{8,9},{9,8},{10,11... | collective-permute-start | bytes 786440 | tf_op jit(solution)/shard_map/ppermute | solution.py:245
  6.1 13.6 %collective-permute-start.5 = (bf16[64,2048]{1,0:T(8,128)(2,1)S(1)}, bf16[64,2048]{1,0:T(8,128)(2,1)S(1)}, u32[]{:S(2)}, u32[]{:S(2)}) collective-permute-start(bf16[64,2048]{1,0:T(8,128)(2,1)S(1)} %get-tuple-element.42), channel_id=1, source_target_pairs={{0,2},{1,3},{2,0},{3,1},{4,6},{5,7},{6,4},{7,5},{8,10},{9,11},{10,... | collective-permute-start | bytes 786440 | tf_op jit(solution)/shard_map/ppermute | solution.py:245
  11.2 15.4 %collective-permute-start.8 = (bf16[64,2048]{1,0:T(8,128)(2,1)S(1)}, bf16[64,2048]{1,0:T(8,128)(2,1)S(1)}, u32[]{:S(2)}, u32[]{:S(2)}) collective-permute-start(bf16[64,2048]{1,0:T(8,128)(2,1)S(1)} %collective-permute-done.6.refs_8_), channel_id=1, source_target_pairs={{0,1},{1,0},{2,3},{3,2},{4,5},{5,4},{6,7},{7,6},{8,9},{9,8},{10,11... | collective-permute-start | bytes 786440 | tf_op jit(solution)/shard_map/ppermute | solution.py:245
  13.3 14.0 %collective-permute-start.7 = (bf16[64,2048]{1,0:T(8,128)(2,1)S(1)}, bf16[64,2048]{1,0:T(8,128)(2,1)S(1)}, u32[]{:S(2)}, u32[]{:S(2)}) collective-permute-start(bf16[64,2048]{1,0:T(8,128)(2,1)S(1)} %collective-permute-done.3.refs_5_), channel_id=1, source_target_pairs={{0,2},{1,3},{2,0},{3,1},{4,6},{5,7},{6,4},{7,5},{8,10},{9,11},{10,... | collective-permute-start | bytes 786440 | tf_op jit(solution)/shard_map/ppermute | solution.py:245
  14.8 0.7 copy-start.17
  17.0 6.2 %collective-permute-start.2 = (bf16[32,128]{1,0:T(8,128)(2,1)}, bf16[32,128]{1,0:T(8,128)(2,1)S(1)}, u32[]{:S(2)}, u32[]{:S(2)}) collective-permute-start(bf16[32,128]{1,0:T(8,128)(2,1)} %shard_map.73.refs_0_), channel_id=1, source_target_pairs={{0,3},{1,2},{2,1},{3,0},{4,7},{5,6},{6,5},{7,4},{8,11},{9,10},{10,... | collective-permute-start | bytes 24584 | tf_op jit(solution)/shard_map/ppermute | solution.py:245
  18.9 0.7 copy-start.19
  19.7 6.1 %collective-permute-start.1 = (bf16[32,128]{1,0:T(8,128)(2,1)}, bf16[32,128]{1,0:T(8,128)(2,1)S(1)}, u32[]{:S(2)}, u32[]{:S(2)}) collective-permute-start(bf16[32,128]{1,0:T(8,128)(2,1)} %shard_map.73.refs_0_), channel_id=1, source_target_pairs={{0,2},{1,3},{2,0},{3,1},{4,6},{5,7},{6,4},{7,5},{8,10},{9,11},{10,... | collective-permute-start | bytes 24584 | tf_op jit(solution)/shard_map/ppermute | solution.py:245
  19.7 0.7 copy-start.21
  20.4 5.8 %collective-permute-start = (bf16[32,128]{1,0:T(8,128)(2,1)}, bf16[32,128]{1,0:T(8,128)(2,1)S(1)}, u32[]{:S(2)}, u32[]{:S(2)}) collective-permute-start(bf16[32,128]{1,0:T(8,128)(2,1)} %shard_map.73.refs_0_), channel_id=1, source_target_pairs={{0,1},{1,0},{2,3},{3,2},{4,5},{5,4},{6,7},{7,6},{8,9},{9,8},{10,11... | collective-permute-start | bytes 24584 | tf_op jit(solution)/shard_map/ppermute | solution.py:245
  23.2 30.2 %collective-permute-start.11 = (bf16[128,2048]{1,0:T(8,128)(2,1)}, bf16[128,2048]{1,0:T(8,128)(2,1)S(1)}, u32[]{:S(2)}, u32[]{:S(2)}) collective-permute-start(bf16[128,2048]{1,0:T(8,128)(2,1)} %refs_0_), channel_id=1, source_target_pairs={{0,3},{1,2},{2,1},{3,0},{4,7},{5,6},{6,5},{7,4},{8,11},{9,10},{10,... | collective-permute-start | bytes 1572872 | tf_op jit(solution)/shard_map/ppermute | solution.py:245
  25.8 28.4 %collective-permute-start.10 = (bf16[128,2048]{1,0:T(8,128)(2,1)}, bf16[128,2048]{1,0:T(8,128)(2,1)S(1)}, u32[]{:S(2)}, u32[]{:S(2)}) collective-permute-start(bf16[128,2048]{1,0:T(8,128)(2,1)} %refs_0_), channel_id=1, source_target_pairs={{0,2},{1,3},{2,0},{3,1},{4,6},{5,7},{6,4},{7,5},{8,10},{9,11},{10,... | collective-permute-start | bytes 1572872 | tf_op jit(solution)/shard_map/ppermute | solution.py:245
  26.3 28.7 %collective-permute-start.9 = (bf16[128,2048]{1,0:T(8,128)(2,1)}, bf16[128,2048]{1,0:T(8,128)(2,1)S(1)}, u32[]{:S(2)}, u32[]{:S(2)}) collective-permute-start(bf16[128,2048]{1,0:T(8,128)(2,1)} %refs_0_), channel_id=1, source_target_pairs={{0,1},{1,0},{2,3},{3,2},{4,5},{5,4},{6,7},{7,6},{8,9},{9,8},{10,11... | collective-permute-start | bytes 1572872 | tf_op jit(solution)/shard_map/ppermute | solution.py:245
  26.7 0.7 copy-start.23
  27.4 0.7 copy-start.25
  28.1 1.0 copy-start.3
  29.1 0.9 copy-start.18
  30.1 0.9 copy-start.20
  31.0 0.9 copy-start.22
  32.0 0.9 copy-start.24
  32.9 0.9 copy-start.26
  33.9 0.7 copy-start.27
  34.6 40.5 %slice-start = ((s8[12582912]{0:T(1024)(128)(4,1)}), s8[4194304]{0:T(1024)(128)(4,1)S(1)}, s32[]{:S(2)}) async-start(s8[12582912]{0:T(1024)(128)(4,1)} %bitcast.2), calls=%async_computation | async-start | bytes 8388608
  34.6 40.5 %slice-start.1 = ((s8[12582912]{0:T(1024)(128)(4,1)}), s8[4194304]{0:T(1024)(128)(4,1)S(1)}, s32[]{:S(2)}) async-start(s8[12582912]{0:T(1024)(128)(4,1)} %bitcast.2), calls=%async_computation.1 | async-start | bytes 8388608
  51.6 1.7 %copy-start = (f32[4,256,768]{2,1,0:T(8,128)}, f32[4,256,768]{2,1,0:T(8,128)S(1)}, u32[]{:S(2)}) copy-start(f32[4,256,768]{2,1,0:T(8,128)S(1)} %get-tuple-element.25.refs_5_) | copy-start | bytes 9437188
  53.3 0.8 copy-start.5
  54.1 0.8 copy-start.7
  55.0 0.8 copy-start.9
  55.7 1.9 %copy-start.1 = (f32[4,256,768]{2,1,0:T(8,128)S(1)}, f32[4,256,768]{2,1,0:T(8,128)}, u32[]{:S(2)}) copy-start(f32[4,256,768]{2,1,0:T(8,128)} %copy-done) | copy-start | bytes 9437188
  57.6 1.9 %copy-start.2 = (f32[4,256,768]{2,1,0:T(8,128)S(1)}, f32[4,256,768]{2,1,0:T(8,128)}, u32[]{:S(2)}) copy-start(f32[4,256,768]{2,1,0:T(8,128)} %get-tuple-element.26.refs_6_) | copy-start | bytes 9437188
  59.5 1.0 copy-start.4
  60.6 1.0 copy-start.6
  61.6 1.0 copy-start.8
  62.7 1.0 copy-start.10
  63.7 11.4 %slice-start.2 = ((s8[12582912]{0:T(1024)(128)(4,1)}), s8[4194304]{0:T(1024)(128)(4,1)S(1)}, s32[]{:S(2)}) async-start(s8[12582912]{0:T(1024)(128)(4,1)} %bitcast.2), calls=%async_computation.2 | async-start | bytes 8388608
  84.1 7.7 %copy-start.11 = (f32[1,128,512]{2,1,0:T(8,128)}, f32[1,128,512]{2,1,0:T(8,128)S(1)}, u32[]{:S(2)}) copy-start(f32[1,128,512]{2,1,0:T(8,128)S(1)} %get-tuple-element.35.refs_6_) | copy-start | bytes 786436
  84.1 13.3 %collective-permute-start.18 = (bf16[2,128,512]{2,1,0:T(8,128)(2,1)S(1)}, bf16[2,128,512]{2,1,0:T(8,128)(2,1)S(1)}, u32[]{:S(2)}, u32[]{:S(2)}) collective-permute-start(bf16[2,128,512]{2,1,0:T(8,128)(2,1)S(1)} %get-tuple-element.39), channel_id=1, source_target_pairs={{0,2},{1,3},{2,0},{3,1},{4,6},{5,7},{6,4},{7,5},{8,10},{9,11},{10,... | collective-permute-start | bytes 786440 | tf_op jit(solution)/shard_map/ppermute | solution.py:245
  85.8 13.3 %collective-permute-start.16 = (bf16[2,128,512]{2,1,0:T(8,128)(2,1)S(1)}, bf16[2,128,512]{2,1,0:T(8,128)(2,1)S(1)}, u32[]{:S(2)}, u32[]{:S(2)}) collective-permute-start(bf16[2,128,512]{2,1,0:T(8,128)(2,1)S(1)} %get-tuple-element.36), channel_id=1, source_target_pairs={{0,1},{1,0},{2,3},{3,2},{4,5},{5,4},{6,7},{7,6},{8,9},{9,8},{10,11... | collective-permute-start | bytes 786440 | tf_op jit(solution)/shard_map/ppermute | solution.py:245
  91.8 4.6 %copy-start.13 = (f32[1,128,512]{2,1,0:T(8,128)}, f32[1,128,512]{2,1,0:T(8,128)S(1)}, u32[]{:S(2)}) copy-start(f32[1,128,512]{2,1,0:T(8,128)S(1)} %get-tuple-element.32.refs_3_) | copy-start | bytes 786436
  96.4 13.4 %copy-start.15 = (f32[1,128,512]{2,1,0:T(8,128)}, f32[1,128,512]{2,1,0:T(8,128)S(1)}, u32[]{:S(2)}) copy-start(f32[1,128,512]{2,1,0:T(8,128)S(1)} %get-tuple-element.29.refs_0_) | copy-start | bytes 786436
  96.4 7.8 %collective-permute-start.14 = (bf16[2,128,512]{2,1,0:T(8,128)(2,1)S(1)}, bf16[2,128,512]{2,1,0:T(8,128)(2,1)S(1)}, u32[]{:S(2)}, u32[]{:S(2)}) collective-permute-start(bf16[2,128,512]{2,1,0:T(8,128)(2,1)S(1)} %get-tuple-element.33), channel_id=1, source_target_pairs={{0,2},{1,3},{2,0},{3,1},{4,6},{5,7},{6,4},{7,5},{8,10},{9,11},{10,... | collective-permute-start | bytes 786440 | tf_op jit(solution)/shard_map/ppermute | solution.py:245
  97.0 7.8 %collective-permute-start.12 = (bf16[2,128,512]{2,1,0:T(8,128)(2,1)S(1)}, bf16[2,128,512]{2,1,0:T(8,128)(2,1)S(1)}, u32[]{:S(2)}, u32[]{:S(2)}) collective-permute-start(bf16[2,128,512]{2,1,0:T(8,128)(2,1)S(1)} %get-tuple-element.30), channel_id=1, source_target_pairs={{0,1},{1,0},{2,3},{3,2},{4,5},{5,4},{6,7},{7,6},{8,9},{9,8},{10,11... | collective-permute-start | bytes 786440 | tf_op jit(solution)/shard_map/ppermute | solution.py:245
  97.4 8.9 %collective-permute-start.19 = (bf16[1,128,512]{2,1,0:T(8,128)(2,1)S(1)}, bf16[1,128,512]{2,1,0:T(8,128)(2,1)S(1)}, u32[]{:S(2)}, u32[]{:S(2)}) collective-permute-start(bf16[1,128,512]{2,1,0:T(8,128)(2,1)S(1)} %add_convert_fusion), channel_id=1, source_target_pairs={{0,1},{1,0},{2,3},{3,2},{4,5},{5,4},{6,7},{7,6},{8,9},{9,8},{10,11... | collective-permute-start | bytes 393224 | tf_op jit(solution)/shard_map/ppermute | solution.py:245
  99.2 7.1 %collective-permute-start.17 = (bf16[1,128,512]{2,1,0:T(8,128)(2,1)S(1)}, bf16[1,128,512]{2,1,0:T(8,128)(2,1)S(1)}, u32[]{:S(2)}, u32[]{:S(2)}) collective-permute-start(bf16[1,128,512]{2,1,0:T(8,128)(2,1)S(1)} %add_convert_fusion.1), channel_id=1, source_target_pairs={{0,2},{1,3},{2,0},{3,1},{4,6},{5,7},{6,4},{7,5},{8,10},{9,11},{10,... | collective-permute-start | bytes 393224 | tf_op jit(solution)/shard_map/ppermute | solution.py:245
  104.3 5.0 %collective-permute-start.15 = (bf16[1,128,512]{2,1,0:T(8,128)(2,1)S(1)}, bf16[1,128,512]{2,1,0:T(8,128)(2,1)S(1)}, u32[]{:S(2)}, u32[]{:S(2)}) collective-permute-start(bf16[1,128,512]{2,1,0:T(8,128)(2,1)S(1)} %add_convert_fusion.2), channel_id=1, source_target_pairs={{0,1},{1,0},{2,3},{3,2},{4,5},{5,4},{6,7},{7,6},{8,9},{9,8},{10,11... | collective-permute-start | bytes 393224 | tf_op jit(solution)/shard_map/ppermute | solution.py:245
  104.8 5.0 %collective-permute-start.13 = (bf16[1,128,512]{2,1,0:T(8,128)(2,1)S(1)}, bf16[1,128,512]{2,1,0:T(8,128)(2,1)S(1)}, u32[]{:S(2)}, u32[]{:S(2)}) collective-permute-start(bf16[1,128,512]{2,1,0:T(8,128)(2,1)S(1)} %add_convert_fusion.3), channel_id=1, source_target_pairs={{0,2},{1,3},{2,0},{3,1},{4,6},{5,7},{6,4},{7,5},{8,10},{9,11},{10,... | collective-permute-start | bytes 393224 | tf_op jit(solution)/shard_map/ppermute | solution.py:245
  109.8 1.0 copy-start.12
  110.8 0.9 copy-start.14
  111.7 0.9 copy-start.16

commit v3 on v2

v3 whole, which is shorter than its diff:
```python
import functools

import jax
import jax.numpy as jnp
from jax import lax
from jax.experimental import pallas as pl
from jax.experimental.pallas import tpu as pltpu
from jax.sharding import PartitionSpec as P

CAP = 56
SLOT = 64
UNUSED = 200.0
MIB = 1 << 20
CHUNKS = 4
PRE_MIB = 8
BACK_MIB = 12
OUT_MIB = 4

NT = (((1,), (1,)), ((), ()))


def dot(a, b, dims=(((1,), (0,)), ((), ()))):
    return lax.dot_general(a, b, dims, preferred_element_type=jnp.float32)


def params(limit):
    return pltpu.CompilerParams(vmem_limit_bytes=limit * MIB)


def rank_kernel(experts, routes_ref, gates_ref, out_ref):
    top, tokens = routes_ref.shape
    chosen = routes_ref[...].astype(jnp.float32)
    gates = gates_ref[...].astype(jnp.float32)
    label = lax.broadcasted_iota(jnp.int32, (experts, tokens), 0).astype(jnp.float32)
    hits = [(chosen[k : k + 1, :] == label).astype(jnp.float32) for k in range(top)]
    before = lax.broadcasted_iota(jnp.int32, (tokens, tokens), 0)
    after = lax.broadcasted_iota(jnp.int32, (tokens, tokens), 1)
    earlier = (before < after).astype(jnp.bfloat16)
    base = jnp.zeros((experts, 1), jnp.float32)
    rank = jnp.zeros((experts, tokens), jnp.float32)
    taken = jnp.zeros((experts, tokens), jnp.float32)
    gate = jnp.zeros((experts, tokens), jnp.float32)
    for k in range(top):
        inside = dot(hits[k].astype(jnp.bfloat16), earlier)
        rank += hits[k] * (inside + base)
        taken += hits[k]
        gate += hits[k] * gates[k : k + 1, :]
        base += jnp.sum(hits[k], axis=1, keepdims=True)
    rank = jnp.where((taken > 0.5) & (rank < CAP), rank, UNUSED)
    out_ref[:experts, :] = rank.astype(jnp.bfloat16)
    out_ref[experts:, :] = gate.astype(jnp.bfloat16)


def rank_table(routes, gates, experts):
    tokens = routes.shape[1]
    return pl.pallas_call(
        functools.partial(rank_kernel, experts),
        out_shape=jax.ShapeDtypeStruct((2 * experts, tokens), jnp.bfloat16),
    )(routes, gates)


def gather_rows(n, local, pick_ref, token_refs, out):
    wide = 2 * SLOT
    features = out.shape[2]
    cols = features // 4
    for p in range(n // 2):
        refs = [ref for pair in token_refs[2 * p : 2 * p + 2] for ref in pair]
        for d in range(0, features, cols):
            part = slice(d, d + cols)
            tokens = jnp.concatenate([ref[:, part] for ref in refs], axis=0)
            rows = dot(pick_ref[p], tokens).astype(jnp.bfloat16)
            for j in range(local):
                out[j, p * wide : (p + 1) * wide, part] = rows[j * wide : (j + 1) * wide, :]


def split(refs, counts):
    parts, first = [], 0
    for count in counts:
        parts.append(refs[first : first + count])
        first += count
    return parts, refs[first:]


def pre_kernel(axis, n, local, counts, *refs):
    table_refs, refs = refs[:n], refs[n:]
    token_refs, refs = split(refs, counts)
    wg_ref, wu_ref, a_ref, b_ref, pick_ref, place_ref, xs, gcol = refs
    experts = n * local
    tokens = table_refs[0].shape[1]
    wide = 2 * SLOT
    hidden = wg_ref.shape[2]
    cols = hidden // 2
    me = lax.axis_index(axis)
    row = lax.broadcasted_iota(jnp.int32, (2 * experts, tokens), 0)
    slot = lax.broadcasted_iota(jnp.int32, (wide, tokens), 0).astype(jnp.float32)
    for p in range(n // 2):
        for j in range(local):
            e = me * local + j
            gates = jnp.zeros((wide, 1), jnp.float32)
            for q in range(2):
                table = table_refs[2 * p + q][...].astype(jnp.float32)
                rank = jnp.sum(jnp.where(row == e, table, 0.0), axis=0, keepdims=True)
                gate = jnp.sum(jnp.where(row == e + experts, table, 0.0), axis=0, keepdims=True)
                pick = (slot == rank + q * SLOT).astype(jnp.float32)
                gates += jnp.sum(pick * gate, axis=1, keepdims=True)
                across = slice(q * tokens, (q + 1) * tokens)
                down = slice(j * wide, (j + 1) * wide)
                pick_ref[p, down, across] = pick.astype(jnp.bfloat16)
                place_ref[p, across, down] = pick.T.astype(jnp.bfloat16)
            gcol[j, p * wide : (p + 1) * wide, :] = gates
    gather_rows(n, local, pick_ref, token_refs, xs)

    @pl.loop(0, local)
    def _(e):
        for f in range(0, hidden, cols):
            part = slice(f, f + cols)
            gate_pre = dot(xs[e], wg_ref[e, :, part])
            up_pre = dot(xs[e], wu_ref[e, :, part])
            sig = jax.nn.sigmoid(gate_pre)
            weighted = gcol[e] * sig
            a_ref[e, part, :] = (weighted * up_pre * (1.0 + gate_pre * (1.0 - sig))).T
            b_ref[e, part, :] = (weighted * gate_pre).T


def vmem(array):
    return pltpu.with_memory_space_constraint(array, pltpu.VMEM)


def load_kernel(count, *refs):
    sources, results, sems = refs[:count], refs[-count - 1 : -1], refs[-1]
    copies = [
        pltpu.make_async_copy(source.at[e], result.at[e], sems.at[i, e])
        for i, (source, result) in enumerate(zip(sources, results))
        for e in range(source.shape[0])
    ]
    for copy in copies:
        copy.start()
    for copy in copies:
        copy.wait()


def load(arrays, after):
    count = len(arrays)
    return pl.pallas_call(
        functools.partial(load_kernel, count),
        in_specs=[pl.BlockSpec(memory_space=pltpu.HBM)] * count + [pl.BlockSpec(memory_space=pl.ANY)],
        out_specs=[pl.BlockSpec(memory_space=pltpu.VMEM)] * count,
        out_shape=[pltpu.VMEM(w.shape, w.dtype) for w in arrays],
        scratch_shapes=[pltpu.SemaphoreType.DMA((count, arrays[0].shape[0]))],
        compiler_params=params(1),
        cost_estimate=pl.CostEstimate(
            flops=0, bytes_accessed=4 * count * arrays[0].size, transcendentals=0
        ),
    )(*[pltpu.with_memory_space_constraint(w, pltpu.HBM) for w in arrays], after)


def pre(axis, n, tables, tokens, wg, wu):
    local, features, hidden = wg.shape
    rows = n * SLOT
    across, down = 2 * tables[0].shape[1], 2 * SLOT * local
    return pl.pallas_call(
        functools.partial(pre_kernel, axis, n, local, [len(t) for t in tokens]),
        out_shape=[
            jax.ShapeDtypeStruct((local, hidden, rows), jnp.float32),
            jax.ShapeDtypeStruct((local, hidden, rows), jnp.float32),
            jax.ShapeDtypeStruct((n // 2, down, across), jnp.bfloat16),
            jax.ShapeDtypeStruct((n // 2, across, down), jnp.bfloat16),
        ],
        scratch_shapes=[
            pltpu.VMEM((local, rows, features), jnp.bfloat16),
            pltpu.VMEM((local, rows, 1), jnp.float32),
        ],
        compiler_params=params(PRE_MIB * max(1, n // 4)),
        cost_estimate=pl.CostEstimate(
            flops=4 * local * rows * features * hidden,
            bytes_accessed=4 * local * features * hidden,
            transcendentals=local * rows * hidden,
        ),
    )(*tables, *[block for t in tokens for block in t], vmem(wg), vmem(wu))


def back_kernel(n, local, counts, pick_ref, *refs):
    token_refs, refs = split(refs, counts)
    wd_ref, a_ref, b_ref, _, _, hg_ref, hu_ref, gs, weight, sems = refs
    hidden = wd_ref.shape[1]
    held = weight.shape[0]
    cols = hidden // 2

    def fetch(e, i):
        part = pl.ds(i * cols, cols)
        slot = lax.rem(e, held)
        return pltpu.make_async_copy(wd_ref.at[e, part], weight.at[slot, part], sems.at[slot, i])

    for e in range(held):
        for i in range(2):
            fetch(e, i).start()
    gather_rows(n, local, pick_ref, token_refs, gs)

    @pl.loop(0, local)
    def _(e):
        for i in range(2):
            part = slice(i * cols, (i + 1) * cols)
            fetch(e, i).wait()
            back = dot(weight[lax.rem(e, held), part, :], gs[e], NT)
            hg_ref[e, part, :] = (back * a_ref[e, part, :]).astype(jnp.bfloat16)
            hu_ref[e, part, :] = (back * b_ref[e, part, :]).astype(jnp.bfloat16)

            @pl.when(e + held < local)
            def _():
                fetch(e + held, i).start()


def back(n, pick, tokens, wd, a, b, wg, wu):
    local, hidden, features = wd.shape
    rows = n * SLOT
    blocks = [block for t in tokens for block in t]
    shape = jax.ShapeDtypeStruct((local, hidden, rows), jnp.bfloat16)
    inside, outside = pl.BlockSpec(memory_space=pltpu.VMEM), pl.BlockSpec(memory_space=pltpu.HBM)
    return pl.pallas_call(
        functools.partial(back_kernel, n, local, [len(t) for t in tokens]),
        in_specs=[inside] * (1 + len(blocks)) + [outside] + [inside] * 4,
        out_shape=[shape, shape],
        scratch_shapes=[
            pltpu.VMEM((local, rows, features), jnp.bfloat16),
            pltpu.VMEM((min(local, 2), hidden, features), jnp.bfloat16),
            pltpu.SemaphoreType.DMA((min(local, 2), 2)),
        ],
        compiler_params=params(BACK_MIB * max(1, n // 8)),
        cost_estimate=pl.CostEstimate(
            flops=2 * local * rows * features * hidden,
            bytes_accessed=2 * local * features * hidden,
            transcendentals=0,
        ),
    )(pick, *blocks, pltpu.with_memory_space_constraint(wd, pltpu.HBM), a, b, vmem(wg), vmem(wu))


def out_kernel(n, local, orders, chunk, place_ref, hg_ref, hu_ref, wg_ref, wu_ref, *rest):
    outs, rows_ref = rest[:-1], rest[-1]
    wide = 2 * SLOT
    cols = wg_ref.shape[1] // CHUNKS
    part = slice(chunk * cols, (chunk + 1) * cols)
    for e in range(local):
        rows = dot(wg_ref[e, part, :], hg_ref[e]) + dot(wu_ref[e, part, :], hu_ref[e])
        rows = rows.astype(jnp.bfloat16)
        for p in range(n // 2):
            rows_ref[p, :, e * wide : (e + 1) * wide] = rows[:, p * wide : (p + 1) * wide]
    tokens = place_ref.shape[1] // 2
    for p in range(n // 2):
        total = dot(place_ref[p], rows_ref[p], NT)
        for out_ref, order in zip(outs, orders):
            for i, g in enumerate(order):
                if g // 2 == p:
                    mine = total[g % 2 * tokens : (g % 2 + 1) * tokens, :]
                    out_ref[i] = mine.astype(out_ref.dtype)


def partial_sums(n, orders, chunk, place, hg, hu, wg, wu):
    local, features, hidden = wg.shape
    tokens = place.shape[1] // 2
    rows = n * SLOT
    cols = features // CHUNKS
    shapes = [(len(order), tokens, cols) for order in orders]
    types = [jnp.float32] + [jnp.bfloat16] * (len(orders) - 1)
    return pl.pallas_call(
        functools.partial(out_kernel, n, local, orders, chunk),
        out_shape=[jax.ShapeDtypeStruct(s, t) for s, t in zip(shapes, types)],
        scratch_shapes=[pltpu.VMEM((n // 2, cols, 2 * SLOT * local), jnp.bfloat16)],
        compiler_params=params(OUT_MIB * max(1, n // 4)),
        cost_estimate=pl.CostEstimate(
            flops=local * rows * cols * hidden,
            bytes_accessed=local * cols * hidden,
            transcendentals=0,
        ),
    )(place, hg, hu, vmem(wg), vmem(wu))


def sum_kernel(*refs):
    parts, out_ref = refs[:-1], refs[-1]
    each = len(parts) // CHUNKS
    cols = out_ref.shape[1] // CHUNKS
    for c in range(CHUNKS):
        own, *others = parts[c * each : (c + 1) * each]
        total = own[0]
        for other in others:
            total += other[0].astype(jnp.float32)
        out_ref[:, c * cols : (c + 1) * cols] = total.astype(jnp.bfloat16)


def body(axis, saved_input, grad_out, routes, route_gates, gate_proj, up_proj, down_proj):
    n = lax.axis_size(axis)
    local = gate_proj.shape[0]
    experts = n * local
    tokens, features = saved_input.shape

    def swap(array, k):
        return lax.ppermute(array, axis, [(i, i ^ k) for i in range(n)])

    table = rank_table(routes.T, route_gates.T, experts)
    tables = [table] + [swap(table, k) for k in range(1, n)]
    if n == 4:
        half = tokens // 2
        upper, lower = saved_input[:half], saved_input[half:]
        near = [[]] + [[swap(upper, k), swap(lower, k)] for k in (1, 2)]
        gate_proj, up_proj = load((gate_proj, up_proj), table)
        relayed = [swap(near[1][0], 2), swap(near[2][1], 1)]
        x_blocks = [[saved_input], near[1], near[2], relayed]
        grad_out, *_ = lax.optimization_barrier((grad_out, near[1], near[2]))
    else:
        x_blocks = [[saved_input]] + [[swap(saved_input, k)] for k in range(1, n)]
        gate_proj, up_proj = load((gate_proj, up_proj), table)
    g_blocks = [[grad_out]] + [[swap(grad_out, k)] for k in range(1, n)]
    a, b, pick, place = pre(axis, n, tables, x_blocks, gate_proj, up_proj)
    hg, hu = back(n, pick, g_blocks, down_proj, a, b, gate_proj, up_proj)
    parts = []
    for chunk in range(CHUNKS):
        if n == 4:
            first, last = (1, 2) if chunk % 2 == 0 else (2, 1)
            orders = ((0,), (first, 3), (last,))
            own, two, one = partial_sums(n, orders, chunk, place, hg, hu, gate_proj, up_proj)
            two = swap(two, first)
            relay = (two[1:2].astype(jnp.float32) + one.astype(jnp.float32)).astype(jnp.bfloat16)
            parts += [own, two[:1], swap(relay, last)]
        else:
            orders = tuple((k,) for k in range(n))
            own, *others = partial_sums(n, orders, chunk, place, hg, hu, gate_proj, up_proj)
            parts += [own] + [swap(other, k + 1) for k, other in enumerate(others)]
    return pl.pallas_call(
        sum_kernel,
        out_shape=jax.ShapeDtypeStruct((tokens, features), jnp.bfloat16),
        compiler_params=params(8),
    )(*parts)


def solution(mesh):
    tokens = P(("dp", "expert"), None)
    weights = P("expert", None, None)
    return jax.shard_map(
        functools.partial(body, "expert"),
        mesh=mesh,
        in_specs=(tokens, tokens, tokens, tokens, weights, weights, weights),
        out_specs=tokens,
        check_vma=False,
    )
```

time: 115 us -> 90.3 us (0.79)
  local copies, waits for them, and re-layouts: 26 us -> 1.84 us
  waiting for transfers between devices: 13.8 us -> 23.1 us
  Pallas kernels: 48.9 us -> 41.2 us
    unnamed x62 -> x6, local copies, waits for them, and re-layouts: 24.9 us -> 0.74 us
    ppermute x20, waiting for transfers between devices: 13.8 us -> 23.1 us  [swap(): return lax.ppermute(array, axis, [(i, i ^ k) for i in range(n)])]
    pallas_call x6 -> x7, Pallas kernels: 46.4 us -> 38.8 us  [the longest x1 11.4 us: pre(): pl.pallas_call(functools.partial(pre_kernel, axis, n, local, [len(t) for...]
  transfers between devices with their start and end apart: 20 -> 20, of which waited for: 8 -> 11; matrix products, arithmetic and copies ran while one was open for 0% -> 0% of each run, Pallas kernels for 24% -> 31%
where the time goes in v3:
time: 90.3 us; the launch traced here: 90 us
  Pallas kernels  41.2 us (46%)
  starting transfers between devices  23.5 us (26%)
  waiting for transfers between devices  23.1 us (26%)
  local copies, waits for them, and re-layouts  1.84 us (2%)
    ppermute x20, starting transfers between devices, swap(): return lax.ppermute(array, axis, [(i, i ^ k) for i in range(n)])  23.5 us
    ppermute x20, waiting for transfers between devices, swap(): return lax.ppermute(array, axis, [(i, i ^ k) for i in range(n)])  23.1 us
    pallas_call x1, Pallas kernels, pre(): pl.pallas_call(functools.partial(pre_kernel, axis, n, local, [len(t) for...  11.4 us
    pallas_call x1, Pallas kernels, back(): pl.pallas_call(functools.partial(back_kernel, n, local, [len(t) for t in...  10.5 us
    pallas_call x4, Pallas kernels, partial_sums(): pl.pallas_call(functools.partial(out_kernel, n, local, orders, chunk), ou...  8.58 us
    pallas_call x1, Pallas kernels, load(): pl.pallas_call(functools.partial(load_kernel, count), in_specs=[pl.BlockS...  8.3 us
  transfers between devices with their start and end apart: 20, of which 11 were waited for; matrix products, arithmetic and copies ran while one was open for 0% of the time, Pallas kernels for 31%

profile of v3, /device:TPU:0, one launch (start us, length us, event | category | flops | bytes accessed | tf_op | source)
XLA Modules:
  0.0 90.0 jit_solution(2316989690878383862)
XLA Ops:
  0.0 1.1 %fusion = (bf16[64,2048]{1,0:T(8,128)(2,1)S(1)}, bf16[64,2048]{1,0:T(8,128)(2,1)S(1)}) fusion(bf16[128,2048]{1,0:T(8,128)(2,1)} %refs_4_.2), kind=kLoop, calls=%fused_computation.4 | loop fusion | bytes 1048576 | tf_op jit(solution)/shard_map/slice | solution.py:302
  1.1 3.0 %collective-permute-start.6 = (bf16[64,2048]{1,0:T(8,128)(2,1)S(1)}, bf16[64,2048]{1,0:T(8,128)(2,1)S(1)}, u32[]{:S(2)}, u32[]{:S(2)}) collective-permute-start(bf16[64,2048]{1,0:T(8,128)(2,1)S(1)} %get-tuple-element.47), channel_id=1, source_target_pairs={{0,2},{1,3},{2,0},{3,1},{4,6},{5,7},{6,4},{7,5},{8,10},{9,11},{10,... | collective-permute-start | bytes 786440 | tf_op jit(solution)/shard_map/ppermute | solution.py:296
  4.1 1.5 %collective-permute-start.3 = (bf16[64,2048]{1,0:T(8,128)(2,1)S(1)}, bf16[64,2048]{1,0:T(8,128)(2,1)S(1)}, u32[]{:S(2)}, u32[]{:S(2)}) collective-permute-start(bf16[64,2048]{1,0:T(8,128)(2,1)S(1)} %get-tuple-element.48), channel_id=1, source_target_pairs={{0,1},{1,0},{2,3},{3,2},{4,5},{5,4},{6,7},{7,6},{8,9},{9,8},{10,11... | collective-permute-start | bytes 786440 | tf_op jit(solution)/shard_map/ppermute | solution.py:296
  5.6 0.5 collective-permute-start.4
  6.1 0.1 collective-permute-start.5
  6.2 5.0 %collective-permute-done.6.refs_8_ = bf16[64,2048]{1,0:T(8,128)(2,1)S(1)} collective-permute-done((bf16[64,2048]{1,0:T(8,128)(2,1)S(1)}, bf16[64,2048]{1,0:T(8,128)(2,1)S(1)}, u32[]{:S(2)}, u32[]{:S(2)}) %collective-permute-start.6) | collective-permute-done | bytes 262176 | tf_op jit(solution)/shard_map/ppermute | solution.py:296
  11.2 2.0 %collective-permute-start.8 = (bf16[64,2048]{1,0:T(8,128)(2,1)S(1)}, bf16[64,2048]{1,0:T(8,128)(2,1)S(1)}, u32[]{:S(2)}, u32[]{:S(2)}) collective-permute-start(bf16[64,2048]{1,0:T(8,128)(2,1)S(1)} %collective-permute-done.6.refs_8_), channel_id=1, source_target_pairs={{0,1},{1,0},{2,3},{3,2},{4,5},{5,4},{6,7},{7,6},{8,9},{9,8},{10,11... | collective-permute-start | bytes 786440 | tf_op jit(solution)/shard_map/ppermute | solution.py:296
  13.3 0.1 collective-permute-done.3.refs_5_
  13.3 1.5 %collective-permute-start.7 = (bf16[64,2048]{1,0:T(8,128)(2,1)S(1)}, bf16[64,2048]{1,0:T(8,128)(2,1)S(1)}, u32[]{:S(2)}, u32[]{:S(2)}) collective-permute-start(bf16[64,2048]{1,0:T(8,128)(2,1)S(1)} %collective-permute-done.3.refs_5_), channel_id=1, source_target_pairs={{0,2},{1,3},{2,0},{3,1},{4,6},{5,7},{6,4},{7,5},{8,10},{9,11},{10,... | collective-permute-start | bytes 786440 | tf_op jit(solution)/shard_map/ppermute | solution.py:296
  14.8 1.5 %shard_map.73.refs_2_.refs_0_ = bf16[32,128]{1,0:T(8,128)(2,1)} custom-call(s32[8,128]{1,0:T(8,128)} %bitcast.2, bf16[8,128]{1,0:T(8,128)(2,1)} %bitcast.3), custom_call_target="tpu_custom_call" | custom-call | tf_op jit(solution)/shard_map/pallas_call | solution.py:56
  16.3 0.0 copy-start.1
  16.3 0.0 copy-start
  16.3 1.5 %collective-permute-start.2 = (bf16[32,128]{1,0:T(8,128)(2,1)}, bf16[32,128]{1,0:T(8,128)(2,1)S(1)}, u32[]{:S(2)}, u32[]{:S(2)}) collective-permute-start(bf16[32,128]{1,0:T(8,128)(2,1)} %shard_map.73.refs_2_.refs_0_), channel_id=1, source_target_pairs={{0,3},{1,2},{2,1},{3,0},{4,7},{5,6},{6,5},{7,4},{8,11},{9,10},{10,... | collective-permute-start | bytes 24584 | tf_op jit(solution)/shard_map/ppermute | solution.py:296
  17.8 1.2 %collective-permute-done.4.refs_6_ = bf16[64,2048]{1,0:T(8,128)(2,1)S(1)} collective-permute-done((bf16[64,2048]{1,0:T(8,128)(2,1)S(1)}, bf16[64,2048]{1,0:T(8,128)(2,1)S(1)}, u32[]{:S(2)}, u32[]{:S(2)}) %collective-permute-start.4) | collective-permute-done | bytes 262176 | tf_op jit(solution)/shard_map/ppermute | solution.py:296
  18.9 0.0 collective-permute-start.1
  19.0 0.0 collective-permute-done.5.refs_7_
  19.0 2.0 %collective-permute-start = (bf16[32,128]{1,0:T(8,128)(2,1)}, bf16[32,128]{1,0:T(8,128)(2,1)S(1)}, u32[]{:S(2)}, u32[]{:S(2)}) collective-permute-start(bf16[32,128]{1,0:T(8,128)(2,1)} %shard_map.73.refs_2_.refs_0_), channel_id=1, source_target_pairs={{0,1},{1,0},{2,3},{3,2},{4,5},{5,4},{6,7},{7,6},{8,9},{9,8},{10,11... | collective-permute-start | bytes 24584 | tf_op jit(solution)/shard_map/ppermute | solution.py:296
  21.0 0.0 copy-start.2
  21.0 0.7 copy-done.2
  21.7 8.3 %shard_map.74 = (bf16[4,2048,768]{2,1,0:T(8,128)(2,1)S(1)}, bf16[4,2048,768]{2,1,0:T(8,128)(2,1)S(1)}) custom-call(bf16[4,2048,768]{2,1,0:T(8,128)(2,1)} %refs_0_.1, bf16[4,2048,768]{2,1,0:T(8,128)(2,1)} %refs_1_.1, bf16[32,128]{1,0:T(8,128)(2,1)S(1)} %copy-done.2), custom_call_target="tpu_custom_call" | custom-call | bytes 50331648 | tf_op jit(solution)/shard_map/pallas_call | solution.py:144
  30.0 0.0 collective-permute-done.2.refs_3_
  30.0 0.0 copy-done.1
  30.0 1.6 %collective-permute-start.11 = (bf16[128,2048]{1,0:T(8,128)(2,1)S(1)}, bf16[128,2048]{1,0:T(8,128)(2,1)S(1)}, u32[]{:S(2)}, u32[]{:S(2)}) collective-permute-start(bf16[128,2048]{1,0:T(8,128)(2,1)S(1)} %copy-done.1), channel_id=1, source_target_pairs={{0,3},{1,2},{2,1},{3,0},{4,7},{5,6},{6,5},{7,4},{8,11},{9,10},{10,... | collective-permute-start | bytes 1572872 | tf_op jit(solution)/shard_map/ppermute | solution.py:296
  31.6 0.0 collective-permute-done.1.refs_2_
  31.6 0.1 collective-permute-start.10
  31.7 0.0 collective-permute-done.refs_1_
  31.7 1.9 %collective-permute-start.9 = (bf16[128,2048]{1,0:T(8,128)(2,1)S(1)}, bf16[128,2048]{1,0:T(8,128)(2,1)S(1)}, u32[]{:S(2)}, u32[]{:S(2)}) collective-permute-start(bf16[128,2048]{1,0:T(8,128)(2,1)S(1)} %copy-done.1), channel_id=1, source_target_pairs={{0,1},{1,0},{2,3},{3,2},{4,5},{5,4},{6,7},{7,6},{8,9},{9,8},{10,11... | collective-permute-start | bytes 1572872 | tf_op jit(solution)/shard_map/ppermute | solution.py:296
  33.6 0.0 collective-permute-done.8.refs_10_
  33.6 0.0 collective-permute-done.7.refs_9_
  33.6 0.0 copy-done
  33.6 11.4 %shard_map.75 = (f32[4,768,256]{2,1,0:T(8,128)S(1)}, f32[4,768,256]{2,1,0:T(8,128)S(1)}, bf16[2,512,256]{2,1,0:T(8,128)(2,1)S(1)}, bf16[2,256,512]{2,1,0:T(8,128)(2,1)S(1)}) custom-call(bf16[32,128]{1,0:T(8,128)(2,1)S(1)} %copy-done.2, bf16[32,128]{1,0:T(8,128)(2,1)S(1)} %collective-permute-done.refs_1_, bf16[32,128]{1,0:T(8,128)(2,1)S(1)} %collective-permute-done.1.refs_2_, ...), custom_call_target="tpu_custom_call" | custom-call | flops 6442450944 | bytes 25165824 | tf_op jit(solution)/shard_map/pallas_call | solution.py:161
  45.0 0.8 collective-permute-done.11.refs_3_
  45.8 6.8 %collective-permute-done.10.refs_2_ = bf16[128,2048]{1,0:T(8,128)(2,1)S(1)} collective-permute-done((bf16[128,2048]{1,0:T(8,128)(2,1)S(1)}, bf16[128,2048]{1,0:T(8,128)(2,1)S(1)}, u32[]{:S(2)}, u32[]{:S(2)}) %collective-permute-start.10) | collective-permute-done | bytes 524320 | tf_op jit(solution)/shard_map/ppermute | solution.py:296
  52.7 0.1 collective-permute-done.9.refs_1_
  52.8 10.5 %shard_map.76 = (bf16[4,768,256]{2,1,0:T(8,128)(2,1)S(1)}, bf16[4,768,256]{2,1,0:T(8,128)(2,1)S(1)}) custom-call(bf16[2,512,256]{2,1,0:T(8,128)(2,1)S(1)} %get-tuple-element.29.pick_ref, bf16[128,2048]{1,0:T(8,128)(2,1)S(1)} %copy-done.1, bf16[128,2048]{1,0:T(8,128)(2,1)S(1)} %collective-permute-done.9.refs_1_, ...), custom_call_target="tpu_custom_call" | custom-call | flops 3221225472 | bytes 12582912 | tf_op jit(solution)/shard_map/pallas_call | solution.py:219
  63.3 2.1 %shard_map.80 = (f32[1,128,512]{2,1,0:T(8,128)S(1)}, bf16[2,128,512]{2,1,0:T(8,128)(2,1)S(1)}, bf16[1,128,512]{2,1,0:T(8,128)(2,1)S(1)}) custom-call(bf16[2,256,512]{2,1,0:T(8,128)(2,1)S(1)} %get-tuple-element.28.place_ref, bf16[4,768,256]{2,1,0:T(8,128)(2,1)S(1)} %get-tuple-element.33.hg_ref, bf16[4,768,256]{2,1,0:T(8,128)(2,1)S(1)} %get-tuple-element.34.hu_ref, ...), custom_call_target="tpu_custom_call" | custom-call | flops 402653184 | bytes 1572864 | tf_op jit(solution)/shard_map/pallas_call | solution.py:264
  65.4 1.0 %collective-permute-start.18 = (bf16[2,128,512]{2,1,0:T(8,128)(2,1)S(1)}, bf16[2,128,512]{2,1,0:T(8,128)(2,1)S(1)}, u32[]{:S(2)}, u32[]{:S(2)}) collective-permute-start(bf16[2,128,512]{2,1,0:T(8,128)(2,1)S(1)} %get-tuple-element.45), channel_id=1, source_target_pairs={{0,2},{1,3},{2,0},{3,1},{4,6},{5,7},{6,4},{7,5},{8,10},{9,11},{10,... | collective-permute-start | bytes 786440 | tf_op jit(solution)/shard_map/ppermute | solution.py:296
  66.4 2.1 %shard_map.79 = (f32[1,128,512]{2,1,0:T(8,128)S(1)}, bf16[2,128,512]{2,1,0:T(8,128)(2,1)S(1)}, bf16[1,128,512]{2,1,0:T(8,128)(2,1)S(1)}) custom-call(bf16[2,256,512]{2,1,0:T(8,128)(2,1)S(1)} %get-tuple-element.28.place_ref, bf16[4,768,256]{2,1,0:T(8,128)(2,1)S(1)} %get-tuple-element.33.hg_ref, bf16[4,768,256]{2,1,0:T(8,128)(2,1)S(1)} %get-tuple-element.34.hu_ref, ...), custom_call_target="tpu_custom_call" | custom-call | flops 402653184 | bytes 1572864 | tf_op jit(solution)/shard_map/pallas_call | solution.py:264
  68.5 1.1 %collective-permute-start.16 = (bf16[2,128,512]{2,1,0:T(8,128)(2,1)S(1)}, bf16[2,128,512]{2,1,0:T(8,128)(2,1)S(1)}, u32[]{:S(2)}, u32[]{:S(2)}) collective-permute-start(bf16[2,128,512]{2,1,0:T(8,128)(2,1)S(1)} %get-tuple-element.42), channel_id=1, source_target_pairs={{0,1},{1,0},{2,3},{3,2},{4,5},{5,4},{6,7},{7,6},{8,9},{9,8},{10,11... | collective-permute-start | bytes 786440 | tf_op jit(solution)/shard_map/ppermute | solution.py:296
  69.7 2.1 %shard_map.78 = (f32[1,128,512]{2,1,0:T(8,128)S(1)}, bf16[2,128,512]{2,1,0:T(8,128)(2,1)S(1)}, bf16[1,128,512]{2,1,0:T(8,128)(2,1)S(1)}) custom-call(bf16[2,256,512]{2,1,0:T(8,128)(2,1)S(1)} %get-tuple-element.28.place_ref, bf16[4,768,256]{2,1,0:T(8,128)(2,1)S(1)} %get-tuple-element.33.hg_ref, bf16[4,768,256]{2,1,0:T(8,128)(2,1)S(1)} %get-tuple-element.34.hu_ref, ...), custom_call_target="tpu_custom_call" | custom-call | flops 402653184 | bytes 1572864 | tf_op jit(solution)/shard_map/pallas_call | solution.py:264
  71.8 0.7 collective-permute-start.14
  72.6 2.1 %shard_map.77 = (f32[1,128,512]{2,1,0:T(8,128)S(1)}, bf16[2,128,512]{2,1,0:T(8,128)(2,1)S(1)}, bf16[1,128,512]{2,1,0:T(8,128)(2,1)S(1)}) custom-call(bf16[2,256,512]{2,1,0:T(8,128)(2,1)S(1)} %get-tuple-element.28.place_ref, bf16[4,768,256]{2,1,0:T(8,128)(2,1)S(1)} %get-tuple-element.33.hg_ref, bf16[4,768,256]{2,1,0:T(8,128)(2,1)S(1)} %get-tuple-element.34.hu_ref, ...), custom_call_target="tpu_custom_call" | custom-call | flops 402653184 | bytes 1572864 | tf_op jit(solution)/shard_map/pallas_call | solution.py:264
  74.7 1.5 %collective-permute-start.12 = (bf16[2,128,512]{2,1,0:T(8,128)(2,1)S(1)}, bf16[2,128,512]{2,1,0:T(8,128)(2,1)S(1)}, u32[]{:S(2)}, u32[]{:S(2)}) collective-permute-start(bf16[2,128,512]{2,1,0:T(8,128)(2,1)S(1)} %get-tuple-element.36), channel_id=1, source_target_pairs={{0,1},{1,0},{2,3},{3,2},{4,5},{5,4},{6,7},{7,6},{8,9},{9,8},{10,11... | collective-permute-start | bytes 786440 | tf_op jit(solution)/shard_map/ppermute | solution.py:296
  76.2 0.0 collective-permute-done.18
  76.2 0.7 collective-permute-start.19
  76.9 0.0 collective-permute-done.16
  77.0 1.4 %collective-permute-start.17 = (bf16[1,128,512]{2,1,0:T(8,128)(2,1)S(1)}, bf16[1,128,512]{2,1,0:T(8,128)(2,1)S(1)}, u32[]{:S(2)}, u32[]{:S(2)}) collective-permute-start(bf16[1,128,512]{2,1,0:T(8,128)(2,1)S(1)} %add_convert_fusion.1), channel_id=1, source_target_pairs={{0,2},{1,3},{2,0},{3,1},{4,6},{5,7},{6,4},{7,5},{8,10},{9,11},{10,... | collective-permute-start | bytes 393224 | tf_op jit(solution)/shard_map/ppermute | solution.py:296
  78.4 2.5 %collective-permute-done.14 = bf16[2,128,512]{2,1,0:T(8,128)(2,1)S(1)} collective-permute-done((bf16[2,128,512]{2,1,0:T(8,128)(2,1)S(1)}, bf16[2,128,512]{2,1,0:T(8,128)(2,1)S(1)}, u32[]{:S(2)}, u32[]{:S(2)}) %collective-permute-start.14) | collective-permute-done | bytes 262176 | tf_op jit(solution)/shard_map/ppermute | solution.py:296
  80.9 0.1 collective-permute-start.15
  80.9 3.1 %collective-permute-done.12 = bf16[2,128,512]{2,1,0:T(8,128)(2,1)S(1)} collective-permute-done((bf16[2,128,512]{2,1,0:T(8,128)(2,1)S(1)}, bf16[2,128,512]{2,1,0:T(8,128)(2,1)S(1)}, u32[]{:S(2)}, u32[]{:S(2)}) %collective-permute-start.12) | collective-permute-done | bytes 262176 | tf_op jit(solution)/shard_map/ppermute | solution.py:296
  84.1 1.4 %collective-permute-start.13 = (bf16[1,128,512]{2,1,0:T(8,128)(2,1)S(1)}, bf16[1,128,512]{2,1,0:T(8,128)(2,1)S(1)}, u32[]{:S(2)}, u32[]{:S(2)}) collective-permute-start(bf16[1,128,512]{2,1,0:T(8,128)(2,1)S(1)} %add_convert_fusion.3), channel_id=1, source_target_pairs={{0,2},{1,3},{2,0},{3,1},{4,6},{5,7},{6,4},{7,5},{8,10},{9,11},{10,... | collective-permute-start | bytes 393224 | tf_op jit(solution)/shard_map/ppermute | solution.py:296
  85.5 0.8 collective-permute-done.19.refs_11_
  86.4 0.0 collective-permute-done.17.refs_8_
  86.4 1.4 %collective-permute-done.15.refs_5_ = bf16[1,128,512]{2,1,0:T(8,128)(2,1)S(1)} collective-permute-done((bf16[1,128,512]{2,1,0:T(8,128)(2,1)S(1)}, bf16[1,128,512]{2,1,0:T(8,128)(2,1)S(1)}, u32[]{:S(2)}, u32[]{:S(2)}) %collective-permute-start.15) | collective-permute-done | bytes 131104 | tf_op jit(solution)/shard_map/ppermute | solution.py:296
  87.8 1.3 %collective-permute-done.13.refs_2_ = bf16[1,128,512]{2,1,0:T(8,128)(2,1)S(1)} collective-permute-done((bf16[1,128,512]{2,1,0:T(8,128)(2,1)S(1)}, bf16[1,128,512]{2,1,0:T(8,128)(2,1)S(1)}, u32[]{:S(2)}, u32[]{:S(2)}) %collective-permute-start.13) | collective-permute-done | bytes 131104 | tf_op jit(solution)/shard_map/ppermute | solution.py:296
  89.1 0.9 %shard_map.81 = bf16[128,2048]{1,0:T(8,128)(2,1)} custom-call(f32[1,128,512]{2,1,0:T(8,128)S(1)} %get-tuple-element.35.refs_0_, bf16[1,128,512]{2,1,0:T(8,128)(2,1)S(1)} %slice.40.refs_1_, bf16[1,128,512]{2,1,0:T(8,128)(2,1)S(1)} %collective-permute-done.13.refs_2_, f32[1,128,512]{2,1,0:T(8,128)S(1)} %get-tuple-element.38.refs_3_, ...), custom_call_target="tpu_custom_call" | custom-call | tf_op jit(solution)/shard_map/pallas_call | solution.py:327
  (8 shorter events, 0.2 us)
Async XLA Ops:
  1.1 10.2 %collective-permute-start.6 = (bf16[64,2048]{1,0:T(8,128)(2,1)S(1)}, bf16[64,2048]{1,0:T(8,128)(2,1)S(1)}, u32[]{:S(2)}, u32[]{:S(2)}) collective-permute-start(bf16[64,2048]{1,0:T(8,128)(2,1)S(1)} %get-tuple-element.47), channel_id=1, source_target_pairs={{0,2},{1,3},{2,0},{3,1},{4,6},{5,7},{6,4},{7,5},{8,10},{9,11},{10,... | collective-permute-start | bytes 786440 | tf_op jit(solution)/shard_map/ppermute | solution.py:296
  4.1 9.2 %collective-permute-start.3 = (bf16[64,2048]{1,0:T(8,128)(2,1)S(1)}, bf16[64,2048]{1,0:T(8,128)(2,1)S(1)}, u32[]{:S(2)}, u32[]{:S(2)}) collective-permute-start(bf16[64,2048]{1,0:T(8,128)(2,1)S(1)} %get-tuple-element.48), channel_id=1, source_target_pairs={{0,1},{1,0},{2,3},{3,2},{4,5},{5,4},{6,7},{7,6},{8,9},{9,8},{10,11... | collective-permute-start | bytes 786440 | tf_op jit(solution)/shard_map/ppermute | solution.py:296
  5.6 13.4 %collective-permute-start.4 = (bf16[64,2048]{1,0:T(8,128)(2,1)S(1)}, bf16[64,2048]{1,0:T(8,128)(2,1)S(1)}, u32[]{:S(2)}, u32[]{:S(2)}) collective-permute-start(bf16[64,2048]{1,0:T(8,128)(2,1)S(1)} %get-tuple-element.47), channel_id=1, source_target_pairs={{0,1},{1,0},{2,3},{3,2},{4,5},{5,4},{6,7},{7,6},{8,9},{9,8},{10,11... | collective-permute-start | bytes 786440 | tf_op jit(solution)/shard_map/ppermute | solution.py:296
  6.1 12.9 %collective-permute-start.5 = (bf16[64,2048]{1,0:T(8,128)(2,1)S(1)}, bf16[64,2048]{1,0:T(8,128)(2,1)S(1)}, u32[]{:S(2)}, u32[]{:S(2)}) collective-permute-start(bf16[64,2048]{1,0:T(8,128)(2,1)S(1)} %get-tuple-element.48), channel_id=1, source_target_pairs={{0,2},{1,3},{2,0},{3,1},{4,6},{5,7},{6,4},{7,5},{8,10},{9,11},{10,... | collective-permute-start | bytes 786440 | tf_op jit(solution)/shard_map/ppermute | solution.py:296
  11.2 22.3 %collective-permute-start.8 = (bf16[64,2048]{1,0:T(8,128)(2,1)S(1)}, bf16[64,2048]{1,0:T(8,128)(2,1)S(1)}, u32[]{:S(2)}, u32[]{:S(2)}) collective-permute-start(bf16[64,2048]{1,0:T(8,128)(2,1)S(1)} %collective-permute-done.6.refs_8_), channel_id=1, source_target_pairs={{0,1},{1,0},{2,3},{3,2},{4,5},{5,4},{6,7},{7,6},{8,9},{9,8},{10,11... | collective-permute-start | bytes 786440 | tf_op jit(solution)/shard_map/ppermute | solution.py:296
  13.3 20.2 %collective-permute-start.7 = (bf16[64,2048]{1,0:T(8,128)(2,1)S(1)}, bf16[64,2048]{1,0:T(8,128)(2,1)S(1)}, u32[]{:S(2)}, u32[]{:S(2)}) collective-permute-start(bf16[64,2048]{1,0:T(8,128)(2,1)S(1)} %collective-permute-done.3.refs_5_), channel_id=1, source_target_pairs={{0,2},{1,3},{2,0},{3,1},{4,6},{5,7},{6,4},{7,5},{8,10},{9,11},{10,... | collective-permute-start | bytes 786440 | tf_op jit(solution)/shard_map/ppermute | solution.py:296
  16.3 13.7 %copy-start.1 = (bf16[128,2048]{1,0:T(8,128)(2,1)S(1)}, bf16[128,2048]{1,0:T(8,128)(2,1)}, u32[]{:S(2)}) copy-start(bf16[128,2048]{1,0:T(8,128)(2,1)} %refs_0_.2) | copy-start | bytes 1572868
  16.3 17.3 %copy-start = (bf16[128,2048]{1,0:T(8,128)(2,1)S(1)}, bf16[128,2048]{1,0:T(8,128)(2,1)}, u32[]{:S(2)}) copy-start(bf16[128,2048]{1,0:T(8,128)(2,1)} %refs_4_.2) | copy-start | bytes 1572868
  16.3 13.7 %collective-permute-start.2 = (bf16[32,128]{1,0:T(8,128)(2,1)}, bf16[32,128]{1,0:T(8,128)(2,1)S(1)}, u32[]{:S(2)}, u32[]{:S(2)}) collective-permute-start(bf16[32,128]{1,0:T(8,128)(2,1)} %shard_map.73.refs_2_.refs_0_), channel_id=1, source_target_pairs={{0,3},{1,2},{2,1},{3,0},{4,7},{5,6},{6,5},{7,4},{8,11},{9,10},{10,... | collective-permute-start | bytes 24584 | tf_op jit(solution)/shard_map/ppermute | solution.py:296
  18.9 12.6 %collective-permute-start.1 = (bf16[32,128]{1,0:T(8,128)(2,1)}, bf16[32,128]{1,0:T(8,128)(2,1)S(1)}, u32[]{:S(2)}, u32[]{:S(2)}) collective-permute-start(bf16[32,128]{1,0:T(8,128)(2,1)} %shard_map.73.refs_2_.refs_0_), channel_id=1, source_target_pairs={{0,2},{1,3},{2,0},{3,1},{4,6},{5,7},{6,4},{7,5},{8,10},{9,11},{10,... | collective-permute-start | bytes 24584 | tf_op jit(solution)/shard_map/ppermute | solution.py:296
  19.0 12.7 %collective-permute-start = (bf16[32,128]{1,0:T(8,128)(2,1)}, bf16[32,128]{1,0:T(8,128)(2,1)S(1)}, u32[]{:S(2)}, u32[]{:S(2)}) collective-permute-start(bf16[32,128]{1,0:T(8,128)(2,1)} %shard_map.73.refs_2_.refs_0_), channel_id=1, source_target_pairs={{0,1},{1,0},{2,3},{3,2},{4,5},{5,4},{6,7},{7,6},{8,9},{9,8},{10,11... | collective-permute-start | bytes 24584 | tf_op jit(solution)/shard_map/ppermute | solution.py:296
  21.0 0.7 copy-start.2
  30.0 15.8 %collective-permute-start.11 = (bf16[128,2048]{1,0:T(8,128)(2,1)S(1)}, bf16[128,2048]{1,0:T(8,128)(2,1)S(1)}, u32[]{:S(2)}, u32[]{:S(2)}) collective-permute-start(bf16[128,2048]{1,0:T(8,128)(2,1)S(1)} %copy-done.1), channel_id=1, source_target_pairs={{0,3},{1,2},{2,1},{3,0},{4,7},{5,6},{6,5},{7,4},{8,11},{9,10},{10,... | collective-permute-start | bytes 1572872 | tf_op jit(solution)/shard_map/ppermute | solution.py:296
  31.6 21.1 %collective-permute-start.10 = (bf16[128,2048]{1,0:T(8,128)(2,1)S(1)}, bf16[128,2048]{1,0:T(8,128)(2,1)S(1)}, u32[]{:S(2)}, u32[]{:S(2)}) collective-permute-start(bf16[128,2048]{1,0:T(8,128)(2,1)S(1)} %copy-done.1), channel_id=1, source_target_pairs={{0,2},{1,3},{2,0},{3,1},{4,6},{5,7},{6,4},{7,5},{8,10},{9,11},{10,... | collective-permute-start | bytes 1572872 | tf_op jit(solution)/shard_map/ppermute | solution.py:296
  31.7 21.1 %collective-permute-start.9 = (bf16[128,2048]{1,0:T(8,128)(2,1)S(1)}, bf16[128,2048]{1,0:T(8,128)(2,1)S(1)}, u32[]{:S(2)}, u32[]{:S(2)}) collective-permute-start(bf16[128,2048]{1,0:T(8,128)(2,1)S(1)} %copy-done.1), channel_id=1, source_target_pairs={{0,1},{1,0},{2,3},{3,2},{4,5},{5,4},{6,7},{7,6},{8,9},{9,8},{10,11... | collective-permute-start | bytes 1572872 | tf_op jit(solution)/shard_map/ppermute | solution.py:296
  65.4 10.8 %collective-permute-start.18 = (bf16[2,128,512]{2,1,0:T(8,128)(2,1)S(1)}, bf16[2,128,512]{2,1,0:T(8,128)(2,1)S(1)}, u32[]{:S(2)}, u32[]{:S(2)}) collective-permute-start(bf16[2,128,512]{2,1,0:T(8,128)(2,1)S(1)} %get-tuple-element.45), channel_id=1, source_target_pairs={{0,2},{1,3},{2,0},{3,1},{4,6},{5,7},{6,4},{7,5},{8,10},{9,11},{10,... | collective-permute-start | bytes 786440 | tf_op jit(solution)/shard_map/ppermute | solution.py:296
  68.5 8.4 %collective-permute-start.16 = (bf16[2,128,512]{2,1,0:T(8,128)(2,1)S(1)}, bf16[2,128,512]{2,1,0:T(8,128)(2,1)S(1)}, u32[]{:S(2)}, u32[]{:S(2)}) collective-permute-start(bf16[2,128,512]{2,1,0:T(8,128)(2,1)S(1)} %get-tuple-element.42), channel_id=1, source_target_pairs={{0,1},{1,0},{2,3},{3,2},{4,5},{5,4},{6,7},{7,6},{8,9},{9,8},{10,11... | collective-permute-start | bytes 786440 | tf_op jit(solution)/shard_map/ppermute | solution.py:296
  71.8 9.0 %collective-permute-start.14 = (bf16[2,128,512]{2,1,0:T(8,128)(2,1)S(1)}, bf16[2,128,512]{2,1,0:T(8,128)(2,1)S(1)}, u32[]{:S(2)}, u32[]{:S(2)}) collective-permute-start(bf16[2,128,512]{2,1,0:T(8,128)(2,1)S(1)} %get-tuple-element.39), channel_id=1, source_target_pairs={{0,2},{1,3},{2,0},{3,1},{4,6},{5,7},{6,4},{7,5},{8,10},{9,11},{10,... | collective-permute-start | bytes 786440 | tf_op jit(solution)/shard_map/ppermute | solution.py:296
  74.7 9.3 %collective-permute-start.12 = (bf16[2,128,512]{2,1,0:T(8,128)(2,1)S(1)}, bf16[2,128,512]{2,1,0:T(8,128)(2,1)S(1)}, u32[]{:S(2)}, u32[]{:S(2)}) collective-permute-start(bf16[2,128,512]{2,1,0:T(8,128)(2,1)S(1)} %get-tuple-element.36), channel_id=1, source_target_pairs={{0,1},{1,0},{2,3},{3,2},{4,5},{5,4},{6,7},{7,6},{8,9},{9,8},{10,11... | collective-permute-start | bytes 786440 | tf_op jit(solution)/shard_map/ppermute | solution.py:296
  76.2 10.1 %collective-permute-start.19 = (bf16[1,128,512]{2,1,0:T(8,128)(2,1)S(1)}, bf16[1,128,512]{2,1,0:T(8,128)(2,1)S(1)}, u32[]{:S(2)}, u32[]{:S(2)}) collective-permute-start(bf16[1,128,512]{2,1,0:T(8,128)(2,1)S(1)} %add_convert_fusion), channel_id=1, source_target_pairs={{0,1},{1,0},{2,3},{3,2},{4,5},{5,4},{6,7},{7,6},{8,9},{9,8},{10,11... | collective-permute-start | bytes 393224 | tf_op jit(solution)/shard_map/ppermute | solution.py:296
  77.0 9.4 %collective-permute-start.17 = (bf16[1,128,512]{2,1,0:T(8,128)(2,1)S(1)}, bf16[1,128,512]{2,1,0:T(8,128)(2,1)S(1)}, u32[]{:S(2)}, u32[]{:S(2)}) collective-permute-start(bf16[1,128,512]{2,1,0:T(8,128)(2,1)S(1)} %add_convert_fusion.1), channel_id=1, source_target_pairs={{0,2},{1,3},{2,0},{3,1},{4,6},{5,7},{6,4},{7,5},{8,10},{9,11},{10,... | collective-permute-start | bytes 393224 | tf_op jit(solution)/shard_map/ppermute | solution.py:296
  80.9 6.9 %collective-permute-start.15 = (bf16[1,128,512]{2,1,0:T(8,128)(2,1)S(1)}, bf16[1,128,512]{2,1,0:T(8,128)(2,1)S(1)}, u32[]{:S(2)}, u32[]{:S(2)}) collective-permute-start(bf16[1,128,512]{2,1,0:T(8,128)(2,1)S(1)} %add_convert_fusion.2), channel_id=1, source_target_pairs={{0,1},{1,0},{2,3},{3,2},{4,5},{5,4},{6,7},{7,6},{8,9},{9,8},{10,11... | collective-permute-start | bytes 393224 | tf_op jit(solution)/shard_map/ppermute | solution.py:296
  84.1 5.0 %collective-permute-start.13 = (bf16[1,128,512]{2,1,0:T(8,128)(2,1)S(1)}, bf16[1,128,512]{2,1,0:T(8,128)(2,1)S(1)}, u32[]{:S(2)}, u32[]{:S(2)}) collective-permute-start(bf16[1,128,512]{2,1,0:T(8,128)(2,1)S(1)} %add_convert_fusion.3), channel_id=1, source_target_pairs={{0,2},{1,3},{2,0},{3,1},{4,6},{5,7},{6,4},{7,5},{8,10},{9,11},{10,... | collective-permute-start | bytes 393224 | tf_op jit(solution)/shard_map/ppermute | solution.py:296

commit v4 on v3

--- a/solution.py
+++ b/solution.py
@@ -73,6 +73,20 @@
                 out[j, p * wide : (p + 1) * wide, part] = rows[j * wide : (j + 1) * wide, :]
 
 
+def gather_columns(n, local, place_ref, token_refs, out):
+    wide = 2 * SLOT
+    features = out.shape[1]
+    size = features // 4
+    for p in range(n // 2):
+        refs = [ref for pair in token_refs[2 * p : 2 * p + 2] for ref in pair]
+        for d in range(0, features, size):
+            part = slice(d, d + size)
+            tokens = jnp.concatenate([ref[:, part] for ref in refs], axis=0)
+            columns = dot(tokens.T, place_ref[p]).astype(jnp.bfloat16)
+            for j in range(local):
+                out[j, part, p * wide : (p + 1) * wide] = columns[:, j * wide : (j + 1) * wide]
+
+
 def split(refs, counts):
     parts, first = [], 0
     for count in counts:
@@ -84,7 +98,7 @@
 def pre_kernel(axis, n, local, counts, *refs):
     table_refs, refs = refs[:n], refs[n:]
     token_refs, refs = split(refs, counts)
-    wg_ref, wu_ref, a_ref, b_ref, pick_ref, place_ref, xs, gcol = refs
+    wg_ref, wu_ref, a_ref, b_ref, place_ref, xs, gcol, pick_ref = refs
     experts = n * local
     tokens = table_refs[0].shape[1]
     wide = 2 * SLOT
@@ -127,7 +141,7 @@
 
 
 def load_kernel(count, *refs):
-    sources, results, sems = refs[:count], refs[-count - 1 : -1], refs[-1]
+    sources, (*results, done_ref, sems) = refs[:count], refs[count + 1 :]
     copies = [
         pltpu.make_async_copy(source.at[e], result.at[e], sems.at[i, e])
         for i, (source, result) in enumerate(zip(sources, results))
@@ -137,6 +151,7 @@
         copy.start()
     for copy in copies:
         copy.wait()
+    done_ref[...] = jnp.zeros_like(done_ref)
 
 
 def load(arrays, after):
@@ -144,8 +159,9 @@
     return pl.pallas_call(
         functools.partial(load_kernel, count),
         in_specs=[pl.BlockSpec(memory_space=pltpu.HBM)] * count + [pl.BlockSpec(memory_space=pl.ANY)],
-        out_specs=[pl.BlockSpec(memory_space=pltpu.VMEM)] * count,
-        out_shape=[pltpu.VMEM(w.shape, w.dtype) for w in arrays],
+        out_specs=[pl.BlockSpec(memory_space=pltpu.VMEM)] * (count + 1),
+        out_shape=[pltpu.VMEM(w.shape, w.dtype) for w in arrays]
+        + [jax.ShapeDtypeStruct((8, 128), jnp.float32)],
         scratch_shapes=[pltpu.SemaphoreType.DMA((count, arrays[0].shape[0]))],
         compiler_params=params(1),
         cost_estimate=pl.CostEstimate(
@@ -154,6 +170,38 @@
     )(*[pltpu.with_memory_space_constraint(w, pltpu.HBM) for w in arrays], after)
 
 
+def relay_kernel(x_ref, y_ref, *refs):
+    upper_ref, lower_ref = refs[-2:]
+    half = upper_ref.shape[0]
+    upper_ref[...] = x_ref[:half, :]
+    lower_ref[...] = y_ref[half:, :]
+
+
+def relay_parts(beside, after):
+    tokens, features = beside[0].shape
+    inside, anywhere = pl.BlockSpec(memory_space=pltpu.VMEM), pl.BlockSpec(memory_space=pl.ANY)
+    half = jax.ShapeDtypeStruct((tokens // 2, features), beside[0].dtype)
+    return pl.pallas_call(
+        relay_kernel,
+        in_specs=[inside] * 2 + [anywhere] * len(after),
+        out_shape=[half, half],
+        compiler_params=params(4),
+    )(*beside, *after)
+
+
+def pass_kernel(array_ref, _, copy_ref):
+    copy_ref[...] = array_ref[...]
+
+
+def passed(array, after):
+    return pl.pallas_call(
+        pass_kernel,
+        in_specs=[pl.BlockSpec(memory_space=pltpu.VMEM), pl.BlockSpec(memory_space=pl.ANY)],
+        out_shape=jax.ShapeDtypeStruct(array.shape, array.dtype),
+        compiler_params=params(4),
+    )(array, after)
+
+
 def pre(axis, n, tables, tokens, wg, wu):
     local, features, hidden = wg.shape
     rows = n * SLOT
@@ -163,12 +211,12 @@
         out_shape=[
             jax.ShapeDtypeStruct((local, hidden, rows), jnp.float32),
             jax.ShapeDtypeStruct((local, hidden, rows), jnp.float32),
-            jax.ShapeDtypeStruct((n // 2, down, across), jnp.bfloat16),
             jax.ShapeDtypeStruct((n // 2, across, down), jnp.bfloat16),
         ],
         scratch_shapes=[
             pltpu.VMEM((local, rows, features), jnp.bfloat16),
             pltpu.VMEM((local, rows, 1), jnp.float32),
+            pltpu.VMEM((n // 2, down, across), jnp.bfloat16),
         ],
         compiler_params=params(PRE_MIB * max(1, n // 4)),
         cost_estimate=pl.CostEstimate(
@@ -179,7 +227,7 @@
     )(*tables, *[block for t in tokens for block in t], vmem(wg), vmem(wu))
 
 
-def back_kernel(n, local, counts, pick_ref, *refs):
+def back_kernel(n, local, counts, place_ref, *refs):
     token_refs, refs = split(refs, counts)
     wd_ref, a_ref, b_ref, _, _, hg_ref, hu_ref, gs, weight, sems = refs
     hidden = wd_ref.shape[1]
@@ -194,14 +242,14 @@
     for e in range(held):
         for i in range(2):
             fetch(e, i).start()
-    gather_rows(n, local, pick_ref, token_refs, gs)
+    gather_columns(n, local, place_ref, token_refs, gs)
 
     @pl.loop(0, local)
     def _(e):
         for i in range(2):
             part = slice(i * cols, (i + 1) * cols)
             fetch(e, i).wait()
-            back = dot(weight[lax.rem(e, held), part, :], gs[e], NT)
+            back = dot(weight[lax.rem(e, held), part, :], gs[e])
             hg_ref[e, part, :] = (back * a_ref[e, part, :]).astype(jnp.bfloat16)
             hu_ref[e, part, :] = (back * b_ref[e, part, :]).astype(jnp.bfloat16)
 
@@ -210,7 +258,7 @@
                 fetch(e + held, i).start()
 
 
-def back(n, pick, tokens, wd, a, b, wg, wu):
+def back(n, place, tokens, wd, a, b, wg, wu):
     local, hidden, features = wd.shape
     rows = n * SLOT
     blocks = [block for t in tokens for block in t]
@@ -221,7 +269,7 @@
         in_specs=[inside] * (1 + len(blocks)) + [outside] + [inside] * 4,
         out_shape=[shape, shape],
         scratch_shapes=[
-            pltpu.VMEM((local, rows, features), jnp.bfloat16),
+            pltpu.VMEM((local, features, rows), jnp.bfloat16),
             pltpu.VMEM((min(local, 2), hidden, features), jnp.bfloat16),
             pltpu.SemaphoreType.DMA((min(local, 2), 2)),
         ],
@@ -231,7 +279,7 @@
             bytes_accessed=2 * local * features * hidden,
             transcendentals=0,
         ),
-    )(pick, *blocks, pltpu.with_memory_space_constraint(wd, pltpu.HBM), a, b, vmem(wg), vmem(wu))
+    )(place, *blocks, pltpu.with_memory_space_constraint(wd, pltpu.HBM), a, b, vmem(wg), vmem(wu))
 
 
 def out_kernel(n, local, orders, chunk, place_ref, hg_ref, hu_ref, wg_ref, wu_ref, *rest):
@@ -297,20 +345,22 @@
 
     table = rank_table(routes.T, route_gates.T, experts)
     tables = [table] + [swap(table, k) for k in range(1, n)]
+    gate_proj, up_proj, done = load((gate_proj, up_proj), table)
     if n == 4:
-        half = tokens // 2
-        upper, lower = saved_input[:half], saved_input[half:]
-        near = [[]] + [[swap(upper, k), swap(lower, k)] for k in (1, 2)]
-        gate_proj, up_proj = load((gate_proj, up_proj), table)
-        relayed = [swap(near[1][0], 2), swap(near[2][1], 1)]
-        x_blocks = [[saved_input], near[1], near[2], relayed]
-        grad_out, *_ = lax.optimization_barrier((grad_out, near[1], near[2]))
+        x_near = [swap(saved_input, 1), swap(saved_input, 2)]
+        upper, lower = relay_parts(x_near, [done, *tables[1:]])
+        sent = passed(grad_out, upper)
+        x_blocks = [[saved_input], *[[x] for x in x_near], [swap(upper, 2), swap(lower, 1)]]
+        g_near = [swap(sent, 1), swap(sent, 2)]
     else:
         x_blocks = [[saved_input]] + [[swap(saved_input, k)] for k in range(1, n)]
-        gate_proj, up_proj = load((gate_proj, up_proj), table)
-    g_blocks = [[grad_out]] + [[swap(grad_out, k)] for k in range(1, n)]
-    a, b, pick, place = pre(axis, n, tables, x_blocks, gate_proj, up_proj)
-    hg, hu = back(n, pick, g_blocks, down_proj, a, b, gate_proj, up_proj)
+    a, b, place = pre(axis, n, tables, x_blocks, gate_proj, up_proj)
+    if n == 4:
+        upper, lower = relay_parts(g_near, [place])
+        g_blocks = [[sent], *[[g] for g in g_near], [swap(upper, 2), swap(lower, 1)]]
+    else:
+        g_blocks = [[grad_out]] + [[swap(grad_out, k)] for k in range(1, n)]
+    hg, hu = back(n, place, g_blocks, down_proj, a, b, gate_proj, up_proj)
     parts = []
     for chunk in range(CHUNKS):
         if n == 4:
@@ -318,8 +368,8 @@
             orders = ((0,), (first, 3), (last,))
             own, two, one = partial_sums(n, orders, chunk, place, hg, hu, gate_proj, up_proj)
             two = swap(two, first)
-            relay = (two[1:2].astype(jnp.float32) + one.astype(jnp.float32)).astype(jnp.bfloat16)
-            parts += [own, two[:1], swap(relay, last)]
+            mixed = (two[1:2].astype(jnp.float32) + one.astype(jnp.float32)).astype(jnp.bfloat16)
+            parts += [own, two[:1], swap(mixed, last)]
         else:
             orders = tuple((k,) for k in range(n))
             own, *others = partial_sums(n, orders, chunk, place, hg, hu, gate_proj, up_proj)

time: 90.3 us -> 82 us (0.908)
  waiting for transfers between devices: 23.1 us -> 16.1 us
  local copies, waits for them, and re-layouts: 1.84 us -> 0.78 us
    ppermute x20 -> x19, waiting for transfers between devices: 23.1 us -> 16.1 us  [swap(): return lax.ppermute(array, axis, [(i, i ^ k) for i in range(n)])]
    slice x5 -> x4, local copies, waits for them, and re-layouts: 1.1 us -> 0.04 us  [body(): parts += [own, two[:1], swap(mixed, last)]]
    ppermute x20 -> x19, starting transfers between devices: 23.5 us -> 23.6 us  [swap(): return lax.ppermute(array, axis, [(i, i ^ k) for i in range(n)])]
  transfers between devices with their start and end apart: 20 -> 19, of which waited for: 11 -> 9; matrix products, arithmetic and copies ran while one was open for 0% -> 0% of each run, Pallas kernels for 31% -> 34%
where the time goes in v4:
time: 82 us; the launch traced here: 81.8 us
  Pallas kernels  41 us (50%)
  starting transfers between devices  23.6 us (29%)
  waiting for transfers between devices  16.1 us (20%)
    ppermute x19, starting transfers between devices, swap(): return lax.ppermute(array, axis, [(i, i ^ k) for i in range(n)])  23.6 us
    ppermute x19, waiting for transfers between devices, swap(): return lax.ppermute(array, axis, [(i, i ^ k) for i in range(n)])  16.1 us
    pallas_call x1, Pallas kernels, pre(): pl.pallas_call(functools.partial(pre_kernel, axis, n, local, [len(t) for...  11.4 us
    pallas_call x1, Pallas kernels, back(): pl.pallas_call(functools.partial(back_kernel, n, local, [len(t) for t in...  10.1 us
    pallas_call x4, Pallas kernels, partial_sums(): pl.pallas_call(functools.partial(out_kernel, n, local, orders, chunk), ou...  8.58 us
    pallas_call x1, Pallas kernels, load(): pl.pallas_call(functools.partial(load_kernel, count), in_specs=[pl.BlockS...  8.31 us
  transfers between devices with their start and end apart: 19, of which 9 were waited for; matrix products, arithmetic and copies ran while one was open for 0% of the time, Pallas kernels for 34%

profile of v4, /device:TPU:0, one launch (start us, length us, event | category | flops | bytes accessed | tf_op | source)
XLA Modules:
  0.0 81.8 jit_solution(14050800186972530818)
XLA Ops:
  0.0 2.9 %collective-permute-start.3 = (bf16[128,2048]{1,0:T(8,128)(2,1)}, bf16[128,2048]{1,0:T(8,128)(2,1)S(1)}, u32[]{:S(2)}, u32[]{:S(2)}) collective-permute-start(bf16[128,2048]{1,0:T(8,128)(2,1)} %refs_4_.1), channel_id=1, source_target_pairs={{0,1},{1,0},{2,3},{3,2},{4,5},{5,4},{6,7},{7,6},{8,9},{9,8},{10,11... | collective-permute-start | bytes 1572872 | tf_op jit(solution)/shard_map/ppermute | solution.py:344
  2.9 1.5 %collective-permute-start.4 = (bf16[128,2048]{1,0:T(8,128)(2,1)}, bf16[128,2048]{1,0:T(8,128)(2,1)S(1)}, u32[]{:S(2)}, u32[]{:S(2)}) collective-permute-start(bf16[128,2048]{1,0:T(8,128)(2,1)} %refs_4_.1), channel_id=1, source_target_pairs={{0,2},{1,3},{2,0},{3,1},{4,6},{5,7},{6,4},{7,5},{8,10},{9,11},{10,... | collective-permute-start | bytes 1572872 | tf_op jit(solution)/shard_map/ppermute | solution.py:344
  4.5 1.5 %shard_map.73.refs_2_.refs_0_ = bf16[32,128]{1,0:T(8,128)(2,1)} custom-call(s32[8,128]{1,0:T(8,128)} %bitcast.2, bf16[8,128]{1,0:T(8,128)(2,1)} %bitcast.3), custom_call_target="tpu_custom_call" | custom-call | tf_op jit(solution)/shard_map/pallas_call | solution.py:56
  5.9 0.0 copy-start
  5.9 0.0 copy-start.1
  6.0 0.0 collective-permute-start.2
  6.0 2.0 %collective-permute-start.1 = (bf16[32,128]{1,0:T(8,128)(2,1)}, bf16[32,128]{1,0:T(8,128)(2,1)S(1)}, u32[]{:S(2)}, u32[]{:S(2)}) collective-permute-start(bf16[32,128]{1,0:T(8,128)(2,1)} %shard_map.73.refs_2_.refs_0_), channel_id=1, source_target_pairs={{0,2},{1,3},{2,0},{3,1},{4,6},{5,7},{6,4},{7,5},{8,10},{9,11},{10,... | collective-permute-start | bytes 24584 | tf_op jit(solution)/shard_map/ppermute | solution.py:344
  7.9 1.5 %collective-permute-start = (bf16[32,128]{1,0:T(8,128)(2,1)}, bf16[32,128]{1,0:T(8,128)(2,1)S(1)}, u32[]{:S(2)}, u32[]{:S(2)}) collective-permute-start(bf16[32,128]{1,0:T(8,128)(2,1)} %shard_map.73.refs_2_.refs_0_), channel_id=1, source_target_pairs={{0,1},{1,0},{2,3},{3,2},{4,5},{5,4},{6,7},{7,6},{8,9},{9,8},{10,11... | collective-permute-start | bytes 24584 | tf_op jit(solution)/shard_map/ppermute | solution.py:344
  9.4 0.0 copy-start.2
  9.4 0.7 copy-done.2
  10.2 0.0 copy-start.3
  10.2 8.3 %shard_map.74 = (bf16[4,2048,768]{2,1,0:T(8,128)(2,1)S(1)}, bf16[4,2048,768]{2,1,0:T(8,128)(2,1)S(1)}, f32[8,128]{1,0:T(8,128)S(1)}) custom-call(bf16[4,2048,768]{2,1,0:T(8,128)(2,1)} %refs_0_.1, bf16[4,2048,768]{2,1,0:T(8,128)(2,1)} %refs_1_.1, bf16[32,128]{1,0:T(8,128)(2,1)S(1)} %copy-done.2), custom_call_target="tpu_custom_call" | custom-call | bytes 50331648 | tf_op jit(solution)/shard_map/pallas_call | solution.py:159
  18.5 0.0 collective-permute-done.2.refs_3_
  18.5 0.0 collective-permute-done.1.refs_2_
  18.5 0.0 collective-permute-done.refs_1_
  18.5 0.0 collective-permute-done.3.x_ref.refs_5_
  18.5 0.0 collective-permute-done.4.y_ref.refs_6_
  18.6 0.6 collective-permute-start.6
  19.2 0.1 collective-permute-start.5
  19.3 0.0 copy-done
  19.3 2.0 %collective-permute-start.8 = (bf16[128,2048]{1,0:T(8,128)(2,1)S(1)}, bf16[128,2048]{1,0:T(8,128)(2,1)S(1)}, u32[]{:S(2)}, u32[]{:S(2)}) collective-permute-start(bf16[128,2048]{1,0:T(8,128)(2,1)S(1)} %shard_map.77.refs_0_), channel_id=1, source_target_pairs={{0,2},{1,3},{2,0},{3,1},{4,6},{5,7},{6,4},{7,5},{8,10},{9,11},{10,... | collective-permute-start | bytes 1572872 | tf_op jit(solution)/shard_map/ppermute | solution.py:344
  21.3 1.5 %collective-permute-start.7 = (bf16[128,2048]{1,0:T(8,128)(2,1)S(1)}, bf16[128,2048]{1,0:T(8,128)(2,1)S(1)}, u32[]{:S(2)}, u32[]{:S(2)}) collective-permute-start(bf16[128,2048]{1,0:T(8,128)(2,1)S(1)} %shard_map.77.refs_0_), channel_id=1, source_target_pairs={{0,1},{1,0},{2,3},{3,2},{4,5},{5,4},{6,7},{7,6},{8,9},{9,8},{10,11... | collective-permute-start | bytes 1572872 | tf_op jit(solution)/shard_map/ppermute | solution.py:344
  22.8 5.1 %collective-permute-done.6.refs_8_ = bf16[64,2048]{1,0:T(8,128)(2,1)S(1)} collective-permute-done((bf16[64,2048]{1,0:T(8,128)(2,1)S(1)}, bf16[64,2048]{1,0:T(8,128)(2,1)S(1)}, u32[]{:S(2)}, u32[]{:S(2)}) %collective-permute-start.6) | collective-permute-done | bytes 262176 | tf_op jit(solution)/shard_map/ppermute | solution.py:344
  27.9 0.5 collective-permute-done.5.refs_7_
  28.4 0.0 copy-done.1
  28.4 0.0 copy-done.3
  28.4 11.4 %shard_map.76 = (f32[4,768,256]{2,1,0:T(8,128)S(1)}, f32[4,768,256]{2,1,0:T(8,128)S(1)}, bf16[2,256,512]{2,1,0:T(8,128)(2,1)S(1)}) custom-call(bf16[32,128]{1,0:T(8,128)(2,1)S(1)} %copy-done.3, bf16[32,128]{1,0:T(8,128)(2,1)S(1)} %collective-permute-done.refs_1_, bf16[32,128]{1,0:T(8,128)(2,1)S(1)} %collective-permute-done.1.refs_2_, ...), custom_call_target="tpu_custom_call" | custom-call | flops 6442450944 | bytes 25165824 | tf_op jit(solution)/shard_map/pallas_call | solution.py:209
  39.9 0.0 collective-permute-done.8.y_ref.refs_2_
  39.9 0.0 collective-permute-done.7.x_ref.refs_1_
  39.9 0.2 collective-permute-start.9
  40.1 1.9 %collective-permute-start.10 = (bf16[64,2048]{1,0:T(8,128)(2,1)S(1)}, bf16[64,2048]{1,0:T(8,128)(2,1)S(1)}, u32[]{:S(2)}, u32[]{:S(2)}) collective-permute-start(bf16[64,2048]{1,0:T(8,128)(2,1)S(1)} %get-tuple-element.36), channel_id=1, source_target_pairs={{0,1},{1,0},{2,3},{3,2},{4,5},{5,4},{6,7},{7,6},{8,9},{9,8},{10,11... | collective-permute-start | bytes 786440 | tf_op jit(solution)/shard_map/ppermute | solution.py:344
  42.0 4.4 %collective-permute-done.9.refs_3_ = bf16[64,2048]{1,0:T(8,128)(2,1)S(1)} collective-permute-done((bf16[64,2048]{1,0:T(8,128)(2,1)S(1)}, bf16[64,2048]{1,0:T(8,128)(2,1)S(1)}, u32[]{:S(2)}, u32[]{:S(2)}) %collective-permute-start.9) | collective-permute-done | bytes 262176 | tf_op jit(solution)/shard_map/ppermute | solution.py:344
  46.4 0.1 collective-permute-done.10.refs_4_
  46.5 10.1 %shard_map.79 = (bf16[4,768,256]{2,1,0:T(8,128)(2,1)S(1)}, bf16[4,768,256]{2,1,0:T(8,128)(2,1)S(1)}) custom-call(bf16[2,256,512]{2,1,0:T(8,128)(2,1)S(1)} %get-tuple-element.34.refs_0_.place_ref, bf16[128,2048]{1,0:T(8,128)(2,1)S(1)} %shard_map.77.refs_0_, bf16[128,2048]{1,0:T(8,128)(2,1)S(1)} %collective-permute-done.7.x_ref.refs_1_, ...), custom_call_target="tpu_custom_call" | custom-call | flops 3221225472 | bytes 12582912 | tf_op jit(solution)/shard_map/pallas_call | solution.py:267
  56.6 2.1 %shard_map.83 = (f32[1,128,512]{2,1,0:T(8,128)S(1)}, bf16[2,128,512]{2,1,0:T(8,128)(2,1)S(1)}, bf16[1,128,512]{2,1,0:T(8,128)(2,1)S(1)}) custom-call(bf16[2,256,512]{2,1,0:T(8,128)(2,1)S(1)} %get-tuple-element.34.refs_0_.place_ref, bf16[4,768,256]{2,1,0:T(8,128)(2,1)S(1)} %get-tuple-element.39.hg_ref, bf16[4,768,256]{2,1,0:T(8,128)(2,1)S(1)} %get-tuple-element.40.hu_ref, ...), custom_call_target="tpu_custom_call" | custom-call | flops 402653184 | bytes 1572864 | tf_op jit(solution)/shard_map/pallas_call | solution.py:312
  58.8 2.0 %collective-permute-start.17 = (bf16[2,128,512]{2,1,0:T(8,128)(2,1)S(1)}, bf16[2,128,512]{2,1,0:T(8,128)(2,1)S(1)}, u32[]{:S(2)}, u32[]{:S(2)}) collective-permute-start(bf16[2,128,512]{2,1,0:T(8,128)(2,1)S(1)} %get-tuple-element.51), channel_id=1, source_target_pairs={{0,2},{1,3},{2,0},{3,1},{4,6},{5,7},{6,4},{7,5},{8,10},{9,11},{10,... | collective-permute-start | bytes 786440 | tf_op jit(solution)/shard_map/ppermute | solution.py:344
  60.7 2.1 %shard_map.82 = (f32[1,128,512]{2,1,0:T(8,128)S(1)}, bf16[2,128,512]{2,1,0:T(8,128)(2,1)S(1)}, bf16[1,128,512]{2,1,0:T(8,128)(2,1)S(1)}) custom-call(bf16[2,256,512]{2,1,0:T(8,128)(2,1)S(1)} %get-tuple-element.34.refs_0_.place_ref, bf16[4,768,256]{2,1,0:T(8,128)(2,1)S(1)} %get-tuple-element.39.hg_ref, bf16[4,768,256]{2,1,0:T(8,128)(2,1)S(1)} %get-tuple-element.40.hu_ref, ...), custom_call_target="tpu_custom_call" | custom-call | flops 402653184 | bytes 1572864 | tf_op jit(solution)/shard_map/pallas_call | solution.py:312
  62.9 1.6 %collective-permute-start.15 = (bf16[2,128,512]{2,1,0:T(8,128)(2,1)S(1)}, bf16[2,128,512]{2,1,0:T(8,128)(2,1)S(1)}, u32[]{:S(2)}, u32[]{:S(2)}) collective-permute-start(bf16[2,128,512]{2,1,0:T(8,128)(2,1)S(1)} %get-tuple-element.48), channel_id=1, source_target_pairs={{0,1},{1,0},{2,3},{3,2},{4,5},{5,4},{6,7},{7,6},{8,9},{9,8},{10,11... | collective-permute-start | bytes 786440 | tf_op jit(solution)/shard_map/ppermute | solution.py:344
  64.5 2.1 %shard_map.81 = (f32[1,128,512]{2,1,0:T(8,128)S(1)}, bf16[2,128,512]{2,1,0:T(8,128)(2,1)S(1)}, bf16[1,128,512]{2,1,0:T(8,128)(2,1)S(1)}) custom-call(bf16[2,256,512]{2,1,0:T(8,128)(2,1)S(1)} %get-tuple-element.34.refs_0_.place_ref, bf16[4,768,256]{2,1,0:T(8,128)(2,1)S(1)} %get-tuple-element.39.hg_ref, bf16[4,768,256]{2,1,0:T(8,128)(2,1)S(1)} %get-tuple-element.40.hu_ref, ...), custom_call_target="tpu_custom_call" | custom-call | flops 402653184 | bytes 1572864 | tf_op jit(solution)/shard_map/pallas_call | solution.py:312
  66.6 0.6 collective-permute-start.13
  67.2 2.1 %shard_map.80 = (f32[1,128,512]{2,1,0:T(8,128)S(1)}, bf16[2,128,512]{2,1,0:T(8,128)(2,1)S(1)}, bf16[1,128,512]{2,1,0:T(8,128)(2,1)S(1)}) custom-call(bf16[2,256,512]{2,1,0:T(8,128)(2,1)S(1)} %get-tuple-element.34.refs_0_.place_ref, bf16[4,768,256]{2,1,0:T(8,128)(2,1)S(1)} %get-tuple-element.39.hg_ref, bf16[4,768,256]{2,1,0:T(8,128)(2,1)S(1)} %get-tuple-element.40.hu_ref, ...), custom_call_target="tpu_custom_call" | custom-call | flops 402653184 | bytes 1572864 | tf_op jit(solution)/shard_map/pallas_call | solution.py:312
  69.3 0.2 collective-permute-start.11
  69.5 0.0 collective-permute-done.17
  69.6 1.9 %collective-permute-start.18 = (bf16[1,128,512]{2,1,0:T(8,128)(2,1)S(1)}, bf16[1,128,512]{2,1,0:T(8,128)(2,1)S(1)}, u32[]{:S(2)}, u32[]{:S(2)}) collective-permute-start(bf16[1,128,512]{2,1,0:T(8,128)(2,1)S(1)} %add_convert_fusion), channel_id=1, source_target_pairs={{0,1},{1,0},{2,3},{3,2},{4,5},{5,4},{6,7},{7,6},{8,9},{9,8},{10,11... | collective-permute-start | bytes 393224 | tf_op jit(solution)/shard_map/ppermute | solution.py:344
  71.5 0.7 collective-permute-done.15
  72.2 0.9 %collective-permute-start.16 = (bf16[1,128,512]{2,1,0:T(8,128)(2,1)S(1)}, bf16[1,128,512]{2,1,0:T(8,128)(2,1)S(1)}, u32[]{:S(2)}, u32[]{:S(2)}) collective-permute-start(bf16[1,128,512]{2,1,0:T(8,128)(2,1)S(1)} %add_convert_fusion.1), channel_id=1, source_target_pairs={{0,2},{1,3},{2,0},{3,1},{4,6},{5,7},{6,4},{7,5},{8,10},{9,11},{10,... | collective-permute-start | bytes 393224 | tf_op jit(solution)/shard_map/ppermute | solution.py:344
  73.1 1.3 %collective-permute-done.13 = bf16[2,128,512]{2,1,0:T(8,128)(2,1)S(1)} collective-permute-done((bf16[2,128,512]{2,1,0:T(8,128)(2,1)S(1)}, bf16[2,128,512]{2,1,0:T(8,128)(2,1)S(1)}, u32[]{:S(2)}, u32[]{:S(2)}) %collective-permute-start.13) | collective-permute-done | bytes 262176 | tf_op jit(solution)/shard_map/ppermute | solution.py:344
  74.5 0.6 collective-permute-start.14
  75.1 0.7 collective-permute-done.11
  75.8 1.6 %collective-permute-start.12 = (bf16[1,128,512]{2,1,0:T(8,128)(2,1)S(1)}, bf16[1,128,512]{2,1,0:T(8,128)(2,1)S(1)}, u32[]{:S(2)}, u32[]{:S(2)}) collective-permute-start(bf16[1,128,512]{2,1,0:T(8,128)(2,1)S(1)} %add_convert_fusion.3), channel_id=1, source_target_pairs={{0,2},{1,3},{2,0},{3,1},{4,6},{5,7},{6,4},{7,5},{8,10},{9,11},{10,... | collective-permute-start | bytes 393224 | tf_op jit(solution)/shard_map/ppermute | solution.py:344
  77.4 0.0 collective-permute-done.18.refs_11_
  77.5 0.0 collective-permute-done.16.refs_8_
  77.5 2.0 %collective-permute-done.14.refs_5_ = bf16[1,128,512]{2,1,0:T(8,128)(2,1)S(1)} collective-permute-done((bf16[1,128,512]{2,1,0:T(8,128)(2,1)S(1)}, bf16[1,128,512]{2,1,0:T(8,128)(2,1)S(1)}, u32[]{:S(2)}, u32[]{:S(2)}) %collective-permute-start.14) | collective-permute-done | bytes 131104 | tf_op jit(solution)/shard_map/ppermute | solution.py:344
  79.5 1.3 %collective-permute-done.12.refs_2_ = bf16[1,128,512]{2,1,0:T(8,128)(2,1)S(1)} collective-permute-done((bf16[1,128,512]{2,1,0:T(8,128)(2,1)S(1)}, bf16[1,128,512]{2,1,0:T(8,128)(2,1)S(1)}, u32[]{:S(2)}, u32[]{:S(2)}) %collective-permute-start.12) | collective-permute-done | bytes 131104 | tf_op jit(solution)/shard_map/ppermute | solution.py:344
  80.8 0.9 %shard_map.84 = bf16[128,2048]{1,0:T(8,128)(2,1)} custom-call(f32[1,128,512]{2,1,0:T(8,128)S(1)} %get-tuple-element.41.refs_0_, bf16[1,128,512]{2,1,0:T(8,128)(2,1)S(1)} %slice.32.refs_1_, bf16[1,128,512]{2,1,0:T(8,128)(2,1)S(1)} %collective-permute-done.12.refs_2_, f32[1,128,512]{2,1,0:T(8,128)S(1)} %get-tuple-element.44.refs_3_, ...), custom_call_target="tpu_custom_call" | custom-call | tf_op jit(solution)/shard_map/pallas_call | solution.py:377
  (11 shorter events, 0.3 us)
Async XLA Ops:
  0.0 18.5 %collective-permute-start.3 = (bf16[128,2048]{1,0:T(8,128)(2,1)}, bf16[128,2048]{1,0:T(8,128)(2,1)S(1)}, u32[]{:S(2)}, u32[]{:S(2)}) collective-permute-start(bf16[128,2048]{1,0:T(8,128)(2,1)} %refs_4_.1), channel_id=1, source_target_pairs={{0,1},{1,0},{2,3},{3,2},{4,5},{5,4},{6,7},{7,6},{8,9},{9,8},{10,11... | collective-permute-start | bytes 1572872 | tf_op jit(solution)/shard_map/ppermute | solution.py:344
  2.9 15.6 %collective-permute-start.4 = (bf16[128,2048]{1,0:T(8,128)(2,1)}, bf16[128,2048]{1,0:T(8,128)(2,1)S(1)}, u32[]{:S(2)}, u32[]{:S(2)}) collective-permute-start(bf16[128,2048]{1,0:T(8,128)(2,1)} %refs_4_.1), channel_id=1, source_target_pairs={{0,2},{1,3},{2,0},{3,1},{4,6},{5,7},{6,4},{7,5},{8,10},{9,11},{10,... | collective-permute-start | bytes 1572872 | tf_op jit(solution)/shard_map/ppermute | solution.py:344
  5.9 13.3 %copy-start = (bf16[128,2048]{1,0:T(8,128)(2,1)S(1)}, bf16[128,2048]{1,0:T(8,128)(2,1)}, u32[]{:S(2)}) copy-start(bf16[128,2048]{1,0:T(8,128)(2,1)} %array_ref.1) | copy-start | bytes 1572868
  5.9 22.5 %copy-start.1 = (bf16[128,2048]{1,0:T(8,128)(2,1)S(1)}, bf16[128,2048]{1,0:T(8,128)(2,1)}, u32[]{:S(2)}) copy-start(bf16[128,2048]{1,0:T(8,128)(2,1)} %refs_4_.1) | copy-start | bytes 1572868
  6.0 12.5 %collective-permute-start.2 = (bf16[32,128]{1,0:T(8,128)(2,1)}, bf16[32,128]{1,0:T(8,128)(2,1)S(1)}, u32[]{:S(2)}, u32[]{:S(2)}) collective-permute-start(bf16[32,128]{1,0:T(8,128)(2,1)} %shard_map.73.refs_2_.refs_0_), channel_id=1, source_target_pairs={{0,3},{1,2},{2,1},{3,0},{4,7},{5,6},{6,5},{7,4},{8,11},{9,10},{10,... | collective-permute-start | bytes 24584 | tf_op jit(solution)/shard_map/ppermute | solution.py:344
  6.0 12.5 %collective-permute-start.1 = (bf16[32,128]{1,0:T(8,128)(2,1)}, bf16[32,128]{1,0:T(8,128)(2,1)S(1)}, u32[]{:S(2)}, u32[]{:S(2)}) collective-permute-start(bf16[32,128]{1,0:T(8,128)(2,1)} %shard_map.73.refs_2_.refs_0_), channel_id=1, source_target_pairs={{0,2},{1,3},{2,0},{3,1},{4,6},{5,7},{6,4},{7,5},{8,10},{9,11},{10,... | collective-permute-start | bytes 24584 | tf_op jit(solution)/shard_map/ppermute | solution.py:344
  7.9 10.6 %collective-permute-start = (bf16[32,128]{1,0:T(8,128)(2,1)}, bf16[32,128]{1,0:T(8,128)(2,1)S(1)}, u32[]{:S(2)}, u32[]{:S(2)}) collective-permute-start(bf16[32,128]{1,0:T(8,128)(2,1)} %shard_map.73.refs_2_.refs_0_), channel_id=1, source_target_pairs={{0,1},{1,0},{2,3},{3,2},{4,5},{5,4},{6,7},{7,6},{8,9},{9,8},{10,11... | collective-permute-start | bytes 24584 | tf_op jit(solution)/shard_map/ppermute | solution.py:344
  9.4 0.7 copy-start.2
  10.2 18.3 %copy-start.3 = (bf16[32,128]{1,0:T(8,128)(2,1)S(1)}, bf16[32,128]{1,0:T(8,128)(2,1)}, u32[]{:S(2)}) copy-start(bf16[32,128]{1,0:T(8,128)(2,1)} %shard_map.73.refs_2_.refs_0_) | copy-start | bytes 24580
  18.6 9.3 %collective-permute-start.6 = (bf16[64,2048]{1,0:T(8,128)(2,1)S(1)}, bf16[64,2048]{1,0:T(8,128)(2,1)S(1)}, u32[]{:S(2)}, u32[]{:S(2)}) collective-permute-start(bf16[64,2048]{1,0:T(8,128)(2,1)S(1)} %get-tuple-element.31), channel_id=1, source_target_pairs={{0,1},{1,0},{2,3},{3,2},{4,5},{5,4},{6,7},{7,6},{8,9},{9,8},{10,11... | collective-permute-start | bytes 786440 | tf_op jit(solution)/shard_map/ppermute | solution.py:344
  19.2 9.2 %collective-permute-start.5 = (bf16[64,2048]{1,0:T(8,128)(2,1)S(1)}, bf16[64,2048]{1,0:T(8,128)(2,1)S(1)}, u32[]{:S(2)}, u32[]{:S(2)}) collective-permute-start(bf16[64,2048]{1,0:T(8,128)(2,1)S(1)} %get-tuple-element.30._), channel_id=1, source_target_pairs={{0,2},{1,3},{2,0},{3,1},{4,6},{5,7},{6,4},{7,5},{8,10},{9,11},{10,... | collective-permute-start | bytes 786440 | tf_op jit(solution)/shard_map/ppermute | solution.py:344
  19.3 20.5 %collective-permute-start.8 = (bf16[128,2048]{1,0:T(8,128)(2,1)S(1)}, bf16[128,2048]{1,0:T(8,128)(2,1)S(1)}, u32[]{:S(2)}, u32[]{:S(2)}) collective-permute-start(bf16[128,2048]{1,0:T(8,128)(2,1)S(1)} %shard_map.77.refs_0_), channel_id=1, source_target_pairs={{0,2},{1,3},{2,0},{3,1},{4,6},{5,7},{6,4},{7,5},{8,10},{9,11},{10,... | collective-permute-start | bytes 1572872 | tf_op jit(solution)/shard_map/ppermute | solution.py:344
  21.3 18.5 %collective-permute-start.7 = (bf16[128,2048]{1,0:T(8,128)(2,1)S(1)}, bf16[128,2048]{1,0:T(8,128)(2,1)S(1)}, u32[]{:S(2)}, u32[]{:S(2)}) collective-permute-start(bf16[128,2048]{1,0:T(8,128)(2,1)S(1)} %shard_map.77.refs_0_), channel_id=1, source_target_pairs={{0,1},{1,0},{2,3},{3,2},{4,5},{5,4},{6,7},{7,6},{8,9},{9,8},{10,11... | collective-permute-start | bytes 1572872 | tf_op jit(solution)/shard_map/ppermute | solution.py:344
  39.9 6.4 %collective-permute-start.9 = (bf16[64,2048]{1,0:T(8,128)(2,1)S(1)}, bf16[64,2048]{1,0:T(8,128)(2,1)S(1)}, u32[]{:S(2)}, u32[]{:S(2)}) collective-permute-start(bf16[64,2048]{1,0:T(8,128)(2,1)S(1)} %get-tuple-element.35), channel_id=1, source_target_pairs={{0,2},{1,3},{2,0},{3,1},{4,6},{5,7},{6,4},{7,5},{8,10},{9,11},{10,... | collective-permute-start | bytes 786440 | tf_op jit(solution)/shard_map/ppermute | solution.py:344
  40.1 6.4 %collective-permute-start.10 = (bf16[64,2048]{1,0:T(8,128)(2,1)S(1)}, bf16[64,2048]{1,0:T(8,128)(2,1)S(1)}, u32[]{:S(2)}, u32[]{:S(2)}) collective-permute-start(bf16[64,2048]{1,0:T(8,128)(2,1)S(1)} %get-tuple-element.36), channel_id=1, source_target_pairs={{0,1},{1,0},{2,3},{3,2},{4,5},{5,4},{6,7},{7,6},{8,9},{9,8},{10,11... | collective-permute-start | bytes 786440 | tf_op jit(solution)/shard_map/ppermute | solution.py:344
  58.8 10.8 %collective-permute-start.17 = (bf16[2,128,512]{2,1,0:T(8,128)(2,1)S(1)}, bf16[2,128,512]{2,1,0:T(8,128)(2,1)S(1)}, u32[]{:S(2)}, u32[]{:S(2)}) collective-permute-start(bf16[2,128,512]{2,1,0:T(8,128)(2,1)S(1)} %get-tuple-element.51), channel_id=1, source_target_pairs={{0,2},{1,3},{2,0},{3,1},{4,6},{5,7},{6,4},{7,5},{8,10},{9,11},{10,... | collective-permute-start | bytes 786440 | tf_op jit(solution)/shard_map/ppermute | solution.py:344
  62.9 9.3 %collective-permute-start.15 = (bf16[2,128,512]{2,1,0:T(8,128)(2,1)S(1)}, bf16[2,128,512]{2,1,0:T(8,128)(2,1)S(1)}, u32[]{:S(2)}, u32[]{:S(2)}) collective-permute-start(bf16[2,128,512]{2,1,0:T(8,128)(2,1)S(1)} %get-tuple-element.48), channel_id=1, source_target_pairs={{0,1},{1,0},{2,3},{3,2},{4,5},{5,4},{6,7},{7,6},{8,9},{9,8},{10,11... | collective-permute-start | bytes 786440 | tf_op jit(solution)/shard_map/ppermute | solution.py:344
  66.6 7.8 %collective-permute-start.13 = (bf16[2,128,512]{2,1,0:T(8,128)(2,1)S(1)}, bf16[2,128,512]{2,1,0:T(8,128)(2,1)S(1)}, u32[]{:S(2)}, u32[]{:S(2)}) collective-permute-start(bf16[2,128,512]{2,1,0:T(8,128)(2,1)S(1)} %get-tuple-element.45), channel_id=1, source_target_pairs={{0,2},{1,3},{2,0},{3,1},{4,6},{5,7},{6,4},{7,5},{8,10},{9,11},{10,... | collective-permute-start | bytes 786440 | tf_op jit(solution)/shard_map/ppermute | solution.py:344
  69.3 6.4 %collective-permute-start.11 = (bf16[2,128,512]{2,1,0:T(8,128)(2,1)S(1)}, bf16[2,128,512]{2,1,0:T(8,128)(2,1)S(1)}, u32[]{:S(2)}, u32[]{:S(2)}) collective-permute-start(bf16[2,128,512]{2,1,0:T(8,128)(2,1)S(1)} %get-tuple-element.42), channel_id=1, source_target_pairs={{0,1},{1,0},{2,3},{3,2},{4,5},{5,4},{6,7},{7,6},{8,9},{9,8},{10,11... | collective-permute-start | bytes 786440 | tf_op jit(solution)/shard_map/ppermute | solution.py:344
  69.6 7.9 %collective-permute-start.18 = (bf16[1,128,512]{2,1,0:T(8,128)(2,1)S(1)}, bf16[1,128,512]{2,1,0:T(8,128)(2,1)S(1)}, u32[]{:S(2)}, u32[]{:S(2)}) collective-permute-start(bf16[1,128,512]{2,1,0:T(8,128)(2,1)S(1)} %add_convert_fusion), channel_id=1, source_target_pairs={{0,1},{1,0},{2,3},{3,2},{4,5},{5,4},{6,7},{7,6},{8,9},{9,8},{10,11... | collective-permute-start | bytes 393224 | tf_op jit(solution)/shard_map/ppermute | solution.py:344
  72.2 5.2 %collective-permute-start.16 = (bf16[1,128,512]{2,1,0:T(8,128)(2,1)S(1)}, bf16[1,128,512]{2,1,0:T(8,128)(2,1)S(1)}, u32[]{:S(2)}, u32[]{:S(2)}) collective-permute-start(bf16[1,128,512]{2,1,0:T(8,128)(2,1)S(1)} %add_convert_fusion.1), channel_id=1, source_target_pairs={{0,2},{1,3},{2,0},{3,1},{4,6},{5,7},{6,4},{7,5},{8,10},{9,11},{10,... | collective-permute-start | bytes 393224 | tf_op jit(solution)/shard_map/ppermute | solution.py:344
  74.5 5.0 %collective-permute-start.14 = (bf16[1,128,512]{2,1,0:T(8,128)(2,1)S(1)}, bf16[1,128,512]{2,1,0:T(8,128)(2,1)S(1)}, u32[]{:S(2)}, u32[]{:S(2)}) collective-permute-start(bf16[1,128,512]{2,1,0:T(8,128)(2,1)S(1)} %add_convert_fusion.2), channel_id=1, source_target_pairs={{0,1},{1,0},{2,3},{3,2},{4,5},{5,4},{6,7},{7,6},{8,9},{9,8},{10,11... | collective-permute-start | bytes 393224 | tf_op jit(solution)/shard_map/ppermute | solution.py:344
  75.8 5.0 %collective-permute-start.12 = (bf16[1,128,512]{2,1,0:T(8,128)(2,1)S(1)}, bf16[1,128,512]{2,1,0:T(8,128)(2,1)S(1)}, u32[]{:S(2)}, u32[]{:S(2)}) collective-permute-start(bf16[1,128,512]{2,1,0:T(8,128)(2,1)S(1)} %add_convert_fusion.3), channel_id=1, source_target_pairs={{0,2},{1,3},{2,0},{3,1},{4,6},{5,7},{6,4},{7,5},{8,10},{9,11},{10,... | collective-permute-start | bytes 393224 | tf_op jit(solution)/shard_map/ppermute | solution.py:344

commit v5 on v4

--- a/solution.py
+++ b/solution.py
@@ -12,8 +12,8 @@
 UNUSED = 200.0
 MIB = 1 << 20
 CHUNKS = 4
-PRE_MIB = 8
-BACK_MIB = 12
+PRE_MIB = 6
+BACK_MIB = 10
 OUT_MIB = 4
 
 NT = (((1,), (1,)), ((), ()))
@@ -59,30 +59,70 @@
     )(routes, gates)
 
 
-def gather_rows(n, local, pick_ref, token_refs, out):
+def slots_kernel(axis, n, local, *refs):
+    table_refs, (pick_ref, place_ref, gate_ref) = refs[:n], refs[n:]
+    experts = n * local
+    tokens = table_refs[0].shape[1]
+    wide = 2 * SLOT
+    me = lax.axis_index(axis)
+    row = lax.broadcasted_iota(jnp.int32, (2 * experts, tokens), 0)
+    slot = lax.broadcasted_iota(jnp.int32, (wide, tokens), 0).astype(jnp.float32)
+    for p in range(n // 2):
+        tables = [table_refs[2 * p + q][...].astype(jnp.float32) for q in range(2)]
+        for j in range(local):
+            e = me * local + j
+            down = slice(j * wide, (j + 1) * wide)
+            gates = jnp.zeros((8, wide), jnp.float32)
+            for q in range(2):
+                rank = jnp.sum(jnp.where(row == e, tables[q], 0.0), axis=0, keepdims=True)
+                gate = jnp.sum(jnp.where(row == e + experts, tables[q], 0.0), axis=0, keepdims=True)
+                pick = (slot == rank + q * SLOT).astype(jnp.float32)
+                place = pick.T.astype(jnp.bfloat16)
+                across = slice(q * tokens, (q + 1) * tokens)
+                pick_ref[p, down, across] = pick.astype(jnp.bfloat16)
+                place_ref[p, across, down] = place
+                gates += dot(jnp.broadcast_to(gate, (8, tokens)).astype(jnp.bfloat16), place)
+            gate_ref[j, :, p * wide : (p + 1) * wide] = gates
+
+
+def slots(axis, n, local, tables):
+    tokens = tables[0].shape[1]
+    across, down = 2 * tokens, 2 * SLOT * local
+    return pl.pallas_call(
+        functools.partial(slots_kernel, axis, n, local),
+        out_shape=[
+            jax.ShapeDtypeStruct((n // 2, down, across), jnp.bfloat16),
+            jax.ShapeDtypeStruct((n // 2, across, down), jnp.bfloat16),
+            jax.ShapeDtypeStruct((local, 8, n * SLOT), jnp.float32),
+        ],
+        compiler_params=params(4 * max(1, n // 8)),
+    )(*tables)
+
+
+def gather_rows(local, pick_ref, token_refs, first, out):
     wide = 2 * SLOT
     features = out.shape[2]
     cols = features // 4
-    for p in range(n // 2):
+    for p in range(len(token_refs) // 2):
         refs = [ref for pair in token_refs[2 * p : 2 * p + 2] for ref in pair]
         for d in range(0, features, cols):
             part = slice(d, d + cols)
             tokens = jnp.concatenate([ref[:, part] for ref in refs], axis=0)
-            rows = dot(pick_ref[p], tokens).astype(jnp.bfloat16)
+            rows = dot(pick_ref[first + p], tokens).astype(jnp.bfloat16)
             for j in range(local):
                 out[j, p * wide : (p + 1) * wide, part] = rows[j * wide : (j + 1) * wide, :]
 
 
-def gather_columns(n, local, place_ref, token_refs, out):
+def gather_columns(local, place_ref, token_refs, first, out):
     wide = 2 * SLOT
     features = out.shape[1]
     size = features // 4
-    for p in range(n // 2):
+    for p in range(len(token_refs) // 2):
         refs = [ref for pair in token_refs[2 * p : 2 * p + 2] for ref in pair]
         for d in range(0, features, size):
             part = slice(d, d + size)
             tokens = jnp.concatenate([ref[:, part] for ref in refs], axis=0)
-            columns = dot(tokens.T, place_ref[p]).astype(jnp.bfloat16)
+            columns = dot(tokens.T, place_ref[first + p]).astype(jnp.bfloat16)
             for j in range(local):
                 out[j, part, p * wide : (p + 1) * wide] = columns[:, j * wide : (j + 1) * wide]
 
@@ -95,49 +135,29 @@
     return parts, refs[first:]
 
 
-def pre_kernel(axis, n, local, counts, *refs):
-    table_refs, refs = refs[:n], refs[n:]
-    token_refs, refs = split(refs, counts)
-    wg_ref, wu_ref, a_ref, b_ref, place_ref, xs, gcol, pick_ref = refs
-    experts = n * local
-    tokens = table_refs[0].shape[1]
-    wide = 2 * SLOT
-    hidden = wg_ref.shape[2]
-    cols = hidden // 2
-    me = lax.axis_index(axis)
-    row = lax.broadcasted_iota(jnp.int32, (2 * experts, tokens), 0)
-    slot = lax.broadcasted_iota(jnp.int32, (wide, tokens), 0).astype(jnp.float32)
-    for p in range(n // 2):
-        for j in range(local):
-            e = me * local + j
-            gates = jnp.zeros((wide, 1), jnp.float32)
-            for q in range(2):
-                table = table_refs[2 * p + q][...].astype(jnp.float32)
-                rank = jnp.sum(jnp.where(row == e, table, 0.0), axis=0, keepdims=True)
-                gate = jnp.sum(jnp.where(row == e + experts, table, 0.0), axis=0, keepdims=True)
-                pick = (slot == rank + q * SLOT).astype(jnp.float32)
-                gates += jnp.sum(pick * gate, axis=1, keepdims=True)
-                across = slice(q * tokens, (q + 1) * tokens)
-                down = slice(j * wide, (j + 1) * wide)
-                pick_ref[p, down, across] = pick.astype(jnp.bfloat16)
-                place_ref[p, across, down] = pick.T.astype(jnp.bfloat16)
-            gcol[j, p * wide : (p + 1) * wide, :] = gates
-    gather_rows(n, local, pick_ref, token_refs, xs)
-
-    @pl.loop(0, local)
-    def _(e):
-        for f in range(0, hidden, cols):
-            part = slice(f, f + cols)
-            gate_pre = dot(xs[e], wg_ref[e, :, part])
-            up_pre = dot(xs[e], wu_ref[e, :, part])
-            sig = jax.nn.sigmoid(gate_pre)
-            weighted = gcol[e] * sig
-            a_ref[e, part, :] = (weighted * up_pre * (1.0 + gate_pre * (1.0 - sig))).T
-            b_ref[e, part, :] = (weighted * gate_pre).T
+def flat(groups):
+    return [block for blocks in groups for block in blocks]
+
+
+def sizes(groups):
+    return [len(blocks) for blocks in groups]
+
+
+INSIDE = pl.BlockSpec(memory_space=pltpu.VMEM)
+OUTSIDE = pl.BlockSpec(memory_space=pltpu.HBM)
+ANYWHERE = pl.BlockSpec(memory_space=pl.ANY)
 
 
 def vmem(array):
     return pltpu.with_memory_space_constraint(array, pltpu.VMEM)
+
+
+def hbm(array):
+    return pltpu.with_memory_space_constraint(array, pltpu.HBM)
+
+
+def fetches(source, result, sems):
+    return [pltpu.make_async_copy(source.at[e], result.at[e], sems.at[e]) for e in range(source.shape[0])]
 
 
 def load_kernel(count, *refs):
@@ -158,7 +178,7 @@
     count = len(arrays)
     return pl.pallas_call(
         functools.partial(load_kernel, count),
-        in_specs=[pl.BlockSpec(memory_space=pltpu.HBM)] * count + [pl.BlockSpec(memory_space=pl.ANY)],
+        in_specs=[OUTSIDE] * count + [pl.BlockSpec(memory_space=pl.ANY)],
         out_specs=[pl.BlockSpec(memory_space=pltpu.VMEM)] * (count + 1),
         out_shape=[pltpu.VMEM(w.shape, w.dtype) for w in arrays]
         + [jax.ShapeDtypeStruct((8, 128), jnp.float32)],
@@ -170,6 +190,36 @@
     )(*[pltpu.with_memory_space_constraint(w, pltpu.HBM) for w in arrays], after)
 
 
+def rows_kernel(local, counts, pick_ref, *refs):
+    token_refs, (_, out_ref) = split(refs, counts)
+    gather_rows(local, pick_ref, token_refs, 0, out_ref)
+
+
+def early_rows(local, pick, tokens, after):
+    features = tokens[0][0].shape[1]
+    return pl.pallas_call(
+        functools.partial(rows_kernel, local, sizes(tokens)),
+        in_specs=[INSIDE] * (1 + len(flat(tokens))) + [ANYWHERE],
+        out_shape=jax.ShapeDtypeStruct((local, 2 * SLOT, features), jnp.bfloat16),
+        compiler_params=params(4),
+    )(pick, *flat(tokens), after)
+
+
+def columns_kernel(local, counts, place_ref, *refs):
+    token_refs, (_, out_ref) = split(refs, counts)
+    gather_columns(local, place_ref, token_refs, 0, out_ref)
+
+
+def early_columns(local, place, tokens, after):
+    features = tokens[0][0].shape[1]
+    return pl.pallas_call(
+        functools.partial(columns_kernel, local, sizes(tokens)),
+        in_specs=[INSIDE] * (1 + len(flat(tokens))) + [ANYWHERE],
+        out_shape=jax.ShapeDtypeStruct((local, features, 2 * SLOT), jnp.bfloat16),
+        compiler_params=params(4),
+    )(place, *flat(tokens), after)
+
+
 def relay_kernel(x_ref, y_ref, *refs):
     upper_ref, lower_ref = refs[-2:]
     half = upper_ref.shape[0]
@@ -202,37 +252,52 @@
     )(array, after)
 
 
-def pre(axis, n, tables, tokens, wg, wu):
+def pre_kernel(local, counts, pick_ref, gate_ref, first_ref, *refs):
+    token_refs, refs = split(refs, counts)
+    wg_ref, wu_ref, a_ref, b_ref, xs = refs
+    hidden = wg_ref.shape[2]
+    cols = hidden // 2
+    gather_rows(local, pick_ref, token_refs, 1, xs)
+
+    @pl.loop(0, local)
+    def _(e):
+        rows = jnp.concatenate([first_ref[e], xs[e]], axis=0)
+        gates = gate_ref[e][:1, :]
+        for f in range(0, hidden, cols):
+            part = slice(f, f + cols)
+            gate_pre = dot(rows, wg_ref[e, :, part])
+            up_pre = dot(rows, wu_ref[e, :, part])
+            sig = jax.nn.sigmoid(gate_pre)
+            a_ref[e, part, :] = (sig * up_pre * (1.0 + gate_pre * (1.0 - sig))).T * gates
+            b_ref[e, part, :] = (sig * gate_pre).T * gates
+
+
+def pre(n, pick, gates, first, tokens, wg, wu):
     local, features, hidden = wg.shape
     rows = n * SLOT
-    across, down = 2 * tables[0].shape[1], 2 * SLOT * local
-    return pl.pallas_call(
-        functools.partial(pre_kernel, axis, n, local, [len(t) for t in tokens]),
+    return pl.pallas_call(
+        functools.partial(pre_kernel, local, sizes(tokens)),
+        in_specs=[INSIDE] * (5 + len(flat(tokens))),
         out_shape=[
             jax.ShapeDtypeStruct((local, hidden, rows), jnp.float32),
             jax.ShapeDtypeStruct((local, hidden, rows), jnp.float32),
-            jax.ShapeDtypeStruct((n // 2, across, down), jnp.bfloat16),
         ],
-        scratch_shapes=[
-            pltpu.VMEM((local, rows, features), jnp.bfloat16),
-            pltpu.VMEM((local, rows, 1), jnp.float32),
-            pltpu.VMEM((n // 2, down, across), jnp.bfloat16),
-        ],
+        scratch_shapes=[pltpu.VMEM((local, rows - 2 * SLOT, features), jnp.bfloat16)],
         compiler_params=params(PRE_MIB * max(1, n // 4)),
         cost_estimate=pl.CostEstimate(
             flops=4 * local * rows * features * hidden,
             bytes_accessed=4 * local * features * hidden,
             transcendentals=local * rows * hidden,
         ),
-    )(*tables, *[block for t in tokens for block in t], vmem(wg), vmem(wu))
-
-
-def back_kernel(n, local, counts, place_ref, *refs):
+    )(pick, gates, first, *flat(tokens), vmem(wg), vmem(wu))
+
+
+def back_kernel(local, counts, place_ref, first_ref, *refs):
     token_refs, refs = split(refs, counts)
     wd_ref, a_ref, b_ref, _, _, hg_ref, hu_ref, gs, weight, sems = refs
     hidden = wd_ref.shape[1]
+    cols = hidden // 2
     held = weight.shape[0]
-    cols = hidden // 2
 
     def fetch(e, i):
         part = pl.ds(i * cols, cols)
@@ -242,14 +307,15 @@
     for e in range(held):
         for i in range(2):
             fetch(e, i).start()
-    gather_columns(n, local, place_ref, token_refs, gs)
+    gather_columns(local, place_ref, token_refs, 1, gs)
 
     @pl.loop(0, local)
     def _(e):
+        rows = jnp.concatenate([first_ref[e], gs[e]], axis=1)
         for i in range(2):
             part = slice(i * cols, (i + 1) * cols)
             fetch(e, i).wait()
-            back = dot(weight[lax.rem(e, held), part, :], gs[e])
+            back = dot(weight[lax.rem(e, held), part, :], rows)
             hg_ref[e, part, :] = (back * a_ref[e, part, :]).astype(jnp.bfloat16)
             hu_ref[e, part, :] = (back * b_ref[e, part, :]).astype(jnp.bfloat16)
 
@@ -258,28 +324,26 @@
                 fetch(e + held, i).start()
 
 
-def back(n, place, tokens, wd, a, b, wg, wu):
+def back(n, place, first, tokens, wd, a, b, wg, wu):
     local, hidden, features = wd.shape
     rows = n * SLOT
-    blocks = [block for t in tokens for block in t]
     shape = jax.ShapeDtypeStruct((local, hidden, rows), jnp.bfloat16)
-    inside, outside = pl.BlockSpec(memory_space=pltpu.VMEM), pl.BlockSpec(memory_space=pltpu.HBM)
-    return pl.pallas_call(
-        functools.partial(back_kernel, n, local, [len(t) for t in tokens]),
-        in_specs=[inside] * (1 + len(blocks)) + [outside] + [inside] * 4,
+    return pl.pallas_call(
+        functools.partial(back_kernel, local, sizes(tokens)),
+        in_specs=[INSIDE] * (2 + len(flat(tokens))) + [OUTSIDE] + [INSIDE] * 4,
         out_shape=[shape, shape],
         scratch_shapes=[
-            pltpu.VMEM((local, features, rows), jnp.bfloat16),
+            pltpu.VMEM((local, features, rows - 2 * SLOT), jnp.bfloat16),
             pltpu.VMEM((min(local, 2), hidden, features), jnp.bfloat16),
             pltpu.SemaphoreType.DMA((min(local, 2), 2)),
         ],
-        compiler_params=params(BACK_MIB * max(1, n // 8)),
+        compiler_params=params(BACK_MIB * max(1, n // 4)),
         cost_estimate=pl.CostEstimate(
             flops=2 * local * rows * features * hidden,
             bytes_accessed=2 * local * features * hidden,
             transcendentals=0,
         ),
-    )(place, *blocks, pltpu.with_memory_space_constraint(wd, pltpu.HBM), a, b, vmem(wg), vmem(wu))
+    )(place, first, *flat(tokens), hbm(wd), a, b, vmem(wg), vmem(wu))
 
 
 def out_kernel(n, local, orders, chunk, place_ref, hg_ref, hu_ref, wg_ref, wu_ref, *rest):
@@ -345,22 +409,27 @@
 
     table = rank_table(routes.T, route_gates.T, experts)
     tables = [table] + [swap(table, k) for k in range(1, n)]
+    pick, place, gates = slots(axis, n, local, tables)
     gate_proj, up_proj, done = load((gate_proj, up_proj), table)
     if n == 4:
         x_near = [swap(saved_input, 1), swap(saved_input, 2)]
-        upper, lower = relay_parts(x_near, [done, *tables[1:]])
+        upper, lower = relay_parts(x_near, [done, place])
         sent = passed(grad_out, upper)
         x_blocks = [[saved_input], *[[x] for x in x_near], [swap(upper, 2), swap(lower, 1)]]
         g_near = [swap(sent, 1), swap(sent, 2)]
     else:
         x_blocks = [[saved_input]] + [[swap(saved_input, k)] for k in range(1, n)]
-    a, b, place = pre(axis, n, tables, x_blocks, gate_proj, up_proj)
+        sent = grad_out
+    x_first = early_rows(local, pick, x_blocks[:2], sent)
+    a, b = pre(n, pick, gates, x_first, x_blocks[2:], gate_proj, up_proj)
     if n == 4:
-        upper, lower = relay_parts(g_near, [place])
+        upper, lower = relay_parts(g_near, [a])
         g_blocks = [[sent], *[[g] for g in g_near], [swap(upper, 2), swap(lower, 1)]]
     else:
         g_blocks = [[grad_out]] + [[swap(grad_out, k)] for k in range(1, n)]
-    hg, hu = back(n, place, g_blocks, down_proj, a, b, gate_proj, up_proj)
+        upper = a
+    g_first = early_columns(local, place, g_blocks[:2], upper)
+    hg, hu = back(n, place, g_first, g_blocks[2:], down_proj, a, b, gate_proj, up_proj)
     parts = []
     for chunk in range(CHUNKS):
         if n == 4:

time: 82 us -> 81.6 us (level)
  starting transfers between devices: 23.6 us -> 21.8 us
  Pallas kernels: 41 us -> 42 us
    ppermute x19, starting transfers between devices: 23.6 us -> 21.8 us  [swap(): return lax.ppermute(array, axis, [(i, i ^ k) for i in range(n)])]
    pallas_call x3 -> x6, Pallas kernels: 29.8 us -> 30.9 us  [the longest x1 10.9 us: pre(): pl.pallas_call(functools.partial(pre_kernel, local, sizes(tokens)), in_sp...]
  transfers between devices with their start and end apart: 19 -> 19, of which waited for: 9 -> 10; matrix products, arithmetic and copies ran while one was open for 0% -> 0% of each run, Pallas kernels for 34% -> 36%
where the time goes in v5:
time: 81.6 us; the launch traced here: 81.4 us
  Pallas kernels  42 us (51%)
  starting transfers between devices  21.8 us (27%)
  waiting for transfers between devices  16.5 us (20%)
    ppermute x19, starting transfers between devices, swap(): return lax.ppermute(array, axis, [(i, i ^ k) for i in range(n)])  21.8 us
    ppermute x19, waiting for transfers between devices, swap(): return lax.ppermute(array, axis, [(i, i ^ k) for i in range(n)])  16.5 us
    pallas_call x1, Pallas kernels, pre(): pl.pallas_call(functools.partial(pre_kernel, local, sizes(tokens)), in_sp...  10.9 us
    pallas_call x1, Pallas kernels, back(): pl.pallas_call(functools.partial(back_kernel, local, sizes(tokens)), in_s...  9.76 us
    pallas_call x4, Pallas kernels, partial_sums(): pl.pallas_call(functools.partial(out_kernel, n, local, orders, chunk), ou...  8.58 us
    pallas_call x1, Pallas kernels, load(): pl.pallas_call(functools.partial(load_kernel, count), in_specs=[OUTSIDE]...  8.3 us
  transfers between devices with their start and end apart: 19, of which 10 were waited for; matrix products, arithmetic and copies ran while one was open for 0% of the time, Pallas kernels for 36%

profile of v5, /device:TPU:0, one launch (start us, length us, event | category | flops | bytes accessed | tf_op | source)
XLA Modules:
  0.0 81.4 jit_solution(8571603602991808926)
XLA Ops:
  0.0 2.9 %collective-permute-start.3 = (bf16[128,2048]{1,0:T(8,128)(2,1)}, bf16[128,2048]{1,0:T(8,128)(2,1)S(1)}, u32[]{:S(2)}, u32[]{:S(2)}) collective-permute-start(bf16[128,2048]{1,0:T(8,128)(2,1)} %refs_0_.3), channel_id=1, source_target_pairs={{0,1},{1,0},{2,3},{3,2},{4,5},{5,4},{6,7},{7,6},{8,9},{9,8},{10,11... | collective-permute-start | bytes 1572872 | tf_op jit(solution)/shard_map/ppermute | solution.py:408
  2.9 1.5 %collective-permute-start.4 = (bf16[128,2048]{1,0:T(8,128)(2,1)}, bf16[128,2048]{1,0:T(8,128)(2,1)S(1)}, u32[]{:S(2)}, u32[]{:S(2)}) collective-permute-start(bf16[128,2048]{1,0:T(8,128)(2,1)} %refs_0_.3), channel_id=1, source_target_pairs={{0,2},{1,3},{2,0},{3,1},{4,6},{5,7},{6,4},{7,5},{8,10},{9,11},{10,... | collective-permute-start | bytes 1572872 | tf_op jit(solution)/shard_map/ppermute | solution.py:408
  4.5 1.5 %shard_map.73.refs_0_.refs_2_ = bf16[32,128]{1,0:T(8,128)(2,1)} custom-call(s32[8,128]{1,0:T(8,128)} %bitcast.2, bf16[8,128]{1,0:T(8,128)(2,1)} %bitcast.3), custom_call_target="tpu_custom_call" | custom-call | tf_op jit(solution)/shard_map/pallas_call | solution.py:56
  5.9 0.0 copy-start
  5.9 0.0 collective-permute-start.2
  6.0 2.0 %collective-permute-start.1 = (bf16[32,128]{1,0:T(8,128)(2,1)}, bf16[32,128]{1,0:T(8,128)(2,1)S(1)}, u32[]{:S(2)}, u32[]{:S(2)}) collective-permute-start(bf16[32,128]{1,0:T(8,128)(2,1)} %shard_map.73.refs_0_.refs_2_), channel_id=1, source_target_pairs={{0,2},{1,3},{2,0},{3,1},{4,6},{5,7},{6,4},{7,5},{8,10},{9,11},{10,... | collective-permute-start | bytes 24584 | tf_op jit(solution)/shard_map/ppermute | solution.py:408
  7.9 1.5 %collective-permute-start = (bf16[32,128]{1,0:T(8,128)(2,1)}, bf16[32,128]{1,0:T(8,128)(2,1)S(1)}, u32[]{:S(2)}, u32[]{:S(2)}) collective-permute-start(bf16[32,128]{1,0:T(8,128)(2,1)} %shard_map.73.refs_0_.refs_2_), channel_id=1, source_target_pairs={{0,1},{1,0},{2,3},{3,2},{4,5},{5,4},{6,7},{7,6},{8,9},{9,8},{10,11... | collective-permute-start | bytes 24584 | tf_op jit(solution)/shard_map/ppermute | solution.py:408
  9.4 0.0 copy-start.2
  9.4 0.7 copy-done.2
  10.2 8.3 %shard_map.75 = (bf16[4,2048,768]{2,1,0:T(8,128)(2,1)S(1)}, bf16[4,2048,768]{2,1,0:T(8,128)(2,1)S(1)}, f32[8,128]{1,0:T(8,128)S(1)}) custom-call(bf16[4,2048,768]{2,1,0:T(8,128)(2,1)} %refs_0_.2, bf16[4,2048,768]{2,1,0:T(8,128)(2,1)} %refs_1_.1, bf16[32,128]{1,0:T(8,128)(2,1)S(1)} %copy-done.2), custom_call_target="tpu_custom_call" | custom-call | bytes 50331648 | tf_op jit(solution)/shard_map/pallas_call | solution.py:179
  18.5 0.0 copy-start.1
  18.5 0.0 collective-permute-done.2.refs_3_
  18.5 0.0 collective-permute-done.1.refs_2_
  18.5 0.0 collective-permute-done.refs_1_
  18.5 0.4 shard_map.74
  19.0 0.0 collective-permute-done.3.x_ref.refs_1_
  19.0 0.0 collective-permute-done.4.y_ref.refs_0_
  19.0 0.6 collective-permute-start.8
  19.6 0.1 collective-permute-start.7
  19.7 0.0 copy-done
  19.7 2.0 %collective-permute-start.6 = (bf16[128,2048]{1,0:T(8,128)(2,1)S(1)}, bf16[128,2048]{1,0:T(8,128)(2,1)S(1)}, u32[]{:S(2)}, u32[]{:S(2)}) collective-permute-start(bf16[128,2048]{1,0:T(8,128)(2,1)S(1)} %shard_map.77.refs_2_.refs_0_), channel_id=1, source_target_pairs={{0,2},{1,3},{2,0},{3,1},{4,6},{5,7},{6,4},{7,5},{8,10},{9,11},{10,... | collective-permute-start | bytes 1572872 | tf_op jit(solution)/shard_map/ppermute | solution.py:408
  21.8 1.5 %collective-permute-start.5 = (bf16[128,2048]{1,0:T(8,128)(2,1)S(1)}, bf16[128,2048]{1,0:T(8,128)(2,1)S(1)}, u32[]{:S(2)}, u32[]{:S(2)}) collective-permute-start(bf16[128,2048]{1,0:T(8,128)(2,1)S(1)} %shard_map.77.refs_2_.refs_0_), channel_id=1, source_target_pairs={{0,1},{1,0},{2,3},{3,2},{4,5},{5,4},{6,7},{7,6},{8,9},{9,8},{10,11... | collective-permute-start | bytes 1572872 | tf_op jit(solution)/shard_map/ppermute | solution.py:408
  23.2 0.0 copy-done.1
  23.2 0.7 shard_map.78.first_ref
  24.0 4.4 %collective-permute-done.8.refs_2_ = bf16[64,2048]{1,0:T(8,128)(2,1)S(1)} collective-permute-done((bf16[64,2048]{1,0:T(8,128)(2,1)S(1)}, bf16[64,2048]{1,0:T(8,128)(2,1)S(1)}, u32[]{:S(2)}, u32[]{:S(2)}) %collective-permute-start.8) | collective-permute-done | bytes 262176 | tf_op jit(solution)/shard_map/ppermute | solution.py:408
  28.3 0.5 collective-permute-done.7.refs_1_
  28.9 10.9 %shard_map.79 = (f32[4,768,256]{2,1,0:T(8,128)S(1)}, f32[4,768,256]{2,1,0:T(8,128)S(1)}) custom-call(bf16[2,512,256]{2,1,0:T(8,128)(2,1)S(1)} %get-tuple-element.34.pick_ref, f32[4,8,256]{2,1,0:T(8,128)S(1)} %get-tuple-element.35.gate_ref, bf16[4,128,2048]{2,1,0:T(8,128)(2,1)S(1)} %shard_map.78.first_ref, ...), custom_call_target="tpu_custom_call" | custom-call | flops 6442450944 | bytes 25165824 | tf_op jit(solution)/shard_map/pallas_call | solution.py:278
  39.8 0.0 collective-permute-done.6.y_ref.refs_0_
  39.8 0.0 collective-permute-done.5.x_ref.refs_1_
  39.8 1.6 %collective-permute-start.10 = (bf16[64,2048]{1,0:T(8,128)(2,1)S(1)}, bf16[64,2048]{1,0:T(8,128)(2,1)S(1)}, u32[]{:S(2)}, u32[]{:S(2)}) collective-permute-start(bf16[64,2048]{1,0:T(8,128)(2,1)S(1)} %get-tuple-element.41), channel_id=1, source_target_pairs={{0,1},{1,0},{2,3},{3,2},{4,5},{5,4},{6,7},{7,6},{8,9},{9,8},{10,11... | collective-permute-start | bytes 786440 | tf_op jit(solution)/shard_map/ppermute | solution.py:408
  41.4 0.5 collective-permute-start.9
  41.9 0.7 shard_map.81.first_ref
  42.6 3.6 %collective-permute-done.10.refs_2_ = bf16[64,2048]{1,0:T(8,128)(2,1)S(1)} collective-permute-done((bf16[64,2048]{1,0:T(8,128)(2,1)S(1)}, bf16[64,2048]{1,0:T(8,128)(2,1)S(1)}, u32[]{:S(2)}, u32[]{:S(2)}) %collective-permute-start.10) | collective-permute-done | bytes 262176 | tf_op jit(solution)/shard_map/ppermute | solution.py:408
  46.3 1.5 %collective-permute-done.9.refs_1_ = bf16[64,2048]{1,0:T(8,128)(2,1)S(1)} collective-permute-done((bf16[64,2048]{1,0:T(8,128)(2,1)S(1)}, bf16[64,2048]{1,0:T(8,128)(2,1)S(1)}, u32[]{:S(2)}, u32[]{:S(2)}) %collective-permute-start.9) | collective-permute-done | bytes 262176 | tf_op jit(solution)/shard_map/ppermute | solution.py:408
  47.8 9.8 %shard_map.82 = (bf16[4,768,256]{2,1,0:T(8,128)(2,1)S(1)}, bf16[4,768,256]{2,1,0:T(8,128)(2,1)S(1)}) custom-call(bf16[2,256,512]{2,1,0:T(8,128)(2,1)S(1)} %get-tuple-element.31.refs_1_.place_ref, bf16[4,2048,128]{2,1,0:T(8,128)(2,1)S(1)} %shard_map.81.first_ref, bf16[128,2048]{1,0:T(8,128)(2,1)S(1)} %collective-permute-done.6.y_ref.refs_0_, ...), custom_call_target="tpu_custom_call" | custom-call | flops 3221225472 | bytes 12582912 | tf_op jit(solution)/shard_map/pallas_call | solution.py:331
  57.5 2.1 %shard_map.86 = (f32[1,128,512]{2,1,0:T(8,128)S(1)}, bf16[2,128,512]{2,1,0:T(8,128)(2,1)S(1)}, bf16[1,128,512]{2,1,0:T(8,128)(2,1)S(1)}) custom-call(bf16[2,256,512]{2,1,0:T(8,128)(2,1)S(1)} %get-tuple-element.31.refs_1_.place_ref, bf16[4,768,256]{2,1,0:T(8,128)(2,1)S(1)} %get-tuple-element.43.hg_ref, bf16[4,768,256]{2,1,0:T(8,128)(2,1)S(1)} %get-tuple-element.44.hu_ref, ...), custom_call_target="tpu_custom_call" | custom-call | flops 402653184 | bytes 1572864 | tf_op jit(solution)/shard_map/pallas_call | solution.py:376
  59.7 0.6 collective-permute-start.17
  60.3 2.1 %shard_map.85 = (f32[1,128,512]{2,1,0:T(8,128)S(1)}, bf16[2,128,512]{2,1,0:T(8,128)(2,1)S(1)}, bf16[1,128,512]{2,1,0:T(8,128)(2,1)S(1)}) custom-call(bf16[2,256,512]{2,1,0:T(8,128)(2,1)S(1)} %get-tuple-element.31.refs_1_.place_ref, bf16[4,768,256]{2,1,0:T(8,128)(2,1)S(1)} %get-tuple-element.43.hg_ref, bf16[4,768,256]{2,1,0:T(8,128)(2,1)S(1)} %get-tuple-element.44.hu_ref, ...), custom_call_target="tpu_custom_call" | custom-call | flops 402653184 | bytes 1572864 | tf_op jit(solution)/shard_map/pallas_call | solution.py:376
  62.4 0.1 collective-permute-start.15
  62.5 2.1 %shard_map.84 = (f32[1,128,512]{2,1,0:T(8,128)S(1)}, bf16[2,128,512]{2,1,0:T(8,128)(2,1)S(1)}, bf16[1,128,512]{2,1,0:T(8,128)(2,1)S(1)}) custom-call(bf16[2,256,512]{2,1,0:T(8,128)(2,1)S(1)} %get-tuple-element.31.refs_1_.place_ref, bf16[4,768,256]{2,1,0:T(8,128)(2,1)S(1)} %get-tuple-element.43.hg_ref, bf16[4,768,256]{2,1,0:T(8,128)(2,1)S(1)} %get-tuple-element.44.hu_ref, ...), custom_call_target="tpu_custom_call" | custom-call | flops 402653184 | bytes 1572864 | tf_op jit(solution)/shard_map/pallas_call | solution.py:376
  64.7 2.0 %collective-permute-start.13 = (bf16[2,128,512]{2,1,0:T(8,128)(2,1)S(1)}, bf16[2,128,512]{2,1,0:T(8,128)(2,1)S(1)}, u32[]{:S(2)}, u32[]{:S(2)}) collective-permute-start(bf16[2,128,512]{2,1,0:T(8,128)(2,1)S(1)} %get-tuple-element.49), channel_id=1, source_target_pairs={{0,2},{1,3},{2,0},{3,1},{4,6},{5,7},{6,4},{7,5},{8,10},{9,11},{10,... | collective-permute-start | bytes 786440 | tf_op jit(solution)/shard_map/ppermute | solution.py:408
  66.7 2.1 %shard_map.83 = (f32[1,128,512]{2,1,0:T(8,128)S(1)}, bf16[2,128,512]{2,1,0:T(8,128)(2,1)S(1)}, bf16[1,128,512]{2,1,0:T(8,128)(2,1)S(1)}) custom-call(bf16[2,256,512]{2,1,0:T(8,128)(2,1)S(1)} %get-tuple-element.31.refs_1_.place_ref, bf16[4,768,256]{2,1,0:T(8,128)(2,1)S(1)} %get-tuple-element.43.hg_ref, bf16[4,768,256]{2,1,0:T(8,128)(2,1)S(1)} %get-tuple-element.44.hu_ref, ...), custom_call_target="tpu_custom_call" | custom-call | flops 402653184 | bytes 1572864 | tf_op jit(solution)/shard_map/pallas_call | solution.py:376
  68.9 1.6 %collective-permute-start.11 = (bf16[2,128,512]{2,1,0:T(8,128)(2,1)S(1)}, bf16[2,128,512]{2,1,0:T(8,128)(2,1)S(1)}, u32[]{:S(2)}, u32[]{:S(2)}) collective-permute-start(bf16[2,128,512]{2,1,0:T(8,128)(2,1)S(1)} %get-tuple-element.46), channel_id=1, source_target_pairs={{0,1},{1,0},{2,3},{3,2},{4,5},{5,4},{6,7},{7,6},{8,9},{9,8},{10,11... | collective-permute-start | bytes 786440 | tf_op jit(solution)/shard_map/ppermute | solution.py:408
  70.4 0.0 collective-permute-done.17
  70.5 0.6 collective-permute-start.18
  71.1 0.6 collective-permute-done.15
  71.8 1.3 %collective-permute-start.16 = (bf16[1,128,512]{2,1,0:T(8,128)(2,1)S(1)}, bf16[1,128,512]{2,1,0:T(8,128)(2,1)S(1)}, u32[]{:S(2)}, u32[]{:S(2)}) collective-permute-start(bf16[1,128,512]{2,1,0:T(8,128)(2,1)S(1)} %add_convert_fusion.1), channel_id=1, source_target_pairs={{0,2},{1,3},{2,0},{3,1},{4,6},{5,7},{6,4},{7,5},{8,10},{9,11},{10,... | collective-permute-start | bytes 393224 | tf_op jit(solution)/shard_map/ppermute | solution.py:408
  73.1 0.0 collective-permute-done.13
  73.1 0.9 %collective-permute-start.14 = (bf16[1,128,512]{2,1,0:T(8,128)(2,1)S(1)}, bf16[1,128,512]{2,1,0:T(8,128)(2,1)S(1)}, u32[]{:S(2)}, u32[]{:S(2)}) collective-permute-start(bf16[1,128,512]{2,1,0:T(8,128)(2,1)S(1)} %add_convert_fusion.2), channel_id=1, source_target_pairs={{0,1},{1,0},{2,3},{3,2},{4,5},{5,4},{6,7},{7,6},{8,9},{9,8},{10,11... | collective-permute-start | bytes 393224 | tf_op jit(solution)/shard_map/ppermute | solution.py:408
  74.0 1.3 %collective-permute-done.11 = bf16[2,128,512]{2,1,0:T(8,128)(2,1)S(1)} collective-permute-done((bf16[2,128,512]{2,1,0:T(8,128)(2,1)S(1)}, bf16[2,128,512]{2,1,0:T(8,128)(2,1)S(1)}, u32[]{:S(2)}, u32[]{:S(2)}) %collective-permute-start.11) | collective-permute-done | bytes 262176 | tf_op jit(solution)/shard_map/ppermute | solution.py:408
  75.4 0.5 collective-permute-start.12
  76.0 0.8 collective-permute-done.18.refs_11_
  76.7 0.1 collective-permute-done.16.refs_8_
  76.8 1.4 %collective-permute-done.14.refs_5_ = bf16[1,128,512]{2,1,0:T(8,128)(2,1)S(1)} collective-permute-done((bf16[1,128,512]{2,1,0:T(8,128)(2,1)S(1)}, bf16[1,128,512]{2,1,0:T(8,128)(2,1)S(1)}, u32[]{:S(2)}, u32[]{:S(2)}) %collective-permute-start.14) | collective-permute-done | bytes 131104 | tf_op jit(solution)/shard_map/ppermute | solution.py:408
  78.1 2.2 %collective-permute-done.12.refs_2_ = bf16[1,128,512]{2,1,0:T(8,128)(2,1)S(1)} collective-permute-done((bf16[1,128,512]{2,1,0:T(8,128)(2,1)S(1)}, bf16[1,128,512]{2,1,0:T(8,128)(2,1)S(1)}, u32[]{:S(2)}, u32[]{:S(2)}) %collective-permute-start.12) | collective-permute-done | bytes 131104 | tf_op jit(solution)/shard_map/ppermute | solution.py:408
  80.4 1.0 %shard_map.87 = bf16[128,2048]{1,0:T(8,128)(2,1)} custom-call(f32[1,128,512]{2,1,0:T(8,128)S(1)} %get-tuple-element.45.refs_0_, bf16[1,128,512]{2,1,0:T(8,128)(2,1)S(1)} %slice.32.refs_1_, bf16[1,128,512]{2,1,0:T(8,128)(2,1)S(1)} %collective-permute-done.12.refs_2_, f32[1,128,512]{2,1,0:T(8,128)S(1)} %get-tuple-element.48.refs_3_, ...), custom_call_target="tpu_custom_call" | custom-call | tf_op jit(solution)/shard_map/pallas_call | solution.py:446
  (11 shorter events, 0.3 us)
Async XLA Ops:
  0.0 19.0 %collective-permute-start.3 = (bf16[128,2048]{1,0:T(8,128)(2,1)}, bf16[128,2048]{1,0:T(8,128)(2,1)S(1)}, u32[]{:S(2)}, u32[]{:S(2)}) collective-permute-start(bf16[128,2048]{1,0:T(8,128)(2,1)} %refs_0_.3), channel_id=1, source_target_pairs={{0,1},{1,0},{2,3},{3,2},{4,5},{5,4},{6,7},{7,6},{8,9},{9,8},{10,11... | collective-permute-start | bytes 1572872 | tf_op jit(solution)/shard_map/ppermute | solution.py:408
  2.9 16.0 %collective-permute-start.4 = (bf16[128,2048]{1,0:T(8,128)(2,1)}, bf16[128,2048]{1,0:T(8,128)(2,1)S(1)}, u32[]{:S(2)}, u32[]{:S(2)}) collective-permute-start(bf16[128,2048]{1,0:T(8,128)(2,1)} %refs_0_.3), channel_id=1, source_target_pairs={{0,2},{1,3},{2,0},{3,1},{4,6},{5,7},{6,4},{7,5},{8,10},{9,11},{10,... | collective-permute-start | bytes 1572872 | tf_op jit(solution)/shard_map/ppermute | solution.py:408
  5.9 13.7 %copy-start = (bf16[128,2048]{1,0:T(8,128)(2,1)S(1)}, bf16[128,2048]{1,0:T(8,128)(2,1)}, u32[]{:S(2)}) copy-start(bf16[128,2048]{1,0:T(8,128)(2,1)} %array_ref.1) | copy-start | bytes 1572868
  5.9 12.5 %collective-permute-start.2 = (bf16[32,128]{1,0:T(8,128)(2,1)}, bf16[32,128]{1,0:T(8,128)(2,1)S(1)}, u32[]{:S(2)}, u32[]{:S(2)}) collective-permute-start(bf16[32,128]{1,0:T(8,128)(2,1)} %shard_map.73.refs_0_.refs_2_), channel_id=1, source_target_pairs={{0,3},{1,2},{2,1},{3,0},{4,7},{5,6},{6,5},{7,4},{8,11},{9,10},{10,... | collective-permute-start | bytes 24584 | tf_op jit(solution)/shard_map/ppermute | solution.py:408
  6.0 12.6 %collective-permute-start.1 = (bf16[32,128]{1,0:T(8,128)(2,1)}, bf16[32,128]{1,0:T(8,128)(2,1)S(1)}, u32[]{:S(2)}, u32[]{:S(2)}) collective-permute-start(bf16[32,128]{1,0:T(8,128)(2,1)} %shard_map.73.refs_0_.refs_2_), channel_id=1, source_target_pairs={{0,2},{1,3},{2,0},{3,1},{4,6},{5,7},{6,4},{7,5},{8,10},{9,11},{10,... | collective-permute-start | bytes 24584 | tf_op jit(solution)/shard_map/ppermute | solution.py:408
  7.9 10.6 %collective-permute-start = (bf16[32,128]{1,0:T(8,128)(2,1)}, bf16[32,128]{1,0:T(8,128)(2,1)S(1)}, u32[]{:S(2)}, u32[]{:S(2)}) collective-permute-start(bf16[32,128]{1,0:T(8,128)(2,1)} %shard_map.73.refs_0_.refs_2_), channel_id=1, source_target_pairs={{0,1},{1,0},{2,3},{3,2},{4,5},{5,4},{6,7},{7,6},{8,9},{9,8},{10,11... | collective-permute-start | bytes 24584 | tf_op jit(solution)/shard_map/ppermute | solution.py:408
  9.4 0.7 copy-start.2
  18.5 4.8 %copy-start.1 = (bf16[128,2048]{1,0:T(8,128)(2,1)S(1)}, bf16[128,2048]{1,0:T(8,128)(2,1)}, u32[]{:S(2)}) copy-start(bf16[128,2048]{1,0:T(8,128)(2,1)} %refs_0_.3) | copy-start | bytes 1572868
  19.0 9.3 %collective-permute-start.8 = (bf16[64,2048]{1,0:T(8,128)(2,1)S(1)}, bf16[64,2048]{1,0:T(8,128)(2,1)S(1)}, u32[]{:S(2)}, u32[]{:S(2)}) collective-permute-start(bf16[64,2048]{1,0:T(8,128)(2,1)S(1)} %get-tuple-element.36), channel_id=1, source_target_pairs={{0,1},{1,0},{2,3},{3,2},{4,5},{5,4},{6,7},{7,6},{8,9},{9,8},{10,11... | collective-permute-start | bytes 786440 | tf_op jit(solution)/shard_map/ppermute | solution.py:408
  19.6 9.2 %collective-permute-start.7 = (bf16[64,2048]{1,0:T(8,128)(2,1)S(1)}, bf16[64,2048]{1,0:T(8,128)(2,1)S(1)}, u32[]{:S(2)}, u32[]{:S(2)}) collective-permute-start(bf16[64,2048]{1,0:T(8,128)(2,1)S(1)} %get-tuple-element.33._), channel_id=1, source_target_pairs={{0,2},{1,3},{2,0},{3,1},{4,6},{5,7},{6,4},{7,5},{8,10},{9,11},{10,... | collective-permute-start | bytes 786440 | tf_op jit(solution)/shard_map/ppermute | solution.py:408
  19.7 20.1 %collective-permute-start.6 = (bf16[128,2048]{1,0:T(8,128)(2,1)S(1)}, bf16[128,2048]{1,0:T(8,128)(2,1)S(1)}, u32[]{:S(2)}, u32[]{:S(2)}) collective-permute-start(bf16[128,2048]{1,0:T(8,128)(2,1)S(1)} %shard_map.77.refs_2_.refs_0_), channel_id=1, source_target_pairs={{0,2},{1,3},{2,0},{3,1},{4,6},{5,7},{6,4},{7,5},{8,10},{9,11},{10,... | collective-permute-start | bytes 1572872 | tf_op jit(solution)/shard_map/ppermute | solution.py:408
  21.8 18.0 %collective-permute-start.5 = (bf16[128,2048]{1,0:T(8,128)(2,1)S(1)}, bf16[128,2048]{1,0:T(8,128)(2,1)S(1)}, u32[]{:S(2)}, u32[]{:S(2)}) collective-permute-start(bf16[128,2048]{1,0:T(8,128)(2,1)S(1)} %shard_map.77.refs_2_.refs_0_), channel_id=1, source_target_pairs={{0,1},{1,0},{2,3},{3,2},{4,5},{5,4},{6,7},{7,6},{8,9},{9,8},{10,11... | collective-permute-start | bytes 1572872 | tf_op jit(solution)/shard_map/ppermute | solution.py:408
  39.8 6.4 %collective-permute-start.10 = (bf16[64,2048]{1,0:T(8,128)(2,1)S(1)}, bf16[64,2048]{1,0:T(8,128)(2,1)S(1)}, u32[]{:S(2)}, u32[]{:S(2)}) collective-permute-start(bf16[64,2048]{1,0:T(8,128)(2,1)S(1)} %get-tuple-element.41), channel_id=1, source_target_pairs={{0,1},{1,0},{2,3},{3,2},{4,5},{5,4},{6,7},{7,6},{8,9},{9,8},{10,11... | collective-permute-start | bytes 786440 | tf_op jit(solution)/shard_map/ppermute | solution.py:408
  41.4 6.4 %collective-permute-start.9 = (bf16[64,2048]{1,0:T(8,128)(2,1)S(1)}, bf16[64,2048]{1,0:T(8,128)(2,1)S(1)}, u32[]{:S(2)}, u32[]{:S(2)}) collective-permute-start(bf16[64,2048]{1,0:T(8,128)(2,1)S(1)} %get-tuple-element.40.refs_2_), channel_id=1, source_target_pairs={{0,2},{1,3},{2,0},{3,1},{4,6},{5,7},{6,4},{7,5},{8,10},{9,11},{10,... | collective-permute-start | bytes 786440 | tf_op jit(solution)/shard_map/ppermute | solution.py:408
  59.7 10.8 %collective-permute-start.17 = (bf16[2,128,512]{2,1,0:T(8,128)(2,1)S(1)}, bf16[2,128,512]{2,1,0:T(8,128)(2,1)S(1)}, u32[]{:S(2)}, u32[]{:S(2)}) collective-permute-start(bf16[2,128,512]{2,1,0:T(8,128)(2,1)S(1)} %get-tuple-element.55), channel_id=1, source_target_pairs={{0,2},{1,3},{2,0},{3,1},{4,6},{5,7},{6,4},{7,5},{8,10},{9,11},{10,... | collective-permute-start | bytes 786440 | tf_op jit(solution)/shard_map/ppermute | solution.py:408
  62.4 9.3 %collective-permute-start.15 = (bf16[2,128,512]{2,1,0:T(8,128)(2,1)S(1)}, bf16[2,128,512]{2,1,0:T(8,128)(2,1)S(1)}, u32[]{:S(2)}, u32[]{:S(2)}) collective-permute-start(bf16[2,128,512]{2,1,0:T(8,128)(2,1)S(1)} %get-tuple-element.52), channel_id=1, source_target_pairs={{0,1},{1,0},{2,3},{3,2},{4,5},{5,4},{6,7},{7,6},{8,9},{9,8},{10,11... | collective-permute-start | bytes 786440 | tf_op jit(solution)/shard_map/ppermute | solution.py:408
  64.7 8.4 %collective-permute-start.13 = (bf16[2,128,512]{2,1,0:T(8,128)(2,1)S(1)}, bf16[2,128,512]{2,1,0:T(8,128)(2,1)S(1)}, u32[]{:S(2)}, u32[]{:S(2)}) collective-permute-start(bf16[2,128,512]{2,1,0:T(8,128)(2,1)S(1)} %get-tuple-element.49), channel_id=1, source_target_pairs={{0,2},{1,3},{2,0},{3,1},{4,6},{5,7},{6,4},{7,5},{8,10},{9,11},{10,... | collective-permute-start | bytes 786440 | tf_op jit(solution)/shard_map/ppermute | solution.py:408
  68.9 6.4 %collective-permute-start.11 = (bf16[2,128,512]{2,1,0:T(8,128)(2,1)S(1)}, bf16[2,128,512]{2,1,0:T(8,128)(2,1)S(1)}, u32[]{:S(2)}, u32[]{:S(2)}) collective-permute-start(bf16[2,128,512]{2,1,0:T(8,128)(2,1)S(1)} %get-tuple-element.46), channel_id=1, source_target_pairs={{0,1},{1,0},{2,3},{3,2},{4,5},{5,4},{6,7},{7,6},{8,9},{9,8},{10,11... | collective-permute-start | bytes 786440 | tf_op jit(solution)/shard_map/ppermute | solution.py:408
  70.5 6.2 %collective-permute-start.18 = (bf16[1,128,512]{2,1,0:T(8,128)(2,1)S(1)}, bf16[1,128,512]{2,1,0:T(8,128)(2,1)S(1)}, u32[]{:S(2)}, u32[]{:S(2)}) collective-permute-start(bf16[1,128,512]{2,1,0:T(8,128)(2,1)S(1)} %add_convert_fusion), channel_id=1, source_target_pairs={{0,1},{1,0},{2,3},{3,2},{4,5},{5,4},{6,7},{7,6},{8,9},{9,8},{10,11... | collective-permute-start | bytes 393224 | tf_op jit(solution)/shard_map/ppermute | solution.py:408
  71.8 5.0 %collective-permute-start.16 = (bf16[1,128,512]{2,1,0:T(8,128)(2,1)S(1)}, bf16[1,128,512]{2,1,0:T(8,128)(2,1)S(1)}, u32[]{:S(2)}, u32[]{:S(2)}) collective-permute-start(bf16[1,128,512]{2,1,0:T(8,128)(2,1)S(1)} %add_convert_fusion.1), channel_id=1, source_target_pairs={{0,2},{1,3},{2,0},{3,1},{4,6},{5,7},{6,4},{7,5},{8,10},{9,11},{10,... | collective-permute-start | bytes 393224 | tf_op jit(solution)/shard_map/ppermute | solution.py:408
  73.1 5.0 %collective-permute-start.14 = (bf16[1,128,512]{2,1,0:T(8,128)(2,1)S(1)}, bf16[1,128,512]{2,1,0:T(8,128)(2,1)S(1)}, u32[]{:S(2)}, u32[]{:S(2)}) collective-permute-start(bf16[1,128,512]{2,1,0:T(8,128)(2,1)S(1)} %add_convert_fusion.2), channel_id=1, source_target_pairs={{0,1},{1,0},{2,3},{3,2},{4,5},{5,4},{6,7},{7,6},{8,9},{9,8},{10,11... | collective-permute-start | bytes 393224 | tf_op jit(solution)/shard_map/ppermute | solution.py:408
  75.4 5.0 %collective-permute-start.12 = (bf16[1,128,512]{2,1,0:T(8,128)(2,1)S(1)}, bf16[1,128,512]{2,1,0:T(8,128)(2,1)S(1)}, u32[]{:S(2)}, u32[]{:S(2)}) collective-permute-start(bf16[1,128,512]{2,1,0:T(8,128)(2,1)S(1)} %add_convert_fusion.3), channel_id=1, source_target_pairs={{0,2},{1,3},{2,0},{3,1},{4,6},{5,7},{6,4},{7,5},{8,10},{9,11},{10,... | collective-permute-start | bytes 393224 | tf_op jit(solution)/shard_map/ppermute | solution.py:408

commit v6 on v5

--- a/solution.py
+++ b/solution.py
@@ -190,17 +190,17 @@
     )(*[pltpu.with_memory_space_constraint(w, pltpu.HBM) for w in arrays], after)
 
 
-def rows_kernel(local, counts, pick_ref, *refs):
+def rows_kernel(local, counts, first, pick_ref, *refs):
     token_refs, (_, out_ref) = split(refs, counts)
-    gather_rows(local, pick_ref, token_refs, 0, out_ref)
-
-
-def early_rows(local, pick, tokens, after):
+    gather_rows(local, pick_ref, token_refs, first, out_ref)
+
+
+def slot_rows(local, pick, tokens, first, after):
     features = tokens[0][0].shape[1]
     return pl.pallas_call(
-        functools.partial(rows_kernel, local, sizes(tokens)),
+        functools.partial(rows_kernel, local, sizes(tokens), first),
         in_specs=[INSIDE] * (1 + len(flat(tokens))) + [ANYWHERE],
-        out_shape=jax.ShapeDtypeStruct((local, 2 * SLOT, features), jnp.bfloat16),
+        out_shape=jax.ShapeDtypeStruct((local, len(tokens) * SLOT, features), jnp.bfloat16),
         compiler_params=params(4),
     )(pick, *flat(tokens), after)
 
@@ -252,56 +252,53 @@
     )(array, after)
 
 
-def pre_kernel(local, counts, pick_ref, gate_ref, first_ref, *refs):
-    token_refs, refs = split(refs, counts)
-    wg_ref, wu_ref, a_ref, b_ref, xs = refs
+def pre_kernel(experts, gate_ref, first_ref, rest_ref, wg_ref, wu_ref, _, a_ref, b_ref):
     hidden = wg_ref.shape[2]
     cols = hidden // 2
-    gather_rows(local, pick_ref, token_refs, 1, xs)
-
-    @pl.loop(0, local)
-    def _(e):
-        rows = jnp.concatenate([first_ref[e], xs[e]], axis=0)
+    for i, e in enumerate(experts):
+        rows = jnp.concatenate([first_ref[e], rest_ref[e]], axis=0)
         gates = gate_ref[e][:1, :]
         for f in range(0, hidden, cols):
             part = slice(f, f + cols)
             gate_pre = dot(rows, wg_ref[e, :, part])
             up_pre = dot(rows, wu_ref[e, :, part])
             sig = jax.nn.sigmoid(gate_pre)
-            a_ref[e, part, :] = (sig * up_pre * (1.0 + gate_pre * (1.0 - sig))).T * gates
-            b_ref[e, part, :] = (sig * gate_pre).T * gates
-
-
-def pre(n, pick, gates, first, tokens, wg, wu):
+            a_ref[i, part, :] = ((sig * up_pre * (1.0 + gate_pre * (1.0 - sig))).T * gates).astype(jnp.bfloat16)
+            b_ref[i, part, :] = ((sig * gate_pre).T * gates).astype(jnp.bfloat16)
+
+
+def pre(n, experts, gates, first, rest, wg, wu, after):
     local, features, hidden = wg.shape
-    rows = n * SLOT
-    return pl.pallas_call(
-        functools.partial(pre_kernel, local, sizes(tokens)),
-        in_specs=[INSIDE] * (5 + len(flat(tokens))),
-        out_shape=[
-            jax.ShapeDtypeStruct((local, hidden, rows), jnp.float32),
-            jax.ShapeDtypeStruct((local, hidden, rows), jnp.float32),
-        ],
-        scratch_shapes=[pltpu.VMEM((local, rows - 2 * SLOT, features), jnp.bfloat16)],
+    rows, count = n * SLOT, len(experts)
+    shape = jax.ShapeDtypeStruct((count, hidden, rows), jnp.bfloat16)
+    return pl.pallas_call(
+        functools.partial(pre_kernel, experts),
+        in_specs=[INSIDE] * 5 + [ANYWHERE],
+        out_shape=[shape, shape],
         compiler_params=params(PRE_MIB * max(1, n // 4)),
         cost_estimate=pl.CostEstimate(
-            flops=4 * local * rows * features * hidden,
-            bytes_accessed=4 * local * features * hidden,
-            transcendentals=local * rows * hidden,
+            flops=4 * count * rows * features * hidden,
+            bytes_accessed=4 * count * features * hidden,
+            transcendentals=count * rows * hidden,
         ),
-    )(pick, gates, first, *flat(tokens), vmem(wg), vmem(wu))
-
-
-def back_kernel(local, counts, place_ref, first_ref, *refs):
-    token_refs, refs = split(refs, counts)
-    wd_ref, a_ref, b_ref, _, _, hg_ref, hu_ref, gs, weight, sems = refs
+    )(gates, first, rest, vmem(wg), vmem(wu), after)
+
+
+def back_kernel(local, counts, halves, place_ref, first_ref, *refs):
+    token_refs, (wd_ref, *refs) = split(refs, counts)
+    factor_refs, (_, _, hg_ref, hu_ref, gs, weight, sems) = refs[: 2 * halves], refs[2 * halves :]
+    factors = [
+        (a_ref, b_ref, i)
+        for a_ref, b_ref in zip(factor_refs[::2], factor_refs[1::2])
+        for i in range(a_ref.shape[0])
+    ]
     hidden = wd_ref.shape[1]
     cols = hidden // 2
     held = weight.shape[0]
 
     def fetch(e, i):
         part = pl.ds(i * cols, cols)
-        slot = lax.rem(e, held)
+        slot = e % held
         return pltpu.make_async_copy(wd_ref.at[e, part], weight.at[slot, part], sems.at[slot, i])
 
     for e in range(held):
@@ -309,28 +306,25 @@
             fetch(e, i).start()
     gather_columns(local, place_ref, token_refs, 1, gs)
 
-    @pl.loop(0, local)
-    def _(e):
+    for e, (a_ref, b_ref, at) in enumerate(factors):
         rows = jnp.concatenate([first_ref[e], gs[e]], axis=1)
         for i in range(2):
             part = slice(i * cols, (i + 1) * cols)
             fetch(e, i).wait()
-            back = dot(weight[lax.rem(e, held), part, :], rows)
-            hg_ref[e, part, :] = (back * a_ref[e, part, :]).astype(jnp.bfloat16)
-            hu_ref[e, part, :] = (back * b_ref[e, part, :]).astype(jnp.bfloat16)
-
-            @pl.when(e + held < local)
-            def _():
+            back = dot(weight[e % held, part, :], rows)
+            hg_ref[e, part, :] = (back * a_ref[at, part, :]).astype(jnp.bfloat16)
+            hu_ref[e, part, :] = (back * b_ref[at, part, :]).astype(jnp.bfloat16)
+            if e + held < local:
                 fetch(e + held, i).start()
 
 
-def back(n, place, first, tokens, wd, a, b, wg, wu):
+def back(n, place, first, tokens, wd, factors, wg, wu):
     local, hidden, features = wd.shape
     rows = n * SLOT
     shape = jax.ShapeDtypeStruct((local, hidden, rows), jnp.bfloat16)
     return pl.pallas_call(
-        functools.partial(back_kernel, local, sizes(tokens)),
-        in_specs=[INSIDE] * (2 + len(flat(tokens))) + [OUTSIDE] + [INSIDE] * 4,
+        functools.partial(back_kernel, local, sizes(tokens), len(factors)),
+        in_specs=[INSIDE] * (2 + len(flat(tokens))) + [OUTSIDE] + [INSIDE] * (2 * len(factors) + 2),
         out_shape=[shape, shape],
         scratch_shapes=[
             pltpu.VMEM((local, features, rows - 2 * SLOT), jnp.bfloat16),
@@ -343,7 +337,7 @@
             bytes_accessed=2 * local * features * hidden,
             transcendentals=0,
         ),
-    )(place, first, *flat(tokens), hbm(wd), a, b, vmem(wg), vmem(wu))
+    )(place, first, *flat(tokens), hbm(wd), *flat(factors), vmem(wg), vmem(wu))
 
 
 def out_kernel(n, local, orders, chunk, place_ref, hg_ref, hu_ref, wg_ref, wu_ref, *rest):
@@ -420,16 +414,20 @@
     else:
         x_blocks = [[saved_input]] + [[swap(saved_input, k)] for k in range(1, n)]
         sent = grad_out
-    x_first = early_rows(local, pick, x_blocks[:2], sent)
-    a, b = pre(n, pick, gates, x_first, x_blocks[2:], gate_proj, up_proj)
+    x_first = slot_rows(local, pick, x_blocks[:2], 0, sent)
+    x_rest = slot_rows(local, pick, x_blocks[2:], 1, sent)
+    half = (local + 1) // 2
+    factors = [pre(n, range(half), gates, x_first, x_rest, gate_proj, up_proj, table)]
     if n == 4:
-        upper, lower = relay_parts(g_near, [a])
+        upper, lower = relay_parts(g_near, [factors[0][0]])
         g_blocks = [[sent], *[[g] for g in g_near], [swap(upper, 2), swap(lower, 1)]]
     else:
         g_blocks = [[grad_out]] + [[swap(grad_out, k)] for k in range(1, n)]
-        upper = a
+        upper = table
+    if half < local:
+        factors.append(pre(n, range(half, local), gates, x_first, x_rest, gate_proj, up_proj, upper))
     g_first = early_columns(local, place, g_blocks[:2], upper)
-    hg, hu = back(n, place, g_first, g_blocks[2:], down_proj, a, b, gate_proj, up_proj)
+    hg, hu = back(n, place, g_first, g_blocks[2:], down_proj, factors, gate_proj, up_proj)
     parts = []
     for chunk in range(CHUNKS):
         if n == 4:

time: 81.6 us -> 86.5 us (1.060)
  local copies, waits for them, and re-layouts: 0.78 us -> 5.36 us
    unnamed x6 -> x10, local copies, waits for them, and re-layouts: 0.74 us -> 5.32 us
    ppermute x19, waiting for transfers between devices: 16.5 us -> 17.3 us  [swap(): return lax.ppermute(array, axis, [(i, i ^ k) for i in range(n)])]
    pallas_call x3 -> x5, Pallas kernels: 21.4 us -> 20.8 us  [the longest x1 9.77 us: back(): pl.pallas_call(functools.partial(back_kernel, local, sizes(tokens), len(f...]
  transfers between devices with their start and end apart: 19 -> 19, of which waited for: 10 -> 10; matrix products, arithmetic and copies ran while one was open for 0% -> 0% of each run, Pallas kernels for 36% -> 33%
where the time goes in v6:
time: 86.5 us; the launch traced here: 86.2 us
  Pallas kernels  41.5 us (48%)
  starting transfers between devices  21.7 us (25%)
  waiting for transfers between devices  17.3 us (20%)
  local copies, waits for them, and re-layouts  5.36 us (6%)
    ppermute x19, starting transfers between devices, swap(): return lax.ppermute(array, axis, [(i, i ^ k) for i in range(n)])  21.7 us
    ppermute x19, waiting for transfers between devices, swap(): return lax.ppermute(array, axis, [(i, i ^ k) for i in range(n)])  17.3 us
    pallas_call x1, Pallas kernels, back(): pl.pallas_call(functools.partial(back_kernel, local, sizes(tokens), len(f...  9.77 us
    pallas_call x2, Pallas kernels, pre(): pl.pallas_call(functools.partial(pre_kernel, experts), in_specs=[INSIDE]...  9.66 us
    pallas_call x4, Pallas kernels, partial_sums(): pl.pallas_call(functools.partial(out_kernel, n, local, orders, chunk), ou...  8.58 us
    pallas_call x1, Pallas kernels, load(): pl.pallas_call(functools.partial(load_kernel, count), in_specs=[OUTSIDE]...  8.3 us
    unnamed x10, local copies, waits for them, and re-layouts  5.32 us
  transfers between devices with their start and end apart: 19, of which 10 were waited for; matrix products, arithmetic and copies ran while one was open for 0% of the time, Pallas kernels for 33%

profile of v6, /device:TPU:0, one launch (start us, length us, event | category | flops | bytes accessed | tf_op | source)
XLA Modules:
  0.0 86.2 jit_solution(2104294220901504636)
XLA Ops:
  0.0 2.9 %collective-permute-start.3 = (bf16[128,2048]{1,0:T(8,128)(2,1)}, bf16[128,2048]{1,0:T(8,128)(2,1)S(1)}, u32[]{:S(2)}, u32[]{:S(2)}) collective-permute-start(bf16[128,2048]{1,0:T(8,128)(2,1)} %refs_0_.3), channel_id=1, source_target_pairs={{0,1},{1,0},{2,3},{3,2},{4,5},{5,4},{6,7},{7,6},{8,9},{9,8},{10,11... | collective-permute-start | bytes 1572872 | tf_op jit(solution)/shard_map/ppermute | solution.py:402
  2.9 1.5 %collective-permute-start.4 = (bf16[128,2048]{1,0:T(8,128)(2,1)}, bf16[128,2048]{1,0:T(8,128)(2,1)S(1)}, u32[]{:S(2)}, u32[]{:S(2)}) collective-permute-start(bf16[128,2048]{1,0:T(8,128)(2,1)} %refs_0_.3), channel_id=1, source_target_pairs={{0,2},{1,3},{2,0},{3,1},{4,6},{5,7},{6,4},{7,5},{8,10},{9,11},{10,... | collective-permute-start | bytes 1572872 | tf_op jit(solution)/shard_map/ppermute | solution.py:402
  4.5 1.5 %shard_map.73.refs_0_.refs_2_._ = bf16[32,128]{1,0:T(8,128)(2,1)} custom-call(s32[8,128]{1,0:T(8,128)} %bitcast.2, bf16[8,128]{1,0:T(8,128)(2,1)} %bitcast.3), custom_call_target="tpu_custom_call" | custom-call | tf_op jit(solution)/shard_map/pallas_call | solution.py:56
  5.9 0.0 copy-start.2
  5.9 0.0 copy-start.3
  6.0 0.0 collective-permute-start.2
  6.0 2.0 %collective-permute-start.1 = (bf16[32,128]{1,0:T(8,128)(2,1)}, bf16[32,128]{1,0:T(8,128)(2,1)S(1)}, u32[]{:S(2)}, u32[]{:S(2)}) collective-permute-start(bf16[32,128]{1,0:T(8,128)(2,1)} %shard_map.73.refs_0_.refs_2_._), channel_id=1, source_target_pairs={{0,2},{1,3},{2,0},{3,1},{4,6},{5,7},{6,4},{7,5},{8,10},{9,11},{10,... | collective-permute-start | bytes 24584 | tf_op jit(solution)/shard_map/ppermute | solution.py:402
  7.9 1.5 %collective-permute-start = (bf16[32,128]{1,0:T(8,128)(2,1)}, bf16[32,128]{1,0:T(8,128)(2,1)S(1)}, u32[]{:S(2)}, u32[]{:S(2)}) collective-permute-start(bf16[32,128]{1,0:T(8,128)(2,1)} %shard_map.73.refs_0_.refs_2_._), channel_id=1, source_target_pairs={{0,1},{1,0},{2,3},{3,2},{4,5},{5,4},{6,7},{7,6},{8,9},{9,8},{10,11... | collective-permute-start | bytes 24584 | tf_op jit(solution)/shard_map/ppermute | solution.py:402
  9.4 0.0 copy-start.4
  9.4 0.7 copy-done.4
  10.2 8.3 %shard_map.75 = (bf16[4,2048,768]{2,1,0:T(8,128)(2,1)S(1)}, bf16[4,2048,768]{2,1,0:T(8,128)(2,1)S(1)}, f32[8,128]{1,0:T(8,128)S(1)}) custom-call(bf16[4,2048,768]{2,1,0:T(8,128)(2,1)} %refs_0_.2, bf16[4,2048,768]{2,1,0:T(8,128)(2,1)} %refs_1_.1, bf16[32,128]{1,0:T(8,128)(2,1)S(1)} %copy-done.4), custom_call_target="tpu_custom_call" | custom-call | bytes 50331648 | tf_op jit(solution)/shard_map/pallas_call | solution.py:179
  18.5 0.0 copy-start
  18.5 0.0 collective-permute-done.2.refs_3_
  18.5 0.0 collective-permute-done.1.refs_2_
  18.5 0.0 collective-permute-done.refs_1_
  18.5 0.4 shard_map.74
  19.0 0.0 collective-permute-done.3.x_ref.refs_1_
  19.0 0.0 collective-permute-done.4.y_ref.refs_0_
  19.0 0.6 collective-permute-start.8
  19.6 0.1 collective-permute-start.7
  19.7 0.0 copy-done.2
  19.8 2.0 %collective-permute-start.6 = (bf16[128,2048]{1,0:T(8,128)(2,1)S(1)}, bf16[128,2048]{1,0:T(8,128)(2,1)S(1)}, u32[]{:S(2)}, u32[]{:S(2)}) collective-permute-start(bf16[128,2048]{1,0:T(8,128)(2,1)S(1)} %shard_map.77.refs_2_.refs_3_.refs_0_), channel_id=1, source_target_pairs={{0,2},{1,3},{2,0},{3,1},{4,6},{5,7},{6,4},{7,5},{8,10},{9,11},{10,... | collective-permute-start | bytes 1572872 | tf_op jit(solution)/shard_map/ppermute | solution.py:402
  21.8 1.5 %collective-permute-start.5 = (bf16[128,2048]{1,0:T(8,128)(2,1)S(1)}, bf16[128,2048]{1,0:T(8,128)(2,1)S(1)}, u32[]{:S(2)}, u32[]{:S(2)}) collective-permute-start(bf16[128,2048]{1,0:T(8,128)(2,1)S(1)} %shard_map.77.refs_2_.refs_3_.refs_0_), channel_id=1, source_target_pairs={{0,1},{1,0},{2,3},{3,2},{4,5},{5,4},{6,7},{7,6},{8,9},{9,8},{10,11... | collective-permute-start | bytes 1572872 | tf_op jit(solution)/shard_map/ppermute | solution.py:402
  23.2 0.0 copy-done.3
  23.2 0.7 shard_map.78.first_ref
  24.0 4.4 %collective-permute-done.8.refs_2_ = bf16[64,2048]{1,0:T(8,128)(2,1)S(1)} collective-permute-done((bf16[64,2048]{1,0:T(8,128)(2,1)S(1)}, bf16[64,2048]{1,0:T(8,128)(2,1)S(1)}, u32[]{:S(2)}, u32[]{:S(2)}) %collective-permute-start.8) | collective-permute-done | bytes 262176 | tf_op jit(solution)/shard_map/ppermute | solution.py:402
  28.3 0.5 collective-permute-done.7.refs_1_
  28.9 0.7 shard_map.79.rest_ref
  29.6 4.7 %shard_map.80 = (bf16[2,768,256]{2,1,0:T(8,128)(2,1)S(1)}, bf16[2,768,256]{2,1,0:T(8,128)(2,1)S(1)}) custom-call(f32[4,8,256]{2,1,0:T(8,128)S(1)} %get-tuple-element.36.gate_ref, bf16[4,128,2048]{2,1,0:T(8,128)(2,1)S(1)} %shard_map.78.first_ref, bf16[4,128,2048]{2,1,0:T(8,128)(2,1)S(1)} %shard_map.79.rest_ref, ...), custom_call_target="tpu_custom_call" | custom-call | flops 3221225472 | bytes 12582912 | tf_op jit(solution)/shard_map/pallas_call | solution.py:274
  34.3 2.9 %collective-permute-done.6.y_ref.refs_0_ = bf16[128,2048]{1,0:T(8,128)(2,1)S(1)} collective-permute-done((bf16[128,2048]{1,0:T(8,128)(2,1)S(1)}, bf16[128,2048]{1,0:T(8,128)(2,1)S(1)}, u32[]{:S(2)}, u32[]{:S(2)}) %collective-permute-start.6) | collective-permute-done | bytes 524320 | tf_op jit(solution)/shard_map/ppermute | solution.py:402
  37.2 0.0 collective-permute-done.5.x_ref.refs_1_
  37.3 1.6 %collective-permute-start.10 = (bf16[64,2048]{1,0:T(8,128)(2,1)S(1)}, bf16[64,2048]{1,0:T(8,128)(2,1)S(1)}, u32[]{:S(2)}, u32[]{:S(2)}) collective-permute-start(bf16[64,2048]{1,0:T(8,128)(2,1)S(1)} %get-tuple-element.43), channel_id=1, source_target_pairs={{0,1},{1,0},{2,3},{3,2},{4,5},{5,4},{6,7},{7,6},{8,9},{9,8},{10,11... | collective-permute-start | bytes 786440 | tf_op jit(solution)/shard_map/ppermute | solution.py:402
  38.8 0.5 collective-permute-start.9
  39.3 0.7 shard_map.82.first_ref
  40.1 0.0 copy-done
  40.1 4.9 %shard_map.83 = (bf16[2,768,256]{2,1,0:T(8,128)(2,1)S(1)}, bf16[2,768,256]{2,1,0:T(8,128)(2,1)S(1)}) custom-call(f32[4,8,256]{2,1,0:T(8,128)S(1)} %get-tuple-element.36.gate_ref, bf16[4,128,2048]{2,1,0:T(8,128)(2,1)S(1)} %shard_map.78.first_ref, bf16[4,128,2048]{2,1,0:T(8,128)(2,1)S(1)} %shard_map.79.rest_ref, ...), custom_call_target="tpu_custom_call" | custom-call | flops 3221225472 | bytes 12582912 | tf_op jit(solution)/shard_map/pallas_call | solution.py:274
  45.0 0.0 collective-permute-done.10.refs_2_
  45.0 0.2 collective-permute-done.9.refs_1_
  45.2 0.0 copy-start.1
  45.2 4.6 %copy-done.1 = bf16[4,2048,768]{2,1,0:T(8,128)(2,1)S(1)} copy-done((bf16[4,2048,768]{2,1,0:T(8,128)(2,1)S(1)}, bf16[4,2048,768]{2,1,0:T(8,128)(2,1)}, u32[]{:S(2)}) %copy-start.1) | copy-done | bytes 12582936
  49.8 9.8 %shard_map.84 = (bf16[4,768,256]{2,1,0:T(8,128)(2,1)S(1)}, bf16[4,768,256]{2,1,0:T(8,128)(2,1)S(1)}) custom-call(bf16[2,256,512]{2,1,0:T(8,128)(2,1)S(1)} %get-tuple-element.33.refs_1_.place_ref, bf16[4,2048,128]{2,1,0:T(8,128)(2,1)S(1)} %shard_map.82.first_ref, bf16[128,2048]{1,0:T(8,128)(2,1)S(1)} %collective-permute-done.6.y_ref.refs_0_, ...), custom_call_target="tpu_custom_call" | custom-call | flops 3221225472 | bytes 12582912 | tf_op jit(solution)/shard_map/pallas_call | solution.py:325
  59.5 2.1 %shard_map.88 = (f32[1,128,512]{2,1,0:T(8,128)S(1)}, bf16[2,128,512]{2,1,0:T(8,128)(2,1)S(1)}, bf16[1,128,512]{2,1,0:T(8,128)(2,1)S(1)}) custom-call(bf16[2,256,512]{2,1,0:T(8,128)(2,1)S(1)} %get-tuple-element.33.refs_1_.place_ref, bf16[4,768,256]{2,1,0:T(8,128)(2,1)S(1)} %get-tuple-element.47.hg_ref, bf16[4,768,256]{2,1,0:T(8,128)(2,1)S(1)} %get-tuple-element.48.hu_ref, ...), custom_call_target="tpu_custom_call" | custom-call | flops 402653184 | bytes 1572864 | tf_op jit(solution)/shard_map/pallas_call | solution.py:370
  61.7 1.4 %collective-permute-start.17 = (bf16[2,128,512]{2,1,0:T(8,128)(2,1)S(1)}, bf16[2,128,512]{2,1,0:T(8,128)(2,1)S(1)}, u32[]{:S(2)}, u32[]{:S(2)}) collective-permute-start(bf16[2,128,512]{2,1,0:T(8,128)(2,1)S(1)} %get-tuple-element.59), channel_id=1, source_target_pairs={{0,2},{1,3},{2,0},{3,1},{4,6},{5,7},{6,4},{7,5},{8,10},{9,11},{10,... | collective-permute-start | bytes 786440 | tf_op jit(solution)/shard_map/ppermute | solution.py:402
  63.1 2.1 %shard_map.87 = (f32[1,128,512]{2,1,0:T(8,128)S(1)}, bf16[2,128,512]{2,1,0:T(8,128)(2,1)S(1)}, bf16[1,128,512]{2,1,0:T(8,128)(2,1)S(1)}) custom-call(bf16[2,256,512]{2,1,0:T(8,128)(2,1)S(1)} %get-tuple-element.33.refs_1_.place_ref, bf16[4,768,256]{2,1,0:T(8,128)(2,1)S(1)} %get-tuple-element.47.hg_ref, bf16[4,768,256]{2,1,0:T(8,128)(2,1)S(1)} %get-tuple-element.48.hu_ref, ...), custom_call_target="tpu_custom_call" | custom-call | flops 402653184 | bytes 1572864 | tf_op jit(solution)/shard_map/pallas_call | solution.py:370
  65.3 0.6 collective-permute-start.15
  65.9 2.1 %shard_map.86 = (f32[1,128,512]{2,1,0:T(8,128)S(1)}, bf16[2,128,512]{2,1,0:T(8,128)(2,1)S(1)}, bf16[1,128,512]{2,1,0:T(8,128)(2,1)S(1)}) custom-call(bf16[2,256,512]{2,1,0:T(8,128)(2,1)S(1)} %get-tuple-element.33.refs_1_.place_ref, bf16[4,768,256]{2,1,0:T(8,128)(2,1)S(1)} %get-tuple-element.47.hg_ref, bf16[4,768,256]{2,1,0:T(8,128)(2,1)S(1)} %get-tuple-element.48.hu_ref, ...), custom_call_target="tpu_custom_call" | custom-call | flops 402653184 | bytes 1572864 | tf_op jit(solution)/shard_map/pallas_call | solution.py:370
  68.0 0.7 collective-permute-start.13
  68.8 2.1 %shard_map.85 = (f32[1,128,512]{2,1,0:T(8,128)S(1)}, bf16[2,128,512]{2,1,0:T(8,128)(2,1)S(1)}, bf16[1,128,512]{2,1,0:T(8,128)(2,1)S(1)}) custom-call(bf16[2,256,512]{2,1,0:T(8,128)(2,1)S(1)} %get-tuple-element.33.refs_1_.place_ref, bf16[4,768,256]{2,1,0:T(8,128)(2,1)S(1)} %get-tuple-element.47.hg_ref, bf16[4,768,256]{2,1,0:T(8,128)(2,1)S(1)} %get-tuple-element.48.hu_ref, ...), custom_call_target="tpu_custom_call" | custom-call | flops 402653184 | bytes 1572864 | tf_op jit(solution)/shard_map/pallas_call | solution.py:370
  70.9 1.5 %collective-permute-start.11 = (bf16[2,128,512]{2,1,0:T(8,128)(2,1)S(1)}, bf16[2,128,512]{2,1,0:T(8,128)(2,1)S(1)}, u32[]{:S(2)}, u32[]{:S(2)}) collective-permute-start(bf16[2,128,512]{2,1,0:T(8,128)(2,1)S(1)} %get-tuple-element.50), channel_id=1, source_target_pairs={{0,1},{1,0},{2,3},{3,2},{4,5},{5,4},{6,7},{7,6},{8,9},{9,8},{10,11... | collective-permute-start | bytes 786440 | tf_op jit(solution)/shard_map/ppermute | solution.py:402
  72.5 0.0 collective-permute-done.17
  72.5 0.6 collective-permute-start.18
  73.1 1.0 %collective-permute-done.15 = bf16[2,128,512]{2,1,0:T(8,128)(2,1)S(1)} collective-permute-done((bf16[2,128,512]{2,1,0:T(8,128)(2,1)S(1)}, bf16[2,128,512]{2,1,0:T(8,128)(2,1)S(1)}, u32[]{:S(2)}, u32[]{:S(2)}) %collective-permute-start.15) | collective-permute-done | bytes 262176 | tf_op jit(solution)/shard_map/ppermute | solution.py:402
  74.2 0.4 collective-permute-start.16
  74.6 0.7 collective-permute-done.13
  75.3 1.4 %collective-permute-start.14 = (bf16[1,128,512]{2,1,0:T(8,128)(2,1)S(1)}, bf16[1,128,512]{2,1,0:T(8,128)(2,1)S(1)}, u32[]{:S(2)}, u32[]{:S(2)}) collective-permute-start(bf16[1,128,512]{2,1,0:T(8,128)(2,1)S(1)} %add_convert_fusion.2), channel_id=1, source_target_pairs={{0,1},{1,0},{2,3},{3,2},{4,5},{5,4},{6,7},{7,6},{8,9},{9,8},{10,11... | collective-permute-start | bytes 393224 | tf_op jit(solution)/shard_map/ppermute | solution.py:402
  76.7 3.4 %collective-permute-done.11 = bf16[2,128,512]{2,1,0:T(8,128)(2,1)S(1)} collective-permute-done((bf16[2,128,512]{2,1,0:T(8,128)(2,1)S(1)}, bf16[2,128,512]{2,1,0:T(8,128)(2,1)S(1)}, u32[]{:S(2)}, u32[]{:S(2)}) %collective-permute-start.11) | collective-permute-done | bytes 262176 | tf_op jit(solution)/shard_map/ppermute | solution.py:402
  80.2 0.7 collective-permute-start.12
  81.0 0.6 collective-permute-done.18.refs_11_
  81.5 0.0 collective-permute-done.16.refs_8_
  81.6 1.4 %collective-permute-done.14.refs_5_ = bf16[1,128,512]{2,1,0:T(8,128)(2,1)S(1)} collective-permute-done((bf16[1,128,512]{2,1,0:T(8,128)(2,1)S(1)}, bf16[1,128,512]{2,1,0:T(8,128)(2,1)S(1)}, u32[]{:S(2)}, u32[]{:S(2)}) %collective-permute-start.14) | collective-permute-done | bytes 131104 | tf_op jit(solution)/shard_map/ppermute | solution.py:402
  83.0 2.3 %collective-permute-done.12.refs_2_ = bf16[1,128,512]{2,1,0:T(8,128)(2,1)S(1)} collective-permute-done((bf16[1,128,512]{2,1,0:T(8,128)(2,1)S(1)}, bf16[1,128,512]{2,1,0:T(8,128)(2,1)S(1)}, u32[]{:S(2)}, u32[]{:S(2)}) %collective-permute-start.12) | collective-permute-done | bytes 131104 | tf_op jit(solution)/shard_map/ppermute | solution.py:402
  85.2 1.0 %shard_map.89 = bf16[128,2048]{1,0:T(8,128)(2,1)} custom-call(f32[1,128,512]{2,1,0:T(8,128)S(1)} %get-tuple-element.49.refs_0_, bf16[1,128,512]{2,1,0:T(8,128)(2,1)S(1)} %slice.32.refs_1_, bf16[1,128,512]{2,1,0:T(8,128)(2,1)S(1)} %collective-permute-done.12.refs_2_, f32[1,128,512]{2,1,0:T(8,128)S(1)} %get-tuple-element.52.refs_3_, ...), custom_call_target="tpu_custom_call" | custom-call | tf_op jit(solution)/shard_map/pallas_call | solution.py:444
  (11 shorter events, 0.3 us)
Async XLA Ops:
  0.0 19.0 %collective-permute-start.3 = (bf16[128,2048]{1,0:T(8,128)(2,1)}, bf16[128,2048]{1,0:T(8,128)(2,1)S(1)}, u32[]{:S(2)}, u32[]{:S(2)}) collective-permute-start(bf16[128,2048]{1,0:T(8,128)(2,1)} %refs_0_.3), channel_id=1, source_target_pairs={{0,1},{1,0},{2,3},{3,2},{4,5},{5,4},{6,7},{7,6},{8,9},{9,8},{10,11... | collective-permute-start | bytes 1572872 | tf_op jit(solution)/shard_map/ppermute | solution.py:402
  2.9 16.0 %collective-permute-start.4 = (bf16[128,2048]{1,0:T(8,128)(2,1)}, bf16[128,2048]{1,0:T(8,128)(2,1)S(1)}, u32[]{:S(2)}, u32[]{:S(2)}) collective-permute-start(bf16[128,2048]{1,0:T(8,128)(2,1)} %refs_0_.3), channel_id=1, source_target_pairs={{0,2},{1,3},{2,0},{3,1},{4,6},{5,7},{6,4},{7,5},{8,10},{9,11},{10,... | collective-permute-start | bytes 1572872 | tf_op jit(solution)/shard_map/ppermute | solution.py:402
  5.9 13.8 %copy-start.2 = (bf16[128,2048]{1,0:T(8,128)(2,1)S(1)}, bf16[128,2048]{1,0:T(8,128)(2,1)}, u32[]{:S(2)}) copy-start(bf16[128,2048]{1,0:T(8,128)(2,1)} %array_ref.1) | copy-start | bytes 1572868
  5.9 17.3 %copy-start.3 = (bf16[128,2048]{1,0:T(8,128)(2,1)S(1)}, bf16[128,2048]{1,0:T(8,128)(2,1)}, u32[]{:S(2)}) copy-start(bf16[128,2048]{1,0:T(8,128)(2,1)} %refs_0_.3) | copy-start | bytes 1572868
  6.0 12.5 %collective-permute-start.2 = (bf16[32,128]{1,0:T(8,128)(2,1)}, bf16[32,128]{1,0:T(8,128)(2,1)S(1)}, u32[]{:S(2)}, u32[]{:S(2)}) collective-permute-start(bf16[32,128]{1,0:T(8,128)(2,1)} %shard_map.73.refs_0_.refs_2_._), channel_id=1, source_target_pairs={{0,3},{1,2},{2,1},{3,0},{4,7},{5,6},{6,5},{7,4},{8,11},{9,10},{10,... | collective-permute-start | bytes 24584 | tf_op jit(solution)/shard_map/ppermute | solution.py:402
  6.0 12.5 %collective-permute-start.1 = (bf16[32,128]{1,0:T(8,128)(2,1)}, bf16[32,128]{1,0:T(8,128)(2,1)S(1)}, u32[]{:S(2)}, u32[]{:S(2)}) collective-permute-start(bf16[32,128]{1,0:T(8,128)(2,1)} %shard_map.73.refs_0_.refs_2_._), channel_id=1, source_target_pairs={{0,2},{1,3},{2,0},{3,1},{4,6},{5,7},{6,4},{7,5},{8,10},{9,11},{10,... | collective-permute-start | bytes 24584 | tf_op jit(solution)/shard_map/ppermute | solution.py:402
  7.9 10.6 %collective-permute-start = (bf16[32,128]{1,0:T(8,128)(2,1)}, bf16[32,128]{1,0:T(8,128)(2,1)S(1)}, u32[]{:S(2)}, u32[]{:S(2)}) collective-permute-start(bf16[32,128]{1,0:T(8,128)(2,1)} %shard_map.73.refs_0_.refs_2_._), channel_id=1, source_target_pairs={{0,1},{1,0},{2,3},{3,2},{4,5},{5,4},{6,7},{7,6},{8,9},{9,8},{10,11... | collective-permute-start | bytes 24584 | tf_op jit(solution)/shard_map/ppermute | solution.py:402
  9.4 0.7 copy-start.4
  18.5 21.6 %copy-start = (bf16[4,2048,768]{2,1,0:T(8,128)(2,1)}, bf16[4,2048,768]{2,1,0:T(8,128)(2,1)S(1)}, u32[]{:S(2)}) copy-start(bf16[4,2048,768]{2,1,0:T(8,128)(2,1)S(1)} %get-tuple-element.40.wu_ref.refs_9_) | copy-start | bytes 37748740
  19.0 9.3 %collective-permute-start.8 = (bf16[64,2048]{1,0:T(8,128)(2,1)S(1)}, bf16[64,2048]{1,0:T(8,128)(2,1)S(1)}, u32[]{:S(2)}, u32[]{:S(2)}) collective-permute-start(bf16[64,2048]{1,0:T(8,128)(2,1)S(1)} %get-tuple-element.38), channel_id=1, source_target_pairs={{0,1},{1,0},{2,3},{3,2},{4,5},{5,4},{6,7},{7,6},{8,9},{9,8},{10,11... | collective-permute-start | bytes 786440 | tf_op jit(solution)/shard_map/ppermute | solution.py:402
  19.6 9.2 %collective-permute-start.7 = (bf16[64,2048]{1,0:T(8,128)(2,1)S(1)}, bf16[64,2048]{1,0:T(8,128)(2,1)S(1)}, u32[]{:S(2)}, u32[]{:S(2)}) collective-permute-start(bf16[64,2048]{1,0:T(8,128)(2,1)S(1)} %get-tuple-element.35._), channel_id=1, source_target_pairs={{0,2},{1,3},{2,0},{3,1},{4,6},{5,7},{6,4},{7,5},{8,10},{9,11},{10,... | collective-permute-start | bytes 786440 | tf_op jit(solution)/shard_map/ppermute | solution.py:402
  19.8 17.5 %collective-permute-start.6 = (bf16[128,2048]{1,0:T(8,128)(2,1)S(1)}, bf16[128,2048]{1,0:T(8,128)(2,1)S(1)}, u32[]{:S(2)}, u32[]{:S(2)}) collective-permute-start(bf16[128,2048]{1,0:T(8,128)(2,1)S(1)} %shard_map.77.refs_2_.refs_3_.refs_0_), channel_id=1, source_target_pairs={{0,2},{1,3},{2,0},{3,1},{4,6},{5,7},{6,4},{7,5},{8,10},{9,11},{10,... | collective-permute-start | bytes 1572872 | tf_op jit(solution)/shard_map/ppermute | solution.py:402
  21.8 15.5 %collective-permute-start.5 = (bf16[128,2048]{1,0:T(8,128)(2,1)S(1)}, bf16[128,2048]{1,0:T(8,128)(2,1)S(1)}, u32[]{:S(2)}, u32[]{:S(2)}) collective-permute-start(bf16[128,2048]{1,0:T(8,128)(2,1)S(1)} %shard_map.77.refs_2_.refs_3_.refs_0_), channel_id=1, source_target_pairs={{0,1},{1,0},{2,3},{3,2},{4,5},{5,4},{6,7},{7,6},{8,9},{9,8},{10,11... | collective-permute-start | bytes 1572872 | tf_op jit(solution)/shard_map/ppermute | solution.py:402
  37.3 7.8 %collective-permute-start.10 = (bf16[64,2048]{1,0:T(8,128)(2,1)S(1)}, bf16[64,2048]{1,0:T(8,128)(2,1)S(1)}, u32[]{:S(2)}, u32[]{:S(2)}) collective-permute-start(bf16[64,2048]{1,0:T(8,128)(2,1)S(1)} %get-tuple-element.43), channel_id=1, source_target_pairs={{0,1},{1,0},{2,3},{3,2},{4,5},{5,4},{6,7},{7,6},{8,9},{9,8},{10,11... | collective-permute-start | bytes 786440 | tf_op jit(solution)/shard_map/ppermute | solution.py:402
  38.8 6.4 %collective-permute-start.9 = (bf16[64,2048]{1,0:T(8,128)(2,1)S(1)}, bf16[64,2048]{1,0:T(8,128)(2,1)S(1)}, u32[]{:S(2)}, u32[]{:S(2)}) collective-permute-start(bf16[64,2048]{1,0:T(8,128)(2,1)S(1)} %get-tuple-element.42.refs_2_._), channel_id=1, source_target_pairs={{0,2},{1,3},{2,0},{3,1},{4,6},{5,7},{6,4},{7,5},{8,10},{9,11},{10,... | collective-permute-start | bytes 786440 | tf_op jit(solution)/shard_map/ppermute | solution.py:402
  45.2 4.6 %copy-start.1 = (bf16[4,2048,768]{2,1,0:T(8,128)(2,1)S(1)}, bf16[4,2048,768]{2,1,0:T(8,128)(2,1)}, u32[]{:S(2)}) copy-start(bf16[4,2048,768]{2,1,0:T(8,128)(2,1)} %copy-done) | copy-start | bytes 37748740
  61.7 10.8 %collective-permute-start.17 = (bf16[2,128,512]{2,1,0:T(8,128)(2,1)S(1)}, bf16[2,128,512]{2,1,0:T(8,128)(2,1)S(1)}, u32[]{:S(2)}, u32[]{:S(2)}) collective-permute-start(bf16[2,128,512]{2,1,0:T(8,128)(2,1)S(1)} %get-tuple-element.59), channel_id=1, source_target_pairs={{0,2},{1,3},{2,0},{3,1},{4,6},{5,7},{6,4},{7,5},{8,10},{9,11},{10,... | collective-permute-start | bytes 786440 | tf_op jit(solution)/shard_map/ppermute | solution.py:402
  65.3 8.8 %collective-permute-start.15 = (bf16[2,128,512]{2,1,0:T(8,128)(2,1)S(1)}, bf16[2,128,512]{2,1,0:T(8,128)(2,1)S(1)}, u32[]{:S(2)}, u32[]{:S(2)}) collective-permute-start(bf16[2,128,512]{2,1,0:T(8,128)(2,1)S(1)} %get-tuple-element.56), channel_id=1, source_target_pairs={{0,1},{1,0},{2,3},{3,2},{4,5},{5,4},{6,7},{7,6},{8,9},{9,8},{10,11... | collective-permute-start | bytes 786440 | tf_op jit(solution)/shard_map/ppermute | solution.py:402
  68.0 7.3 %collective-permute-start.13 = (bf16[2,128,512]{2,1,0:T(8,128)(2,1)S(1)}, bf16[2,128,512]{2,1,0:T(8,128)(2,1)S(1)}, u32[]{:S(2)}, u32[]{:S(2)}) collective-permute-start(bf16[2,128,512]{2,1,0:T(8,128)(2,1)S(1)} %get-tuple-element.53), channel_id=1, source_target_pairs={{0,2},{1,3},{2,0},{3,1},{4,6},{5,7},{6,4},{7,5},{8,10},{9,11},{10,... | collective-permute-start | bytes 786440 | tf_op jit(solution)/shard_map/ppermute | solution.py:402
  70.9 9.2 %collective-permute-start.11 = (bf16[2,128,512]{2,1,0:T(8,128)(2,1)S(1)}, bf16[2,128,512]{2,1,0:T(8,128)(2,1)S(1)}, u32[]{:S(2)}, u32[]{:S(2)}) collective-permute-start(bf16[2,128,512]{2,1,0:T(8,128)(2,1)S(1)} %get-tuple-element.50), channel_id=1, source_target_pairs={{0,1},{1,0},{2,3},{3,2},{4,5},{5,4},{6,7},{7,6},{8,9},{9,8},{10,11... | collective-permute-start | bytes 786440 | tf_op jit(solution)/shard_map/ppermute | solution.py:402
  72.5 9.1 %collective-permute-start.18 = (bf16[1,128,512]{2,1,0:T(8,128)(2,1)S(1)}, bf16[1,128,512]{2,1,0:T(8,128)(2,1)S(1)}, u32[]{:S(2)}, u32[]{:S(2)}) collective-permute-start(bf16[1,128,512]{2,1,0:T(8,128)(2,1)S(1)} %add_convert_fusion), channel_id=1, source_target_pairs={{0,1},{1,0},{2,3},{3,2},{4,5},{5,4},{6,7},{7,6},{8,9},{9,8},{10,11... | collective-permute-start | bytes 393224 | tf_op jit(solution)/shard_map/ppermute | solution.py:402
  74.2 7.4 %collective-permute-start.16 = (bf16[1,128,512]{2,1,0:T(8,128)(2,1)S(1)}, bf16[1,128,512]{2,1,0:T(8,128)(2,1)S(1)}, u32[]{:S(2)}, u32[]{:S(2)}) collective-permute-start(bf16[1,128,512]{2,1,0:T(8,128)(2,1)S(1)} %add_convert_fusion.1), channel_id=1, source_target_pairs={{0,2},{1,3},{2,0},{3,1},{4,6},{5,7},{6,4},{7,5},{8,10},{9,11},{10,... | collective-permute-start | bytes 393224 | tf_op jit(solution)/shard_map/ppermute | solution.py:402
  75.3 7.6 %collective-permute-start.14 = (bf16[1,128,512]{2,1,0:T(8,128)(2,1)S(1)}, bf16[1,128,512]{2,1,0:T(8,128)(2,1)S(1)}, u32[]{:S(2)}, u32[]{:S(2)}) collective-permute-start(bf16[1,128,512]{2,1,0:T(8,128)(2,1)S(1)} %add_convert_fusion.2), channel_id=1, source_target_pairs={{0,1},{1,0},{2,3},{3,2},{4,5},{5,4},{6,7},{7,6},{8,9},{9,8},{10,11... | collective-permute-start | bytes 393224 | tf_op jit(solution)/shard_map/ppermute | solution.py:402
  80.2 5.0 %collective-permute-start.12 = (bf16[1,128,512]{2,1,0:T(8,128)(2,1)S(1)}, bf16[1,128,512]{2,1,0:T(8,128)(2,1)S(1)}, u32[]{:S(2)}, u32[]{:S(2)}) collective-permute-start(bf16[1,128,512]{2,1,0:T(8,128)(2,1)S(1)} %add_convert_fusion.3), channel_id=1, source_target_pairs={{0,2},{1,3},{2,0},{3,1},{4,6},{5,7},{6,4},{7,5},{8,10},{9,11},{10,... | collective-permute-start | bytes 393224 | tf_op jit(solution)/shard_map/ppermute | solution.py:402

commit v7 on v6

--- a/solution.py
+++ b/solution.py
@@ -12,9 +12,11 @@
 UNUSED = 200.0
 MIB = 1 << 20
 CHUNKS = 4
+RING = 8
+COPIES = 4
 PRE_MIB = 6
-BACK_MIB = 10
-OUT_MIB = 4
+BACK_MIB = 18
+OUT_MIB = 12
 
 NT = (((1,), (1,)), ((), ()))
 
@@ -263,14 +265,14 @@
             gate_pre = dot(rows, wg_ref[e, :, part])
             up_pre = dot(rows, wu_ref[e, :, part])
             sig = jax.nn.sigmoid(gate_pre)
-            a_ref[i, part, :] = ((sig * up_pre * (1.0 + gate_pre * (1.0 - sig))).T * gates).astype(jnp.bfloat16)
-            b_ref[i, part, :] = ((sig * gate_pre).T * gates).astype(jnp.bfloat16)
+            a_ref[i, part, :] = (sig * up_pre * (1.0 + gate_pre * (1.0 - sig))).T * gates
+            b_ref[i, part, :] = (sig * gate_pre).T * gates
 
 
 def pre(n, experts, gates, first, rest, wg, wu, after):
     local, features, hidden = wg.shape
     rows, count = n * SLOT, len(experts)
-    shape = jax.ShapeDtypeStruct((count, hidden, rows), jnp.bfloat16)
+    shape = jax.ShapeDtypeStruct((count, hidden, rows), jnp.float32)
     return pl.pallas_call(
         functools.partial(pre_kernel, experts),
         in_specs=[INSIDE] * 5 + [ANYWHERE],
@@ -286,7 +288,7 @@
 
 def back_kernel(local, counts, halves, place_ref, first_ref, *refs):
     token_refs, (wd_ref, *refs) = split(refs, counts)
-    factor_refs, (_, _, hg_ref, hu_ref, gs, weight, sems) = refs[: 2 * halves], refs[2 * halves :]
+    factor_refs, (_, hg_ref, hu_ref, gs, weight, sems) = refs[: 2 * halves], refs[2 * halves :]
     factors = [
         (a_ref, b_ref, i)
         for a_ref, b_ref in zip(factor_refs[::2], factor_refs[1::2])
@@ -294,60 +296,89 @@
     ]
     hidden = wd_ref.shape[1]
     cols = hidden // 2
-    held = weight.shape[0]
-
-    def fetch(e, i):
-        part = pl.ds(i * cols, cols)
-        slot = e % held
-        return pltpu.make_async_copy(wd_ref.at[e, part], weight.at[slot, part], sems.at[slot, i])
-
-    for e in range(held):
-        for i in range(2):
-            fetch(e, i).start()
+    ring, rows_each = weight.shape[0], cols // COPIES
+    pieces = [(e, i) for e in range(local) for i in range(2)]
+
+    def fetch(piece):
+        e, i = pieces[piece]
+        at = piece % ring
+        return [
+            pltpu.make_async_copy(
+                wd_ref.at[e, pl.ds(i * cols + c * rows_each, rows_each)],
+                weight.at[at, pl.ds(c * rows_each, rows_each)],
+                sems.at[at, c],
+            )
+            for c in range(COPIES)
+        ]
+
+    def start(piece):
+        if piece < len(pieces):
+            for copy in fetch(piece):
+                copy.start()
+
+    for piece in range(ring):
+        start(piece)
     gather_columns(local, place_ref, token_refs, 1, gs)
 
     for e, (a_ref, b_ref, at) in enumerate(factors):
         rows = jnp.concatenate([first_ref[e], gs[e]], axis=1)
         for i in range(2):
             part = slice(i * cols, (i + 1) * cols)
-            fetch(e, i).wait()
-            back = dot(weight[e % held, part, :], rows)
+            piece = 2 * e + i
+            for copy in fetch(piece):
+                copy.wait()
+            back = dot(weight[piece % ring], rows)
             hg_ref[e, part, :] = (back * a_ref[at, part, :]).astype(jnp.bfloat16)
             hu_ref[e, part, :] = (back * b_ref[at, part, :]).astype(jnp.bfloat16)
-            if e + held < local:
-                fetch(e + held, i).start()
-
-
-def back(n, place, first, tokens, wd, factors, wg, wu):
+            start(piece + ring)
+
+
+def back(n, place, first, tokens, wd, factors, wg):
     local, hidden, features = wd.shape
     rows = n * SLOT
     shape = jax.ShapeDtypeStruct((local, hidden, rows), jnp.bfloat16)
     return pl.pallas_call(
         functools.partial(back_kernel, local, sizes(tokens), len(factors)),
-        in_specs=[INSIDE] * (2 + len(flat(tokens))) + [OUTSIDE] + [INSIDE] * (2 * len(factors) + 2),
+        in_specs=[INSIDE] * (2 + len(flat(tokens))) + [OUTSIDE] + [INSIDE] * (2 * len(factors) + 1),
         out_shape=[shape, shape],
         scratch_shapes=[
             pltpu.VMEM((local, features, rows - 2 * SLOT), jnp.bfloat16),
-            pltpu.VMEM((min(local, 2), hidden, features), jnp.bfloat16),
-            pltpu.SemaphoreType.DMA((min(local, 2), 2)),
+            pltpu.VMEM((min(2 * local, RING), hidden // 2, features), jnp.bfloat16),
+            pltpu.SemaphoreType.DMA((min(2 * local, RING), COPIES)),
         ],
-        compiler_params=params(BACK_MIB * max(1, n // 4)),
+        compiler_params=params(BACK_MIB),
         cost_estimate=pl.CostEstimate(
             flops=2 * local * rows * features * hidden,
             bytes_accessed=2 * local * features * hidden,
             transcendentals=0,
         ),
-    )(place, first, *flat(tokens), hbm(wd), *flat(factors), vmem(wg), vmem(wu))
+    )(place, first, *flat(tokens), hbm(wd), *flat(factors), vmem(wg))
 
 
 def out_kernel(n, local, orders, chunk, place_ref, hg_ref, hu_ref, wg_ref, wu_ref, *rest):
-    outs, rows_ref = rest[:-1], rest[-1]
+    outs, (rows_ref, half_ref, weight, sems) = rest[:-4], rest[-4:]
     wide = 2 * SLOT
     cols = wg_ref.shape[1] // CHUNKS
     part = slice(chunk * cols, (chunk + 1) * cols)
+    copies = [
+        [
+            pltpu.make_async_copy(
+                wu_ref.at[e, pl.ds(chunk * cols + c * cols // 2, cols // 2)],
+                weight.at[e, pl.ds(c * cols // 2, cols // 2)],
+                sems.at[e, c],
+            )
+            for c in range(2)
+        ]
+        for e in range(local)
+    ]
+    for copy in flat(copies):
+        copy.start()
     for e in range(local):
-        rows = dot(wg_ref[e, part, :], hg_ref[e]) + dot(wu_ref[e, part, :], hu_ref[e])
-        rows = rows.astype(jnp.bfloat16)
+        half_ref[e] = dot(wg_ref[e, part, :], hg_ref[e])
+    for e in range(local):
+        for copy in copies[e]:
+            copy.wait()
+        rows = (half_ref[e] + dot(weight[e], hu_ref[e])).astype(jnp.bfloat16)
         for p in range(n // 2):
             rows_ref[p, :, e * wide : (e + 1) * wide] = rows[:, p * wide : (p + 1) * wide]
     tokens = place_ref.shape[1] // 2
@@ -369,15 +400,21 @@
     types = [jnp.float32] + [jnp.bfloat16] * (len(orders) - 1)
     return pl.pallas_call(
         functools.partial(out_kernel, n, local, orders, chunk),
+        in_specs=[INSIDE] * 4 + [OUTSIDE],
         out_shape=[jax.ShapeDtypeStruct(s, t) for s, t in zip(shapes, types)],
-        scratch_shapes=[pltpu.VMEM((n // 2, cols, 2 * SLOT * local), jnp.bfloat16)],
-        compiler_params=params(OUT_MIB * max(1, n // 4)),
+        scratch_shapes=[
+            pltpu.VMEM((n // 2, cols, 2 * SLOT * local), jnp.bfloat16),
+            pltpu.VMEM((local, cols, rows), jnp.float32),
+            pltpu.VMEM((local, cols, hidden), jnp.bfloat16),
+            pltpu.SemaphoreType.DMA((local, 2)),
+        ],
+        compiler_params=params(OUT_MIB * max(1, n // 8)),
         cost_estimate=pl.CostEstimate(
             flops=local * rows * cols * hidden,
             bytes_accessed=local * cols * hidden,
             transcendentals=0,
         ),
-    )(place, hg, hu, vmem(wg), vmem(wu))
+    )(place, hg, hu, vmem(wg), hbm(wu))
 
 
 def sum_kernel(*refs):
@@ -404,7 +441,7 @@
     table = rank_table(routes.T, route_gates.T, experts)
     tables = [table] + [swap(table, k) for k in range(1, n)]
     pick, place, gates = slots(axis, n, local, tables)
-    gate_proj, up_proj, done = load((gate_proj, up_proj), table)
+    gate_proj, up_near, done = load((gate_proj, up_proj), table)
     if n == 4:
         x_near = [swap(saved_input, 1), swap(saved_input, 2)]
         upper, lower = relay_parts(x_near, [done, place])
@@ -417,7 +454,7 @@
     x_first = slot_rows(local, pick, x_blocks[:2], 0, sent)
     x_rest = slot_rows(local, pick, x_blocks[2:], 1, sent)
     half = (local + 1) // 2
-    factors = [pre(n, range(half), gates, x_first, x_rest, gate_proj, up_proj, table)]
+    factors = [pre(n, range(half), gates, x_first, x_rest, gate_proj, up_near, table)]
     if n == 4:
         upper, lower = relay_parts(g_near, [factors[0][0]])
         g_blocks = [[sent], *[[g] for g in g_near], [swap(upper, 2), swap(lower, 1)]]
@@ -425,9 +462,9 @@
         g_blocks = [[grad_out]] + [[swap(grad_out, k)] for k in range(1, n)]
         upper = table
     if half < local:
-        factors.append(pre(n, range(half, local), gates, x_first, x_rest, gate_proj, up_proj, upper))
+        factors.append(pre(n, range(half, local), gates, x_first, x_rest, gate_proj, up_near, upper))
     g_first = early_columns(local, place, g_blocks[:2], upper)
-    hg, hu = back(n, place, g_first, g_blocks[2:], down_proj, factors, gate_proj, up_proj)
+    hg, hu = back(n, place, g_first, g_blocks[2:], down_proj, factors, gate_proj)
     parts = []
     for chunk in range(CHUNKS):
         if n == 4:

time: 86.5 us -> 88.4 us (1.022)
  Pallas kernels: 41.5 us -> 50.4 us
  local copies, waits for them, and re-layouts: 5.36 us -> 0.78 us
  waiting for transfers between devices: 17.3 us -> 13 us
  starting transfers between devices: 21.7 us -> 23.6 us
    pallas_call x4, Pallas kernels: 8.58 us -> 17.3 us  [partial_sums(): pl.pallas_call(functools.partial(out_kernel, n, local, orders, chunk), in...]
    unnamed x10 -> x6, local copies, waits for them, and re-layouts: 5.32 us -> 0.74 us
    ppermute x19, waiting for transfers between devices: 17.3 us -> 13 us  [swap(): return lax.ppermute(array, axis, [(i, i ^ k) for i in range(n)])]
    ppermute x19, starting transfers between devices: 21.7 us -> 23.6 us  [swap(): return lax.ppermute(array, axis, [(i, i ^ k) for i in range(n)])]
  transfers between devices with their start and end apart: 19 -> 19, of which waited for: 10 -> 7; matrix products, arithmetic and copies ran while one was open for 0% -> 0% of each run, Pallas kernels for 33% -> 40%
where the time goes in v7:
time: 88.4 us; the launch traced here: 88.2 us
  Pallas kernels  50.4 us (57%)
  starting transfers between devices  23.6 us (27%)
  waiting for transfers between devices  13 us (15%)
    ppermute x19, starting transfers between devices, swap(): return lax.ppermute(array, axis, [(i, i ^ k) for i in range(n)])  23.6 us
    pallas_call x4, Pallas kernels, partial_sums(): pl.pallas_call(functools.partial(out_kernel, n, local, orders, chunk), in...  17.3 us
    ppermute x19, waiting for transfers between devices, swap(): return lax.ppermute(array, axis, [(i, i ^ k) for i in range(n)])  13 us
    pallas_call x1, Pallas kernels, back(): pl.pallas_call(functools.partial(back_kernel, local, sizes(tokens), len(f...  9.99 us
    pallas_call x2, Pallas kernels, pre(): pl.pallas_call(functools.partial(pre_kernel, experts), in_specs=[INSIDE]...  9.66 us
    pallas_call x1, Pallas kernels, load(): pl.pallas_call(functools.partial(load_kernel, count), in_specs=[OUTSIDE]...  8.3 us
  transfers between devices with their start and end apart: 19, of which 7 were waited for; matrix products, arithmetic and copies ran while one was open for 0% of the time, Pallas kernels for 40%

profile of v7, /device:TPU:0, one launch (start us, length us, event | category | flops | bytes accessed | tf_op | source)
XLA Modules:
  0.0 88.2 jit_solution(16691592527105816190)
XLA Ops:
  0.0 2.9 %collective-permute-start.3 = (bf16[128,2048]{1,0:T(8,128)(2,1)}, bf16[128,2048]{1,0:T(8,128)(2,1)S(1)}, u32[]{:S(2)}, u32[]{:S(2)}) collective-permute-start(bf16[128,2048]{1,0:T(8,128)(2,1)} %refs_0_.3), channel_id=1, source_target_pairs={{0,1},{1,0},{2,3},{3,2},{4,5},{5,4},{6,7},{7,6},{8,9},{9,8},{10,11... | collective-permute-start | bytes 1572872 | tf_op jit(solution)/shard_map/ppermute | solution.py:439
  2.9 1.5 %collective-permute-start.4 = (bf16[128,2048]{1,0:T(8,128)(2,1)}, bf16[128,2048]{1,0:T(8,128)(2,1)S(1)}, u32[]{:S(2)}, u32[]{:S(2)}) collective-permute-start(bf16[128,2048]{1,0:T(8,128)(2,1)} %refs_0_.3), channel_id=1, source_target_pairs={{0,2},{1,3},{2,0},{3,1},{4,6},{5,7},{6,4},{7,5},{8,10},{9,11},{10,... | collective-permute-start | bytes 1572872 | tf_op jit(solution)/shard_map/ppermute | solution.py:439
  4.5 1.5 %shard_map.73.refs_0_.refs_2_._ = bf16[32,128]{1,0:T(8,128)(2,1)} custom-call(s32[8,128]{1,0:T(8,128)} %bitcast.2, bf16[8,128]{1,0:T(8,128)(2,1)} %bitcast.3), custom_call_target="tpu_custom_call" | custom-call | tf_op jit(solution)/shard_map/pallas_call | solution.py:58
  5.9 0.0 copy-start
  5.9 0.0 collective-permute-start.2
  6.0 2.0 %collective-permute-start.1 = (bf16[32,128]{1,0:T(8,128)(2,1)}, bf16[32,128]{1,0:T(8,128)(2,1)S(1)}, u32[]{:S(2)}, u32[]{:S(2)}) collective-permute-start(bf16[32,128]{1,0:T(8,128)(2,1)} %shard_map.73.refs_0_.refs_2_._), channel_id=1, source_target_pairs={{0,2},{1,3},{2,0},{3,1},{4,6},{5,7},{6,4},{7,5},{8,10},{9,11},{10,... | collective-permute-start | bytes 24584 | tf_op jit(solution)/shard_map/ppermute | solution.py:439
  7.9 1.5 %collective-permute-start = (bf16[32,128]{1,0:T(8,128)(2,1)}, bf16[32,128]{1,0:T(8,128)(2,1)S(1)}, u32[]{:S(2)}, u32[]{:S(2)}) collective-permute-start(bf16[32,128]{1,0:T(8,128)(2,1)} %shard_map.73.refs_0_.refs_2_._), channel_id=1, source_target_pairs={{0,1},{1,0},{2,3},{3,2},{4,5},{5,4},{6,7},{7,6},{8,9},{9,8},{10,11... | collective-permute-start | bytes 24584 | tf_op jit(solution)/shard_map/ppermute | solution.py:439
  9.4 0.0 copy-start.2
  9.4 0.7 copy-done.2
  10.2 8.3 %shard_map.75 = (bf16[4,2048,768]{2,1,0:T(8,128)(2,1)S(1)}, bf16[4,2048,768]{2,1,0:T(8,128)(2,1)S(1)}, f32[8,128]{1,0:T(8,128)S(1)}) custom-call(bf16[4,2048,768]{2,1,0:T(8,128)(2,1)} %refs_0_.2, bf16[4,2048,768]{2,1,0:T(8,128)(2,1)} %wu_ref.7, bf16[32,128]{1,0:T(8,128)(2,1)S(1)} %copy-done.2), custom_call_target="tpu_custom_call" | custom-call | bytes 50331648 | tf_op jit(solution)/shard_map/pallas_call | solution.py:181
  18.5 0.0 copy-start.1
  18.5 0.0 collective-permute-done.2.refs_3_
  18.5 0.0 collective-permute-done.1.refs_2_
  18.5 0.0 collective-permute-done.refs_1_
  18.5 0.4 shard_map.74
  19.0 0.0 collective-permute-done.3.x_ref.refs_1_
  19.0 0.0 collective-permute-done.4.y_ref.refs_0_
  19.0 0.6 collective-permute-start.8
  19.6 0.1 collective-permute-start.7
  19.7 0.0 copy-done
  19.7 2.0 %collective-permute-start.6 = (bf16[128,2048]{1,0:T(8,128)(2,1)S(1)}, bf16[128,2048]{1,0:T(8,128)(2,1)S(1)}, u32[]{:S(2)}, u32[]{:S(2)}) collective-permute-start(bf16[128,2048]{1,0:T(8,128)(2,1)S(1)} %shard_map.77.refs_2_.refs_3_.refs_0_), channel_id=1, source_target_pairs={{0,2},{1,3},{2,0},{3,1},{4,6},{5,7},{6,4},{7,5},{8,10},{9,11},{10,... | collective-permute-start | bytes 1572872 | tf_op jit(solution)/shard_map/ppermute | solution.py:439
  21.8 1.5 %collective-permute-start.5 = (bf16[128,2048]{1,0:T(8,128)(2,1)S(1)}, bf16[128,2048]{1,0:T(8,128)(2,1)S(1)}, u32[]{:S(2)}, u32[]{:S(2)}) collective-permute-start(bf16[128,2048]{1,0:T(8,128)(2,1)S(1)} %shard_map.77.refs_2_.refs_3_.refs_0_), channel_id=1, source_target_pairs={{0,1},{1,0},{2,3},{3,2},{4,5},{5,4},{6,7},{7,6},{8,9},{9,8},{10,11... | collective-permute-start | bytes 1572872 | tf_op jit(solution)/shard_map/ppermute | solution.py:439
  23.2 0.0 copy-done.1
  23.2 0.7 shard_map.78.first_ref
  24.0 4.4 %collective-permute-done.8.refs_2_ = bf16[64,2048]{1,0:T(8,128)(2,1)S(1)} collective-permute-done((bf16[64,2048]{1,0:T(8,128)(2,1)S(1)}, bf16[64,2048]{1,0:T(8,128)(2,1)S(1)}, u32[]{:S(2)}, u32[]{:S(2)}) %collective-permute-start.8) | collective-permute-done | bytes 262176 | tf_op jit(solution)/shard_map/ppermute | solution.py:439
  28.3 0.5 collective-permute-done.7.refs_1_
  28.9 0.7 shard_map.79.rest_ref
  29.6 4.7 %shard_map.80 = (f32[2,768,256]{2,1,0:T(8,128)S(1)}, f32[2,768,256]{2,1,0:T(8,128)S(1)}) custom-call(f32[4,8,256]{2,1,0:T(8,128)S(1)} %get-tuple-element.36.gate_ref, bf16[4,128,2048]{2,1,0:T(8,128)(2,1)S(1)} %shard_map.78.first_ref, bf16[4,128,2048]{2,1,0:T(8,128)(2,1)S(1)} %shard_map.79.rest_ref, ...), custom_call_target="tpu_custom_call" | custom-call | flops 3221225472 | bytes 12582912 | tf_op jit(solution)/shard_map/pallas_call | solution.py:276
  34.3 2.9 %collective-permute-done.6.y_ref.refs_0_ = bf16[128,2048]{1,0:T(8,128)(2,1)S(1)} collective-permute-done((bf16[128,2048]{1,0:T(8,128)(2,1)S(1)}, bf16[128,2048]{1,0:T(8,128)(2,1)S(1)}, u32[]{:S(2)}, u32[]{:S(2)}) %collective-permute-start.6) | collective-permute-done | bytes 524320 | tf_op jit(solution)/shard_map/ppermute | solution.py:439
  37.2 0.0 collective-permute-done.5.x_ref.refs_1_
  37.3 1.6 %collective-permute-start.10 = (bf16[64,2048]{1,0:T(8,128)(2,1)S(1)}, bf16[64,2048]{1,0:T(8,128)(2,1)S(1)}, u32[]{:S(2)}, u32[]{:S(2)}) collective-permute-start(bf16[64,2048]{1,0:T(8,128)(2,1)S(1)} %get-tuple-element.43), channel_id=1, source_target_pairs={{0,1},{1,0},{2,3},{3,2},{4,5},{5,4},{6,7},{7,6},{8,9},{9,8},{10,11... | collective-permute-start | bytes 786440 | tf_op jit(solution)/shard_map/ppermute | solution.py:439
  38.8 0.5 collective-permute-start.9
  39.3 0.7 shard_map.82.first_ref
  40.1 4.9 %shard_map.83 = (f32[2,768,256]{2,1,0:T(8,128)S(1)}, f32[2,768,256]{2,1,0:T(8,128)S(1)}) custom-call(f32[4,8,256]{2,1,0:T(8,128)S(1)} %get-tuple-element.36.gate_ref, bf16[4,128,2048]{2,1,0:T(8,128)(2,1)S(1)} %shard_map.78.first_ref, bf16[4,128,2048]{2,1,0:T(8,128)(2,1)S(1)} %shard_map.79.rest_ref, ...), custom_call_target="tpu_custom_call" | custom-call | flops 3221225472 | bytes 12582912 | tf_op jit(solution)/shard_map/pallas_call | solution.py:276
  45.0 0.0 collective-permute-done.10.refs_2_
  45.0 0.2 collective-permute-done.9.refs_1_
  45.2 10.0 %shard_map.84 = (bf16[4,768,256]{2,1,0:T(8,128)(2,1)S(1)}, bf16[4,768,256]{2,1,0:T(8,128)(2,1)S(1)}) custom-call(bf16[2,256,512]{2,1,0:T(8,128)(2,1)S(1)} %get-tuple-element.33.refs_1_.place_ref, bf16[4,2048,128]{2,1,0:T(8,128)(2,1)S(1)} %shard_map.82.first_ref, bf16[128,2048]{1,0:T(8,128)(2,1)S(1)} %collective-permute-done.6.y_ref.refs_0_, ...), custom_call_target="tpu_custom_call" | custom-call | flops 3221225472 | bytes 12582912 | tf_op jit(solution)/shard_map/pallas_call | solution.py:340
  55.2 4.3 %shard_map.88 = (f32[1,128,512]{2,1,0:T(8,128)S(1)}, bf16[2,128,512]{2,1,0:T(8,128)(2,1)S(1)}, bf16[1,128,512]{2,1,0:T(8,128)(2,1)S(1)}) custom-call(bf16[2,256,512]{2,1,0:T(8,128)(2,1)S(1)} %get-tuple-element.33.refs_1_.place_ref, bf16[4,768,256]{2,1,0:T(8,128)(2,1)S(1)} %get-tuple-element.47.hg_ref, bf16[4,768,256]{2,1,0:T(8,128)(2,1)S(1)} %get-tuple-element.48.hu_ref, ...), custom_call_target="tpu_custom_call" | custom-call | flops 402653184 | bytes 1572864 | tf_op jit(solution)/shard_map/pallas_call | solution.py:401
  59.5 1.4 %collective-permute-start.17 = (bf16[2,128,512]{2,1,0:T(8,128)(2,1)S(1)}, bf16[2,128,512]{2,1,0:T(8,128)(2,1)S(1)}, u32[]{:S(2)}, u32[]{:S(2)}) collective-permute-start(bf16[2,128,512]{2,1,0:T(8,128)(2,1)S(1)} %get-tuple-element.59), channel_id=1, source_target_pairs={{0,2},{1,3},{2,0},{3,1},{4,6},{5,7},{6,4},{7,5},{8,10},{9,11},{10,... | collective-permute-start | bytes 786440 | tf_op jit(solution)/shard_map/ppermute | solution.py:439
  61.0 4.3 %shard_map.87 = (f32[1,128,512]{2,1,0:T(8,128)S(1)}, bf16[2,128,512]{2,1,0:T(8,128)(2,1)S(1)}, bf16[1,128,512]{2,1,0:T(8,128)(2,1)S(1)}) custom-call(bf16[2,256,512]{2,1,0:T(8,128)(2,1)S(1)} %get-tuple-element.33.refs_1_.place_ref, bf16[4,768,256]{2,1,0:T(8,128)(2,1)S(1)} %get-tuple-element.47.hg_ref, bf16[4,768,256]{2,1,0:T(8,128)(2,1)S(1)} %get-tuple-element.48.hu_ref, ...), custom_call_target="tpu_custom_call" | custom-call | flops 402653184 | bytes 1572864 | tf_op jit(solution)/shard_map/pallas_call | solution.py:401
  65.3 0.6 collective-permute-start.15
  65.9 4.3 %shard_map.86 = (f32[1,128,512]{2,1,0:T(8,128)S(1)}, bf16[2,128,512]{2,1,0:T(8,128)(2,1)S(1)}, bf16[1,128,512]{2,1,0:T(8,128)(2,1)S(1)}) custom-call(bf16[2,256,512]{2,1,0:T(8,128)(2,1)S(1)} %get-tuple-element.33.refs_1_.place_ref, bf16[4,768,256]{2,1,0:T(8,128)(2,1)S(1)} %get-tuple-element.47.hg_ref, bf16[4,768,256]{2,1,0:T(8,128)(2,1)S(1)} %get-tuple-element.48.hu_ref, ...), custom_call_target="tpu_custom_call" | custom-call | flops 402653184 | bytes 1572864 | tf_op jit(solution)/shard_map/pallas_call | solution.py:401
  70.2 0.7 collective-permute-start.13
  70.9 4.3 %shard_map.85 = (f32[1,128,512]{2,1,0:T(8,128)S(1)}, bf16[2,128,512]{2,1,0:T(8,128)(2,1)S(1)}, bf16[1,128,512]{2,1,0:T(8,128)(2,1)S(1)}) custom-call(bf16[2,256,512]{2,1,0:T(8,128)(2,1)S(1)} %get-tuple-element.33.refs_1_.place_ref, bf16[4,768,256]{2,1,0:T(8,128)(2,1)S(1)} %get-tuple-element.47.hg_ref, bf16[4,768,256]{2,1,0:T(8,128)(2,1)S(1)} %get-tuple-element.48.hu_ref, ...), custom_call_target="tpu_custom_call" | custom-call | flops 402653184 | bytes 1572864 | tf_op jit(solution)/shard_map/pallas_call | solution.py:401
  75.3 1.6 %collective-permute-start.11 = (bf16[2,128,512]{2,1,0:T(8,128)(2,1)S(1)}, bf16[2,128,512]{2,1,0:T(8,128)(2,1)S(1)}, u32[]{:S(2)}, u32[]{:S(2)}) collective-permute-start(bf16[2,128,512]{2,1,0:T(8,128)(2,1)S(1)} %get-tuple-element.50), channel_id=1, source_target_pairs={{0,1},{1,0},{2,3},{3,2},{4,5},{5,4},{6,7},{7,6},{8,9},{9,8},{10,11... | collective-permute-start | bytes 786440 | tf_op jit(solution)/shard_map/ppermute | solution.py:439
  76.8 0.0 collective-permute-done.17
  76.9 0.6 collective-permute-start.18
  77.5 0.0 collective-permute-done.15
  77.5 1.4 %collective-permute-start.16 = (bf16[1,128,512]{2,1,0:T(8,128)(2,1)S(1)}, bf16[1,128,512]{2,1,0:T(8,128)(2,1)S(1)}, u32[]{:S(2)}, u32[]{:S(2)}) collective-permute-start(bf16[1,128,512]{2,1,0:T(8,128)(2,1)S(1)} %add_convert_fusion.1), channel_id=1, source_target_pairs={{0,2},{1,3},{2,0},{3,1},{4,6},{5,7},{6,4},{7,5},{8,10},{9,11},{10,... | collective-permute-start | bytes 393224 | tf_op jit(solution)/shard_map/ppermute | solution.py:439
  78.9 0.0 collective-permute-done.13
  79.0 1.6 %collective-permute-start.14 = (bf16[1,128,512]{2,1,0:T(8,128)(2,1)S(1)}, bf16[1,128,512]{2,1,0:T(8,128)(2,1)S(1)}, u32[]{:S(2)}, u32[]{:S(2)}) collective-permute-start(bf16[1,128,512]{2,1,0:T(8,128)(2,1)S(1)} %add_convert_fusion.2), channel_id=1, source_target_pairs={{0,1},{1,0},{2,3},{3,2},{4,5},{5,4},{6,7},{7,6},{8,9},{9,8},{10,11... | collective-permute-start | bytes 393224 | tf_op jit(solution)/shard_map/ppermute | solution.py:439
  80.5 1.6 %collective-permute-done.11 = bf16[2,128,512]{2,1,0:T(8,128)(2,1)S(1)} collective-permute-done((bf16[2,128,512]{2,1,0:T(8,128)(2,1)S(1)}, bf16[2,128,512]{2,1,0:T(8,128)(2,1)S(1)}, u32[]{:S(2)}, u32[]{:S(2)}) %collective-permute-start.11) | collective-permute-done | bytes 262176 | tf_op jit(solution)/shard_map/ppermute | solution.py:439
  82.2 1.5 %collective-permute-start.12 = (bf16[1,128,512]{2,1,0:T(8,128)(2,1)S(1)}, bf16[1,128,512]{2,1,0:T(8,128)(2,1)S(1)}, u32[]{:S(2)}, u32[]{:S(2)}) collective-permute-start(bf16[1,128,512]{2,1,0:T(8,128)(2,1)S(1)} %add_convert_fusion.3), channel_id=1, source_target_pairs={{0,2},{1,3},{2,0},{3,1},{4,6},{5,7},{6,4},{7,5},{8,10},{9,11},{10,... | collective-permute-start | bytes 393224 | tf_op jit(solution)/shard_map/ppermute | solution.py:439
  83.7 0.0 collective-permute-done.18.refs_11_
  83.8 0.0 collective-permute-done.16.refs_8_
  83.8 1.2 %collective-permute-done.14.refs_5_ = bf16[1,128,512]{2,1,0:T(8,128)(2,1)S(1)} collective-permute-done((bf16[1,128,512]{2,1,0:T(8,128)(2,1)S(1)}, bf16[1,128,512]{2,1,0:T(8,128)(2,1)S(1)}, u32[]{:S(2)}, u32[]{:S(2)}) %collective-permute-start.14) | collective-permute-done | bytes 131104 | tf_op jit(solution)/shard_map/ppermute | solution.py:439
  84.9 2.3 %collective-permute-done.12.refs_2_ = bf16[1,128,512]{2,1,0:T(8,128)(2,1)S(1)} collective-permute-done((bf16[1,128,512]{2,1,0:T(8,128)(2,1)S(1)}, bf16[1,128,512]{2,1,0:T(8,128)(2,1)S(1)}, u32[]{:S(2)}, u32[]{:S(2)}) %collective-permute-start.12) | collective-permute-done | bytes 131104 | tf_op jit(solution)/shard_map/ppermute | solution.py:439
  87.2 1.0 %shard_map.89 = bf16[128,2048]{1,0:T(8,128)(2,1)} custom-call(f32[1,128,512]{2,1,0:T(8,128)S(1)} %get-tuple-element.49.refs_0_, bf16[1,128,512]{2,1,0:T(8,128)(2,1)S(1)} %slice.32.refs_1_, bf16[1,128,512]{2,1,0:T(8,128)(2,1)S(1)} %collective-permute-done.12.refs_2_, f32[1,128,512]{2,1,0:T(8,128)S(1)} %get-tuple-element.52.refs_3_, ...), custom_call_target="tpu_custom_call" | custom-call | tf_op jit(solution)/shard_map/pallas_call | solution.py:481
  (11 shorter events, 0.3 us)
Async XLA Ops:
  0.0 19.0 %collective-permute-start.3 = (bf16[128,2048]{1,0:T(8,128)(2,1)}, bf16[128,2048]{1,0:T(8,128)(2,1)S(1)}, u32[]{:S(2)}, u32[]{:S(2)}) collective-permute-start(bf16[128,2048]{1,0:T(8,128)(2,1)} %refs_0_.3), channel_id=1, source_target_pairs={{0,1},{1,0},{2,3},{3,2},{4,5},{5,4},{6,7},{7,6},{8,9},{9,8},{10,11... | collective-permute-start | bytes 1572872 | tf_op jit(solution)/shard_map/ppermute | solution.py:439
  2.9 16.0 %collective-permute-start.4 = (bf16[128,2048]{1,0:T(8,128)(2,1)}, bf16[128,2048]{1,0:T(8,128)(2,1)S(1)}, u32[]{:S(2)}, u32[]{:S(2)}) collective-permute-start(bf16[128,2048]{1,0:T(8,128)(2,1)} %refs_0_.3), channel_id=1, source_target_pairs={{0,2},{1,3},{2,0},{3,1},{4,6},{5,7},{6,4},{7,5},{8,10},{9,11},{10,... | collective-permute-start | bytes 1572872 | tf_op jit(solution)/shard_map/ppermute | solution.py:439
  5.9 13.7 %copy-start = (bf16[128,2048]{1,0:T(8,128)(2,1)S(1)}, bf16[128,2048]{1,0:T(8,128)(2,1)}, u32[]{:S(2)}) copy-start(bf16[128,2048]{1,0:T(8,128)(2,1)} %array_ref.1) | copy-start | bytes 1572868
  5.9 12.5 %collective-permute-start.2 = (bf16[32,128]{1,0:T(8,128)(2,1)}, bf16[32,128]{1,0:T(8,128)(2,1)S(1)}, u32[]{:S(2)}, u32[]{:S(2)}) collective-permute-start(bf16[32,128]{1,0:T(8,128)(2,1)} %shard_map.73.refs_0_.refs_2_._), channel_id=1, source_target_pairs={{0,3},{1,2},{2,1},{3,0},{4,7},{5,6},{6,5},{7,4},{8,11},{9,10},{10,... | collective-permute-start | bytes 24584 | tf_op jit(solution)/shard_map/ppermute | solution.py:439
  6.0 12.6 %collective-permute-start.1 = (bf16[32,128]{1,0:T(8,128)(2,1)}, bf16[32,128]{1,0:T(8,128)(2,1)S(1)}, u32[]{:S(2)}, u32[]{:S(2)}) collective-permute-start(bf16[32,128]{1,0:T(8,128)(2,1)} %shard_map.73.refs_0_.refs_2_._), channel_id=1, source_target_pairs={{0,2},{1,3},{2,0},{3,1},{4,6},{5,7},{6,4},{7,5},{8,10},{9,11},{10,... | collective-permute-start | bytes 24584 | tf_op jit(solution)/shard_map/ppermute | solution.py:439
  7.9 10.6 %collective-permute-start = (bf16[32,128]{1,0:T(8,128)(2,1)}, bf16[32,128]{1,0:T(8,128)(2,1)S(1)}, u32[]{:S(2)}, u32[]{:S(2)}) collective-permute-start(bf16[32,128]{1,0:T(8,128)(2,1)} %shard_map.73.refs_0_.refs_2_._), channel_id=1, source_target_pairs={{0,1},{1,0},{2,3},{3,2},{4,5},{5,4},{6,7},{7,6},{8,9},{9,8},{10,11... | collective-permute-start | bytes 24584 | tf_op jit(solution)/shard_map/ppermute | solution.py:439
  9.4 0.7 copy-start.2
  18.5 4.8 %copy-start.1 = (bf16[128,2048]{1,0:T(8,128)(2,1)S(1)}, bf16[128,2048]{1,0:T(8,128)(2,1)}, u32[]{:S(2)}) copy-start(bf16[128,2048]{1,0:T(8,128)(2,1)} %refs_0_.3) | copy-start | bytes 1572868
  19.0 9.3 %collective-permute-start.8 = (bf16[64,2048]{1,0:T(8,128)(2,1)S(1)}, bf16[64,2048]{1,0:T(8,128)(2,1)S(1)}, u32[]{:S(2)}, u32[]{:S(2)}) collective-permute-start(bf16[64,2048]{1,0:T(8,128)(2,1)S(1)} %get-tuple-element.38), channel_id=1, source_target_pairs={{0,1},{1,0},{2,3},{3,2},{4,5},{5,4},{6,7},{7,6},{8,9},{9,8},{10,11... | collective-permute-start | bytes 786440 | tf_op jit(solution)/shard_map/ppermute | solution.py:439
  19.6 9.2 %collective-permute-start.7 = (bf16[64,2048]{1,0:T(8,128)(2,1)S(1)}, bf16[64,2048]{1,0:T(8,128)(2,1)S(1)}, u32[]{:S(2)}, u32[]{:S(2)}) collective-permute-start(bf16[64,2048]{1,0:T(8,128)(2,1)S(1)} %get-tuple-element.35._), channel_id=1, source_target_pairs={{0,2},{1,3},{2,0},{3,1},{4,6},{5,7},{6,4},{7,5},{8,10},{9,11},{10,... | collective-permute-start | bytes 786440 | tf_op jit(solution)/shard_map/ppermute | solution.py:439
  19.7 17.5 %collective-permute-start.6 = (bf16[128,2048]{1,0:T(8,128)(2,1)S(1)}, bf16[128,2048]{1,0:T(8,128)(2,1)S(1)}, u32[]{:S(2)}, u32[]{:S(2)}) collective-permute-start(bf16[128,2048]{1,0:T(8,128)(2,1)S(1)} %shard_map.77.refs_2_.refs_3_.refs_0_), channel_id=1, source_target_pairs={{0,2},{1,3},{2,0},{3,1},{4,6},{5,7},{6,4},{7,5},{8,10},{9,11},{10,... | collective-permute-start | bytes 1572872 | tf_op jit(solution)/shard_map/ppermute | solution.py:439
  21.8 15.5 %collective-permute-start.5 = (bf16[128,2048]{1,0:T(8,128)(2,1)S(1)}, bf16[128,2048]{1,0:T(8,128)(2,1)S(1)}, u32[]{:S(2)}, u32[]{:S(2)}) collective-permute-start(bf16[128,2048]{1,0:T(8,128)(2,1)S(1)} %shard_map.77.refs_2_.refs_3_.refs_0_), channel_id=1, source_target_pairs={{0,1},{1,0},{2,3},{3,2},{4,5},{5,4},{6,7},{7,6},{8,9},{9,8},{10,11... | collective-permute-start | bytes 1572872 | tf_op jit(solution)/shard_map/ppermute | solution.py:439
  37.3 7.8 %collective-permute-start.10 = (bf16[64,2048]{1,0:T(8,128)(2,1)S(1)}, bf16[64,2048]{1,0:T(8,128)(2,1)S(1)}, u32[]{:S(2)}, u32[]{:S(2)}) collective-permute-start(bf16[64,2048]{1,0:T(8,128)(2,1)S(1)} %get-tuple-element.43), channel_id=1, source_target_pairs={{0,1},{1,0},{2,3},{3,2},{4,5},{5,4},{6,7},{7,6},{8,9},{9,8},{10,11... | collective-permute-start | bytes 786440 | tf_op jit(solution)/shard_map/ppermute | solution.py:439
  38.8 6.4 %collective-permute-start.9 = (bf16[64,2048]{1,0:T(8,128)(2,1)S(1)}, bf16[64,2048]{1,0:T(8,128)(2,1)S(1)}, u32[]{:S(2)}, u32[]{:S(2)}) collective-permute-start(bf16[64,2048]{1,0:T(8,128)(2,1)S(1)} %get-tuple-element.42.refs_2_._), channel_id=1, source_target_pairs={{0,2},{1,3},{2,0},{3,1},{4,6},{5,7},{6,4},{7,5},{8,10},{9,11},{10,... | collective-permute-start | bytes 786440 | tf_op jit(solution)/shard_map/ppermute | solution.py:439
  59.5 17.3 %collective-permute-start.17 = (bf16[2,128,512]{2,1,0:T(8,128)(2,1)S(1)}, bf16[2,128,512]{2,1,0:T(8,128)(2,1)S(1)}, u32[]{:S(2)}, u32[]{:S(2)}) collective-permute-start(bf16[2,128,512]{2,1,0:T(8,128)(2,1)S(1)} %get-tuple-element.59), channel_id=1, source_target_pairs={{0,2},{1,3},{2,0},{3,1},{4,6},{5,7},{6,4},{7,5},{8,10},{9,11},{10,... | collective-permute-start | bytes 786440 | tf_op jit(solution)/shard_map/ppermute | solution.py:439
  65.3 12.2 %collective-permute-start.15 = (bf16[2,128,512]{2,1,0:T(8,128)(2,1)S(1)}, bf16[2,128,512]{2,1,0:T(8,128)(2,1)S(1)}, u32[]{:S(2)}, u32[]{:S(2)}) collective-permute-start(bf16[2,128,512]{2,1,0:T(8,128)(2,1)S(1)} %get-tuple-element.56), channel_id=1, source_target_pairs={{0,1},{1,0},{2,3},{3,2},{4,5},{5,4},{6,7},{7,6},{8,9},{9,8},{10,11... | collective-permute-start | bytes 786440 | tf_op jit(solution)/shard_map/ppermute | solution.py:439
  70.2 8.7 %collective-permute-start.13 = (bf16[2,128,512]{2,1,0:T(8,128)(2,1)S(1)}, bf16[2,128,512]{2,1,0:T(8,128)(2,1)S(1)}, u32[]{:S(2)}, u32[]{:S(2)}) collective-permute-start(bf16[2,128,512]{2,1,0:T(8,128)(2,1)S(1)} %get-tuple-element.53), channel_id=1, source_target_pairs={{0,2},{1,3},{2,0},{3,1},{4,6},{5,7},{6,4},{7,5},{8,10},{9,11},{10,... | collective-permute-start | bytes 786440 | tf_op jit(solution)/shard_map/ppermute | solution.py:439
  75.3 6.9 %collective-permute-start.11 = (bf16[2,128,512]{2,1,0:T(8,128)(2,1)S(1)}, bf16[2,128,512]{2,1,0:T(8,128)(2,1)S(1)}, u32[]{:S(2)}, u32[]{:S(2)}) collective-permute-start(bf16[2,128,512]{2,1,0:T(8,128)(2,1)S(1)} %get-tuple-element.50), channel_id=1, source_target_pairs={{0,1},{1,0},{2,3},{3,2},{4,5},{5,4},{6,7},{7,6},{8,9},{9,8},{10,11... | collective-permute-start | bytes 786440 | tf_op jit(solution)/shard_map/ppermute | solution.py:439
  76.9 6.9 %collective-permute-start.18 = (bf16[1,128,512]{2,1,0:T(8,128)(2,1)S(1)}, bf16[1,128,512]{2,1,0:T(8,128)(2,1)S(1)}, u32[]{:S(2)}, u32[]{:S(2)}) collective-permute-start(bf16[1,128,512]{2,1,0:T(8,128)(2,1)S(1)} %add_convert_fusion), channel_id=1, source_target_pairs={{0,1},{1,0},{2,3},{3,2},{4,5},{5,4},{6,7},{7,6},{8,9},{9,8},{10,11... | collective-permute-start | bytes 393224 | tf_op jit(solution)/shard_map/ppermute | solution.py:439
  77.5 6.3 %collective-permute-start.16 = (bf16[1,128,512]{2,1,0:T(8,128)(2,1)S(1)}, bf16[1,128,512]{2,1,0:T(8,128)(2,1)S(1)}, u32[]{:S(2)}, u32[]{:S(2)}) collective-permute-start(bf16[1,128,512]{2,1,0:T(8,128)(2,1)S(1)} %add_convert_fusion.1), channel_id=1, source_target_pairs={{0,2},{1,3},{2,0},{3,1},{4,6},{5,7},{6,4},{7,5},{8,10},{9,11},{10,... | collective-permute-start | bytes 393224 | tf_op jit(solution)/shard_map/ppermute | solution.py:439
  79.0 6.0 %collective-permute-start.14 = (bf16[1,128,512]{2,1,0:T(8,128)(2,1)S(1)}, bf16[1,128,512]{2,1,0:T(8,128)(2,1)S(1)}, u32[]{:S(2)}, u32[]{:S(2)}) collective-permute-start(bf16[1,128,512]{2,1,0:T(8,128)(2,1)S(1)} %add_convert_fusion.2), channel_id=1, source_target_pairs={{0,1},{1,0},{2,3},{3,2},{4,5},{5,4},{6,7},{7,6},{8,9},{9,8},{10,11... | collective-permute-start | bytes 393224 | tf_op jit(solution)/shard_map/ppermute | solution.py:439
  82.2 5.0 %collective-permute-start.12 = (bf16[1,128,512]{2,1,0:T(8,128)(2,1)S(1)}, bf16[1,128,512]{2,1,0:T(8,128)(2,1)S(1)}, u32[]{:S(2)}, u32[]{:S(2)}) collective-permute-start(bf16[1,128,512]{2,1,0:T(8,128)(2,1)S(1)} %add_convert_fusion.3), channel_id=1, source_target_pairs={{0,2},{1,3},{2,0},{3,1},{4,6},{5,7},{6,4},{7,5},{8,10},{9,11},{10,... | collective-permute-start | bytes 393224 | tf_op jit(solution)/shard_map/ppermute | solution.py:439

commit v8 on v6

--- a/solution.py
+++ b/solution.py
@@ -13,8 +13,8 @@
 MIB = 1 << 20
 CHUNKS = 4
 PRE_MIB = 6
-BACK_MIB = 10
-OUT_MIB = 4
+BACK_MIB = 6
+OUT_MIB = 5
 
 NT = (((1,), (1,)), ((), ()))
 
@@ -156,17 +156,35 @@
     return pltpu.with_memory_space_constraint(array, pltpu.HBM)
 
 
-def fetches(source, result, sems):
-    return [pltpu.make_async_copy(source.at[e], result.at[e], sems.at[e]) for e in range(source.shape[0])]
-
-
-def load_kernel(count, *refs):
-    sources, (*results, done_ref, sems) = refs[:count], refs[count + 1 :]
-    copies = [
-        pltpu.make_async_copy(source.at[e], result.at[e], sems.at[i, e])
-        for i, (source, result) in enumerate(zip(sources, results))
-        for e in range(source.shape[0])
-    ]
+class Ahead:
+    def __init__(self, array, first, count, first_row=0, rows=None):
+        self.array, self.first, self.count = array, first, count
+        self.first_row, self.rows = first_row, rows or array.shape[1]
+        self.pieces = 4
+
+    def result(self):
+        return pltpu.VMEM((self.count, self.rows, self.array.shape[2]), self.array.dtype)
+
+    def semaphores(self):
+        return pltpu.SemaphoreType.DMA((self.count, self.pieces))
+
+    def copies(self, source, result, sems):
+        size = self.rows // self.pieces
+        return [
+            pltpu.make_async_copy(
+                source.at[self.first + e, pl.ds(self.first_row + c * size, size)],
+                result.at[e, pl.ds(c * size, size)],
+                sems.at[e, c],
+            )
+            for e in range(self.count)
+            for c in range(self.pieces)
+        ]
+
+
+def load_kernel(aheads, *refs):
+    count = len(aheads)
+    sources, results, done_ref, sems = refs[:count], refs[count + 1 : -count - 1], refs[-count - 1], refs[-count:]
+    copies = flat(ahead.copies(*each) for ahead, *each in zip(aheads, sources, results, sems))
     for copy in copies:
         copy.start()
     for copy in copies:
@@ -174,20 +192,20 @@
     done_ref[...] = jnp.zeros_like(done_ref)
 
 
-def load(arrays, after):
-    count = len(arrays)
-    return pl.pallas_call(
-        functools.partial(load_kernel, count),
-        in_specs=[OUTSIDE] * count + [pl.BlockSpec(memory_space=pl.ANY)],
-        out_specs=[pl.BlockSpec(memory_space=pltpu.VMEM)] * (count + 1),
-        out_shape=[pltpu.VMEM(w.shape, w.dtype) for w in arrays]
-        + [jax.ShapeDtypeStruct((8, 128), jnp.float32)],
-        scratch_shapes=[pltpu.SemaphoreType.DMA((count, arrays[0].shape[0]))],
+def load(aheads, after):
+    return pl.pallas_call(
+        functools.partial(load_kernel, aheads),
+        in_specs=[OUTSIDE] * len(aheads) + [ANYWHERE],
+        out_specs=[INSIDE] * (len(aheads) + 1),
+        out_shape=[ahead.result() for ahead in aheads] + [jax.ShapeDtypeStruct((8, 128), jnp.float32)],
+        scratch_shapes=[ahead.semaphores() for ahead in aheads],
         compiler_params=params(1),
         cost_estimate=pl.CostEstimate(
-            flops=0, bytes_accessed=4 * count * arrays[0].size, transcendentals=0
+            flops=0,
+            bytes_accessed=4 * sum(ahead.count * ahead.array[0].size for ahead in aheads),
+            transcendentals=0,
         ),
-    )(*[pltpu.with_memory_space_constraint(w, pltpu.HBM) for w in arrays], after)
+    )(*[hbm(ahead.array) for ahead in aheads], after)
 
 
 def rows_kernel(local, counts, first, pick_ref, *refs):
@@ -205,17 +223,17 @@
     )(pick, *flat(tokens), after)
 
 
-def columns_kernel(local, counts, place_ref, *refs):
+def columns_kernel(local, counts, first, place_ref, *refs):
     token_refs, (_, out_ref) = split(refs, counts)
-    gather_columns(local, place_ref, token_refs, 0, out_ref)
-
-
-def early_columns(local, place, tokens, after):
+    gather_columns(local, place_ref, token_refs, first, out_ref)
+
+
+def slot_columns(local, place, tokens, first, after):
     features = tokens[0][0].shape[1]
     return pl.pallas_call(
-        functools.partial(columns_kernel, local, sizes(tokens)),
+        functools.partial(columns_kernel, local, sizes(tokens), first),
         in_specs=[INSIDE] * (1 + len(flat(tokens))) + [ANYWHERE],
-        out_shape=jax.ShapeDtypeStruct((local, features, 2 * SLOT), jnp.bfloat16),
+        out_shape=jax.ShapeDtypeStruct((local, features, len(tokens) * SLOT), jnp.bfloat16),
         compiler_params=params(4),
     )(place, *flat(tokens), after)
 
@@ -252,101 +270,101 @@
     )(array, after)
 
 
-def pre_kernel(experts, gate_ref, first_ref, rest_ref, wg_ref, wu_ref, _, a_ref, b_ref):
+def pre_kernel(experts, ahead, gate_ref, first_ref, rest_ref, wg_ref, wu_ref, source, _, a_ref, b_ref, result, sems):
     hidden = wg_ref.shape[2]
     cols = hidden // 2
+    copies = ahead.copies(source, result, sems)
+    for copy in copies:
+        copy.start()
     for i, e in enumerate(experts):
         rows = jnp.concatenate([first_ref[e], rest_ref[e]], axis=0)
         gates = gate_ref[e][:1, :]
         for f in range(0, hidden, cols):
             part = slice(f, f + cols)
             gate_pre = dot(rows, wg_ref[e, :, part])
-            up_pre = dot(rows, wu_ref[e, :, part])
+            up_pre = dot(rows, wu_ref[i, :, part])
             sig = jax.nn.sigmoid(gate_pre)
-            a_ref[i, part, :] = ((sig * up_pre * (1.0 + gate_pre * (1.0 - sig))).T * gates).astype(jnp.bfloat16)
-            b_ref[i, part, :] = ((sig * gate_pre).T * gates).astype(jnp.bfloat16)
-
-
-def pre(n, experts, gates, first, rest, wg, wu, after):
+            a_ref[i, part, :] = (sig * up_pre * (1.0 + gate_pre * (1.0 - sig))).T * gates
+            b_ref[i, part, :] = (sig * gate_pre).T * gates
+    for copy in copies:
+        copy.wait()
+
+
+def pre(n, experts, ahead, gates, first, rest, wg, wu, after):
     local, features, hidden = wg.shape
     rows, count = n * SLOT, len(experts)
-    shape = jax.ShapeDtypeStruct((count, hidden, rows), jnp.bfloat16)
-    return pl.pallas_call(
-        functools.partial(pre_kernel, experts),
-        in_specs=[INSIDE] * 5 + [ANYWHERE],
-        out_shape=[shape, shape],
+    shape = jax.ShapeDtypeStruct((count, hidden, rows), jnp.float32)
+    return pl.pallas_call(
+        functools.partial(pre_kernel, experts, ahead),
+        in_specs=[INSIDE] * 5 + [OUTSIDE, ANYWHERE],
+        out_specs=[INSIDE] * 3,
+        out_shape=[shape, shape, ahead.result()],
+        scratch_shapes=[ahead.semaphores()],
         compiler_params=params(PRE_MIB * max(1, n // 4)),
         cost_estimate=pl.CostEstimate(
             flops=4 * count * rows * features * hidden,
             bytes_accessed=4 * count * features * hidden,
             transcendentals=count * rows * hidden,
         ),
-    )(gates, first, rest, vmem(wg), vmem(wu), after)
-
-
-def back_kernel(local, counts, halves, place_ref, first_ref, *refs):
-    token_refs, (wd_ref, *refs) = split(refs, counts)
-    factor_refs, (_, _, hg_ref, hu_ref, gs, weight, sems) = refs[: 2 * halves], refs[2 * halves :]
-    factors = [
-        (a_ref, b_ref, i)
-        for a_ref, b_ref in zip(factor_refs[::2], factor_refs[1::2])
-        for i in range(a_ref.shape[0])
-    ]
+    )(gates, first, rest, vmem(wg), vmem(wu), hbm(ahead.array), after)
+
+
+def back_kernel(experts, ahead, first_ref, rest_ref, wd_ref, a_ref, b_ref, _, source, hg_ref, hu_ref, result, sems):
     hidden = wd_ref.shape[1]
     cols = hidden // 2
-    held = weight.shape[0]
-
-    def fetch(e, i):
-        part = pl.ds(i * cols, cols)
-        slot = e % held
-        return pltpu.make_async_copy(wd_ref.at[e, part], weight.at[slot, part], sems.at[slot, i])
-
-    for e in range(held):
-        for i in range(2):
-            fetch(e, i).start()
-    gather_columns(local, place_ref, token_refs, 1, gs)
-
-    for e, (a_ref, b_ref, at) in enumerate(factors):
-        rows = jnp.concatenate([first_ref[e], gs[e]], axis=1)
-        for i in range(2):
-            part = slice(i * cols, (i + 1) * cols)
-            fetch(e, i).wait()
-            back = dot(weight[e % held, part, :], rows)
-            hg_ref[e, part, :] = (back * a_ref[at, part, :]).astype(jnp.bfloat16)
-            hu_ref[e, part, :] = (back * b_ref[at, part, :]).astype(jnp.bfloat16)
-            if e + held < local:
-                fetch(e + held, i).start()
-
-
-def back(n, place, first, tokens, wd, factors, wg, wu):
-    local, hidden, features = wd.shape
+    copies = ahead.copies(source, result, sems)
+    for copy in copies:
+        copy.start()
+    for i, e in enumerate(experts):
+        columns = jnp.concatenate([first_ref[e], rest_ref[e]], axis=1)
+        for f in range(0, hidden, cols):
+            part = slice(f, f + cols)
+            back = dot(wd_ref[i, part, :], columns)
+            hg_ref[i, part, :] = (back * a_ref[i, part, :]).astype(jnp.bfloat16)
+            hu_ref[i, part, :] = (back * b_ref[i, part, :]).astype(jnp.bfloat16)
+    for copy in copies:
+        copy.wait()
+
+
+def back(n, experts, ahead, first, rest, wd, a, b, wg):
+    count, hidden, features = wd.shape
     rows = n * SLOT
-    shape = jax.ShapeDtypeStruct((local, hidden, rows), jnp.bfloat16)
-    return pl.pallas_call(
-        functools.partial(back_kernel, local, sizes(tokens), len(factors)),
-        in_specs=[INSIDE] * (2 + len(flat(tokens))) + [OUTSIDE] + [INSIDE] * (2 * len(factors) + 2),
-        out_shape=[shape, shape],
-        scratch_shapes=[
-            pltpu.VMEM((local, features, rows - 2 * SLOT), jnp.bfloat16),
-            pltpu.VMEM((min(local, 2), hidden, features), jnp.bfloat16),
-            pltpu.SemaphoreType.DMA((min(local, 2), 2)),
-        ],
+    shape = jax.ShapeDtypeStruct((count, hidden, rows), jnp.bfloat16)
+    return pl.pallas_call(
+        functools.partial(back_kernel, experts, ahead),
+        in_specs=[INSIDE] * 6 + [OUTSIDE],
+        out_specs=[INSIDE] * 3,
+        out_shape=[shape, shape, ahead.result()],
+        scratch_shapes=[ahead.semaphores()],
         compiler_params=params(BACK_MIB * max(1, n // 4)),
         cost_estimate=pl.CostEstimate(
-            flops=2 * local * rows * features * hidden,
-            bytes_accessed=2 * local * features * hidden,
+            flops=2 * count * rows * features * hidden,
+            bytes_accessed=2 * count * features * hidden,
             transcendentals=0,
         ),
-    )(place, first, *flat(tokens), hbm(wd), *flat(factors), vmem(wg), vmem(wu))
-
-
-def out_kernel(n, local, orders, chunk, place_ref, hg_ref, hu_ref, wg_ref, wu_ref, *rest):
-    outs, rows_ref = rest[:-1], rest[-1]
+    )(first, rest, vmem(wd), a, b, vmem(wg), hbm(ahead.array))
+
+
+def out_kernel(n, local, orders, chunk, ahead, parts, place_ref, *refs):
+    h_refs, (wg_ref, wu_ref, *refs) = refs[: 2 * parts], refs[2 * parts :]
+    copies = []
+    if ahead:
+        source, *outs, result, rows_ref, sems = refs
+        copies = ahead.copies(source, result, sems)
+    else:
+        *outs, rows_ref = refs
+    for copy in copies:
+        copy.start()
     wide = 2 * SLOT
-    cols = wg_ref.shape[1] // CHUNKS
+    cols = wu_ref.shape[1]
     part = slice(chunk * cols, (chunk + 1) * cols)
-    for e in range(local):
-        rows = dot(wg_ref[e, part, :], hg_ref[e]) + dot(wu_ref[e, part, :], hu_ref[e])
+    hidden_refs = [
+        (hg_ref.at[i], hu_ref.at[i])
+        for hg_ref, hu_ref in zip(h_refs[::2], h_refs[1::2])
+        for i in range(hg_ref.shape[0])
+    ]
+    for e, (hg_ref, hu_ref) in enumerate(hidden_refs):
+        rows = dot(wg_ref[e, part, :], hg_ref[...]) + dot(wu_ref[e], hu_ref[...])
         rows = rows.astype(jnp.bfloat16)
         for p in range(n // 2):
             rows_ref[p, :, e * wide : (e + 1) * wide] = rows[:, p * wide : (p + 1) * wide]
@@ -358,26 +376,31 @@
                 if g // 2 == p:
                     mine = total[g % 2 * tokens : (g % 2 + 1) * tokens, :]
                     out_ref[i] = mine.astype(out_ref.dtype)
-
-
-def partial_sums(n, orders, chunk, place, hg, hu, wg, wu):
+    for copy in copies:
+        copy.wait()
+
+
+def partial_sums(n, orders, chunk, ahead, place, hidden_grads, wg, wu):
     local, features, hidden = wg.shape
     tokens = place.shape[1] // 2
     rows = n * SLOT
-    cols = features // CHUNKS
+    cols = wu.shape[1]
     shapes = [(len(order), tokens, cols) for order in orders]
     types = [jnp.float32] + [jnp.bfloat16] * (len(orders) - 1)
-    return pl.pallas_call(
-        functools.partial(out_kernel, n, local, orders, chunk),
-        out_shape=[jax.ShapeDtypeStruct(s, t) for s, t in zip(shapes, types)],
-        scratch_shapes=[pltpu.VMEM((n // 2, cols, 2 * SLOT * local), jnp.bfloat16)],
+    more = [ahead] if ahead else []
+    return pl.pallas_call(
+        functools.partial(out_kernel, n, local, orders, chunk, ahead, len(hidden_grads)),
+        in_specs=[INSIDE] * (3 + 2 * len(hidden_grads)) + [OUTSIDE] * len(more),
+        out_specs=[INSIDE] * (len(orders) + len(more)),
+        out_shape=[jax.ShapeDtypeStruct(s, t) for s, t in zip(shapes, types)] + [m.result() for m in more],
+        scratch_shapes=[pltpu.VMEM((n // 2, cols, 2 * SLOT * local), jnp.bfloat16)] + [m.semaphores() for m in more],
         compiler_params=params(OUT_MIB * max(1, n // 4)),
         cost_estimate=pl.CostEstimate(
             flops=local * rows * cols * hidden,
             bytes_accessed=local * cols * hidden,
             transcendentals=0,
         ),
-    )(place, hg, hu, vmem(wg), vmem(wu))
+    )(place, *flat(hidden_grads), vmem(wg), vmem(wu), *[hbm(m.array) for m in more])
 
 
 def sum_kernel(*refs):
@@ -404,7 +427,13 @@
     table = rank_table(routes.T, route_gates.T, experts)
     tables = [table] + [swap(table, k) for k in range(1, n)]
     pick, place, gates = slots(axis, n, local, tables)
-    gate_proj, up_proj, done = load((gate_proj, up_proj), table)
+    half = (local + 1) // 2
+    experts_of = [part for part in (range(half), range(half, local)) if len(part)]
+    cols = features // CHUNKS
+    ups = [Ahead(up_proj, part[0], len(part)) for part in experts_of]
+    downs = [Ahead(down_proj, part[0], len(part)) for part in experts_of]
+    chunks = [Ahead(up_proj, 0, local, c * cols, cols) for c in range(CHUNKS)]
+    gate_proj, near, done = load([Ahead(gate_proj, 0, local), ups[0]], table)
     if n == 4:
         x_near = [swap(saved_input, 1), swap(saved_input, 2)]
         upper, lower = relay_parts(x_near, [done, place])
@@ -416,30 +445,41 @@
         sent = grad_out
     x_first = slot_rows(local, pick, x_blocks[:2], 0, sent)
     x_rest = slot_rows(local, pick, x_blocks[2:], 1, sent)
-    half = (local + 1) // 2
-    factors = [pre(n, range(half), gates, x_first, x_rest, gate_proj, up_proj, table)]
-    if n == 4:
-        upper, lower = relay_parts(g_near, [factors[0][0]])
-        g_blocks = [[sent], *[[g] for g in g_near], [swap(upper, 2), swap(lower, 1)]]
-    else:
-        g_blocks = [[grad_out]] + [[swap(grad_out, k)] for k in range(1, n)]
-        upper = table
-    if half < local:
-        factors.append(pre(n, range(half, local), gates, x_first, x_rest, gate_proj, up_proj, upper))
-    g_first = early_columns(local, place, g_blocks[:2], upper)
-    hg, hu = back(n, place, g_first, g_blocks[2:], down_proj, factors, gate_proj, up_proj)
+    after = table
+    factors = []
+    for i, part in enumerate(experts_of):
+        following = [*ups, downs[0]][i + 1]
+        a, b, near = pre(n, part, following, gates, x_first, x_rest, gate_proj, near, after)
+        factors.append((a, b))
+        if i == 0 and n == 4:
+            after, lower = relay_parts(g_near, [a])
+            g_blocks = [[sent], *[[g] for g in g_near], [swap(after, 2), swap(lower, 1)]]
+        elif i == 0:
+            g_blocks = [[grad_out]] + [[swap(grad_out, k)] for k in range(1, n)]
+    g_first = slot_columns(local, place, g_blocks[:2], 0, after)
+    g_rest = slot_columns(local, place, g_blocks[2:], 1, after)
+    hidden_grads = []
+    for i, (part, (a, b)) in enumerate(zip(experts_of, factors)):
+        following = [*downs, chunks[0]][i + 1]
+        hg, hu, near = back(n, part, following, g_first, g_rest, near, a, b, gate_proj)
+        hidden_grads.append((hg, hu))
     parts = []
     for chunk in range(CHUNKS):
+        following = chunks[chunk + 1] if chunk + 1 < CHUNKS else None
         if n == 4:
             first, last = (1, 2) if chunk % 2 == 0 else (2, 1)
             orders = ((0,), (first, 3), (last,))
-            own, two, one = partial_sums(n, orders, chunk, place, hg, hu, gate_proj, up_proj)
+        else:
+            orders = tuple((k,) for k in range(n))
+        own, *others = partial_sums(n, orders, chunk, following, place, hidden_grads, gate_proj, near)
+        if following:
+            *others, near = others
+        if n == 4:
+            two, one = others
             two = swap(two, first)
             mixed = (two[1:2].astype(jnp.float32) + one.astype(jnp.float32)).astype(jnp.bfloat16)
             parts += [own, two[:1], swap(mixed, last)]
         else:
-            orders = tuple((k,) for k in range(n))
-            own, *others = partial_sums(n, orders, chunk, place, hg, hu, gate_proj, up_proj)
             parts += [own] + [swap(other, k + 1) for k, other in enumerate(others)]
     return pl.pallas_call(
         sum_kernel,

time: 86.5 us -> 85.7 us (level)
  Pallas kernels: 41.5 us -> 49.1 us
  waiting for transfers between devices: 17.3 us -> 11.9 us
  local copies, waits for them, and re-layouts: 5.36 us -> 0.78 us
  starting transfers between devices: 21.7 us -> 23.2 us
    pallas_call x9 -> x11, Pallas kernels: 37 us -> 44.7 us  [the longest x2 15.1 us: pre(): pl.pallas_call(functools.partial(pre_kernel, experts, ahead), in_specs=[I...]
    ppermute x19, waiting for transfers between devices: 17.3 us -> 11.9 us  [swap(): return lax.ppermute(array, axis, [(i, i ^ k) for i in range(n)])]
    unnamed x10 -> x8, local copies, waits for them, and re-layouts: 5.32 us -> 0.74 us
    ppermute x19, starting transfers between devices: 21.7 us -> 23.2 us  [swap(): return lax.ppermute(array, axis, [(i, i ^ k) for i in range(n)])]
  transfers between devices with their start and end apart: 19 -> 19, of which waited for: 10 -> 8; matrix products, arithmetic and copies ran while one was open for 0% -> 0% of each run, Pallas kernels for 33% -> 42%
where the time goes in v8:
time: 85.7 us; the launch traced here: 85.4 us
  Pallas kernels  49.1 us (57%)
  starting transfers between devices  23.2 us (27%)
  waiting for transfers between devices  11.9 us (14%)
    ppermute x19, starting transfers between devices, swap(): return lax.ppermute(array, axis, [(i, i ^ k) for i in range(n)])  23.2 us
    pallas_call x2, Pallas kernels, pre(): pl.pallas_call(functools.partial(pre_kernel, experts, ahead), in_specs=[I...  15.1 us
    pallas_call x4, Pallas kernels, partial_sums(): pl.pallas_call(functools.partial(out_kernel, n, local, orders, chunk, ahe...  13.8 us
    ppermute x19, waiting for transfers between devices, swap(): return lax.ppermute(array, axis, [(i, i ^ k) for i in range(n)])  11.9 us
    pallas_call x2, Pallas kernels, back(): pl.pallas_call(functools.partial(back_kernel, experts, ahead), in_specs=[...  7.74 us
    pallas_call x1, Pallas kernels, load(): pl.pallas_call(functools.partial(load_kernel, aheads), in_specs=[OUTSIDE]...  6.6 us
  transfers between devices with their start and end apart: 19, of which 8 were waited for; matrix products, arithmetic and copies ran while one was open for 0% of the time, Pallas kernels for 42%

profile of v8, /device:TPU:0, one launch (start us, length us, event | category | flops | bytes accessed | tf_op | source)
XLA Modules:
  0.0 85.4 jit_solution(1673755294039959677)
XLA Ops:
  0.0 2.9 %collective-permute-start.3 = (bf16[128,2048]{1,0:T(8,128)(2,1)}, bf16[128,2048]{1,0:T(8,128)(2,1)S(1)}, u32[]{:S(2)}, u32[]{:S(2)}) collective-permute-start(bf16[128,2048]{1,0:T(8,128)(2,1)} %refs_0_.3), channel_id=1, source_target_pairs={{0,1},{1,0},{2,3},{3,2},{4,5},{5,4},{6,7},{7,6},{8,9},{9,8},{10,11... | collective-permute-start | bytes 1572872 | tf_op jit(solution)/shard_map/ppermute | solution.py:425
  2.9 1.5 %collective-permute-start.4 = (bf16[128,2048]{1,0:T(8,128)(2,1)}, bf16[128,2048]{1,0:T(8,128)(2,1)S(1)}, u32[]{:S(2)}, u32[]{:S(2)}) collective-permute-start(bf16[128,2048]{1,0:T(8,128)(2,1)} %refs_0_.3), channel_id=1, source_target_pairs={{0,2},{1,3},{2,0},{3,1},{4,6},{5,7},{6,4},{7,5},{8,10},{9,11},{10,... | collective-permute-start | bytes 1572872 | tf_op jit(solution)/shard_map/ppermute | solution.py:425
  4.5 1.5 %shard_map.73.refs_0_.refs_2_._ = bf16[32,128]{1,0:T(8,128)(2,1)} custom-call(s32[8,128]{1,0:T(8,128)} %bitcast.2, bf16[8,128]{1,0:T(8,128)(2,1)} %bitcast.3), custom_call_target="tpu_custom_call" | custom-call | tf_op jit(solution)/shard_map/pallas_call | solution.py:56
  5.9 0.0 copy-start
  5.9 0.0 collective-permute-start.2
  6.0 2.0 %collective-permute-start.1 = (bf16[32,128]{1,0:T(8,128)(2,1)}, bf16[32,128]{1,0:T(8,128)(2,1)S(1)}, u32[]{:S(2)}, u32[]{:S(2)}) collective-permute-start(bf16[32,128]{1,0:T(8,128)(2,1)} %shard_map.73.refs_0_.refs_2_._), channel_id=1, source_target_pairs={{0,2},{1,3},{2,0},{3,1},{4,6},{5,7},{6,4},{7,5},{8,10},{9,11},{10,... | collective-permute-start | bytes 24584 | tf_op jit(solution)/shard_map/ppermute | solution.py:425
  7.9 1.5 %collective-permute-start = (bf16[32,128]{1,0:T(8,128)(2,1)}, bf16[32,128]{1,0:T(8,128)(2,1)S(1)}, u32[]{:S(2)}, u32[]{:S(2)}) collective-permute-start(bf16[32,128]{1,0:T(8,128)(2,1)} %shard_map.73.refs_0_.refs_2_._), channel_id=1, source_target_pairs={{0,1},{1,0},{2,3},{3,2},{4,5},{5,4},{6,7},{7,6},{8,9},{9,8},{10,11... | collective-permute-start | bytes 24584 | tf_op jit(solution)/shard_map/ppermute | solution.py:425
  9.4 0.0 copy-start.2
  9.4 0.7 copy-done.2
  10.2 0.0 copy-start.3
  10.2 6.6 %shard_map.75 = (bf16[4,2048,768]{2,1,0:T(8,128)(2,1)S(1)}, bf16[2,2048,768]{2,1,0:T(8,128)(2,1)S(1)}, f32[8,128]{1,0:T(8,128)S(1)}) custom-call(bf16[4,2048,768]{2,1,0:T(8,128)(2,1)} %refs_0_.2, bf16[4,2048,768]{2,1,0:T(8,128)(2,1)} %refs_6_.5, bf16[32,128]{1,0:T(8,128)(2,1)S(1)} %copy-done.2), custom_call_target="tpu_custom_call" | custom-call | bytes 37748736 | tf_op jit(solution)/shard_map/pallas_call | solution.py:196
  16.8 0.0 copy-start.1
  16.8 0.0 collective-permute-done.2.refs_3_
  16.8 0.1 collective-permute-done.1.refs_2_
  16.9 0.0 collective-permute-done.refs_1_
  16.9 0.0 copy-done.3
  16.9 0.4 shard_map.74
  17.3 0.0 collective-permute-done.3.x_ref.refs_1_
  17.3 0.0 collective-permute-done.4.y_ref.refs_0_
  17.4 1.2 %collective-permute-start.8 = (bf16[64,2048]{1,0:T(8,128)(2,1)S(1)}, bf16[64,2048]{1,0:T(8,128)(2,1)S(1)}, u32[]{:S(2)}, u32[]{:S(2)}) collective-permute-start(bf16[64,2048]{1,0:T(8,128)(2,1)S(1)} %get-tuple-element.47), channel_id=1, source_target_pairs={{0,1},{1,0},{2,3},{3,2},{4,5},{5,4},{6,7},{7,6},{8,9},{9,8},{10,11... | collective-permute-start | bytes 786440 | tf_op jit(solution)/shard_map/ppermute | solution.py:425
  18.6 0.9 %collective-permute-start.7 = (bf16[64,2048]{1,0:T(8,128)(2,1)S(1)}, bf16[64,2048]{1,0:T(8,128)(2,1)S(1)}, u32[]{:S(2)}, u32[]{:S(2)}) collective-permute-start(bf16[64,2048]{1,0:T(8,128)(2,1)S(1)} %get-tuple-element.44._), channel_id=1, source_target_pairs={{0,2},{1,3},{2,0},{3,1},{4,6},{5,7},{6,4},{7,5},{8,10},{9,11},{10,... | collective-permute-start | bytes 786440 | tf_op jit(solution)/shard_map/ppermute | solution.py:425
  19.5 0.0 copy-done
  19.5 1.2 %collective-permute-start.6 = (bf16[128,2048]{1,0:T(8,128)(2,1)S(1)}, bf16[128,2048]{1,0:T(8,128)(2,1)S(1)}, u32[]{:S(2)}, u32[]{:S(2)}) collective-permute-start(bf16[128,2048]{1,0:T(8,128)(2,1)S(1)} %shard_map.77.refs_2_.refs_3_.refs_0_), channel_id=1, source_target_pairs={{0,2},{1,3},{2,0},{3,1},{4,6},{5,7},{6,4},{7,5},{8,10},{9,11},{10,... | collective-permute-start | bytes 1572872 | tf_op jit(solution)/shard_map/ppermute | solution.py:425
  20.7 0.9 %collective-permute-start.5 = (bf16[128,2048]{1,0:T(8,128)(2,1)S(1)}, bf16[128,2048]{1,0:T(8,128)(2,1)S(1)}, u32[]{:S(2)}, u32[]{:S(2)}) collective-permute-start(bf16[128,2048]{1,0:T(8,128)(2,1)S(1)} %shard_map.77.refs_2_.refs_3_.refs_0_), channel_id=1, source_target_pairs={{0,1},{1,0},{2,3},{3,2},{4,5},{5,4},{6,7},{7,6},{8,9},{9,8},{10,11... | collective-permute-start | bytes 1572872 | tf_op jit(solution)/shard_map/ppermute | solution.py:425
  21.6 0.0 copy-done.1
  21.6 0.7 shard_map.78.first_ref
  22.3 4.4 %collective-permute-done.8.refs_2_ = bf16[64,2048]{1,0:T(8,128)(2,1)S(1)} collective-permute-done((bf16[64,2048]{1,0:T(8,128)(2,1)S(1)}, bf16[64,2048]{1,0:T(8,128)(2,1)S(1)}, u32[]{:S(2)}, u32[]{:S(2)}) %collective-permute-start.8) | collective-permute-done | bytes 262176 | tf_op jit(solution)/shard_map/ppermute | solution.py:425
  26.7 1.2 %collective-permute-done.7.refs_1_ = bf16[64,2048]{1,0:T(8,128)(2,1)S(1)} collective-permute-done((bf16[64,2048]{1,0:T(8,128)(2,1)S(1)}, bf16[64,2048]{1,0:T(8,128)(2,1)S(1)}, u32[]{:S(2)}, u32[]{:S(2)}) %collective-permute-start.7) | collective-permute-done | bytes 262176 | tf_op jit(solution)/shard_map/ppermute | solution.py:425
  27.9 0.7 shard_map.79.rest_ref
  28.6 7.5 %shard_map.80 = (f32[2,768,256]{2,1,0:T(8,128)S(1)}, f32[2,768,256]{2,1,0:T(8,128)S(1)}, bf16[2,2048,768]{2,1,0:T(8,128)(2,1)S(1)}) custom-call(f32[4,8,256]{2,1,0:T(8,128)S(1)} %get-tuple-element.45.gate_ref, bf16[4,128,2048]{2,1,0:T(8,128)(2,1)S(1)} %shard_map.78.first_ref, bf16[4,128,2048]{2,1,0:T(8,128)(2,1)S(1)} %shard_map.79.rest_ref, ...), custom_call_target="tpu_custom_call" | custom-call | flops 3221225472 | bytes 12582912 | tf_op jit(solution)/shard_map/pallas_call | solution.py:297
  36.1 0.3 collective-permute-done.6.y_ref.refs_0_
  36.4 0.0 collective-permute-done.5.x_ref.refs_1_
  36.4 0.9 %collective-permute-start.10 = (bf16[64,2048]{1,0:T(8,128)(2,1)S(1)}, bf16[64,2048]{1,0:T(8,128)(2,1)S(1)}, u32[]{:S(2)}, u32[]{:S(2)}) collective-permute-start(bf16[64,2048]{1,0:T(8,128)(2,1)S(1)} %get-tuple-element.52), channel_id=1, source_target_pairs={{0,1},{1,0},{2,3},{3,2},{4,5},{5,4},{6,7},{7,6},{8,9},{9,8},{10,11... | collective-permute-start | bytes 786440 | tf_op jit(solution)/shard_map/ppermute | solution.py:425
  37.3 1.6 %collective-permute-start.9 = (bf16[64,2048]{1,0:T(8,128)(2,1)S(1)}, bf16[64,2048]{1,0:T(8,128)(2,1)S(1)}, u32[]{:S(2)}, u32[]{:S(2)}) collective-permute-start(bf16[64,2048]{1,0:T(8,128)(2,1)S(1)} %get-tuple-element.51.refs_2_.refs_3_._), channel_id=1, source_target_pairs={{0,2},{1,3},{2,0},{3,1},{4,6},{5,7},{6,4},{7,5},{8,10},{9,11},{10,... | collective-permute-start | bytes 786440 | tf_op jit(solution)/shard_map/ppermute | solution.py:425
  38.9 0.7 shard_map.82.first_ref
  39.7 7.7 %shard_map.84 = (f32[2,768,256]{2,1,0:T(8,128)S(1)}, f32[2,768,256]{2,1,0:T(8,128)S(1)}, bf16[2,768,2048]{2,1,0:T(8,128)(2,1)S(1)}) custom-call(f32[4,8,256]{2,1,0:T(8,128)S(1)} %get-tuple-element.45.gate_ref, bf16[4,128,2048]{2,1,0:T(8,128)(2,1)S(1)} %shard_map.78.first_ref, bf16[4,128,2048]{2,1,0:T(8,128)(2,1)S(1)} %shard_map.79.rest_ref, ...), custom_call_target="tpu_custom_call" | custom-call | flops 3221225472 | bytes 12582912 | tf_op jit(solution)/shard_map/pallas_call | solution.py:297
  47.3 0.0 collective-permute-done.10.refs_2_
  47.4 0.0 collective-permute-done.9.refs_1_
  47.4 0.7 shard_map.83.rest_ref
  48.1 4.2 %shard_map.85 = (bf16[2,768,256]{2,1,0:T(8,128)(2,1)S(1)}, bf16[2,768,256]{2,1,0:T(8,128)(2,1)S(1)}, bf16[2,768,2048]{2,1,0:T(8,128)(2,1)S(1)}) custom-call(bf16[4,2048,128]{2,1,0:T(8,128)(2,1)S(1)} %shard_map.82.first_ref, bf16[4,2048,128]{2,1,0:T(8,128)(2,1)S(1)} %shard_map.83.rest_ref, bf16[2,768,2048]{2,1,0:T(8,128)(2,1)S(1)} %get-tuple-element.54.wd_ref, ...), custom_call_target="tpu_custom_call" | custom-call | flops 1610612736 | bytes 6291456 | tf_op jit(solution)/shard_map/pallas_call | solution.py:333
  52.4 3.5 %shard_map.86 = (bf16[2,768,256]{2,1,0:T(8,128)(2,1)S(1)}, bf16[2,768,256]{2,1,0:T(8,128)(2,1)S(1)}, bf16[4,512,768]{2,1,0:T(8,128)(2,1)S(1)}) custom-call(bf16[4,2048,128]{2,1,0:T(8,128)(2,1)S(1)} %shard_map.82.first_ref, bf16[4,2048,128]{2,1,0:T(8,128)(2,1)S(1)} %shard_map.83.rest_ref, bf16[2,768,2048]{2,1,0:T(8,128)(2,1)S(1)} %get-tuple-element.58.wd_ref, ...), custom_call_target="tpu_custom_call" | custom-call | flops 1610612736 | bytes 6291456 | tf_op jit(solution)/shard_map/pallas_call | solution.py:333
  55.9 3.8 %shard_map.87 = (f32[1,128,512]{2,1,0:T(8,128)S(1)}, bf16[2,128,512]{2,1,0:T(8,128)(2,1)S(1)}, bf16[1,128,512]{2,1,0:T(8,128)(2,1)S(1)}, bf16[4,512,768]{2,1,0:T(8,128)(2,1)S(1)}) custom-call(bf16[2,256,512]{2,1,0:T(8,128)(2,1)S(1)} %get-tuple-element.42.refs_1_.place_ref, bf16[2,768,256]{2,1,0:T(8,128)(2,1)S(1)} %get-tuple-element.56.refs_0_, ...), custom_call_target="tpu_custom_call" | custom-call | flops 402653184 | bytes 1572864 | tf_op jit(solution)/shard_map/pallas_call | solution.py:391
  59.7 0.7 collective-permute-start.11
  60.3 4.0 %shard_map.88 = (f32[1,128,512]{2,1,0:T(8,128)S(1)}, bf16[2,128,512]{2,1,0:T(8,128)(2,1)S(1)}, bf16[1,128,512]{2,1,0:T(8,128)(2,1)S(1)}, bf16[4,512,768]{2,1,0:T(8,128)(2,1)S(1)}) custom-call(bf16[2,256,512]{2,1,0:T(8,128)(2,1)S(1)} %get-tuple-element.42.refs_1_.place_ref, bf16[2,768,256]{2,1,0:T(8,128)(2,1)S(1)} %get-tuple-element.56.refs_0_, ...), custom_call_target="tpu_custom_call" | custom-call | flops 402653184 | bytes 1572864 | tf_op jit(solution)/shard_map/pallas_call | solution.py:391
  64.3 1.1 %collective-permute-start.13 = (bf16[2,128,512]{2,1,0:T(8,128)(2,1)S(1)}, bf16[2,128,512]{2,1,0:T(8,128)(2,1)S(1)}, u32[]{:S(2)}, u32[]{:S(2)}) collective-permute-start(bf16[2,128,512]{2,1,0:T(8,128)(2,1)S(1)} %get-tuple-element.69), channel_id=1, source_target_pairs={{0,2},{1,3},{2,0},{3,1},{4,6},{5,7},{6,4},{7,5},{8,10},{9,11},{10,... | collective-permute-start | bytes 786440 | tf_op jit(solution)/shard_map/ppermute | solution.py:425
  65.4 3.8 %shard_map.89 = (f32[1,128,512]{2,1,0:T(8,128)S(1)}, bf16[2,128,512]{2,1,0:T(8,128)(2,1)S(1)}, bf16[1,128,512]{2,1,0:T(8,128)(2,1)S(1)}, bf16[4,512,768]{2,1,0:T(8,128)(2,1)S(1)}) custom-call(bf16[2,256,512]{2,1,0:T(8,128)(2,1)S(1)} %get-tuple-element.42.refs_1_.place_ref, bf16[2,768,256]{2,1,0:T(8,128)(2,1)S(1)} %get-tuple-element.56.refs_0_, ...), custom_call_target="tpu_custom_call" | custom-call | flops 402653184 | bytes 1572864 | tf_op jit(solution)/shard_map/pallas_call | solution.py:391
  69.2 0.9 %collective-permute-start.15 = (bf16[2,128,512]{2,1,0:T(8,128)(2,1)S(1)}, bf16[2,128,512]{2,1,0:T(8,128)(2,1)S(1)}, u32[]{:S(2)}, u32[]{:S(2)}) collective-permute-start(bf16[2,128,512]{2,1,0:T(8,128)(2,1)S(1)} %get-tuple-element.73), channel_id=1, source_target_pairs={{0,1},{1,0},{2,3},{3,2},{4,5},{5,4},{6,7},{7,6},{8,9},{9,8},{10,11... | collective-permute-start | bytes 786440 | tf_op jit(solution)/shard_map/ppermute | solution.py:425
  70.2 2.1 %shard_map.90 = (f32[1,128,512]{2,1,0:T(8,128)S(1)}, bf16[2,128,512]{2,1,0:T(8,128)(2,1)S(1)}, bf16[1,128,512]{2,1,0:T(8,128)(2,1)S(1)}) custom-call(bf16[2,256,512]{2,1,0:T(8,128)(2,1)S(1)} %get-tuple-element.42.refs_1_.place_ref, bf16[2,768,256]{2,1,0:T(8,128)(2,1)S(1)} %get-tuple-element.56.refs_0_, bf16[2,768,256]{2,1,0:T(8,128)(2,1)S(1)} %get-tuple-element.57.refs_1_, ...), custom_call_target="tpu_custom_call" | custom-call | flops 402653184 | bytes 1572864 | tf_op jit(solution)/shard_map/pallas_call | solution.py:391
  72.3 1.7 %collective-permute-start.17 = (bf16[2,128,512]{2,1,0:T(8,128)(2,1)S(1)}, bf16[2,128,512]{2,1,0:T(8,128)(2,1)S(1)}, u32[]{:S(2)}, u32[]{:S(2)}) collective-permute-start(bf16[2,128,512]{2,1,0:T(8,128)(2,1)S(1)} %get-tuple-element.77), channel_id=1, source_target_pairs={{0,2},{1,3},{2,0},{3,1},{4,6},{5,7},{6,4},{7,5},{8,10},{9,11},{10,... | collective-permute-start | bytes 786440 | tf_op jit(solution)/shard_map/ppermute | solution.py:425
  74.0 0.0 collective-permute-done.11
  74.0 0.5 collective-permute-start.12
  74.5 0.0 collective-permute-done.13
  74.5 1.2 %collective-permute-start.14 = (bf16[1,128,512]{2,1,0:T(8,128)(2,1)S(1)}, bf16[1,128,512]{2,1,0:T(8,128)(2,1)S(1)}, u32[]{:S(2)}, u32[]{:S(2)}) collective-permute-start(bf16[1,128,512]{2,1,0:T(8,128)(2,1)S(1)} %add_convert_fusion.2), channel_id=1, source_target_pairs={{0,1},{1,0},{2,3},{3,2},{4,5},{5,4},{6,7},{7,6},{8,9},{9,8},{10,11... | collective-permute-start | bytes 393224 | tf_op jit(solution)/shard_map/ppermute | solution.py:425
  75.8 1.2 %collective-permute-done.15 = bf16[2,128,512]{2,1,0:T(8,128)(2,1)S(1)} collective-permute-done((bf16[2,128,512]{2,1,0:T(8,128)(2,1)S(1)}, bf16[2,128,512]{2,1,0:T(8,128)(2,1)S(1)}, u32[]{:S(2)}, u32[]{:S(2)}) %collective-permute-start.15) | collective-permute-done | bytes 262176 | tf_op jit(solution)/shard_map/ppermute | solution.py:425
  77.0 1.1 %collective-permute-start.16 = (bf16[1,128,512]{2,1,0:T(8,128)(2,1)S(1)}, bf16[1,128,512]{2,1,0:T(8,128)(2,1)S(1)}, u32[]{:S(2)}, u32[]{:S(2)}) collective-permute-start(bf16[1,128,512]{2,1,0:T(8,128)(2,1)S(1)} %add_convert_fusion.1), channel_id=1, source_target_pairs={{0,2},{1,3},{2,0},{3,1},{4,6},{5,7},{6,4},{7,5},{8,10},{9,11},{10,... | collective-permute-start | bytes 393224 | tf_op jit(solution)/shard_map/ppermute | solution.py:425
  78.2 1.1 %collective-permute-done.17 = bf16[2,128,512]{2,1,0:T(8,128)(2,1)S(1)} collective-permute-done((bf16[2,128,512]{2,1,0:T(8,128)(2,1)S(1)}, bf16[2,128,512]{2,1,0:T(8,128)(2,1)S(1)}, u32[]{:S(2)}, u32[]{:S(2)}) %collective-permute-start.17) | collective-permute-done | bytes 262176 | tf_op jit(solution)/shard_map/ppermute | solution.py:425
  79.4 1.4 %collective-permute-start.18 = (bf16[1,128,512]{2,1,0:T(8,128)(2,1)S(1)}, bf16[1,128,512]{2,1,0:T(8,128)(2,1)S(1)}, u32[]{:S(2)}, u32[]{:S(2)}) collective-permute-start(bf16[1,128,512]{2,1,0:T(8,128)(2,1)S(1)} %add_convert_fusion), channel_id=1, source_target_pairs={{0,1},{1,0},{2,3},{3,2},{4,5},{5,4},{6,7},{7,6},{8,9},{9,8},{10,11... | collective-permute-start | bytes 393224 | tf_op jit(solution)/shard_map/ppermute | solution.py:425
  80.8 0.0 collective-permute-done.12.refs_2_
  80.8 0.0 collective-permute-done.14.refs_5_
  80.8 1.3 %collective-permute-done.16.refs_8_ = bf16[1,128,512]{2,1,0:T(8,128)(2,1)S(1)} collective-permute-done((bf16[1,128,512]{2,1,0:T(8,128)(2,1)S(1)}, bf16[1,128,512]{2,1,0:T(8,128)(2,1)S(1)}, u32[]{:S(2)}, u32[]{:S(2)}) %collective-permute-start.16) | collective-permute-done | bytes 131104 | tf_op jit(solution)/shard_map/ppermute | solution.py:425
  82.2 2.3 %collective-permute-done.18.refs_11_ = bf16[1,128,512]{2,1,0:T(8,128)(2,1)S(1)} collective-permute-done((bf16[1,128,512]{2,1,0:T(8,128)(2,1)S(1)}, bf16[1,128,512]{2,1,0:T(8,128)(2,1)S(1)}, u32[]{:S(2)}, u32[]{:S(2)}) %collective-permute-start.18) | collective-permute-done | bytes 131104 | tf_op jit(solution)/shard_map/ppermute | solution.py:425
  84.4 1.0 %shard_map.91 = bf16[128,2048]{1,0:T(8,128)(2,1)} custom-call(f32[1,128,512]{2,1,0:T(8,128)S(1)} %get-tuple-element.64.refs_0_, bf16[1,128,512]{2,1,0:T(8,128)(2,1)S(1)} %slice.32.refs_1_, bf16[1,128,512]{2,1,0:T(8,128)(2,1)S(1)} %collective-permute-done.12.refs_2_, f32[1,128,512]{2,1,0:T(8,128)S(1)} %get-tuple-element.68.refs_3_, ...), custom_call_target="tpu_custom_call" | custom-call | tf_op jit(solution)/shard_map/pallas_call | solution.py:484
  (11 shorter events, 0.3 us)
Async XLA Ops:
  0.0 17.3 %collective-permute-start.3 = (bf16[128,2048]{1,0:T(8,128)(2,1)}, bf16[128,2048]{1,0:T(8,128)(2,1)S(1)}, u32[]{:S(2)}, u32[]{:S(2)}) collective-permute-start(bf16[128,2048]{1,0:T(8,128)(2,1)} %refs_0_.3), channel_id=1, source_target_pairs={{0,1},{1,0},{2,3},{3,2},{4,5},{5,4},{6,7},{7,6},{8,9},{9,8},{10,11... | collective-permute-start | bytes 1572872 | tf_op jit(solution)/shard_map/ppermute | solution.py:425
  2.9 14.4 %collective-permute-start.4 = (bf16[128,2048]{1,0:T(8,128)(2,1)}, bf16[128,2048]{1,0:T(8,128)(2,1)S(1)}, u32[]{:S(2)}, u32[]{:S(2)}) collective-permute-start(bf16[128,2048]{1,0:T(8,128)(2,1)} %refs_0_.3), channel_id=1, source_target_pairs={{0,2},{1,3},{2,0},{3,1},{4,6},{5,7},{6,4},{7,5},{8,10},{9,11},{10,... | collective-permute-start | bytes 1572872 | tf_op jit(solution)/shard_map/ppermute | solution.py:425
  5.9 13.6 %copy-start = (bf16[128,2048]{1,0:T(8,128)(2,1)S(1)}, bf16[128,2048]{1,0:T(8,128)(2,1)}, u32[]{:S(2)}) copy-start(bf16[128,2048]{1,0:T(8,128)(2,1)} %array_ref.1) | copy-start | bytes 1572868
  5.9 10.8 %collective-permute-start.2 = (bf16[32,128]{1,0:T(8,128)(2,1)}, bf16[32,128]{1,0:T(8,128)(2,1)S(1)}, u32[]{:S(2)}, u32[]{:S(2)}) collective-permute-start(bf16[32,128]{1,0:T(8,128)(2,1)} %shard_map.73.refs_0_.refs_2_._), channel_id=1, source_target_pairs={{0,3},{1,2},{2,1},{3,0},{4,7},{5,6},{6,5},{7,4},{8,11},{9,10},{10,... | collective-permute-start | bytes 24584 | tf_op jit(solution)/shard_map/ppermute | solution.py:425
  6.0 10.9 %collective-permute-start.1 = (bf16[32,128]{1,0:T(8,128)(2,1)}, bf16[32,128]{1,0:T(8,128)(2,1)S(1)}, u32[]{:S(2)}, u32[]{:S(2)}) collective-permute-start(bf16[32,128]{1,0:T(8,128)(2,1)} %shard_map.73.refs_0_.refs_2_._), channel_id=1, source_target_pairs={{0,2},{1,3},{2,0},{3,1},{4,6},{5,7},{6,4},{7,5},{8,10},{9,11},{10,... | collective-permute-start | bytes 24584 | tf_op jit(solution)/shard_map/ppermute | solution.py:425
  7.9 8.9 %collective-permute-start = (bf16[32,128]{1,0:T(8,128)(2,1)}, bf16[32,128]{1,0:T(8,128)(2,1)S(1)}, u32[]{:S(2)}, u32[]{:S(2)}) collective-permute-start(bf16[32,128]{1,0:T(8,128)(2,1)} %shard_map.73.refs_0_.refs_2_._), channel_id=1, source_target_pairs={{0,1},{1,0},{2,3},{3,2},{4,5},{5,4},{6,7},{7,6},{8,9},{9,8},{10,11... | collective-permute-start | bytes 24584 | tf_op jit(solution)/shard_map/ppermute | solution.py:425
  9.4 0.7 copy-start.2
  10.2 6.7 %copy-start.3 = (bf16[32,128]{1,0:T(8,128)(2,1)S(1)}, bf16[32,128]{1,0:T(8,128)(2,1)}, u32[]{:S(2)}) copy-start(bf16[32,128]{1,0:T(8,128)(2,1)} %shard_map.73.refs_0_.refs_2_._) | copy-start | bytes 24580
  16.8 4.8 %copy-start.1 = (bf16[128,2048]{1,0:T(8,128)(2,1)S(1)}, bf16[128,2048]{1,0:T(8,128)(2,1)}, u32[]{:S(2)}) copy-start(bf16[128,2048]{1,0:T(8,128)(2,1)} %refs_0_.3) | copy-start | bytes 1572868
  17.4 9.3 %collective-permute-start.8 = (bf16[64,2048]{1,0:T(8,128)(2,1)S(1)}, bf16[64,2048]{1,0:T(8,128)(2,1)S(1)}, u32[]{:S(2)}, u32[]{:S(2)}) collective-permute-start(bf16[64,2048]{1,0:T(8,128)(2,1)S(1)} %get-tuple-element.47), channel_id=1, source_target_pairs={{0,1},{1,0},{2,3},{3,2},{4,5},{5,4},{6,7},{7,6},{8,9},{9,8},{10,11... | collective-permute-start | bytes 786440 | tf_op jit(solution)/shard_map/ppermute | solution.py:425
  18.6 9.2 %collective-permute-start.7 = (bf16[64,2048]{1,0:T(8,128)(2,1)S(1)}, bf16[64,2048]{1,0:T(8,128)(2,1)S(1)}, u32[]{:S(2)}, u32[]{:S(2)}) collective-permute-start(bf16[64,2048]{1,0:T(8,128)(2,1)S(1)} %get-tuple-element.44._), channel_id=1, source_target_pairs={{0,2},{1,3},{2,0},{3,1},{4,6},{5,7},{6,4},{7,5},{8,10},{9,11},{10,... | collective-permute-start | bytes 786440 | tf_op jit(solution)/shard_map/ppermute | solution.py:425
  19.5 16.8 %collective-permute-start.6 = (bf16[128,2048]{1,0:T(8,128)(2,1)S(1)}, bf16[128,2048]{1,0:T(8,128)(2,1)S(1)}, u32[]{:S(2)}, u32[]{:S(2)}) collective-permute-start(bf16[128,2048]{1,0:T(8,128)(2,1)S(1)} %shard_map.77.refs_2_.refs_3_.refs_0_), channel_id=1, source_target_pairs={{0,2},{1,3},{2,0},{3,1},{4,6},{5,7},{6,4},{7,5},{8,10},{9,11},{10,... | collective-permute-start | bytes 1572872 | tf_op jit(solution)/shard_map/ppermute | solution.py:425
  20.7 15.6 %collective-permute-start.5 = (bf16[128,2048]{1,0:T(8,128)(2,1)S(1)}, bf16[128,2048]{1,0:T(8,128)(2,1)S(1)}, u32[]{:S(2)}, u32[]{:S(2)}) collective-permute-start(bf16[128,2048]{1,0:T(8,128)(2,1)S(1)} %shard_map.77.refs_2_.refs_3_.refs_0_), channel_id=1, source_target_pairs={{0,1},{1,0},{2,3},{3,2},{4,5},{5,4},{6,7},{7,6},{8,9},{9,8},{10,11... | collective-permute-start | bytes 1572872 | tf_op jit(solution)/shard_map/ppermute | solution.py:425
  36.4 10.9 %collective-permute-start.10 = (bf16[64,2048]{1,0:T(8,128)(2,1)S(1)}, bf16[64,2048]{1,0:T(8,128)(2,1)S(1)}, u32[]{:S(2)}, u32[]{:S(2)}) collective-permute-start(bf16[64,2048]{1,0:T(8,128)(2,1)S(1)} %get-tuple-element.52), channel_id=1, source_target_pairs={{0,1},{1,0},{2,3},{3,2},{4,5},{5,4},{6,7},{7,6},{8,9},{9,8},{10,11... | collective-permute-start | bytes 786440 | tf_op jit(solution)/shard_map/ppermute | solution.py:425
  37.3 10.0 %collective-permute-start.9 = (bf16[64,2048]{1,0:T(8,128)(2,1)S(1)}, bf16[64,2048]{1,0:T(8,128)(2,1)S(1)}, u32[]{:S(2)}, u32[]{:S(2)}) collective-permute-start(bf16[64,2048]{1,0:T(8,128)(2,1)S(1)} %get-tuple-element.51.refs_2_.refs_3_._), channel_id=1, source_target_pairs={{0,2},{1,3},{2,0},{3,1},{4,6},{5,7},{6,4},{7,5},{8,10},{9,11},{10,... | collective-permute-start | bytes 786440 | tf_op jit(solution)/shard_map/ppermute | solution.py:425
  59.7 14.3 %collective-permute-start.11 = (bf16[2,128,512]{2,1,0:T(8,128)(2,1)S(1)}, bf16[2,128,512]{2,1,0:T(8,128)(2,1)S(1)}, u32[]{:S(2)}, u32[]{:S(2)}) collective-permute-start(bf16[2,128,512]{2,1,0:T(8,128)(2,1)S(1)} %get-tuple-element.65), channel_id=1, source_target_pairs={{0,1},{1,0},{2,3},{3,2},{4,5},{5,4},{6,7},{7,6},{8,9},{9,8},{10,11... | collective-permute-start | bytes 786440 | tf_op jit(solution)/shard_map/ppermute | solution.py:425
  64.3 10.2 %collective-permute-start.13 = (bf16[2,128,512]{2,1,0:T(8,128)(2,1)S(1)}, bf16[2,128,512]{2,1,0:T(8,128)(2,1)S(1)}, u32[]{:S(2)}, u32[]{:S(2)}) collective-permute-start(bf16[2,128,512]{2,1,0:T(8,128)(2,1)S(1)} %get-tuple-element.69), channel_id=1, source_target_pairs={{0,2},{1,3},{2,0},{3,1},{4,6},{5,7},{6,4},{7,5},{8,10},{9,11},{10,... | collective-permute-start | bytes 786440 | tf_op jit(solution)/shard_map/ppermute | solution.py:425
  69.2 7.8 %collective-permute-start.15 = (bf16[2,128,512]{2,1,0:T(8,128)(2,1)S(1)}, bf16[2,128,512]{2,1,0:T(8,128)(2,1)S(1)}, u32[]{:S(2)}, u32[]{:S(2)}) collective-permute-start(bf16[2,128,512]{2,1,0:T(8,128)(2,1)S(1)} %get-tuple-element.73), channel_id=1, source_target_pairs={{0,1},{1,0},{2,3},{3,2},{4,5},{5,4},{6,7},{7,6},{8,9},{9,8},{10,11... | collective-permute-start | bytes 786440 | tf_op jit(solution)/shard_map/ppermute | solution.py:425
  72.3 7.0 %collective-permute-start.17 = (bf16[2,128,512]{2,1,0:T(8,128)(2,1)S(1)}, bf16[2,128,512]{2,1,0:T(8,128)(2,1)S(1)}, u32[]{:S(2)}, u32[]{:S(2)}) collective-permute-start(bf16[2,128,512]{2,1,0:T(8,128)(2,1)S(1)} %get-tuple-element.77), channel_id=1, source_target_pairs={{0,2},{1,3},{2,0},{3,1},{4,6},{5,7},{6,4},{7,5},{8,10},{9,11},{10,... | collective-permute-start | bytes 786440 | tf_op jit(solution)/shard_map/ppermute | solution.py:425
  74.0 6.8 %collective-permute-start.12 = (bf16[1,128,512]{2,1,0:T(8,128)(2,1)S(1)}, bf16[1,128,512]{2,1,0:T(8,128)(2,1)S(1)}, u32[]{:S(2)}, u32[]{:S(2)}) collective-permute-start(bf16[1,128,512]{2,1,0:T(8,128)(2,1)S(1)} %add_convert_fusion.3), channel_id=1, source_target_pairs={{0,2},{1,3},{2,0},{3,1},{4,6},{5,7},{6,4},{7,5},{8,10},{9,11},{10,... | collective-permute-start | bytes 393224 | tf_op jit(solution)/shard_map/ppermute | solution.py:425
  74.5 6.3 %collective-permute-start.14 = (bf16[1,128,512]{2,1,0:T(8,128)(2,1)S(1)}, bf16[1,128,512]{2,1,0:T(8,128)(2,1)S(1)}, u32[]{:S(2)}, u32[]{:S(2)}) collective-permute-start(bf16[1,128,512]{2,1,0:T(8,128)(2,1)S(1)} %add_convert_fusion.2), channel_id=1, source_target_pairs={{0,1},{1,0},{2,3},{3,2},{4,5},{5,4},{6,7},{7,6},{8,9},{9,8},{10,11... | collective-permute-start | bytes 393224 | tf_op jit(solution)/shard_map/ppermute | solution.py:425
  77.0 5.1 %collective-permute-start.16 = (bf16[1,128,512]{2,1,0:T(8,128)(2,1)S(1)}, bf16[1,128,512]{2,1,0:T(8,128)(2,1)S(1)}, u32[]{:S(2)}, u32[]{:S(2)}) collective-permute-start(bf16[1,128,512]{2,1,0:T(8,128)(2,1)S(1)} %add_convert_fusion.1), channel_id=1, source_target_pairs={{0,2},{1,3},{2,0},{3,1},{4,6},{5,7},{6,4},{7,5},{8,10},{9,11},{10,... | collective-permute-start | bytes 393224 | tf_op jit(solution)/shard_map/ppermute | solution.py:425
  79.4 5.0 %collective-permute-start.18 = (bf16[1,128,512]{2,1,0:T(8,128)(2,1)S(1)}, bf16[1,128,512]{2,1,0:T(8,128)(2,1)S(1)}, u32[]{:S(2)}, u32[]{:S(2)}) collective-permute-start(bf16[1,128,512]{2,1,0:T(8,128)(2,1)S(1)} %add_convert_fusion), channel_id=1, source_target_pairs={{0,1},{1,0},{2,3},{3,2},{4,5},{5,4},{6,7},{7,6},{8,9},{9,8},{10,11... | collective-permute-start | bytes 393224 | tf_op jit(solution)/shard_map/ppermute | solution.py:425

commit v9 on v6

--- a/solution.py
+++ b/solution.py
@@ -12,8 +12,10 @@
 UNUSED = 200.0
 MIB = 1 << 20
 CHUNKS = 4
-PRE_MIB = 6
-BACK_MIB = 10
+RING = 2
+COPIES = 4
+PRE_MIB = 5
+BACK_MIB = 7
 OUT_MIB = 4
 
 NT = (((1,), (1,)), ((), ()))
@@ -263,14 +265,14 @@
             gate_pre = dot(rows, wg_ref[e, :, part])
             up_pre = dot(rows, wu_ref[e, :, part])
             sig = jax.nn.sigmoid(gate_pre)
-            a_ref[i, part, :] = ((sig * up_pre * (1.0 + gate_pre * (1.0 - sig))).T * gates).astype(jnp.bfloat16)
-            b_ref[i, part, :] = ((sig * gate_pre).T * gates).astype(jnp.bfloat16)
+            a_ref[i, part, :] = (sig * up_pre * (1.0 + gate_pre * (1.0 - sig))).T * gates
+            b_ref[i, part, :] = (sig * gate_pre).T * gates
 
 
 def pre(n, experts, gates, first, rest, wg, wu, after):
     local, features, hidden = wg.shape
     rows, count = n * SLOT, len(experts)
-    shape = jax.ShapeDtypeStruct((count, hidden, rows), jnp.bfloat16)
+    shape = jax.ShapeDtypeStruct((count, hidden, rows), jnp.float32)
     return pl.pallas_call(
         functools.partial(pre_kernel, experts),
         in_specs=[INSIDE] * 5 + [ANYWHERE],
@@ -294,28 +296,41 @@
     ]
     hidden = wd_ref.shape[1]
     cols = hidden // 2
-    held = weight.shape[0]
-
-    def fetch(e, i):
-        part = pl.ds(i * cols, cols)
-        slot = e % held
-        return pltpu.make_async_copy(wd_ref.at[e, part], weight.at[slot, part], sems.at[slot, i])
-
-    for e in range(held):
-        for i in range(2):
-            fetch(e, i).start()
+    ring, rows_each = weight.shape[0], cols // COPIES
+    pieces = [(e, i) for e in range(local) for i in range(2)]
+
+    def fetch(piece):
+        e, i = pieces[piece]
+        at = piece % ring
+        return [
+            pltpu.make_async_copy(
+                wd_ref.at[e, pl.ds(i * cols + c * rows_each, rows_each)],
+                weight.at[at, pl.ds(c * rows_each, rows_each)],
+                sems.at[at, c],
+            )
+            for c in range(COPIES)
+        ]
+
+    def start(piece):
+        if piece < len(pieces):
+            for copy in fetch(piece):
+                copy.start()
+
+    for piece in range(ring):
+        start(piece)
     gather_columns(local, place_ref, token_refs, 1, gs)
 
     for e, (a_ref, b_ref, at) in enumerate(factors):
         rows = jnp.concatenate([first_ref[e], gs[e]], axis=1)
         for i in range(2):
             part = slice(i * cols, (i + 1) * cols)
-            fetch(e, i).wait()
-            back = dot(weight[e % held, part, :], rows)
+            piece = 2 * e + i
+            for copy in fetch(piece):
+                copy.wait()
+            back = dot(weight[piece % ring], rows)
             hg_ref[e, part, :] = (back * a_ref[at, part, :]).astype(jnp.bfloat16)
             hu_ref[e, part, :] = (back * b_ref[at, part, :]).astype(jnp.bfloat16)
-            if e + held < local:
-                fetch(e + held, i).start()
+            start(piece + ring)
 
 
 def back(n, place, first, tokens, wd, factors, wg, wu):
@@ -328,8 +343,8 @@
         out_shape=[shape, shape],
         scratch_shapes=[
             pltpu.VMEM((local, features, rows - 2 * SLOT), jnp.bfloat16),
-            pltpu.VMEM((min(local, 2), hidden, features), jnp.bfloat16),
-            pltpu.SemaphoreType.DMA((min(local, 2), 2)),
+            pltpu.VMEM((min(2 * local, RING), hidden // 2, features), jnp.bfloat16),
+            pltpu.SemaphoreType.DMA((min(2 * local, RING), COPIES)),
         ],
         compiler_params=params(BACK_MIB * max(1, n // 4)),
         cost_estimate=pl.CostEstimate(

time: 86.5 us -> 82.9 us (0.958)
  local copies, waits for them, and re-layouts: 5.36 us -> 0.78 us
  Pallas kernels: 41.5 us -> 42.4 us
    unnamed x10 -> x8, local copies, waits for them, and re-layouts: 5.32 us -> 0.74 us
    pallas_call x1, Pallas kernels: 9.77 us -> 10.7 us  [back(): pl.pallas_call(functools.partial(back_kernel, local, sizes(tokens), len(f...]
  transfers between devices with their start and end apart: 19 -> 19, of which waited for: 10 -> 10; matrix products, arithmetic and copies ran while one was open for 0% -> 0% of each run, Pallas kernels for 33% -> 35%
where the time goes in v9:
time: 82.9 us; the launch traced here: 82.5 us
  Pallas kernels  42.4 us (51%)
  starting transfers between devices  21.6 us (26%)
  waiting for transfers between devices  17.4 us (21%)
    ppermute x19, starting transfers between devices, swap(): return lax.ppermute(array, axis, [(i, i ^ k) for i in range(n)])  21.6 us
    ppermute x19, waiting for transfers between devices, swap(): return lax.ppermute(array, axis, [(i, i ^ k) for i in range(n)])  17.4 us
    pallas_call x1, Pallas kernels, back(): pl.pallas_call(functools.partial(back_kernel, local, sizes(tokens), len(f...  10.7 us
    pallas_call x2, Pallas kernels, pre(): pl.pallas_call(functools.partial(pre_kernel, experts), in_specs=[INSIDE]...  9.66 us
    pallas_call x4, Pallas kernels, partial_sums(): pl.pallas_call(functools.partial(out_kernel, n, local, orders, chunk), ou...  8.58 us
    pallas_call x1, Pallas kernels, load(): pl.pallas_call(functools.partial(load_kernel, count), in_specs=[OUTSIDE]...  8.31 us
  transfers between devices with their start and end apart: 19, of which 10 were waited for; matrix products, arithmetic and copies ran while one was open for 0% of the time, Pallas kernels for 35%

profile of v9, /device:TPU:0, one launch (start us, length us, event | category | flops | bytes accessed | tf_op | source)
XLA Modules:
  0.0 82.5 jit_solution(10831707778305766451)
XLA Ops:
  0.0 2.9 %collective-permute-start.3 = (bf16[128,2048]{1,0:T(8,128)(2,1)}, bf16[128,2048]{1,0:T(8,128)(2,1)S(1)}, u32[]{:S(2)}, u32[]{:S(2)}) collective-permute-start(bf16[128,2048]{1,0:T(8,128)(2,1)} %refs_0_.3), channel_id=1, source_target_pairs={{0,1},{1,0},{2,3},{3,2},{4,5},{5,4},{6,7},{7,6},{8,9},{9,8},{10,11... | collective-permute-start | bytes 1572872 | tf_op jit(solution)/shard_map/ppermute | solution.py:417
  2.9 1.5 %collective-permute-start.4 = (bf16[128,2048]{1,0:T(8,128)(2,1)}, bf16[128,2048]{1,0:T(8,128)(2,1)S(1)}, u32[]{:S(2)}, u32[]{:S(2)}) collective-permute-start(bf16[128,2048]{1,0:T(8,128)(2,1)} %refs_0_.3), channel_id=1, source_target_pairs={{0,2},{1,3},{2,0},{3,1},{4,6},{5,7},{6,4},{7,5},{8,10},{9,11},{10,... | collective-permute-start | bytes 1572872 | tf_op jit(solution)/shard_map/ppermute | solution.py:417
  4.5 1.5 %shard_map.73.refs_0_.refs_2_._ = bf16[32,128]{1,0:T(8,128)(2,1)} custom-call(s32[8,128]{1,0:T(8,128)} %bitcast.2, bf16[8,128]{1,0:T(8,128)(2,1)} %bitcast.3), custom_call_target="tpu_custom_call" | custom-call | tf_op jit(solution)/shard_map/pallas_call | solution.py:58
  5.9 0.0 copy-start
  5.9 0.0 collective-permute-start.2
  6.0 2.0 %collective-permute-start.1 = (bf16[32,128]{1,0:T(8,128)(2,1)}, bf16[32,128]{1,0:T(8,128)(2,1)S(1)}, u32[]{:S(2)}, u32[]{:S(2)}) collective-permute-start(bf16[32,128]{1,0:T(8,128)(2,1)} %shard_map.73.refs_0_.refs_2_._), channel_id=1, source_target_pairs={{0,2},{1,3},{2,0},{3,1},{4,6},{5,7},{6,4},{7,5},{8,10},{9,11},{10,... | collective-permute-start | bytes 24584 | tf_op jit(solution)/shard_map/ppermute | solution.py:417
  7.9 1.5 %collective-permute-start = (bf16[32,128]{1,0:T(8,128)(2,1)}, bf16[32,128]{1,0:T(8,128)(2,1)S(1)}, u32[]{:S(2)}, u32[]{:S(2)}) collective-permute-start(bf16[32,128]{1,0:T(8,128)(2,1)} %shard_map.73.refs_0_.refs_2_._), channel_id=1, source_target_pairs={{0,1},{1,0},{2,3},{3,2},{4,5},{5,4},{6,7},{7,6},{8,9},{9,8},{10,11... | collective-permute-start | bytes 24584 | tf_op jit(solution)/shard_map/ppermute | solution.py:417
  9.4 0.0 copy-start.2
  9.4 0.7 copy-done.2
  10.2 0.0 copy-start.3
  10.2 8.3 %shard_map.75 = (bf16[4,2048,768]{2,1,0:T(8,128)(2,1)S(1)}, bf16[4,2048,768]{2,1,0:T(8,128)(2,1)S(1)}, f32[8,128]{1,0:T(8,128)S(1)}) custom-call(bf16[4,2048,768]{2,1,0:T(8,128)(2,1)} %refs_0_.2, bf16[4,2048,768]{2,1,0:T(8,128)(2,1)} %refs_1_.1, bf16[32,128]{1,0:T(8,128)(2,1)S(1)} %copy-done.2), custom_call_target="tpu_custom_call" | custom-call | bytes 50331648 | tf_op jit(solution)/shard_map/pallas_call | solution.py:181
  18.5 0.0 copy-start.1
  18.5 0.0 collective-permute-done.2.refs_3_
  18.5 0.0 collective-permute-done.1.refs_2_
  18.5 0.0 collective-permute-done.refs_1_
  18.5 0.0 copy-done.3
  18.5 0.4 shard_map.74
  19.0 0.0 collective-permute-done.3.x_ref.refs_1_
  19.0 0.0 collective-permute-done.4.y_ref.refs_0_
  19.0 0.6 collective-permute-start.8
  19.6 0.1 collective-permute-start.7
  19.7 0.0 copy-done
  19.7 2.0 %collective-permute-start.6 = (bf16[128,2048]{1,0:T(8,128)(2,1)S(1)}, bf16[128,2048]{1,0:T(8,128)(2,1)S(1)}, u32[]{:S(2)}, u32[]{:S(2)}) collective-permute-start(bf16[128,2048]{1,0:T(8,128)(2,1)S(1)} %shard_map.77.refs_2_.refs_3_.refs_0_), channel_id=1, source_target_pairs={{0,2},{1,3},{2,0},{3,1},{4,6},{5,7},{6,4},{7,5},{8,10},{9,11},{10,... | collective-permute-start | bytes 1572872 | tf_op jit(solution)/shard_map/ppermute | solution.py:417
  21.8 1.5 %collective-permute-start.5 = (bf16[128,2048]{1,0:T(8,128)(2,1)S(1)}, bf16[128,2048]{1,0:T(8,128)(2,1)S(1)}, u32[]{:S(2)}, u32[]{:S(2)}) collective-permute-start(bf16[128,2048]{1,0:T(8,128)(2,1)S(1)} %shard_map.77.refs_2_.refs_3_.refs_0_), channel_id=1, source_target_pairs={{0,1},{1,0},{2,3},{3,2},{4,5},{5,4},{6,7},{7,6},{8,9},{9,8},{10,11... | collective-permute-start | bytes 1572872 | tf_op jit(solution)/shard_map/ppermute | solution.py:417
  23.3 0.0 copy-done.1
  23.3 0.7 shard_map.78.first_ref
  24.0 4.4 %collective-permute-done.8.refs_2_ = bf16[64,2048]{1,0:T(8,128)(2,1)S(1)} collective-permute-done((bf16[64,2048]{1,0:T(8,128)(2,1)S(1)}, bf16[64,2048]{1,0:T(8,128)(2,1)S(1)}, u32[]{:S(2)}, u32[]{:S(2)}) %collective-permute-start.8) | collective-permute-done | bytes 262176 | tf_op jit(solution)/shard_map/ppermute | solution.py:417
  28.4 0.5 collective-permute-done.7.refs_1_
  28.9 0.7 shard_map.79.rest_ref
  29.6 4.7 %shard_map.80 = (f32[2,768,256]{2,1,0:T(8,128)S(1)}, f32[2,768,256]{2,1,0:T(8,128)S(1)}) custom-call(f32[4,8,256]{2,1,0:T(8,128)S(1)} %get-tuple-element.36.gate_ref, bf16[4,128,2048]{2,1,0:T(8,128)(2,1)S(1)} %shard_map.78.first_ref, bf16[4,128,2048]{2,1,0:T(8,128)(2,1)S(1)} %shard_map.79.rest_ref, ...), custom_call_target="tpu_custom_call" | custom-call | flops 3221225472 | bytes 12582912 | tf_op jit(solution)/shard_map/pallas_call | solution.py:276
  34.3 2.9 %collective-permute-done.6.y_ref.refs_0_ = bf16[128,2048]{1,0:T(8,128)(2,1)S(1)} collective-permute-done((bf16[128,2048]{1,0:T(8,128)(2,1)S(1)}, bf16[128,2048]{1,0:T(8,128)(2,1)S(1)}, u32[]{:S(2)}, u32[]{:S(2)}) %collective-permute-start.6) | collective-permute-done | bytes 524320 | tf_op jit(solution)/shard_map/ppermute | solution.py:417
  37.2 0.0 collective-permute-done.5.x_ref.refs_1_
  37.3 1.6 %collective-permute-start.10 = (bf16[64,2048]{1,0:T(8,128)(2,1)S(1)}, bf16[64,2048]{1,0:T(8,128)(2,1)S(1)}, u32[]{:S(2)}, u32[]{:S(2)}) collective-permute-start(bf16[64,2048]{1,0:T(8,128)(2,1)S(1)} %get-tuple-element.43), channel_id=1, source_target_pairs={{0,1},{1,0},{2,3},{3,2},{4,5},{5,4},{6,7},{7,6},{8,9},{9,8},{10,11... | collective-permute-start | bytes 786440 | tf_op jit(solution)/shard_map/ppermute | solution.py:417
  38.8 0.5 collective-permute-start.9
  39.3 0.7 shard_map.82.first_ref
  40.1 4.9 %shard_map.83 = (f32[2,768,256]{2,1,0:T(8,128)S(1)}, f32[2,768,256]{2,1,0:T(8,128)S(1)}) custom-call(f32[4,8,256]{2,1,0:T(8,128)S(1)} %get-tuple-element.36.gate_ref, bf16[4,128,2048]{2,1,0:T(8,128)(2,1)S(1)} %shard_map.78.first_ref, bf16[4,128,2048]{2,1,0:T(8,128)(2,1)S(1)} %shard_map.79.rest_ref, ...), custom_call_target="tpu_custom_call" | custom-call | flops 3221225472 | bytes 12582912 | tf_op jit(solution)/shard_map/pallas_call | solution.py:276
  45.0 0.0 collective-permute-done.10.refs_2_
  45.0 0.2 collective-permute-done.9.refs_1_
  45.2 10.7 %shard_map.84 = (bf16[4,768,256]{2,1,0:T(8,128)(2,1)S(1)}, bf16[4,768,256]{2,1,0:T(8,128)(2,1)S(1)}) custom-call(bf16[2,256,512]{2,1,0:T(8,128)(2,1)S(1)} %get-tuple-element.33.refs_1_.place_ref, bf16[4,2048,128]{2,1,0:T(8,128)(2,1)S(1)} %shard_map.82.first_ref, bf16[128,2048]{1,0:T(8,128)(2,1)S(1)} %collective-permute-done.6.y_ref.refs_0_, ...), custom_call_target="tpu_custom_call" | custom-call | flops 3221225472 | bytes 12582912 | tf_op jit(solution)/shard_map/pallas_call | solution.py:340
  55.9 2.1 %shard_map.88 = (f32[1,128,512]{2,1,0:T(8,128)S(1)}, bf16[2,128,512]{2,1,0:T(8,128)(2,1)S(1)}, bf16[1,128,512]{2,1,0:T(8,128)(2,1)S(1)}) custom-call(bf16[2,256,512]{2,1,0:T(8,128)(2,1)S(1)} %get-tuple-element.33.refs_1_.place_ref, bf16[4,768,256]{2,1,0:T(8,128)(2,1)S(1)} %get-tuple-element.47.hg_ref, bf16[4,768,256]{2,1,0:T(8,128)(2,1)S(1)} %get-tuple-element.48.hu_ref, ...), custom_call_target="tpu_custom_call" | custom-call | flops 402653184 | bytes 1572864 | tf_op jit(solution)/shard_map/pallas_call | solution.py:385
  58.1 1.4 %collective-permute-start.17 = (bf16[2,128,512]{2,1,0:T(8,128)(2,1)S(1)}, bf16[2,128,512]{2,1,0:T(8,128)(2,1)S(1)}, u32[]{:S(2)}, u32[]{:S(2)}) collective-permute-start(bf16[2,128,512]{2,1,0:T(8,128)(2,1)S(1)} %get-tuple-element.59), channel_id=1, source_target_pairs={{0,2},{1,3},{2,0},{3,1},{4,6},{5,7},{6,4},{7,5},{8,10},{9,11},{10,... | collective-permute-start | bytes 786440 | tf_op jit(solution)/shard_map/ppermute | solution.py:417
  59.5 2.1 %shard_map.87 = (f32[1,128,512]{2,1,0:T(8,128)S(1)}, bf16[2,128,512]{2,1,0:T(8,128)(2,1)S(1)}, bf16[1,128,512]{2,1,0:T(8,128)(2,1)S(1)}) custom-call(bf16[2,256,512]{2,1,0:T(8,128)(2,1)S(1)} %get-tuple-element.33.refs_1_.place_ref, bf16[4,768,256]{2,1,0:T(8,128)(2,1)S(1)} %get-tuple-element.47.hg_ref, bf16[4,768,256]{2,1,0:T(8,128)(2,1)S(1)} %get-tuple-element.48.hu_ref, ...), custom_call_target="tpu_custom_call" | custom-call | flops 402653184 | bytes 1572864 | tf_op jit(solution)/shard_map/pallas_call | solution.py:385
  61.6 0.6 collective-permute-start.15
  62.2 2.1 %shard_map.86 = (f32[1,128,512]{2,1,0:T(8,128)S(1)}, bf16[2,128,512]{2,1,0:T(8,128)(2,1)S(1)}, bf16[1,128,512]{2,1,0:T(8,128)(2,1)S(1)}) custom-call(bf16[2,256,512]{2,1,0:T(8,128)(2,1)S(1)} %get-tuple-element.33.refs_1_.place_ref, bf16[4,768,256]{2,1,0:T(8,128)(2,1)S(1)} %get-tuple-element.47.hg_ref, bf16[4,768,256]{2,1,0:T(8,128)(2,1)S(1)} %get-tuple-element.48.hu_ref, ...), custom_call_target="tpu_custom_call" | custom-call | flops 402653184 | bytes 1572864 | tf_op jit(solution)/shard_map/pallas_call | solution.py:385
  64.4 0.7 collective-permute-start.13
  65.1 2.1 %shard_map.85 = (f32[1,128,512]{2,1,0:T(8,128)S(1)}, bf16[2,128,512]{2,1,0:T(8,128)(2,1)S(1)}, bf16[1,128,512]{2,1,0:T(8,128)(2,1)S(1)}) custom-call(bf16[2,256,512]{2,1,0:T(8,128)(2,1)S(1)} %get-tuple-element.33.refs_1_.place_ref, bf16[4,768,256]{2,1,0:T(8,128)(2,1)S(1)} %get-tuple-element.47.hg_ref, bf16[4,768,256]{2,1,0:T(8,128)(2,1)S(1)} %get-tuple-element.48.hu_ref, ...), custom_call_target="tpu_custom_call" | custom-call | flops 402653184 | bytes 1572864 | tf_op jit(solution)/shard_map/pallas_call | solution.py:385
  67.3 1.6 %collective-permute-start.11 = (bf16[2,128,512]{2,1,0:T(8,128)(2,1)S(1)}, bf16[2,128,512]{2,1,0:T(8,128)(2,1)S(1)}, u32[]{:S(2)}, u32[]{:S(2)}) collective-permute-start(bf16[2,128,512]{2,1,0:T(8,128)(2,1)S(1)} %get-tuple-element.50), channel_id=1, source_target_pairs={{0,1},{1,0},{2,3},{3,2},{4,5},{5,4},{6,7},{7,6},{8,9},{9,8},{10,11... | collective-permute-start | bytes 786440 | tf_op jit(solution)/shard_map/ppermute | solution.py:417
  68.8 0.0 collective-permute-done.17
  68.9 0.6 collective-permute-start.18
  69.5 1.1 %collective-permute-done.15 = bf16[2,128,512]{2,1,0:T(8,128)(2,1)S(1)} collective-permute-done((bf16[2,128,512]{2,1,0:T(8,128)(2,1)S(1)}, bf16[2,128,512]{2,1,0:T(8,128)(2,1)S(1)}, u32[]{:S(2)}, u32[]{:S(2)}) %collective-permute-start.15) | collective-permute-done | bytes 262176 | tf_op jit(solution)/shard_map/ppermute | solution.py:417
  70.6 0.3 collective-permute-start.16
  70.9 0.7 collective-permute-done.13
  71.6 1.5 %collective-permute-start.14 = (bf16[1,128,512]{2,1,0:T(8,128)(2,1)S(1)}, bf16[1,128,512]{2,1,0:T(8,128)(2,1)S(1)}, u32[]{:S(2)}, u32[]{:S(2)}) collective-permute-start(bf16[1,128,512]{2,1,0:T(8,128)(2,1)S(1)} %add_convert_fusion.2), channel_id=1, source_target_pairs={{0,1},{1,0},{2,3},{3,2},{4,5},{5,4},{6,7},{7,6},{8,9},{9,8},{10,11... | collective-permute-start | bytes 393224 | tf_op jit(solution)/shard_map/ppermute | solution.py:417
  73.1 3.4 %collective-permute-done.11 = bf16[2,128,512]{2,1,0:T(8,128)(2,1)S(1)} collective-permute-done((bf16[2,128,512]{2,1,0:T(8,128)(2,1)S(1)}, bf16[2,128,512]{2,1,0:T(8,128)(2,1)S(1)}, u32[]{:S(2)}, u32[]{:S(2)}) %collective-permute-start.11) | collective-permute-done | bytes 262176 | tf_op jit(solution)/shard_map/ppermute | solution.py:417
  76.5 0.7 collective-permute-start.12
  77.3 0.6 collective-permute-done.18.refs_11_
  77.9 0.0 collective-permute-done.16.refs_8_
  77.9 1.4 %collective-permute-done.14.refs_5_ = bf16[1,128,512]{2,1,0:T(8,128)(2,1)S(1)} collective-permute-done((bf16[1,128,512]{2,1,0:T(8,128)(2,1)S(1)}, bf16[1,128,512]{2,1,0:T(8,128)(2,1)S(1)}, u32[]{:S(2)}, u32[]{:S(2)}) %collective-permute-start.14) | collective-permute-done | bytes 131104 | tf_op jit(solution)/shard_map/ppermute | solution.py:417
  79.3 2.3 %collective-permute-done.12.refs_2_ = bf16[1,128,512]{2,1,0:T(8,128)(2,1)S(1)} collective-permute-done((bf16[1,128,512]{2,1,0:T(8,128)(2,1)S(1)}, bf16[1,128,512]{2,1,0:T(8,128)(2,1)S(1)}, u32[]{:S(2)}, u32[]{:S(2)}) %collective-permute-start.12) | collective-permute-done | bytes 131104 | tf_op jit(solution)/shard_map/ppermute | solution.py:417
  81.6 1.0 %shard_map.89 = bf16[128,2048]{1,0:T(8,128)(2,1)} custom-call(f32[1,128,512]{2,1,0:T(8,128)S(1)} %get-tuple-element.49.refs_0_, bf16[1,128,512]{2,1,0:T(8,128)(2,1)S(1)} %slice.32.refs_1_, bf16[1,128,512]{2,1,0:T(8,128)(2,1)S(1)} %collective-permute-done.12.refs_2_, f32[1,128,512]{2,1,0:T(8,128)S(1)} %get-tuple-element.52.refs_3_, ...), custom_call_target="tpu_custom_call" | custom-call | tf_op jit(solution)/shard_map/pallas_call | solution.py:459
  (11 shorter events, 0.3 us)
Async XLA Ops:
  0.0 19.0 %collective-permute-start.3 = (bf16[128,2048]{1,0:T(8,128)(2,1)}, bf16[128,2048]{1,0:T(8,128)(2,1)S(1)}, u32[]{:S(2)}, u32[]{:S(2)}) collective-permute-start(bf16[128,2048]{1,0:T(8,128)(2,1)} %refs_0_.3), channel_id=1, source_target_pairs={{0,1},{1,0},{2,3},{3,2},{4,5},{5,4},{6,7},{7,6},{8,9},{9,8},{10,11... | collective-permute-start | bytes 1572872 | tf_op jit(solution)/shard_map/ppermute | solution.py:417
  2.9 16.1 %collective-permute-start.4 = (bf16[128,2048]{1,0:T(8,128)(2,1)}, bf16[128,2048]{1,0:T(8,128)(2,1)S(1)}, u32[]{:S(2)}, u32[]{:S(2)}) collective-permute-start(bf16[128,2048]{1,0:T(8,128)(2,1)} %refs_0_.3), channel_id=1, source_target_pairs={{0,2},{1,3},{2,0},{3,1},{4,6},{5,7},{6,4},{7,5},{8,10},{9,11},{10,... | collective-permute-start | bytes 1572872 | tf_op jit(solution)/shard_map/ppermute | solution.py:417
  5.9 13.7 %copy-start = (bf16[128,2048]{1,0:T(8,128)(2,1)S(1)}, bf16[128,2048]{1,0:T(8,128)(2,1)}, u32[]{:S(2)}) copy-start(bf16[128,2048]{1,0:T(8,128)(2,1)} %array_ref.1) | copy-start | bytes 1572868
  5.9 12.6 %collective-permute-start.2 = (bf16[32,128]{1,0:T(8,128)(2,1)}, bf16[32,128]{1,0:T(8,128)(2,1)S(1)}, u32[]{:S(2)}, u32[]{:S(2)}) collective-permute-start(bf16[32,128]{1,0:T(8,128)(2,1)} %shard_map.73.refs_0_.refs_2_._), channel_id=1, source_target_pairs={{0,3},{1,2},{2,1},{3,0},{4,7},{5,6},{6,5},{7,4},{8,11},{9,10},{10,... | collective-permute-start | bytes 24584 | tf_op jit(solution)/shard_map/ppermute | solution.py:417
  6.0 12.6 %collective-permute-start.1 = (bf16[32,128]{1,0:T(8,128)(2,1)}, bf16[32,128]{1,0:T(8,128)(2,1)S(1)}, u32[]{:S(2)}, u32[]{:S(2)}) collective-permute-start(bf16[32,128]{1,0:T(8,128)(2,1)} %shard_map.73.refs_0_.refs_2_._), channel_id=1, source_target_pairs={{0,2},{1,3},{2,0},{3,1},{4,6},{5,7},{6,4},{7,5},{8,10},{9,11},{10,... | collective-permute-start | bytes 24584 | tf_op jit(solution)/shard_map/ppermute | solution.py:417
  7.9 10.6 %collective-permute-start = (bf16[32,128]{1,0:T(8,128)(2,1)}, bf16[32,128]{1,0:T(8,128)(2,1)S(1)}, u32[]{:S(2)}, u32[]{:S(2)}) collective-permute-start(bf16[32,128]{1,0:T(8,128)(2,1)} %shard_map.73.refs_0_.refs_2_._), channel_id=1, source_target_pairs={{0,1},{1,0},{2,3},{3,2},{4,5},{5,4},{6,7},{7,6},{8,9},{9,8},{10,11... | collective-permute-start | bytes 24584 | tf_op jit(solution)/shard_map/ppermute | solution.py:417
  9.4 0.7 copy-start.2
  10.2 8.4 %copy-start.3 = (bf16[32,128]{1,0:T(8,128)(2,1)S(1)}, bf16[32,128]{1,0:T(8,128)(2,1)}, u32[]{:S(2)}) copy-start(bf16[32,128]{1,0:T(8,128)(2,1)} %shard_map.73.refs_0_.refs_2_._) | copy-start | bytes 24580
  18.5 4.8 %copy-start.1 = (bf16[128,2048]{1,0:T(8,128)(2,1)S(1)}, bf16[128,2048]{1,0:T(8,128)(2,1)}, u32[]{:S(2)}) copy-start(bf16[128,2048]{1,0:T(8,128)(2,1)} %refs_0_.3) | copy-start | bytes 1572868
  19.0 9.3 %collective-permute-start.8 = (bf16[64,2048]{1,0:T(8,128)(2,1)S(1)}, bf16[64,2048]{1,0:T(8,128)(2,1)S(1)}, u32[]{:S(2)}, u32[]{:S(2)}) collective-permute-start(bf16[64,2048]{1,0:T(8,128)(2,1)S(1)} %get-tuple-element.38), channel_id=1, source_target_pairs={{0,1},{1,0},{2,3},{3,2},{4,5},{5,4},{6,7},{7,6},{8,9},{9,8},{10,11... | collective-permute-start | bytes 786440 | tf_op jit(solution)/shard_map/ppermute | solution.py:417
  19.6 9.2 %collective-permute-start.7 = (bf16[64,2048]{1,0:T(8,128)(2,1)S(1)}, bf16[64,2048]{1,0:T(8,128)(2,1)S(1)}, u32[]{:S(2)}, u32[]{:S(2)}) collective-permute-start(bf16[64,2048]{1,0:T(8,128)(2,1)S(1)} %get-tuple-element.35._), channel_id=1, source_target_pairs={{0,2},{1,3},{2,0},{3,1},{4,6},{5,7},{6,4},{7,5},{8,10},{9,11},{10,... | collective-permute-start | bytes 786440 | tf_op jit(solution)/shard_map/ppermute | solution.py:417
  19.7 17.5 %collective-permute-start.6 = (bf16[128,2048]{1,0:T(8,128)(2,1)S(1)}, bf16[128,2048]{1,0:T(8,128)(2,1)S(1)}, u32[]{:S(2)}, u32[]{:S(2)}) collective-permute-start(bf16[128,2048]{1,0:T(8,128)(2,1)S(1)} %shard_map.77.refs_2_.refs_3_.refs_0_), channel_id=1, source_target_pairs={{0,2},{1,3},{2,0},{3,1},{4,6},{5,7},{6,4},{7,5},{8,10},{9,11},{10,... | collective-permute-start | bytes 1572872 | tf_op jit(solution)/shard_map/ppermute | solution.py:417
  21.8 15.5 %collective-permute-start.5 = (bf16[128,2048]{1,0:T(8,128)(2,1)S(1)}, bf16[128,2048]{1,0:T(8,128)(2,1)S(1)}, u32[]{:S(2)}, u32[]{:S(2)}) collective-permute-start(bf16[128,2048]{1,0:T(8,128)(2,1)S(1)} %shard_map.77.refs_2_.refs_3_.refs_0_), channel_id=1, source_target_pairs={{0,1},{1,0},{2,3},{3,2},{4,5},{5,4},{6,7},{7,6},{8,9},{9,8},{10,11... | collective-permute-start | bytes 1572872 | tf_op jit(solution)/shard_map/ppermute | solution.py:417
  37.3 7.8 %collective-permute-start.10 = (bf16[64,2048]{1,0:T(8,128)(2,1)S(1)}, bf16[64,2048]{1,0:T(8,128)(2,1)S(1)}, u32[]{:S(2)}, u32[]{:S(2)}) collective-permute-start(bf16[64,2048]{1,0:T(8,128)(2,1)S(1)} %get-tuple-element.43), channel_id=1, source_target_pairs={{0,1},{1,0},{2,3},{3,2},{4,5},{5,4},{6,7},{7,6},{8,9},{9,8},{10,11... | collective-permute-start | bytes 786440 | tf_op jit(solution)/shard_map/ppermute | solution.py:417
  38.8 6.4 %collective-permute-start.9 = (bf16[64,2048]{1,0:T(8,128)(2,1)S(1)}, bf16[64,2048]{1,0:T(8,128)(2,1)S(1)}, u32[]{:S(2)}, u32[]{:S(2)}) collective-permute-start(bf16[64,2048]{1,0:T(8,128)(2,1)S(1)} %get-tuple-element.42.refs_2_._), channel_id=1, source_target_pairs={{0,2},{1,3},{2,0},{3,1},{4,6},{5,7},{6,4},{7,5},{8,10},{9,11},{10,... | collective-permute-start | bytes 786440 | tf_op jit(solution)/shard_map/ppermute | solution.py:417
  58.1 10.8 %collective-permute-start.17 = (bf16[2,128,512]{2,1,0:T(8,128)(2,1)S(1)}, bf16[2,128,512]{2,1,0:T(8,128)(2,1)S(1)}, u32[]{:S(2)}, u32[]{:S(2)}) collective-permute-start(bf16[2,128,512]{2,1,0:T(8,128)(2,1)S(1)} %get-tuple-element.59), channel_id=1, source_target_pairs={{0,2},{1,3},{2,0},{3,1},{4,6},{5,7},{6,4},{7,5},{8,10},{9,11},{10,... | collective-permute-start | bytes 786440 | tf_op jit(solution)/shard_map/ppermute | solution.py:417
  61.6 8.9 %collective-permute-start.15 = (bf16[2,128,512]{2,1,0:T(8,128)(2,1)S(1)}, bf16[2,128,512]{2,1,0:T(8,128)(2,1)S(1)}, u32[]{:S(2)}, u32[]{:S(2)}) collective-permute-start(bf16[2,128,512]{2,1,0:T(8,128)(2,1)S(1)} %get-tuple-element.56), channel_id=1, source_target_pairs={{0,1},{1,0},{2,3},{3,2},{4,5},{5,4},{6,7},{7,6},{8,9},{9,8},{10,11... | collective-permute-start | bytes 786440 | tf_op jit(solution)/shard_map/ppermute | solution.py:417
  64.4 7.2 %collective-permute-start.13 = (bf16[2,128,512]{2,1,0:T(8,128)(2,1)S(1)}, bf16[2,128,512]{2,1,0:T(8,128)(2,1)S(1)}, u32[]{:S(2)}, u32[]{:S(2)}) collective-permute-start(bf16[2,128,512]{2,1,0:T(8,128)(2,1)S(1)} %get-tuple-element.53), channel_id=1, source_target_pairs={{0,2},{1,3},{2,0},{3,1},{4,6},{5,7},{6,4},{7,5},{8,10},{9,11},{10,... | collective-permute-start | bytes 786440 | tf_op jit(solution)/shard_map/ppermute | solution.py:417
  67.3 9.2 %collective-permute-start.11 = (bf16[2,128,512]{2,1,0:T(8,128)(2,1)S(1)}, bf16[2,128,512]{2,1,0:T(8,128)(2,1)S(1)}, u32[]{:S(2)}, u32[]{:S(2)}) collective-permute-start(bf16[2,128,512]{2,1,0:T(8,128)(2,1)S(1)} %get-tuple-element.50), channel_id=1, source_target_pairs={{0,1},{1,0},{2,3},{3,2},{4,5},{5,4},{6,7},{7,6},{8,9},{9,8},{10,11... | collective-permute-start | bytes 786440 | tf_op jit(solution)/shard_map/ppermute | solution.py:417
  68.9 9.0 %collective-permute-start.18 = (bf16[1,128,512]{2,1,0:T(8,128)(2,1)S(1)}, bf16[1,128,512]{2,1,0:T(8,128)(2,1)S(1)}, u32[]{:S(2)}, u32[]{:S(2)}) collective-permute-start(bf16[1,128,512]{2,1,0:T(8,128)(2,1)S(1)} %add_convert_fusion), channel_id=1, source_target_pairs={{0,1},{1,0},{2,3},{3,2},{4,5},{5,4},{6,7},{7,6},{8,9},{9,8},{10,11... | collective-permute-start | bytes 393224 | tf_op jit(solution)/shard_map/ppermute | solution.py:417
  70.6 7.3 %collective-permute-start.16 = (bf16[1,128,512]{2,1,0:T(8,128)(2,1)S(1)}, bf16[1,128,512]{2,1,0:T(8,128)(2,1)S(1)}, u32[]{:S(2)}, u32[]{:S(2)}) collective-permute-start(bf16[1,128,512]{2,1,0:T(8,128)(2,1)S(1)} %add_convert_fusion.1), channel_id=1, source_target_pairs={{0,2},{1,3},{2,0},{3,1},{4,6},{5,7},{6,4},{7,5},{8,10},{9,11},{10,... | collective-permute-start | bytes 393224 | tf_op jit(solution)/shard_map/ppermute | solution.py:417
  71.6 7.7 %collective-permute-start.14 = (bf16[1,128,512]{2,1,0:T(8,128)(2,1)S(1)}, bf16[1,128,512]{2,1,0:T(8,128)(2,1)S(1)}, u32[]{:S(2)}, u32[]{:S(2)}) collective-permute-start(bf16[1,128,512]{2,1,0:T(8,128)(2,1)S(1)} %add_convert_fusion.2), channel_id=1, source_target_pairs={{0,1},{1,0},{2,3},{3,2},{4,5},{5,4},{6,7},{7,6},{8,9},{9,8},{10,11... | collective-permute-start | bytes 393224 | tf_op jit(solution)/shard_map/ppermute | solution.py:417
  76.5 5.0 %collective-permute-start.12 = (bf16[1,128,512]{2,1,0:T(8,128)(2,1)S(1)}, bf16[1,128,512]{2,1,0:T(8,128)(2,1)S(1)}, u32[]{:S(2)}, u32[]{:S(2)}) collective-permute-start(bf16[1,128,512]{2,1,0:T(8,128)(2,1)S(1)} %add_convert_fusion.3), channel_id=1, source_target_pairs={{0,2},{1,3},{2,0},{3,1},{4,6},{5,7},{6,4},{7,5},{8,10},{9,11},{10,... | collective-permute-start | bytes 393224 | tf_op jit(solution)/shard_map/ppermute | solution.py:417

commit v10 on v9

--- a/solution.py
+++ b/solution.py
@@ -12,6 +12,7 @@
 UNUSED = 200.0
 MIB = 1 << 20
 CHUNKS = 4
+DIRECT = (0, 1)
 RING = 2
 COPIES = 4
 PRE_MIB = 5
@@ -395,12 +396,11 @@
     )(place, hg, hu, vmem(wg), vmem(wu))
 
 
-def sum_kernel(*refs):
-    parts, out_ref = refs[:-1], refs[-1]
-    each = len(parts) // CHUNKS
+def sum_kernel(counts, *refs):
+    parts, _ = split(refs, counts)
+    out_ref = refs[-1]
     cols = out_ref.shape[1] // CHUNKS
-    for c in range(CHUNKS):
-        own, *others = parts[c * each : (c + 1) * each]
+    for c, (own, *others) in enumerate(parts):
         total = own[0]
         for other in others:
             total += other[0].astype(jnp.float32)
@@ -445,22 +445,22 @@
     hg, hu = back(n, place, g_first, g_blocks[2:], down_proj, factors, gate_proj, up_proj)
     parts = []
     for chunk in range(CHUNKS):
-        if n == 4:
+        if n == 4 and chunk not in DIRECT:
             first, last = (1, 2) if chunk % 2 == 0 else (2, 1)
             orders = ((0,), (first, 3), (last,))
             own, two, one = partial_sums(n, orders, chunk, place, hg, hu, gate_proj, up_proj)
             two = swap(two, first)
             mixed = (two[1:2].astype(jnp.float32) + one.astype(jnp.float32)).astype(jnp.bfloat16)
-            parts += [own, two[:1], swap(mixed, last)]
+            parts.append([own, two[:1], swap(mixed, last)])
         else:
             orders = tuple((k,) for k in range(n))
             own, *others = partial_sums(n, orders, chunk, place, hg, hu, gate_proj, up_proj)
-            parts += [own] + [swap(other, k + 1) for k, other in enumerate(others)]
-    return pl.pallas_call(
-        sum_kernel,
+            parts.append([own] + [swap(other, k + 1) for k, other in enumerate(others)])
+    return pl.pallas_call(
+        functools.partial(sum_kernel, sizes(parts)),
         out_shape=jax.ShapeDtypeStruct((tokens, features), jnp.bfloat16),
         compiler_params=params(8),
-    )(*parts)
+    )(*flat(parts))
 
 
 def solution(mesh):

time: 82.9 us -> 85.2 us (1.028)
  starting transfers between devices: 21.6 us -> 25.5 us
  waiting for transfers between devices: 17.4 us -> 15.9 us
    ppermute x19 -> x21, starting transfers between devices: 21.6 us -> 25.5 us  [swap(): return lax.ppermute(array, axis, [(i, i ^ k) for i in range(n)])]
    ppermute x19 -> x21, waiting for transfers between devices: 17.4 us -> 15.9 us  [swap(): return lax.ppermute(array, axis, [(i, i ^ k) for i in range(n)])]
  transfers between devices with their start and end apart: 19 -> 21, of which waited for: 10 -> 9; matrix products, arithmetic and copies ran while one was open for 0% -> 0% of each run, Pallas kernels for 35% -> 34%
where the time goes in v10:
time: 85.2 us; the launch traced here: 84.9 us
  Pallas kernels  42.4 us (50%)
  starting transfers between devices  25.5 us (30%)
  waiting for transfers between devices  15.9 us (19%)
    ppermute x21, starting transfers between devices, swap(): return lax.ppermute(array, axis, [(i, i ^ k) for i in range(n)])  25.5 us
    ppermute x21, waiting for transfers between devices, swap(): return lax.ppermute(array, axis, [(i, i ^ k) for i in range(n)])  15.9 us
    pallas_call x1, Pallas kernels, back(): pl.pallas_call(functools.partial(back_kernel, local, sizes(tokens), len(f...  10.7 us
    pallas_call x2, Pallas kernels, pre(): pl.pallas_call(functools.partial(pre_kernel, experts), in_specs=[INSIDE]...  9.66 us
    pallas_call x4, Pallas kernels, partial_sums(): pl.pallas_call(functools.partial(out_kernel, n, local, orders, chunk), ou...  8.58 us
    pallas_call x1, Pallas kernels, load(): pl.pallas_call(functools.partial(load_kernel, count), in_specs=[OUTSIDE]...  8.31 us
  transfers between devices with their start and end apart: 21, of which 9 were waited for; matrix products, arithmetic and copies ran while one was open for 0% of the time, Pallas kernels for 34%

profile of v10, /device:TPU:0, one launch (start us, length us, event | category | flops | bytes accessed | tf_op | source)
XLA Modules:
  0.0 84.9 jit_solution(12358254249836075046)
XLA Ops:
  0.0 2.9 %collective-permute-start.3 = (bf16[128,2048]{1,0:T(8,128)(2,1)}, bf16[128,2048]{1,0:T(8,128)(2,1)S(1)}, u32[]{:S(2)}, u32[]{:S(2)}) collective-permute-start(bf16[128,2048]{1,0:T(8,128)(2,1)} %refs_0_.3), channel_id=1, source_target_pairs={{0,1},{1,0},{2,3},{3,2},{4,5},{5,4},{6,7},{7,6},{8,9},{9,8},{10,11... | collective-permute-start | bytes 1572872 | tf_op jit(solution)/shard_map/ppermute | solution.py:417
  2.9 1.5 %collective-permute-start.4 = (bf16[128,2048]{1,0:T(8,128)(2,1)}, bf16[128,2048]{1,0:T(8,128)(2,1)S(1)}, u32[]{:S(2)}, u32[]{:S(2)}) collective-permute-start(bf16[128,2048]{1,0:T(8,128)(2,1)} %refs_0_.3), channel_id=1, source_target_pairs={{0,2},{1,3},{2,0},{3,1},{4,6},{5,7},{6,4},{7,5},{8,10},{9,11},{10,... | collective-permute-start | bytes 1572872 | tf_op jit(solution)/shard_map/ppermute | solution.py:417
  4.5 1.5 %shard_map.73.refs_0_.refs_2_._ = bf16[32,128]{1,0:T(8,128)(2,1)} custom-call(s32[8,128]{1,0:T(8,128)} %bitcast.2, bf16[8,128]{1,0:T(8,128)(2,1)} %bitcast.3), custom_call_target="tpu_custom_call" | custom-call | tf_op jit(solution)/shard_map/pallas_call | solution.py:59
  5.9 0.0 copy-start
  5.9 0.0 collective-permute-start.2
  6.0 2.0 %collective-permute-start.1 = (bf16[32,128]{1,0:T(8,128)(2,1)}, bf16[32,128]{1,0:T(8,128)(2,1)S(1)}, u32[]{:S(2)}, u32[]{:S(2)}) collective-permute-start(bf16[32,128]{1,0:T(8,128)(2,1)} %shard_map.73.refs_0_.refs_2_._), channel_id=1, source_target_pairs={{0,2},{1,3},{2,0},{3,1},{4,6},{5,7},{6,4},{7,5},{8,10},{9,11},{10,... | collective-permute-start | bytes 24584 | tf_op jit(solution)/shard_map/ppermute | solution.py:417
  7.9 1.5 %collective-permute-start = (bf16[32,128]{1,0:T(8,128)(2,1)}, bf16[32,128]{1,0:T(8,128)(2,1)S(1)}, u32[]{:S(2)}, u32[]{:S(2)}) collective-permute-start(bf16[32,128]{1,0:T(8,128)(2,1)} %shard_map.73.refs_0_.refs_2_._), channel_id=1, source_target_pairs={{0,1},{1,0},{2,3},{3,2},{4,5},{5,4},{6,7},{7,6},{8,9},{9,8},{10,11... | collective-permute-start | bytes 24584 | tf_op jit(solution)/shard_map/ppermute | solution.py:417
  9.4 0.0 copy-start.2
  9.4 0.7 copy-done.2
  10.2 0.0 copy-start.3
  10.2 8.3 %shard_map.75 = (bf16[4,2048,768]{2,1,0:T(8,128)(2,1)S(1)}, bf16[4,2048,768]{2,1,0:T(8,128)(2,1)S(1)}, f32[8,128]{1,0:T(8,128)S(1)}) custom-call(bf16[4,2048,768]{2,1,0:T(8,128)(2,1)} %refs_0_.2, bf16[4,2048,768]{2,1,0:T(8,128)(2,1)} %refs_1_.1, bf16[32,128]{1,0:T(8,128)(2,1)S(1)} %copy-done.2), custom_call_target="tpu_custom_call" | custom-call | bytes 50331648 | tf_op jit(solution)/shard_map/pallas_call | solution.py:182
  18.5 0.0 copy-start.1
  18.5 0.0 collective-permute-done.2.refs_3_
  18.5 0.0 collective-permute-done.1.refs_2_
  18.5 0.0 collective-permute-done.refs_1_
  18.5 0.0 copy-done.3
  18.5 0.4 shard_map.74
  19.0 0.0 collective-permute-done.3.x_ref.refs_1_
  19.0 0.0 collective-permute-done.4.y_ref.refs_0_
  19.0 0.6 collective-permute-start.8
  19.6 0.1 collective-permute-start.7
  19.7 0.0 copy-done
  19.7 2.0 %collective-permute-start.6 = (bf16[128,2048]{1,0:T(8,128)(2,1)S(1)}, bf16[128,2048]{1,0:T(8,128)(2,1)S(1)}, u32[]{:S(2)}, u32[]{:S(2)}) collective-permute-start(bf16[128,2048]{1,0:T(8,128)(2,1)S(1)} %shard_map.77.refs_2_.refs_3_.refs_0_), channel_id=1, source_target_pairs={{0,2},{1,3},{2,0},{3,1},{4,6},{5,7},{6,4},{7,5},{8,10},{9,11},{10,... | collective-permute-start | bytes 1572872 | tf_op jit(solution)/shard_map/ppermute | solution.py:417
  21.8 1.5 %collective-permute-start.5 = (bf16[128,2048]{1,0:T(8,128)(2,1)S(1)}, bf16[128,2048]{1,0:T(8,128)(2,1)S(1)}, u32[]{:S(2)}, u32[]{:S(2)}) collective-permute-start(bf16[128,2048]{1,0:T(8,128)(2,1)S(1)} %shard_map.77.refs_2_.refs_3_.refs_0_), channel_id=1, source_target_pairs={{0,1},{1,0},{2,3},{3,2},{4,5},{5,4},{6,7},{7,6},{8,9},{9,8},{10,11... | collective-permute-start | bytes 1572872 | tf_op jit(solution)/shard_map/ppermute | solution.py:417
  23.3 0.0 copy-done.1
  23.3 0.7 shard_map.78.first_ref
  24.0 4.4 %collective-permute-done.8.refs_2_ = bf16[64,2048]{1,0:T(8,128)(2,1)S(1)} collective-permute-done((bf16[64,2048]{1,0:T(8,128)(2,1)S(1)}, bf16[64,2048]{1,0:T(8,128)(2,1)S(1)}, u32[]{:S(2)}, u32[]{:S(2)}) %collective-permute-start.8) | collective-permute-done | bytes 262176 | tf_op jit(solution)/shard_map/ppermute | solution.py:417
  28.4 0.5 collective-permute-done.7.refs_1_
  28.9 0.7 shard_map.79.rest_ref
  29.6 4.7 %shard_map.80 = (f32[2,768,256]{2,1,0:T(8,128)S(1)}, f32[2,768,256]{2,1,0:T(8,128)S(1)}) custom-call(f32[4,8,256]{2,1,0:T(8,128)S(1)} %get-tuple-element.38.gate_ref, bf16[4,128,2048]{2,1,0:T(8,128)(2,1)S(1)} %shard_map.78.first_ref, bf16[4,128,2048]{2,1,0:T(8,128)(2,1)S(1)} %shard_map.79.rest_ref, ...), custom_call_target="tpu_custom_call" | custom-call | flops 3221225472 | bytes 12582912 | tf_op jit(solution)/shard_map/pallas_call | solution.py:277
  34.3 2.9 %collective-permute-done.6.y_ref.refs_0_ = bf16[128,2048]{1,0:T(8,128)(2,1)S(1)} collective-permute-done((bf16[128,2048]{1,0:T(8,128)(2,1)S(1)}, bf16[128,2048]{1,0:T(8,128)(2,1)S(1)}, u32[]{:S(2)}, u32[]{:S(2)}) %collective-permute-start.6) | collective-permute-done | bytes 524320 | tf_op jit(solution)/shard_map/ppermute | solution.py:417
  37.2 0.0 collective-permute-done.5.x_ref.refs_1_
  37.3 1.6 %collective-permute-start.10 = (bf16[64,2048]{1,0:T(8,128)(2,1)S(1)}, bf16[64,2048]{1,0:T(8,128)(2,1)S(1)}, u32[]{:S(2)}, u32[]{:S(2)}) collective-permute-start(bf16[64,2048]{1,0:T(8,128)(2,1)S(1)} %get-tuple-element.45), channel_id=1, source_target_pairs={{0,1},{1,0},{2,3},{3,2},{4,5},{5,4},{6,7},{7,6},{8,9},{9,8},{10,11... | collective-permute-start | bytes 786440 | tf_op jit(solution)/shard_map/ppermute | solution.py:417
  38.8 0.5 collective-permute-start.9
  39.3 0.7 shard_map.82.first_ref
  40.1 4.9 %shard_map.83 = (f32[2,768,256]{2,1,0:T(8,128)S(1)}, f32[2,768,256]{2,1,0:T(8,128)S(1)}) custom-call(f32[4,8,256]{2,1,0:T(8,128)S(1)} %get-tuple-element.38.gate_ref, bf16[4,128,2048]{2,1,0:T(8,128)(2,1)S(1)} %shard_map.78.first_ref, bf16[4,128,2048]{2,1,0:T(8,128)(2,1)S(1)} %shard_map.79.rest_ref, ...), custom_call_target="tpu_custom_call" | custom-call | flops 3221225472 | bytes 12582912 | tf_op jit(solution)/shard_map/pallas_call | solution.py:277
  45.0 0.0 collective-permute-done.10.refs_2_
  45.0 0.2 collective-permute-done.9.refs_1_
  45.2 10.7 %shard_map.84 = (bf16[4,768,256]{2,1,0:T(8,128)(2,1)S(1)}, bf16[4,768,256]{2,1,0:T(8,128)(2,1)S(1)}) custom-call(bf16[2,256,512]{2,1,0:T(8,128)(2,1)S(1)} %get-tuple-element.35.refs_1_.place_ref, bf16[4,2048,128]{2,1,0:T(8,128)(2,1)S(1)} %shard_map.82.first_ref, bf16[128,2048]{1,0:T(8,128)(2,1)S(1)} %collective-permute-done.6.y_ref.refs_0_, ...), custom_call_target="tpu_custom_call" | custom-call | flops 3221225472 | bytes 12582912 | tf_op jit(solution)/shard_map/pallas_call | solution.py:341
  55.9 2.1 %shard_map.88 = (f32[1,128,512]{2,1,0:T(8,128)S(1)}, bf16[2,128,512]{2,1,0:T(8,128)(2,1)S(1)}, bf16[1,128,512]{2,1,0:T(8,128)(2,1)S(1)}) custom-call(bf16[2,256,512]{2,1,0:T(8,128)(2,1)S(1)} %get-tuple-element.35.refs_1_.place_ref, bf16[4,768,256]{2,1,0:T(8,128)(2,1)S(1)} %get-tuple-element.49.hg_ref, bf16[4,768,256]{2,1,0:T(8,128)(2,1)S(1)} %get-tuple-element.50.hu_ref, ...), custom_call_target="tpu_custom_call" | custom-call | flops 402653184 | bytes 1572864 | tf_op jit(solution)/shard_map/pallas_call | solution.py:386
  58.1 1.4 %collective-permute-start.19 = (bf16[2,128,512]{2,1,0:T(8,128)(2,1)S(1)}, bf16[2,128,512]{2,1,0:T(8,128)(2,1)S(1)}, u32[]{:S(2)}, u32[]{:S(2)}) collective-permute-start(bf16[2,128,512]{2,1,0:T(8,128)(2,1)S(1)} %get-tuple-element.63), channel_id=1, source_target_pairs={{0,2},{1,3},{2,0},{3,1},{4,6},{5,7},{6,4},{7,5},{8,10},{9,11},{10,... | collective-permute-start | bytes 786440 | tf_op jit(solution)/shard_map/ppermute | solution.py:417
  59.5 2.1 %shard_map.86 = (f32[1,128,512]{2,1,0:T(8,128)S(1)}, bf16[1,128,512]{2,1,0:T(8,128)(2,1)S(1)}, bf16[1,128,512]{2,1,0:T(8,128)(2,1)S(1)}, bf16[1,128,512]{2,1,0:T(8,128)(2,1)S(1)}) custom-call(bf16[2,256,512]{2,1,0:T(8,128)(2,1)S(1)} %get-tuple-element.35.refs_1_.place_ref, bf16[4,768,256]{2,1,0:T(8,128)(2,1)S(1)} %get-tuple-element.49.hg_ref, ...), custom_call_target="tpu_custom_call" | custom-call | flops 402653184 | bytes 1572864 | tf_op jit(solution)/shard_map/pallas_call | solution.py:386
  61.6 0.6 collective-permute-start.14
  62.2 0.7 collective-permute-start.15
  62.9 2.3 %collective-permute-start.16 = (bf16[1,128,512]{2,1,0:T(8,128)(2,1)S(1)}, bf16[1,128,512]{2,1,0:T(8,128)(2,1)S(1)}, u32[]{:S(2)}, u32[]{:S(2)}) collective-permute-start(bf16[1,128,512]{2,1,0:T(8,128)(2,1)S(1)} %get-tuple-element.58), channel_id=1, source_target_pairs={{0,3},{1,2},{2,1},{3,0},{4,7},{5,6},{6,5},{7,4},{8,11},{9,10},{10,... | collective-permute-start | bytes 393224 | tf_op jit(solution)/shard_map/ppermute | solution.py:417
  65.2 2.1 %shard_map.87 = (f32[1,128,512]{2,1,0:T(8,128)S(1)}, bf16[2,128,512]{2,1,0:T(8,128)(2,1)S(1)}, bf16[1,128,512]{2,1,0:T(8,128)(2,1)S(1)}) custom-call(bf16[2,256,512]{2,1,0:T(8,128)(2,1)S(1)} %get-tuple-element.35.refs_1_.place_ref, bf16[4,768,256]{2,1,0:T(8,128)(2,1)S(1)} %get-tuple-element.49.hg_ref, bf16[4,768,256]{2,1,0:T(8,128)(2,1)S(1)} %get-tuple-element.50.hu_ref, ...), custom_call_target="tpu_custom_call" | custom-call | flops 402653184 | bytes 1572864 | tf_op jit(solution)/shard_map/pallas_call | solution.py:386
  67.3 0.6 collective-permute-start.17
  67.9 2.1 %shard_map.85 = (f32[1,128,512]{2,1,0:T(8,128)S(1)}, bf16[1,128,512]{2,1,0:T(8,128)(2,1)S(1)}, bf16[1,128,512]{2,1,0:T(8,128)(2,1)S(1)}, bf16[1,128,512]{2,1,0:T(8,128)(2,1)S(1)}) custom-call(bf16[2,256,512]{2,1,0:T(8,128)(2,1)S(1)} %get-tuple-element.35.refs_1_.place_ref, bf16[4,768,256]{2,1,0:T(8,128)(2,1)S(1)} %get-tuple-element.49.hg_ref, ...), custom_call_target="tpu_custom_call" | custom-call | flops 402653184 | bytes 1572864 | tf_op jit(solution)/shard_map/pallas_call | solution.py:386
  70.1 0.0 collective-permute-done.19
  70.1 1.6 %collective-permute-start.11 = (bf16[1,128,512]{2,1,0:T(8,128)(2,1)S(1)}, bf16[1,128,512]{2,1,0:T(8,128)(2,1)S(1)}, u32[]{:S(2)}, u32[]{:S(2)}) collective-permute-start(bf16[1,128,512]{2,1,0:T(8,128)(2,1)S(1)} %get-tuple-element.52), channel_id=1, source_target_pairs={{0,1},{1,0},{2,3},{3,2},{4,5},{5,4},{6,7},{7,6},{8,9},{9,8},{10,11... | collective-permute-start | bytes 393224 | tf_op jit(solution)/shard_map/ppermute | solution.py:417
  71.7 3.6 %collective-permute-done.17 = bf16[2,128,512]{2,1,0:T(8,128)(2,1)S(1)} collective-permute-done((bf16[2,128,512]{2,1,0:T(8,128)(2,1)S(1)}, bf16[2,128,512]{2,1,0:T(8,128)(2,1)S(1)}, u32[]{:S(2)}, u32[]{:S(2)}) %collective-permute-start.17) | collective-permute-done | bytes 262176 | tf_op jit(solution)/shard_map/ppermute | solution.py:417
  75.3 0.6 collective-permute-start.12
  75.9 0.0 collective-permute-done.14.refs_5_
  75.9 1.6 %collective-permute-start.13 = (bf16[1,128,512]{2,1,0:T(8,128)(2,1)S(1)}, bf16[1,128,512]{2,1,0:T(8,128)(2,1)S(1)}, u32[]{:S(2)}, u32[]{:S(2)}) collective-permute-start(bf16[1,128,512]{2,1,0:T(8,128)(2,1)S(1)} %get-tuple-element.54), channel_id=1, source_target_pairs={{0,3},{1,2},{2,1},{3,0},{4,7},{5,6},{6,5},{7,4},{8,11},{9,10},{10,... | collective-permute-start | bytes 393224 | tf_op jit(solution)/shard_map/ppermute | solution.py:417
  77.6 0.0 collective-permute-done.15.refs_6_
  77.6 1.3 %collective-permute-start.20 = (bf16[1,128,512]{2,1,0:T(8,128)(2,1)S(1)}, bf16[1,128,512]{2,1,0:T(8,128)(2,1)S(1)}, u32[]{:S(2)}, u32[]{:S(2)}) collective-permute-start(bf16[1,128,512]{2,1,0:T(8,128)(2,1)S(1)} %add_convert_fusion), channel_id=1, source_target_pairs={{0,1},{1,0},{2,3},{3,2},{4,5},{5,4},{6,7},{7,6},{8,9},{9,8},{10,11... | collective-permute-start | bytes 393224 | tf_op jit(solution)/shard_map/ppermute | solution.py:417
  78.9 0.0 collective-permute-done.16.refs_7_
  78.9 0.6 collective-permute-start.18
  79.5 0.0 collective-permute-done.11.refs_1_
  79.5 0.7 collective-permute-done.12.refs_2_
  80.2 1.6 %collective-permute-done.13.refs_3_ = bf16[1,128,512]{2,1,0:T(8,128)(2,1)S(1)} collective-permute-done((bf16[1,128,512]{2,1,0:T(8,128)(2,1)S(1)}, bf16[1,128,512]{2,1,0:T(8,128)(2,1)S(1)}, u32[]{:S(2)}, u32[]{:S(2)}) %collective-permute-start.13) | collective-permute-done | bytes 131104 | tf_op jit(solution)/shard_map/ppermute | solution.py:417
  81.9 1.3 %collective-permute-done.20.refs_13_ = bf16[1,128,512]{2,1,0:T(8,128)(2,1)S(1)} collective-permute-done((bf16[1,128,512]{2,1,0:T(8,128)(2,1)S(1)}, bf16[1,128,512]{2,1,0:T(8,128)(2,1)S(1)}, u32[]{:S(2)}, u32[]{:S(2)}) %collective-permute-start.20) | collective-permute-done | bytes 131104 | tf_op jit(solution)/shard_map/ppermute | solution.py:417
  83.2 0.6 collective-permute-done.18.refs_10_
  83.8 1.0 %shard_map.89 = bf16[128,2048]{1,0:T(8,128)(2,1)} custom-call(f32[1,128,512]{2,1,0:T(8,128)S(1)} %get-tuple-element.51.refs_0_, bf16[1,128,512]{2,1,0:T(8,128)(2,1)S(1)} %collective-permute-done.11.refs_1_, bf16[1,128,512]{2,1,0:T(8,128)(2,1)S(1)} %collective-permute-done.12.refs_2_, bf16[1,128,512]{2,1,0:T(8,128)(2,1)S(1)} %collective-permute-done.13.refs_3_, ...), custom_call_target="tpu_custom_call" | custom-call | tf_op jit(solution)/shard_map/pallas_call | solution.py:459
  (7 shorter events, 0.2 us)
Async XLA Ops:
  0.0 19.0 %collective-permute-start.3 = (bf16[128,2048]{1,0:T(8,128)(2,1)}, bf16[128,2048]{1,0:T(8,128)(2,1)S(1)}, u32[]{:S(2)}, u32[]{:S(2)}) collective-permute-start(bf16[128,2048]{1,0:T(8,128)(2,1)} %refs_0_.3), channel_id=1, source_target_pairs={{0,1},{1,0},{2,3},{3,2},{4,5},{5,4},{6,7},{7,6},{8,9},{9,8},{10,11... | collective-permute-start | bytes 1572872 | tf_op jit(solution)/shard_map/ppermute | solution.py:417
  2.9 16.1 %collective-permute-start.4 = (bf16[128,2048]{1,0:T(8,128)(2,1)}, bf16[128,2048]{1,0:T(8,128)(2,1)S(1)}, u32[]{:S(2)}, u32[]{:S(2)}) collective-permute-start(bf16[128,2048]{1,0:T(8,128)(2,1)} %refs_0_.3), channel_id=1, source_target_pairs={{0,2},{1,3},{2,0},{3,1},{4,6},{5,7},{6,4},{7,5},{8,10},{9,11},{10,... | collective-permute-start | bytes 1572872 | tf_op jit(solution)/shard_map/ppermute | solution.py:417
  5.9 13.7 %copy-start = (bf16[128,2048]{1,0:T(8,128)(2,1)S(1)}, bf16[128,2048]{1,0:T(8,128)(2,1)}, u32[]{:S(2)}) copy-start(bf16[128,2048]{1,0:T(8,128)(2,1)} %array_ref.1) | copy-start | bytes 1572868
  5.9 12.6 %collective-permute-start.2 = (bf16[32,128]{1,0:T(8,128)(2,1)}, bf16[32,128]{1,0:T(8,128)(2,1)S(1)}, u32[]{:S(2)}, u32[]{:S(2)}) collective-permute-start(bf16[32,128]{1,0:T(8,128)(2,1)} %shard_map.73.refs_0_.refs_2_._), channel_id=1, source_target_pairs={{0,3},{1,2},{2,1},{3,0},{4,7},{5,6},{6,5},{7,4},{8,11},{9,10},{10,... | collective-permute-start | bytes 24584 | tf_op jit(solution)/shard_map/ppermute | solution.py:417
  6.0 12.6 %collective-permute-start.1 = (bf16[32,128]{1,0:T(8,128)(2,1)}, bf16[32,128]{1,0:T(8,128)(2,1)S(1)}, u32[]{:S(2)}, u32[]{:S(2)}) collective-permute-start(bf16[32,128]{1,0:T(8,128)(2,1)} %shard_map.73.refs_0_.refs_2_._), channel_id=1, source_target_pairs={{0,2},{1,3},{2,0},{3,1},{4,6},{5,7},{6,4},{7,5},{8,10},{9,11},{10,... | collective-permute-start | bytes 24584 | tf_op jit(solution)/shard_map/ppermute | solution.py:417
  7.9 10.6 %collective-permute-start = (bf16[32,128]{1,0:T(8,128)(2,1)}, bf16[32,128]{1,0:T(8,128)(2,1)S(1)}, u32[]{:S(2)}, u32[]{:S(2)}) collective-permute-start(bf16[32,128]{1,0:T(8,128)(2,1)} %shard_map.73.refs_0_.refs_2_._), channel_id=1, source_target_pairs={{0,1},{1,0},{2,3},{3,2},{4,5},{5,4},{6,7},{7,6},{8,9},{9,8},{10,11... | collective-permute-start | bytes 24584 | tf_op jit(solution)/shard_map/ppermute | solution.py:417
  9.4 0.7 copy-start.2
  10.2 8.4 %copy-start.3 = (bf16[32,128]{1,0:T(8,128)(2,1)S(1)}, bf16[32,128]{1,0:T(8,128)(2,1)}, u32[]{:S(2)}) copy-start(bf16[32,128]{1,0:T(8,128)(2,1)} %shard_map.73.refs_0_.refs_2_._) | copy-start | bytes 24580
  18.5 4.8 %copy-start.1 = (bf16[128,2048]{1,0:T(8,128)(2,1)S(1)}, bf16[128,2048]{1,0:T(8,128)(2,1)}, u32[]{:S(2)}) copy-start(bf16[128,2048]{1,0:T(8,128)(2,1)} %refs_0_.3) | copy-start | bytes 1572868
  19.0 9.3 %collective-permute-start.8 = (bf16[64,2048]{1,0:T(8,128)(2,1)S(1)}, bf16[64,2048]{1,0:T(8,128)(2,1)S(1)}, u32[]{:S(2)}, u32[]{:S(2)}) collective-permute-start(bf16[64,2048]{1,0:T(8,128)(2,1)S(1)} %get-tuple-element.40), channel_id=1, source_target_pairs={{0,1},{1,0},{2,3},{3,2},{4,5},{5,4},{6,7},{7,6},{8,9},{9,8},{10,11... | collective-permute-start | bytes 786440 | tf_op jit(solution)/shard_map/ppermute | solution.py:417
  19.6 9.2 %collective-permute-start.7 = (bf16[64,2048]{1,0:T(8,128)(2,1)S(1)}, bf16[64,2048]{1,0:T(8,128)(2,1)S(1)}, u32[]{:S(2)}, u32[]{:S(2)}) collective-permute-start(bf16[64,2048]{1,0:T(8,128)(2,1)S(1)} %get-tuple-element.37._), channel_id=1, source_target_pairs={{0,2},{1,3},{2,0},{3,1},{4,6},{5,7},{6,4},{7,5},{8,10},{9,11},{10,... | collective-permute-start | bytes 786440 | tf_op jit(solution)/shard_map/ppermute | solution.py:417
  19.7 17.5 %collective-permute-start.6 = (bf16[128,2048]{1,0:T(8,128)(2,1)S(1)}, bf16[128,2048]{1,0:T(8,128)(2,1)S(1)}, u32[]{:S(2)}, u32[]{:S(2)}) collective-permute-start(bf16[128,2048]{1,0:T(8,128)(2,1)S(1)} %shard_map.77.refs_2_.refs_3_.refs_0_), channel_id=1, source_target_pairs={{0,2},{1,3},{2,0},{3,1},{4,6},{5,7},{6,4},{7,5},{8,10},{9,11},{10,... | collective-permute-start | bytes 1572872 | tf_op jit(solution)/shard_map/ppermute | solution.py:417
  21.8 15.5 %collective-permute-start.5 = (bf16[128,2048]{1,0:T(8,128)(2,1)S(1)}, bf16[128,2048]{1,0:T(8,128)(2,1)S(1)}, u32[]{:S(2)}, u32[]{:S(2)}) collective-permute-start(bf16[128,2048]{1,0:T(8,128)(2,1)S(1)} %shard_map.77.refs_2_.refs_3_.refs_0_), channel_id=1, source_target_pairs={{0,1},{1,0},{2,3},{3,2},{4,5},{5,4},{6,7},{7,6},{8,9},{9,8},{10,11... | collective-permute-start | bytes 1572872 | tf_op jit(solution)/shard_map/ppermute | solution.py:417
  37.3 7.8 %collective-permute-start.10 = (bf16[64,2048]{1,0:T(8,128)(2,1)S(1)}, bf16[64,2048]{1,0:T(8,128)(2,1)S(1)}, u32[]{:S(2)}, u32[]{:S(2)}) collective-permute-start(bf16[64,2048]{1,0:T(8,128)(2,1)S(1)} %get-tuple-element.45), channel_id=1, source_target_pairs={{0,1},{1,0},{2,3},{3,2},{4,5},{5,4},{6,7},{7,6},{8,9},{9,8},{10,11... | collective-permute-start | bytes 786440 | tf_op jit(solution)/shard_map/ppermute | solution.py:417
  38.8 6.4 %collective-permute-start.9 = (bf16[64,2048]{1,0:T(8,128)(2,1)S(1)}, bf16[64,2048]{1,0:T(8,128)(2,1)S(1)}, u32[]{:S(2)}, u32[]{:S(2)}) collective-permute-start(bf16[64,2048]{1,0:T(8,128)(2,1)S(1)} %get-tuple-element.44.refs_2_._), channel_id=1, source_target_pairs={{0,2},{1,3},{2,0},{3,1},{4,6},{5,7},{6,4},{7,5},{8,10},{9,11},{10,... | collective-permute-start | bytes 786440 | tf_op jit(solution)/shard_map/ppermute | solution.py:417
  58.1 12.0 %collective-permute-start.19 = (bf16[2,128,512]{2,1,0:T(8,128)(2,1)S(1)}, bf16[2,128,512]{2,1,0:T(8,128)(2,1)S(1)}, u32[]{:S(2)}, u32[]{:S(2)}) collective-permute-start(bf16[2,128,512]{2,1,0:T(8,128)(2,1)S(1)} %get-tuple-element.63), channel_id=1, source_target_pairs={{0,2},{1,3},{2,0},{3,1},{4,6},{5,7},{6,4},{7,5},{8,10},{9,11},{10,... | collective-permute-start | bytes 786440 | tf_op jit(solution)/shard_map/ppermute | solution.py:417
  61.6 14.3 %collective-permute-start.14 = (bf16[1,128,512]{2,1,0:T(8,128)(2,1)S(1)}, bf16[1,128,512]{2,1,0:T(8,128)(2,1)S(1)}, u32[]{:S(2)}, u32[]{:S(2)}) collective-permute-start(bf16[1,128,512]{2,1,0:T(8,128)(2,1)S(1)} %get-tuple-element.56), channel_id=1, source_target_pairs={{0,1},{1,0},{2,3},{3,2},{4,5},{5,4},{6,7},{7,6},{8,9},{9,8},{10,11... | collective-permute-start | bytes 393224 | tf_op jit(solution)/shard_map/ppermute | solution.py:417
  62.2 15.3 %collective-permute-start.15 = (bf16[1,128,512]{2,1,0:T(8,128)(2,1)S(1)}, bf16[1,128,512]{2,1,0:T(8,128)(2,1)S(1)}, u32[]{:S(2)}, u32[]{:S(2)}) collective-permute-start(bf16[1,128,512]{2,1,0:T(8,128)(2,1)S(1)} %get-tuple-element.57), channel_id=1, source_target_pairs={{0,2},{1,3},{2,0},{3,1},{4,6},{5,7},{6,4},{7,5},{8,10},{9,11},{10,... | collective-permute-start | bytes 393224 | tf_op jit(solution)/shard_map/ppermute | solution.py:417
  62.9 16.0 %collective-permute-start.16 = (bf16[1,128,512]{2,1,0:T(8,128)(2,1)S(1)}, bf16[1,128,512]{2,1,0:T(8,128)(2,1)S(1)}, u32[]{:S(2)}, u32[]{:S(2)}) collective-permute-start(bf16[1,128,512]{2,1,0:T(8,128)(2,1)S(1)} %get-tuple-element.58), channel_id=1, source_target_pairs={{0,3},{1,2},{2,1},{3,0},{4,7},{5,6},{6,5},{7,4},{8,11},{9,10},{10,... | collective-permute-start | bytes 393224 | tf_op jit(solution)/shard_map/ppermute | solution.py:417
  67.3 7.9 %collective-permute-start.17 = (bf16[2,128,512]{2,1,0:T(8,128)(2,1)S(1)}, bf16[2,128,512]{2,1,0:T(8,128)(2,1)S(1)}, u32[]{:S(2)}, u32[]{:S(2)}) collective-permute-start(bf16[2,128,512]{2,1,0:T(8,128)(2,1)S(1)} %get-tuple-element.60), channel_id=1, source_target_pairs={{0,1},{1,0},{2,3},{3,2},{4,5},{5,4},{6,7},{7,6},{8,9},{9,8},{10,11... | collective-permute-start | bytes 786440 | tf_op jit(solution)/shard_map/ppermute | solution.py:417
  70.1 9.4 %collective-permute-start.11 = (bf16[1,128,512]{2,1,0:T(8,128)(2,1)S(1)}, bf16[1,128,512]{2,1,0:T(8,128)(2,1)S(1)}, u32[]{:S(2)}, u32[]{:S(2)}) collective-permute-start(bf16[1,128,512]{2,1,0:T(8,128)(2,1)S(1)} %get-tuple-element.52), channel_id=1, source_target_pairs={{0,1},{1,0},{2,3},{3,2},{4,5},{5,4},{6,7},{7,6},{8,9},{9,8},{10,11... | collective-permute-start | bytes 393224 | tf_op jit(solution)/shard_map/ppermute | solution.py:417
  75.3 5.0 %collective-permute-start.12 = (bf16[1,128,512]{2,1,0:T(8,128)(2,1)S(1)}, bf16[1,128,512]{2,1,0:T(8,128)(2,1)S(1)}, u32[]{:S(2)}, u32[]{:S(2)}) collective-permute-start(bf16[1,128,512]{2,1,0:T(8,128)(2,1)S(1)} %get-tuple-element.53), channel_id=1, source_target_pairs={{0,2},{1,3},{2,0},{3,1},{4,6},{5,7},{6,4},{7,5},{8,10},{9,11},{10,... | collective-permute-start | bytes 393224 | tf_op jit(solution)/shard_map/ppermute | solution.py:417
  75.9 5.9 %collective-permute-start.13 = (bf16[1,128,512]{2,1,0:T(8,128)(2,1)S(1)}, bf16[1,128,512]{2,1,0:T(8,128)(2,1)S(1)}, u32[]{:S(2)}, u32[]{:S(2)}) collective-permute-start(bf16[1,128,512]{2,1,0:T(8,128)(2,1)S(1)} %get-tuple-element.54), channel_id=1, source_target_pairs={{0,3},{1,2},{2,1},{3,0},{4,7},{5,6},{6,5},{7,4},{8,11},{9,10},{10,... | collective-permute-start | bytes 393224 | tf_op jit(solution)/shard_map/ppermute | solution.py:417
  77.6 5.7 %collective-permute-start.20 = (bf16[1,128,512]{2,1,0:T(8,128)(2,1)S(1)}, bf16[1,128,512]{2,1,0:T(8,128)(2,1)S(1)}, u32[]{:S(2)}, u32[]{:S(2)}) collective-permute-start(bf16[1,128,512]{2,1,0:T(8,128)(2,1)S(1)} %add_convert_fusion), channel_id=1, source_target_pairs={{0,1},{1,0},{2,3},{3,2},{4,5},{5,4},{6,7},{7,6},{8,9},{9,8},{10,11... | collective-permute-start | bytes 393224 | tf_op jit(solution)/shard_map/ppermute | solution.py:417
  78.9 5.0 %collective-permute-start.18 = (bf16[1,128,512]{2,1,0:T(8,128)(2,1)S(1)}, bf16[1,128,512]{2,1,0:T(8,128)(2,1)S(1)}, u32[]{:S(2)}, u32[]{:S(2)}) collective-permute-start(bf16[1,128,512]{2,1,0:T(8,128)(2,1)S(1)} %add_convert_fusion.1), channel_id=1, source_target_pairs={{0,2},{1,3},{2,0},{3,1},{4,6},{5,7},{6,4},{7,5},{8,10},{9,11},{10,... | collective-permute-start | bytes 393224 | tf_op jit(solution)/shard_map/ppermute | solution.py:417

commit v11 on v9

--- a/solution.py
+++ b/solution.py
@@ -419,16 +419,16 @@
     table = rank_table(routes.T, route_gates.T, experts)
     tables = [table] + [swap(table, k) for k in range(1, n)]
     pick, place, gates = slots(axis, n, local, tables)
-    gate_proj, up_proj, done = load((gate_proj, up_proj), table)
     if n == 4:
         x_near = [swap(saved_input, 1), swap(saved_input, 2)]
-        upper, lower = relay_parts(x_near, [done, place])
+        upper, lower = relay_parts(x_near, [place])
         sent = passed(grad_out, upper)
         x_blocks = [[saved_input], *[[x] for x in x_near], [swap(upper, 2), swap(lower, 1)]]
         g_near = [swap(sent, 1), swap(sent, 2)]
     else:
         x_blocks = [[saved_input]] + [[swap(saved_input, k)] for k in range(1, n)]
         sent = grad_out
+    gate_proj, up_proj, _ = load((gate_proj, up_proj), sent)
     x_first = slot_rows(local, pick, x_blocks[:2], 0, sent)
     x_rest = slot_rows(local, pick, x_blocks[2:], 1, sent)
     half = (local + 1) // 2

time: 82.9 us -> 84 us (1.013)
  waiting for transfers between devices: 17.4 us -> 15.4 us
  starting transfers between devices: 21.6 us -> 22.9 us
  local copies, waits for them, and re-layouts: 0.78 us -> 1.79 us
    ppermute x19, waiting for transfers between devices: 17.4 us -> 15.4 us  [swap(): return lax.ppermute(array, axis, [(i, i ^ k) for i in range(n)])]
    ppermute x19, starting transfers between devices: 21.6 us -> 22.9 us  [swap(): return lax.ppermute(array, axis, [(i, i ^ k) for i in range(n)])]
    unnamed x8, local copies, waits for them, and re-layouts: 0.74 us -> 1.75 us
  transfers between devices with their start and end apart: 19 -> 19, of which waited for: 10 -> 7; matrix products, arithmetic and copies ran while one was open for 0% -> 0% of each run, Pallas kernels for 35% -> 35%
where the time goes in v11:
time: 84 us; the launch traced here: 83.6 us
  Pallas kernels  43.1 us (51%)
  starting transfers between devices  22.9 us (27%)
  waiting for transfers between devices  15.4 us (18%)
  local copies, waits for them, and re-layouts  1.79 us (2%)
    ppermute x19, starting transfers between devices, swap(): return lax.ppermute(array, axis, [(i, i ^ k) for i in range(n)])  22.9 us
    ppermute x19, waiting for transfers between devices, swap(): return lax.ppermute(array, axis, [(i, i ^ k) for i in range(n)])  15.4 us
    pallas_call x1, Pallas kernels, back(): pl.pallas_call(functools.partial(back_kernel, local, sizes(tokens), len(f...  10.7 us
    pallas_call x2, Pallas kernels, pre(): pl.pallas_call(functools.partial(pre_kernel, experts), in_specs=[INSIDE]...  9.81 us
    pallas_call x1, Pallas kernels, load(): pl.pallas_call(functools.partial(load_kernel, count), in_specs=[OUTSIDE]...  8.89 us
    pallas_call x4, Pallas kernels, partial_sums(): pl.pallas_call(functools.partial(out_kernel, n, local, orders, chunk), ou...  8.59 us
    unnamed x8, local copies, waits for them, and re-layouts  1.75 us
  transfers between devices with their start and end apart: 19, of which 7 were waited for; matrix products, arithmetic and copies ran while one was open for 0% of the time, Pallas kernels for 35%

profile of v11, /device:TPU:0, one launch (start us, length us, event | category | flops | bytes accessed | tf_op | source)
XLA Modules:
  0.0 83.6 jit_solution(4061438889234279401)
XLA Ops:
  0.0 2.9 %collective-permute-start.3 = (bf16[128,2048]{1,0:T(8,128)(2,1)}, bf16[128,2048]{1,0:T(8,128)(2,1)S(1)}, u32[]{:S(2)}, u32[]{:S(2)}) collective-permute-start(bf16[128,2048]{1,0:T(8,128)(2,1)} %refs_0_.2), channel_id=1, source_target_pairs={{0,1},{1,0},{2,3},{3,2},{4,5},{5,4},{6,7},{7,6},{8,9},{9,8},{10,11... | collective-permute-start | bytes 1572872 | tf_op jit(solution)/shard_map/ppermute | solution.py:417
  2.9 1.5 %collective-permute-start.4 = (bf16[128,2048]{1,0:T(8,128)(2,1)}, bf16[128,2048]{1,0:T(8,128)(2,1)S(1)}, u32[]{:S(2)}, u32[]{:S(2)}) collective-permute-start(bf16[128,2048]{1,0:T(8,128)(2,1)} %refs_0_.2), channel_id=1, source_target_pairs={{0,2},{1,3},{2,0},{3,1},{4,6},{5,7},{6,4},{7,5},{8,10},{9,11},{10,... | collective-permute-start | bytes 1572872 | tf_op jit(solution)/shard_map/ppermute | solution.py:417
  4.5 1.5 %shard_map.73.refs_0_._ = bf16[32,128]{1,0:T(8,128)(2,1)} custom-call(s32[8,128]{1,0:T(8,128)} %bitcast.2, bf16[8,128]{1,0:T(8,128)(2,1)} %bitcast.3), custom_call_target="tpu_custom_call" | custom-call | tf_op jit(solution)/shard_map/pallas_call | solution.py:58
  5.9 0.0 collective-permute-start.2
  6.0 2.0 %collective-permute-start.1 = (bf16[32,128]{1,0:T(8,128)(2,1)}, bf16[32,128]{1,0:T(8,128)(2,1)S(1)}, u32[]{:S(2)}, u32[]{:S(2)}) collective-permute-start(bf16[32,128]{1,0:T(8,128)(2,1)} %shard_map.73.refs_0_._), channel_id=1, source_target_pairs={{0,2},{1,3},{2,0},{3,1},{4,6},{5,7},{6,4},{7,5},{8,10},{9,11},{10,... | collective-permute-start | bytes 24584 | tf_op jit(solution)/shard_map/ppermute | solution.py:417
  7.9 1.5 %collective-permute-start = (bf16[32,128]{1,0:T(8,128)(2,1)}, bf16[32,128]{1,0:T(8,128)(2,1)S(1)}, u32[]{:S(2)}, u32[]{:S(2)}) collective-permute-start(bf16[32,128]{1,0:T(8,128)(2,1)} %shard_map.73.refs_0_._), channel_id=1, source_target_pairs={{0,1},{1,0},{2,3},{3,2},{4,5},{5,4},{6,7},{7,6},{8,9},{9,8},{10,11... | collective-permute-start | bytes 24584 | tf_op jit(solution)/shard_map/ppermute | solution.py:417
  9.4 7.2 %collective-permute-done.2.refs_3_ = bf16[32,128]{1,0:T(8,128)(2,1)S(1)} collective-permute-done((bf16[32,128]{1,0:T(8,128)(2,1)}, bf16[32,128]{1,0:T(8,128)(2,1)S(1)}, u32[]{:S(2)}, u32[]{:S(2)}) %collective-permute-start.2) | collective-permute-done | bytes 8224 | tf_op jit(solution)/shard_map/ppermute | solution.py:417
  16.6 0.2 collective-permute-done.1.refs_2_
  16.9 0.0 collective-permute-done.refs_1_
  16.9 0.0 copy-start.2
  16.9 0.7 copy-done.2
  17.6 0.4 shard_map.74
  18.0 0.0 collective-permute-done.3.x_ref.refs_1_
  18.0 0.0 collective-permute-done.4.y_ref.refs_0_
  18.1 1.2 %collective-permute-start.8 = (bf16[64,2048]{1,0:T(8,128)(2,1)S(1)}, bf16[64,2048]{1,0:T(8,128)(2,1)S(1)}, u32[]{:S(2)}, u32[]{:S(2)}) collective-permute-start(bf16[64,2048]{1,0:T(8,128)(2,1)S(1)} %get-tuple-element.36), channel_id=1, source_target_pairs={{0,1},{1,0},{2,3},{3,2},{4,5},{5,4},{6,7},{7,6},{8,9},{9,8},{10,11... | collective-permute-start | bytes 786440 | tf_op jit(solution)/shard_map/ppermute | solution.py:417
  19.3 0.9 %collective-permute-start.7 = (bf16[64,2048]{1,0:T(8,128)(2,1)S(1)}, bf16[64,2048]{1,0:T(8,128)(2,1)S(1)}, u32[]{:S(2)}, u32[]{:S(2)}) collective-permute-start(bf16[64,2048]{1,0:T(8,128)(2,1)S(1)} %get-tuple-element.33._), channel_id=1, source_target_pairs={{0,2},{1,3},{2,0},{3,1},{4,6},{5,7},{6,4},{7,5},{8,10},{9,11},{10,... | collective-permute-start | bytes 786440 | tf_op jit(solution)/shard_map/ppermute | solution.py:417
  20.2 0.0 copy-start
  20.2 1.0 %copy-done = bf16[128,2048]{1,0:T(8,128)(2,1)S(1)} copy-done((bf16[128,2048]{1,0:T(8,128)(2,1)S(1)}, bf16[128,2048]{1,0:T(8,128)(2,1)}, u32[]{:S(2)}) %copy-start) | copy-done | bytes 524312
  21.3 0.0 copy-start.1
  21.3 1.2 %collective-permute-start.6 = (bf16[128,2048]{1,0:T(8,128)(2,1)S(1)}, bf16[128,2048]{1,0:T(8,128)(2,1)S(1)}, u32[]{:S(2)}, u32[]{:S(2)}) collective-permute-start(bf16[128,2048]{1,0:T(8,128)(2,1)S(1)} %shard_map.76.refs_2_.refs_3_.refs_0_), channel_id=1, source_target_pairs={{0,2},{1,3},{2,0},{3,1},{4,6},{5,7},{6,4},{7,5},{8,10},{9,11},{10,... | collective-permute-start | bytes 1572872 | tf_op jit(solution)/shard_map/ppermute | solution.py:417
  22.5 0.9 %collective-permute-start.5 = (bf16[128,2048]{1,0:T(8,128)(2,1)S(1)}, bf16[128,2048]{1,0:T(8,128)(2,1)S(1)}, u32[]{:S(2)}, u32[]{:S(2)}) collective-permute-start(bf16[128,2048]{1,0:T(8,128)(2,1)S(1)} %shard_map.76.refs_2_.refs_3_.refs_0_), channel_id=1, source_target_pairs={{0,1},{1,0},{2,3},{3,2},{4,5},{5,4},{6,7},{7,6},{8,9},{9,8},{10,11... | collective-permute-start | bytes 1572872 | tf_op jit(solution)/shard_map/ppermute | solution.py:417
  23.4 8.9 %shard_map.79 = (bf16[4,2048,768]{2,1,0:T(8,128)(2,1)S(1)}, bf16[4,2048,768]{2,1,0:T(8,128)(2,1)S(1)}, f32[8,128]{1,0:T(8,128)}) custom-call(bf16[4,2048,768]{2,1,0:T(8,128)(2,1)} %refs_0_.3, bf16[4,2048,768]{2,1,0:T(8,128)(2,1)} %refs_1_.1, bf16[128,2048]{1,0:T(8,128)(2,1)S(1)} %shard_map.76.refs_2_.refs_3_.refs_0_), custom_call_target="tpu_custom_call" | custom-call | bytes 50331648 | tf_op jit(solution)/shard_map/pallas_call | solution.py:181
  32.3 0.0 copy-done.1
  32.3 0.7 shard_map.77.first_ref
  33.0 0.0 copy-start.3
  33.0 0.0 collective-permute-done.8.refs_2_
  33.0 0.0 collective-permute-done.7.refs_1_
  33.0 0.7 shard_map.78.rest_ref
  33.7 0.0 copy-done.3
  33.7 4.8 %shard_map.80 = (f32[2,768,256]{2,1,0:T(8,128)S(1)}, f32[2,768,256]{2,1,0:T(8,128)S(1)}) custom-call(f32[4,8,256]{2,1,0:T(8,128)S(1)} %get-tuple-element.34.gate_ref, bf16[4,128,2048]{2,1,0:T(8,128)(2,1)S(1)} %shard_map.77.first_ref, bf16[4,128,2048]{2,1,0:T(8,128)(2,1)S(1)} %shard_map.78.rest_ref, ...), custom_call_target="tpu_custom_call" | custom-call | flops 3221225472 | bytes 12582912 | tf_op jit(solution)/shard_map/pallas_call | solution.py:276
  38.6 0.0 collective-permute-done.6.y_ref.refs_0_
  38.6 0.0 collective-permute-done.5.x_ref.refs_1_
  38.6 1.2 %collective-permute-start.10 = (bf16[64,2048]{1,0:T(8,128)(2,1)S(1)}, bf16[64,2048]{1,0:T(8,128)(2,1)S(1)}, u32[]{:S(2)}, u32[]{:S(2)}) collective-permute-start(bf16[64,2048]{1,0:T(8,128)(2,1)S(1)} %get-tuple-element.41), channel_id=1, source_target_pairs={{0,1},{1,0},{2,3},{3,2},{4,5},{5,4},{6,7},{7,6},{8,9},{9,8},{10,11... | collective-permute-start | bytes 786440 | tf_op jit(solution)/shard_map/ppermute | solution.py:417
  39.8 0.9 %collective-permute-start.9 = (bf16[64,2048]{1,0:T(8,128)(2,1)S(1)}, bf16[64,2048]{1,0:T(8,128)(2,1)S(1)}, u32[]{:S(2)}, u32[]{:S(2)}) collective-permute-start(bf16[64,2048]{1,0:T(8,128)(2,1)S(1)} %get-tuple-element.40.refs_2_._), channel_id=1, source_target_pairs={{0,2},{1,3},{2,0},{3,1},{4,6},{5,7},{6,4},{7,5},{8,10},{9,11},{10,... | collective-permute-start | bytes 786440 | tf_op jit(solution)/shard_map/ppermute | solution.py:417
  40.7 0.7 shard_map.82.first_ref
  41.5 5.0 %shard_map.83 = (f32[2,768,256]{2,1,0:T(8,128)S(1)}, f32[2,768,256]{2,1,0:T(8,128)S(1)}) custom-call(f32[4,8,256]{2,1,0:T(8,128)S(1)} %get-tuple-element.34.gate_ref, bf16[4,128,2048]{2,1,0:T(8,128)(2,1)S(1)} %shard_map.77.first_ref, bf16[4,128,2048]{2,1,0:T(8,128)(2,1)S(1)} %shard_map.78.rest_ref, ...), custom_call_target="tpu_custom_call" | custom-call | flops 3221225472 | bytes 12582912 | tf_op jit(solution)/shard_map/pallas_call | solution.py:276
  46.5 0.0 collective-permute-done.10.refs_2_
  46.5 0.0 collective-permute-done.9.refs_1_
  46.5 10.7 %shard_map.84 = (bf16[4,768,256]{2,1,0:T(8,128)(2,1)S(1)}, bf16[4,768,256]{2,1,0:T(8,128)(2,1)S(1)}) custom-call(bf16[2,256,512]{2,1,0:T(8,128)(2,1)S(1)} %get-tuple-element.32.refs_0_.place_ref, bf16[4,2048,128]{2,1,0:T(8,128)(2,1)S(1)} %shard_map.82.first_ref, bf16[128,2048]{1,0:T(8,128)(2,1)S(1)} %collective-permute-done.6.y_ref.refs_0_, ...), custom_call_target="tpu_custom_call" | custom-call | flops 3221225472 | bytes 12582912 | tf_op jit(solution)/shard_map/pallas_call | solution.py:340
  57.2 2.2 %shard_map.88 = (f32[1,128,512]{2,1,0:T(8,128)S(1)}, bf16[2,128,512]{2,1,0:T(8,128)(2,1)S(1)}, bf16[1,128,512]{2,1,0:T(8,128)(2,1)S(1)}) custom-call(bf16[2,256,512]{2,1,0:T(8,128)(2,1)S(1)} %get-tuple-element.32.refs_0_.place_ref, bf16[4,768,256]{2,1,0:T(8,128)(2,1)S(1)} %get-tuple-element.45.hg_ref, bf16[4,768,256]{2,1,0:T(8,128)(2,1)S(1)} %get-tuple-element.46.hu_ref, ...), custom_call_target="tpu_custom_call" | custom-call | flops 402653184 | bytes 1572864 | tf_op jit(solution)/shard_map/pallas_call | solution.py:385
  59.4 1.2 %collective-permute-start.17 = (bf16[2,128,512]{2,1,0:T(8,128)(2,1)S(1)}, bf16[2,128,512]{2,1,0:T(8,128)(2,1)S(1)}, u32[]{:S(2)}, u32[]{:S(2)}) collective-permute-start(bf16[2,128,512]{2,1,0:T(8,128)(2,1)S(1)} %get-tuple-element.57), channel_id=1, source_target_pairs={{0,2},{1,3},{2,0},{3,1},{4,6},{5,7},{6,4},{7,5},{8,10},{9,11},{10,... | collective-permute-start | bytes 786440 | tf_op jit(solution)/shard_map/ppermute | solution.py:417
  60.6 2.1 %shard_map.87 = (f32[1,128,512]{2,1,0:T(8,128)S(1)}, bf16[2,128,512]{2,1,0:T(8,128)(2,1)S(1)}, bf16[1,128,512]{2,1,0:T(8,128)(2,1)S(1)}) custom-call(bf16[2,256,512]{2,1,0:T(8,128)(2,1)S(1)} %get-tuple-element.32.refs_0_.place_ref, bf16[4,768,256]{2,1,0:T(8,128)(2,1)S(1)} %get-tuple-element.45.hg_ref, bf16[4,768,256]{2,1,0:T(8,128)(2,1)S(1)} %get-tuple-element.46.hu_ref, ...), custom_call_target="tpu_custom_call" | custom-call | flops 402653184 | bytes 1572864 | tf_op jit(solution)/shard_map/pallas_call | solution.py:385
  62.7 1.0 %collective-permute-start.15 = (bf16[2,128,512]{2,1,0:T(8,128)(2,1)S(1)}, bf16[2,128,512]{2,1,0:T(8,128)(2,1)S(1)}, u32[]{:S(2)}, u32[]{:S(2)}) collective-permute-start(bf16[2,128,512]{2,1,0:T(8,128)(2,1)S(1)} %get-tuple-element.54), channel_id=1, source_target_pairs={{0,1},{1,0},{2,3},{3,2},{4,5},{5,4},{6,7},{7,6},{8,9},{9,8},{10,11... | collective-permute-start | bytes 786440 | tf_op jit(solution)/shard_map/ppermute | solution.py:417
  63.7 2.1 %shard_map.86 = (f32[1,128,512]{2,1,0:T(8,128)S(1)}, bf16[2,128,512]{2,1,0:T(8,128)(2,1)S(1)}, bf16[1,128,512]{2,1,0:T(8,128)(2,1)S(1)}) custom-call(bf16[2,256,512]{2,1,0:T(8,128)(2,1)S(1)} %get-tuple-element.32.refs_0_.place_ref, bf16[4,768,256]{2,1,0:T(8,128)(2,1)S(1)} %get-tuple-element.45.hg_ref, bf16[4,768,256]{2,1,0:T(8,128)(2,1)S(1)} %get-tuple-element.46.hu_ref, ...), custom_call_target="tpu_custom_call" | custom-call | flops 402653184 | bytes 1572864 | tf_op jit(solution)/shard_map/pallas_call | solution.py:385
  65.9 1.5 %collective-permute-start.13 = (bf16[2,128,512]{2,1,0:T(8,128)(2,1)S(1)}, bf16[2,128,512]{2,1,0:T(8,128)(2,1)S(1)}, u32[]{:S(2)}, u32[]{:S(2)}) collective-permute-start(bf16[2,128,512]{2,1,0:T(8,128)(2,1)S(1)} %get-tuple-element.51), channel_id=1, source_target_pairs={{0,2},{1,3},{2,0},{3,1},{4,6},{5,7},{6,4},{7,5},{8,10},{9,11},{10,... | collective-permute-start | bytes 786440 | tf_op jit(solution)/shard_map/ppermute | solution.py:417
  67.4 2.1 %shard_map.85 = (f32[1,128,512]{2,1,0:T(8,128)S(1)}, bf16[2,128,512]{2,1,0:T(8,128)(2,1)S(1)}, bf16[1,128,512]{2,1,0:T(8,128)(2,1)S(1)}) custom-call(bf16[2,256,512]{2,1,0:T(8,128)(2,1)S(1)} %get-tuple-element.32.refs_0_.place_ref, bf16[4,768,256]{2,1,0:T(8,128)(2,1)S(1)} %get-tuple-element.45.hg_ref, bf16[4,768,256]{2,1,0:T(8,128)(2,1)S(1)} %get-tuple-element.46.hu_ref, ...), custom_call_target="tpu_custom_call" | custom-call | flops 402653184 | bytes 1572864 | tf_op jit(solution)/shard_map/pallas_call | solution.py:385
  69.5 0.6 collective-permute-start.11
  70.1 0.0 collective-permute-done.17
  70.2 1.6 %collective-permute-start.18 = (bf16[1,128,512]{2,1,0:T(8,128)(2,1)S(1)}, bf16[1,128,512]{2,1,0:T(8,128)(2,1)S(1)}, u32[]{:S(2)}, u32[]{:S(2)}) collective-permute-start(bf16[1,128,512]{2,1,0:T(8,128)(2,1)S(1)} %add_convert_fusion), channel_id=1, source_target_pairs={{0,1},{1,0},{2,3},{3,2},{4,5},{5,4},{6,7},{7,6},{8,9},{9,8},{10,11... | collective-permute-start | bytes 393224 | tf_op jit(solution)/shard_map/ppermute | solution.py:417
  71.7 0.0 collective-permute-done.15
  71.8 0.7 collective-permute-start.16
  72.4 1.3 %collective-permute-done.13 = bf16[2,128,512]{2,1,0:T(8,128)(2,1)S(1)} collective-permute-done((bf16[2,128,512]{2,1,0:T(8,128)(2,1)S(1)}, bf16[2,128,512]{2,1,0:T(8,128)(2,1)S(1)}, u32[]{:S(2)}, u32[]{:S(2)}) %collective-permute-start.13) | collective-permute-done | bytes 262176 | tf_op jit(solution)/shard_map/ppermute | solution.py:417
  73.8 1.1 %collective-permute-start.14 = (bf16[1,128,512]{2,1,0:T(8,128)(2,1)S(1)}, bf16[1,128,512]{2,1,0:T(8,128)(2,1)S(1)}, u32[]{:S(2)}, u32[]{:S(2)}) collective-permute-start(bf16[1,128,512]{2,1,0:T(8,128)(2,1)S(1)} %add_convert_fusion.2), channel_id=1, source_target_pairs={{0,1},{1,0},{2,3},{3,2},{4,5},{5,4},{6,7},{7,6},{8,9},{9,8},{10,11... | collective-permute-start | bytes 393224 | tf_op jit(solution)/shard_map/ppermute | solution.py:417
  74.9 2.7 %collective-permute-done.11 = bf16[2,128,512]{2,1,0:T(8,128)(2,1)S(1)} collective-permute-done((bf16[2,128,512]{2,1,0:T(8,128)(2,1)S(1)}, bf16[2,128,512]{2,1,0:T(8,128)(2,1)S(1)}, u32[]{:S(2)}, u32[]{:S(2)}) %collective-permute-start.11) | collective-permute-done | bytes 262176 | tf_op jit(solution)/shard_map/ppermute | solution.py:417
  77.6 1.0 %collective-permute-start.12 = (bf16[1,128,512]{2,1,0:T(8,128)(2,1)S(1)}, bf16[1,128,512]{2,1,0:T(8,128)(2,1)S(1)}, u32[]{:S(2)}, u32[]{:S(2)}) collective-permute-start(bf16[1,128,512]{2,1,0:T(8,128)(2,1)S(1)} %add_convert_fusion.3), channel_id=1, source_target_pairs={{0,2},{1,3},{2,0},{3,1},{4,6},{5,7},{6,4},{7,5},{8,10},{9,11},{10,... | collective-permute-start | bytes 393224 | tf_op jit(solution)/shard_map/ppermute | solution.py:417
  78.7 0.3 collective-permute-done.18.refs_11_
  79.0 0.0 collective-permute-done.16.refs_8_
  79.0 1.4 %collective-permute-done.14.refs_5_ = bf16[1,128,512]{2,1,0:T(8,128)(2,1)S(1)} collective-permute-done((bf16[1,128,512]{2,1,0:T(8,128)(2,1)S(1)}, bf16[1,128,512]{2,1,0:T(8,128)(2,1)S(1)}, u32[]{:S(2)}, u32[]{:S(2)}) %collective-permute-start.14) | collective-permute-done | bytes 131104 | tf_op jit(solution)/shard_map/ppermute | solution.py:417
  80.4 2.3 %collective-permute-done.12.refs_2_ = bf16[1,128,512]{2,1,0:T(8,128)(2,1)S(1)} collective-permute-done((bf16[1,128,512]{2,1,0:T(8,128)(2,1)S(1)}, bf16[1,128,512]{2,1,0:T(8,128)(2,1)S(1)}, u32[]{:S(2)}, u32[]{:S(2)}) %collective-permute-start.12) | collective-permute-done | bytes 131104 | tf_op jit(solution)/shard_map/ppermute | solution.py:417
  82.7 0.9 %shard_map.89 = bf16[128,2048]{1,0:T(8,128)(2,1)} custom-call(f32[1,128,512]{2,1,0:T(8,128)S(1)} %get-tuple-element.47.refs_0_, bf16[1,128,512]{2,1,0:T(8,128)(2,1)S(1)} %slice.32.refs_1_, bf16[1,128,512]{2,1,0:T(8,128)(2,1)S(1)} %collective-permute-done.12.refs_2_, f32[1,128,512]{2,1,0:T(8,128)S(1)} %get-tuple-element.50.refs_3_, ...), custom_call_target="tpu_custom_call" | custom-call | tf_op jit(solution)/shard_map/pallas_call | solution.py:459
  (11 shorter events, 0.3 us)
Async XLA Ops:
  0.0 18.0 %collective-permute-start.3 = (bf16[128,2048]{1,0:T(8,128)(2,1)}, bf16[128,2048]{1,0:T(8,128)(2,1)S(1)}, u32[]{:S(2)}, u32[]{:S(2)}) collective-permute-start(bf16[128,2048]{1,0:T(8,128)(2,1)} %refs_0_.2), channel_id=1, source_target_pairs={{0,1},{1,0},{2,3},{3,2},{4,5},{5,4},{6,7},{7,6},{8,9},{9,8},{10,11... | collective-permute-start | bytes 1572872 | tf_op jit(solution)/shard_map/ppermute | solution.py:417
  2.9 15.1 %collective-permute-start.4 = (bf16[128,2048]{1,0:T(8,128)(2,1)}, bf16[128,2048]{1,0:T(8,128)(2,1)S(1)}, u32[]{:S(2)}, u32[]{:S(2)}) collective-permute-start(bf16[128,2048]{1,0:T(8,128)(2,1)} %refs_0_.2), channel_id=1, source_target_pairs={{0,2},{1,3},{2,0},{3,1},{4,6},{5,7},{6,4},{7,5},{8,10},{9,11},{10,... | collective-permute-start | bytes 1572872 | tf_op jit(solution)/shard_map/ppermute | solution.py:417
  5.9 10.7 %collective-permute-start.2 = (bf16[32,128]{1,0:T(8,128)(2,1)}, bf16[32,128]{1,0:T(8,128)(2,1)S(1)}, u32[]{:S(2)}, u32[]{:S(2)}) collective-permute-start(bf16[32,128]{1,0:T(8,128)(2,1)} %shard_map.73.refs_0_._), channel_id=1, source_target_pairs={{0,3},{1,2},{2,1},{3,0},{4,7},{5,6},{6,5},{7,4},{8,11},{9,10},{10,... | collective-permute-start | bytes 24584 | tf_op jit(solution)/shard_map/ppermute | solution.py:417
  6.0 10.9 %collective-permute-start.1 = (bf16[32,128]{1,0:T(8,128)(2,1)}, bf16[32,128]{1,0:T(8,128)(2,1)S(1)}, u32[]{:S(2)}, u32[]{:S(2)}) collective-permute-start(bf16[32,128]{1,0:T(8,128)(2,1)} %shard_map.73.refs_0_._), channel_id=1, source_target_pairs={{0,2},{1,3},{2,0},{3,1},{4,6},{5,7},{6,4},{7,5},{8,10},{9,11},{10,... | collective-permute-start | bytes 24584 | tf_op jit(solution)/shard_map/ppermute | solution.py:417
  7.9 8.9 %collective-permute-start = (bf16[32,128]{1,0:T(8,128)(2,1)}, bf16[32,128]{1,0:T(8,128)(2,1)S(1)}, u32[]{:S(2)}, u32[]{:S(2)}) collective-permute-start(bf16[32,128]{1,0:T(8,128)(2,1)} %shard_map.73.refs_0_._), channel_id=1, source_target_pairs={{0,1},{1,0},{2,3},{3,2},{4,5},{5,4},{6,7},{7,6},{8,9},{9,8},{10,11... | collective-permute-start | bytes 24584 | tf_op jit(solution)/shard_map/ppermute | solution.py:417
  16.9 0.7 copy-start.2
  18.1 14.9 %collective-permute-start.8 = (bf16[64,2048]{1,0:T(8,128)(2,1)S(1)}, bf16[64,2048]{1,0:T(8,128)(2,1)S(1)}, u32[]{:S(2)}, u32[]{:S(2)}) collective-permute-start(bf16[64,2048]{1,0:T(8,128)(2,1)S(1)} %get-tuple-element.36), channel_id=1, source_target_pairs={{0,1},{1,0},{2,3},{3,2},{4,5},{5,4},{6,7},{7,6},{8,9},{9,8},{10,11... | collective-permute-start | bytes 786440 | tf_op jit(solution)/shard_map/ppermute | solution.py:417
  19.3 13.7 %collective-permute-start.7 = (bf16[64,2048]{1,0:T(8,128)(2,1)S(1)}, bf16[64,2048]{1,0:T(8,128)(2,1)S(1)}, u32[]{:S(2)}, u32[]{:S(2)}) collective-permute-start(bf16[64,2048]{1,0:T(8,128)(2,1)S(1)} %get-tuple-element.33._), channel_id=1, source_target_pairs={{0,2},{1,3},{2,0},{3,1},{4,6},{5,7},{6,4},{7,5},{8,10},{9,11},{10,... | collective-permute-start | bytes 786440 | tf_op jit(solution)/shard_map/ppermute | solution.py:417
  20.2 1.0 %copy-start = (bf16[128,2048]{1,0:T(8,128)(2,1)S(1)}, bf16[128,2048]{1,0:T(8,128)(2,1)}, u32[]{:S(2)}) copy-start(bf16[128,2048]{1,0:T(8,128)(2,1)} %array_ref.1) | copy-start | bytes 1572868
  21.3 11.0 %copy-start.1 = (bf16[128,2048]{1,0:T(8,128)(2,1)S(1)}, bf16[128,2048]{1,0:T(8,128)(2,1)}, u32[]{:S(2)}) copy-start(bf16[128,2048]{1,0:T(8,128)(2,1)} %refs_0_.2) | copy-start | bytes 1572868
  21.3 17.3 %collective-permute-start.6 = (bf16[128,2048]{1,0:T(8,128)(2,1)S(1)}, bf16[128,2048]{1,0:T(8,128)(2,1)S(1)}, u32[]{:S(2)}, u32[]{:S(2)}) collective-permute-start(bf16[128,2048]{1,0:T(8,128)(2,1)S(1)} %shard_map.76.refs_2_.refs_3_.refs_0_), channel_id=1, source_target_pairs={{0,2},{1,3},{2,0},{3,1},{4,6},{5,7},{6,4},{7,5},{8,10},{9,11},{10,... | collective-permute-start | bytes 1572872 | tf_op jit(solution)/shard_map/ppermute | solution.py:417
  22.5 16.1 %collective-permute-start.5 = (bf16[128,2048]{1,0:T(8,128)(2,1)S(1)}, bf16[128,2048]{1,0:T(8,128)(2,1)S(1)}, u32[]{:S(2)}, u32[]{:S(2)}) collective-permute-start(bf16[128,2048]{1,0:T(8,128)(2,1)S(1)} %shard_map.76.refs_2_.refs_3_.refs_0_), channel_id=1, source_target_pairs={{0,1},{1,0},{2,3},{3,2},{4,5},{5,4},{6,7},{7,6},{8,9},{9,8},{10,11... | collective-permute-start | bytes 1572872 | tf_op jit(solution)/shard_map/ppermute | solution.py:417
  33.0 0.8 copy-start.3
  38.6 7.9 %collective-permute-start.10 = (bf16[64,2048]{1,0:T(8,128)(2,1)S(1)}, bf16[64,2048]{1,0:T(8,128)(2,1)S(1)}, u32[]{:S(2)}, u32[]{:S(2)}) collective-permute-start(bf16[64,2048]{1,0:T(8,128)(2,1)S(1)} %get-tuple-element.41), channel_id=1, source_target_pairs={{0,1},{1,0},{2,3},{3,2},{4,5},{5,4},{6,7},{7,6},{8,9},{9,8},{10,11... | collective-permute-start | bytes 786440 | tf_op jit(solution)/shard_map/ppermute | solution.py:417
  39.8 6.7 %collective-permute-start.9 = (bf16[64,2048]{1,0:T(8,128)(2,1)S(1)}, bf16[64,2048]{1,0:T(8,128)(2,1)S(1)}, u32[]{:S(2)}, u32[]{:S(2)}) collective-permute-start(bf16[64,2048]{1,0:T(8,128)(2,1)S(1)} %get-tuple-element.40.refs_2_._), channel_id=1, source_target_pairs={{0,2},{1,3},{2,0},{3,1},{4,6},{5,7},{6,4},{7,5},{8,10},{9,11},{10,... | collective-permute-start | bytes 786440 | tf_op jit(solution)/shard_map/ppermute | solution.py:417
  59.4 10.8 %collective-permute-start.17 = (bf16[2,128,512]{2,1,0:T(8,128)(2,1)S(1)}, bf16[2,128,512]{2,1,0:T(8,128)(2,1)S(1)}, u32[]{:S(2)}, u32[]{:S(2)}) collective-permute-start(bf16[2,128,512]{2,1,0:T(8,128)(2,1)S(1)} %get-tuple-element.57), channel_id=1, source_target_pairs={{0,2},{1,3},{2,0},{3,1},{4,6},{5,7},{6,4},{7,5},{8,10},{9,11},{10,... | collective-permute-start | bytes 786440 | tf_op jit(solution)/shard_map/ppermute | solution.py:417
  62.7 9.0 %collective-permute-start.15 = (bf16[2,128,512]{2,1,0:T(8,128)(2,1)S(1)}, bf16[2,128,512]{2,1,0:T(8,128)(2,1)S(1)}, u32[]{:S(2)}, u32[]{:S(2)}) collective-permute-start(bf16[2,128,512]{2,1,0:T(8,128)(2,1)S(1)} %get-tuple-element.54), channel_id=1, source_target_pairs={{0,1},{1,0},{2,3},{3,2},{4,5},{5,4},{6,7},{7,6},{8,9},{9,8},{10,11... | collective-permute-start | bytes 786440 | tf_op jit(solution)/shard_map/ppermute | solution.py:417
  65.9 7.8 %collective-permute-start.13 = (bf16[2,128,512]{2,1,0:T(8,128)(2,1)S(1)}, bf16[2,128,512]{2,1,0:T(8,128)(2,1)S(1)}, u32[]{:S(2)}, u32[]{:S(2)}) collective-permute-start(bf16[2,128,512]{2,1,0:T(8,128)(2,1)S(1)} %get-tuple-element.51), channel_id=1, source_target_pairs={{0,2},{1,3},{2,0},{3,1},{4,6},{5,7},{6,4},{7,5},{8,10},{9,11},{10,... | collective-permute-start | bytes 786440 | tf_op jit(solution)/shard_map/ppermute | solution.py:417
  69.5 8.0 %collective-permute-start.11 = (bf16[2,128,512]{2,1,0:T(8,128)(2,1)S(1)}, bf16[2,128,512]{2,1,0:T(8,128)(2,1)S(1)}, u32[]{:S(2)}, u32[]{:S(2)}) collective-permute-start(bf16[2,128,512]{2,1,0:T(8,128)(2,1)S(1)} %get-tuple-element.48), channel_id=1, source_target_pairs={{0,1},{1,0},{2,3},{3,2},{4,5},{5,4},{6,7},{7,6},{8,9},{9,8},{10,11... | collective-permute-start | bytes 786440 | tf_op jit(solution)/shard_map/ppermute | solution.py:417
  70.2 8.8 %collective-permute-start.18 = (bf16[1,128,512]{2,1,0:T(8,128)(2,1)S(1)}, bf16[1,128,512]{2,1,0:T(8,128)(2,1)S(1)}, u32[]{:S(2)}, u32[]{:S(2)}) collective-permute-start(bf16[1,128,512]{2,1,0:T(8,128)(2,1)S(1)} %add_convert_fusion), channel_id=1, source_target_pairs={{0,1},{1,0},{2,3},{3,2},{4,5},{5,4},{6,7},{7,6},{8,9},{9,8},{10,11... | collective-permute-start | bytes 393224 | tf_op jit(solution)/shard_map/ppermute | solution.py:417
  71.8 7.2 %collective-permute-start.16 = (bf16[1,128,512]{2,1,0:T(8,128)(2,1)S(1)}, bf16[1,128,512]{2,1,0:T(8,128)(2,1)S(1)}, u32[]{:S(2)}, u32[]{:S(2)}) collective-permute-start(bf16[1,128,512]{2,1,0:T(8,128)(2,1)S(1)} %add_convert_fusion.1), channel_id=1, source_target_pairs={{0,2},{1,3},{2,0},{3,1},{4,6},{5,7},{6,4},{7,5},{8,10},{9,11},{10,... | collective-permute-start | bytes 393224 | tf_op jit(solution)/shard_map/ppermute | solution.py:417
  73.8 6.6 %collective-permute-start.14 = (bf16[1,128,512]{2,1,0:T(8,128)(2,1)S(1)}, bf16[1,128,512]{2,1,0:T(8,128)(2,1)S(1)}, u32[]{:S(2)}, u32[]{:S(2)}) collective-permute-start(bf16[1,128,512]{2,1,0:T(8,128)(2,1)S(1)} %add_convert_fusion.2), channel_id=1, source_target_pairs={{0,1},{1,0},{2,3},{3,2},{4,5},{5,4},{6,7},{7,6},{8,9},{9,8},{10,11... | collective-permute-start | bytes 393224 | tf_op jit(solution)/shard_map/ppermute | solution.py:417
  77.6 5.0 %collective-permute-start.12 = (bf16[1,128,512]{2,1,0:T(8,128)(2,1)S(1)}, bf16[1,128,512]{2,1,0:T(8,128)(2,1)S(1)}, u32[]{:S(2)}, u32[]{:S(2)}) collective-permute-start(bf16[1,128,512]{2,1,0:T(8,128)(2,1)S(1)} %add_convert_fusion.3), channel_id=1, source_target_pairs={{0,2},{1,3},{2,0},{3,1},{4,6},{5,7},{6,4},{7,5},{8,10},{9,11},{10,... | collective-permute-start | bytes 393224 | tf_op jit(solution)/shard_map/ppermute | solution.py:417

commit v12 on v5

--- a/solution.py
+++ b/solution.py
@@ -259,8 +259,7 @@
     cols = hidden // 2
     gather_rows(local, pick_ref, token_refs, 1, xs)
 
-    @pl.loop(0, local)
-    def _(e):
+    for e in range(local):
         rows = jnp.concatenate([first_ref[e], xs[e]], axis=0)
         gates = gate_ref[e][:1, :]
         for f in range(0, hidden, cols):

time: 81.6 us -> 81.5 us (level)
  Pallas kernels: 42 us -> 41.1 us
    pallas_call x1, Pallas kernels: 10.9 us -> 9.77 us  [pre(): pl.pallas_call(functools.partial(pre_kernel, local, sizes(tokens)), in_sp...]
  transfers between devices with their start and end apart: 19 -> 19, of which waited for: 10 -> 9; matrix products, arithmetic and copies ran while one was open for 0% -> 0% of each run, Pallas kernels for 36% -> 35%
where the time goes in v12:
time: 81.5 us; the launch traced here: 81.2 us
  Pallas kernels  41.1 us (50%)
  starting transfers between devices  22 us (27%)
  waiting for transfers between devices  17.1 us (21%)
    ppermute x19, starting transfers between devices, swap(): return lax.ppermute(array, axis, [(i, i ^ k) for i in range(n)])  22 us
    ppermute x19, waiting for transfers between devices, swap(): return lax.ppermute(array, axis, [(i, i ^ k) for i in range(n)])  17.1 us
    pallas_call x1, Pallas kernels, pre(): pl.pallas_call(functools.partial(pre_kernel, local, sizes(tokens)), in_sp...  9.77 us
    pallas_call x1, Pallas kernels, back(): pl.pallas_call(functools.partial(back_kernel, local, sizes(tokens)), in_s...  9.76 us
    pallas_call x4, Pallas kernels, partial_sums(): pl.pallas_call(functools.partial(out_kernel, n, local, orders, chunk), ou...  8.58 us
    pallas_call x1, Pallas kernels, load(): pl.pallas_call(functools.partial(load_kernel, count), in_specs=[OUTSIDE]...  8.3 us
  transfers between devices with their start and end apart: 19, of which 9 were waited for; matrix products, arithmetic and copies ran while one was open for 0% of the time, Pallas kernels for 35%

profile of v12, /device:TPU:0, one launch (start us, length us, event | category | flops | bytes accessed | tf_op | source)
XLA Modules:
  0.0 81.2 jit_solution(17973434770024978918)
XLA Ops:
  0.0 2.9 %collective-permute-start.3 = (bf16[128,2048]{1,0:T(8,128)(2,1)}, bf16[128,2048]{1,0:T(8,128)(2,1)S(1)}, u32[]{:S(2)}, u32[]{:S(2)}) collective-permute-start(bf16[128,2048]{1,0:T(8,128)(2,1)} %refs_0_.3), channel_id=1, source_target_pairs={{0,1},{1,0},{2,3},{3,2},{4,5},{5,4},{6,7},{7,6},{8,9},{9,8},{10,11... | collective-permute-start | bytes 1572872 | tf_op jit(solution)/shard_map/ppermute | solution.py:407
  2.9 1.5 %collective-permute-start.4 = (bf16[128,2048]{1,0:T(8,128)(2,1)}, bf16[128,2048]{1,0:T(8,128)(2,1)S(1)}, u32[]{:S(2)}, u32[]{:S(2)}) collective-permute-start(bf16[128,2048]{1,0:T(8,128)(2,1)} %refs_0_.3), channel_id=1, source_target_pairs={{0,2},{1,3},{2,0},{3,1},{4,6},{5,7},{6,4},{7,5},{8,10},{9,11},{10,... | collective-permute-start | bytes 1572872 | tf_op jit(solution)/shard_map/ppermute | solution.py:407
  4.5 1.5 %shard_map.73.refs_0_.refs_2_ = bf16[32,128]{1,0:T(8,128)(2,1)} custom-call(s32[8,128]{1,0:T(8,128)} %bitcast.2, bf16[8,128]{1,0:T(8,128)(2,1)} %bitcast.3), custom_call_target="tpu_custom_call" | custom-call | tf_op jit(solution)/shard_map/pallas_call | solution.py:56
  5.9 0.0 copy-start
  5.9 0.0 collective-permute-start.2
  6.0 2.0 %collective-permute-start.1 = (bf16[32,128]{1,0:T(8,128)(2,1)}, bf16[32,128]{1,0:T(8,128)(2,1)S(1)}, u32[]{:S(2)}, u32[]{:S(2)}) collective-permute-start(bf16[32,128]{1,0:T(8,128)(2,1)} %shard_map.73.refs_0_.refs_2_), channel_id=1, source_target_pairs={{0,2},{1,3},{2,0},{3,1},{4,6},{5,7},{6,4},{7,5},{8,10},{9,11},{10,... | collective-permute-start | bytes 24584 | tf_op jit(solution)/shard_map/ppermute | solution.py:407
  7.9 1.5 %collective-permute-start = (bf16[32,128]{1,0:T(8,128)(2,1)}, bf16[32,128]{1,0:T(8,128)(2,1)S(1)}, u32[]{:S(2)}, u32[]{:S(2)}) collective-permute-start(bf16[32,128]{1,0:T(8,128)(2,1)} %shard_map.73.refs_0_.refs_2_), channel_id=1, source_target_pairs={{0,1},{1,0},{2,3},{3,2},{4,5},{5,4},{6,7},{7,6},{8,9},{9,8},{10,11... | collective-permute-start | bytes 24584 | tf_op jit(solution)/shard_map/ppermute | solution.py:407
  9.4 0.0 copy-start.2
  9.4 0.7 copy-done.2
  10.2 8.3 %shard_map.75 = (bf16[4,2048,768]{2,1,0:T(8,128)(2,1)S(1)}, bf16[4,2048,768]{2,1,0:T(8,128)(2,1)S(1)}, f32[8,128]{1,0:T(8,128)S(1)}) custom-call(bf16[4,2048,768]{2,1,0:T(8,128)(2,1)} %refs_0_.2, bf16[4,2048,768]{2,1,0:T(8,128)(2,1)} %refs_1_.1, bf16[32,128]{1,0:T(8,128)(2,1)S(1)} %copy-done.2), custom_call_target="tpu_custom_call" | custom-call | bytes 50331648 | tf_op jit(solution)/shard_map/pallas_call | solution.py:179
  18.5 0.0 copy-start.1
  18.5 0.0 collective-permute-done.2.refs_3_
  18.5 0.0 collective-permute-done.1.refs_2_
  18.5 0.0 collective-permute-done.refs_1_
  18.5 0.4 shard_map.74
  19.0 0.0 collective-permute-done.3.x_ref.refs_1_
  19.0 0.0 collective-permute-done.4.y_ref.refs_0_
  19.0 0.6 collective-permute-start.8
  19.6 0.1 collective-permute-start.7
  19.7 0.0 copy-done
  19.7 2.0 %collective-permute-start.6 = (bf16[128,2048]{1,0:T(8,128)(2,1)S(1)}, bf16[128,2048]{1,0:T(8,128)(2,1)S(1)}, u32[]{:S(2)}, u32[]{:S(2)}) collective-permute-start(bf16[128,2048]{1,0:T(8,128)(2,1)S(1)} %shard_map.77.refs_2_.refs_0_), channel_id=1, source_target_pairs={{0,2},{1,3},{2,0},{3,1},{4,6},{5,7},{6,4},{7,5},{8,10},{9,11},{10,... | collective-permute-start | bytes 1572872 | tf_op jit(solution)/shard_map/ppermute | solution.py:407
  21.8 1.5 %collective-permute-start.5 = (bf16[128,2048]{1,0:T(8,128)(2,1)S(1)}, bf16[128,2048]{1,0:T(8,128)(2,1)S(1)}, u32[]{:S(2)}, u32[]{:S(2)}) collective-permute-start(bf16[128,2048]{1,0:T(8,128)(2,1)S(1)} %shard_map.77.refs_2_.refs_0_), channel_id=1, source_target_pairs={{0,1},{1,0},{2,3},{3,2},{4,5},{5,4},{6,7},{7,6},{8,9},{9,8},{10,11... | collective-permute-start | bytes 1572872 | tf_op jit(solution)/shard_map/ppermute | solution.py:407
  23.2 0.0 copy-done.1
  23.2 0.7 shard_map.78.first_ref
  24.0 4.4 %collective-permute-done.8.refs_2_ = bf16[64,2048]{1,0:T(8,128)(2,1)S(1)} collective-permute-done((bf16[64,2048]{1,0:T(8,128)(2,1)S(1)}, bf16[64,2048]{1,0:T(8,128)(2,1)S(1)}, u32[]{:S(2)}, u32[]{:S(2)}) %collective-permute-start.8) | collective-permute-done | bytes 262176 | tf_op jit(solution)/shard_map/ppermute | solution.py:407
  28.3 0.5 collective-permute-done.7.refs_1_
  28.9 9.8 %shard_map.79 = (f32[4,768,256]{2,1,0:T(8,128)S(1)}, f32[4,768,256]{2,1,0:T(8,128)S(1)}) custom-call(bf16[2,512,256]{2,1,0:T(8,128)(2,1)S(1)} %get-tuple-element.34.pick_ref, f32[4,8,256]{2,1,0:T(8,128)S(1)} %get-tuple-element.35.gate_ref, bf16[4,128,2048]{2,1,0:T(8,128)(2,1)S(1)} %shard_map.78.first_ref, ...), custom_call_target="tpu_custom_call" | custom-call | flops 6442450944 | bytes 25165824 | tf_op jit(solution)/shard_map/pallas_call | solution.py:277
  38.6 0.0 collective-permute-done.6.y_ref.refs_0_
  38.7 0.0 collective-permute-done.5.x_ref.refs_1_
  38.7 1.6 %collective-permute-start.10 = (bf16[64,2048]{1,0:T(8,128)(2,1)S(1)}, bf16[64,2048]{1,0:T(8,128)(2,1)S(1)}, u32[]{:S(2)}, u32[]{:S(2)}) collective-permute-start(bf16[64,2048]{1,0:T(8,128)(2,1)S(1)} %get-tuple-element.41), channel_id=1, source_target_pairs={{0,1},{1,0},{2,3},{3,2},{4,5},{5,4},{6,7},{7,6},{8,9},{9,8},{10,11... | collective-permute-start | bytes 786440 | tf_op jit(solution)/shard_map/ppermute | solution.py:407
  40.3 0.5 collective-permute-start.9
  40.8 0.9 %shard_map.81.first_ref = bf16[4,2048,128]{2,1,0:T(8,128)(2,1)S(1)} custom-call(bf16[2,256,512]{2,1,0:T(8,128)(2,1)S(1)} %get-tuple-element.31.refs_1_.place_ref, bf16[128,2048]{1,0:T(8,128)(2,1)S(1)} %shard_map.77.refs_2_.refs_0_, bf16[128,2048]{1,0:T(8,128)(2,1)S(1)} %collective-permute-done.5.x_ref.refs_1_, bf16[64,2048]{1,0:T(8,128)(2,1)S(1)} %get-tuple-element.40.refs_2_), custom_call_target="tpu_custom_call" | custom-call | tf_op jit(solution)/shard_map/pallas_call | solution.py:215
  41.7 3.4 %collective-permute-done.10.refs_2_ = bf16[64,2048]{1,0:T(8,128)(2,1)S(1)} collective-permute-done((bf16[64,2048]{1,0:T(8,128)(2,1)S(1)}, bf16[64,2048]{1,0:T(8,128)(2,1)S(1)}, u32[]{:S(2)}, u32[]{:S(2)}) %collective-permute-start.10) | collective-permute-done | bytes 262176 | tf_op jit(solution)/shard_map/ppermute | solution.py:407
  45.1 1.5 %collective-permute-done.9.refs_1_ = bf16[64,2048]{1,0:T(8,128)(2,1)S(1)} collective-permute-done((bf16[64,2048]{1,0:T(8,128)(2,1)S(1)}, bf16[64,2048]{1,0:T(8,128)(2,1)S(1)}, u32[]{:S(2)}, u32[]{:S(2)}) %collective-permute-start.9) | collective-permute-done | bytes 262176 | tf_op jit(solution)/shard_map/ppermute | solution.py:407
  46.6 9.8 %shard_map.82 = (bf16[4,768,256]{2,1,0:T(8,128)(2,1)S(1)}, bf16[4,768,256]{2,1,0:T(8,128)(2,1)S(1)}) custom-call(bf16[2,256,512]{2,1,0:T(8,128)(2,1)S(1)} %get-tuple-element.31.refs_1_.place_ref, bf16[4,2048,128]{2,1,0:T(8,128)(2,1)S(1)} %shard_map.81.first_ref, bf16[128,2048]{1,0:T(8,128)(2,1)S(1)} %collective-permute-done.6.y_ref.refs_0_, ...), custom_call_target="tpu_custom_call" | custom-call | flops 3221225472 | bytes 12582912 | tf_op jit(solution)/shard_map/pallas_call | solution.py:330
  56.4 2.1 %shard_map.86 = (f32[1,128,512]{2,1,0:T(8,128)S(1)}, bf16[2,128,512]{2,1,0:T(8,128)(2,1)S(1)}, bf16[1,128,512]{2,1,0:T(8,128)(2,1)S(1)}) custom-call(bf16[2,256,512]{2,1,0:T(8,128)(2,1)S(1)} %get-tuple-element.31.refs_1_.place_ref, bf16[4,768,256]{2,1,0:T(8,128)(2,1)S(1)} %get-tuple-element.43.hg_ref, bf16[4,768,256]{2,1,0:T(8,128)(2,1)S(1)} %get-tuple-element.44.hu_ref, ...), custom_call_target="tpu_custom_call" | custom-call | flops 402653184 | bytes 1572864 | tf_op jit(solution)/shard_map/pallas_call | solution.py:375
  58.6 0.6 collective-permute-start.17
  59.1 2.1 %shard_map.85 = (f32[1,128,512]{2,1,0:T(8,128)S(1)}, bf16[2,128,512]{2,1,0:T(8,128)(2,1)S(1)}, bf16[1,128,512]{2,1,0:T(8,128)(2,1)S(1)}) custom-call(bf16[2,256,512]{2,1,0:T(8,128)(2,1)S(1)} %get-tuple-element.31.refs_1_.place_ref, bf16[4,768,256]{2,1,0:T(8,128)(2,1)S(1)} %get-tuple-element.43.hg_ref, bf16[4,768,256]{2,1,0:T(8,128)(2,1)S(1)} %get-tuple-element.44.hu_ref, ...), custom_call_target="tpu_custom_call" | custom-call | flops 402653184 | bytes 1572864 | tf_op jit(solution)/shard_map/pallas_call | solution.py:375
  61.3 0.1 collective-permute-start.15
  61.4 2.1 %shard_map.84 = (f32[1,128,512]{2,1,0:T(8,128)S(1)}, bf16[2,128,512]{2,1,0:T(8,128)(2,1)S(1)}, bf16[1,128,512]{2,1,0:T(8,128)(2,1)S(1)}) custom-call(bf16[2,256,512]{2,1,0:T(8,128)(2,1)S(1)} %get-tuple-element.31.refs_1_.place_ref, bf16[4,768,256]{2,1,0:T(8,128)(2,1)S(1)} %get-tuple-element.43.hg_ref, bf16[4,768,256]{2,1,0:T(8,128)(2,1)S(1)} %get-tuple-element.44.hu_ref, ...), custom_call_target="tpu_custom_call" | custom-call | flops 402653184 | bytes 1572864 | tf_op jit(solution)/shard_map/pallas_call | solution.py:375
  63.6 2.0 %collective-permute-start.13 = (bf16[2,128,512]{2,1,0:T(8,128)(2,1)S(1)}, bf16[2,128,512]{2,1,0:T(8,128)(2,1)S(1)}, u32[]{:S(2)}, u32[]{:S(2)}) collective-permute-start(bf16[2,128,512]{2,1,0:T(8,128)(2,1)S(1)} %get-tuple-element.49), channel_id=1, source_target_pairs={{0,2},{1,3},{2,0},{3,1},{4,6},{5,7},{6,4},{7,5},{8,10},{9,11},{10,... | collective-permute-start | bytes 786440 | tf_op jit(solution)/shard_map/ppermute | solution.py:407
  65.6 2.1 %shard_map.83 = (f32[1,128,512]{2,1,0:T(8,128)S(1)}, bf16[2,128,512]{2,1,0:T(8,128)(2,1)S(1)}, bf16[1,128,512]{2,1,0:T(8,128)(2,1)S(1)}) custom-call(bf16[2,256,512]{2,1,0:T(8,128)(2,1)S(1)} %get-tuple-element.31.refs_1_.place_ref, bf16[4,768,256]{2,1,0:T(8,128)(2,1)S(1)} %get-tuple-element.43.hg_ref, bf16[4,768,256]{2,1,0:T(8,128)(2,1)S(1)} %get-tuple-element.44.hu_ref, ...), custom_call_target="tpu_custom_call" | custom-call | flops 402653184 | bytes 1572864 | tf_op jit(solution)/shard_map/pallas_call | solution.py:375
  67.8 1.6 %collective-permute-start.11 = (bf16[2,128,512]{2,1,0:T(8,128)(2,1)S(1)}, bf16[2,128,512]{2,1,0:T(8,128)(2,1)S(1)}, u32[]{:S(2)}, u32[]{:S(2)}) collective-permute-start(bf16[2,128,512]{2,1,0:T(8,128)(2,1)S(1)} %get-tuple-element.46), channel_id=1, source_target_pairs={{0,1},{1,0},{2,3},{3,2},{4,5},{5,4},{6,7},{7,6},{8,9},{9,8},{10,11... | collective-permute-start | bytes 786440 | tf_op jit(solution)/shard_map/ppermute | solution.py:407
  69.3 0.0 collective-permute-done.17
  69.4 0.6 collective-permute-start.18
  70.0 0.6 collective-permute-done.15
  70.6 1.7 %collective-permute-start.16 = (bf16[1,128,512]{2,1,0:T(8,128)(2,1)S(1)}, bf16[1,128,512]{2,1,0:T(8,128)(2,1)S(1)}, u32[]{:S(2)}, u32[]{:S(2)}) collective-permute-start(bf16[1,128,512]{2,1,0:T(8,128)(2,1)S(1)} %add_convert_fusion.1), channel_id=1, source_target_pairs={{0,2},{1,3},{2,0},{3,1},{4,6},{5,7},{6,4},{7,5},{8,10},{9,11},{10,... | collective-permute-start | bytes 393224 | tf_op jit(solution)/shard_map/ppermute | solution.py:407
  72.2 0.0 collective-permute-done.13
  72.3 0.5 collective-permute-start.14
  72.8 2.4 %collective-permute-done.11 = bf16[2,128,512]{2,1,0:T(8,128)(2,1)S(1)} collective-permute-done((bf16[2,128,512]{2,1,0:T(8,128)(2,1)S(1)}, bf16[2,128,512]{2,1,0:T(8,128)(2,1)S(1)}, u32[]{:S(2)}, u32[]{:S(2)}) %collective-permute-start.11) | collective-permute-done | bytes 262176 | tf_op jit(solution)/shard_map/ppermute | solution.py:407
  75.2 0.7 collective-permute-start.12
  76.0 0.6 collective-permute-done.18.refs_11_
  76.6 0.0 collective-permute-done.16.refs_8_
  76.6 1.4 %collective-permute-done.14.refs_5_ = bf16[1,128,512]{2,1,0:T(8,128)(2,1)S(1)} collective-permute-done((bf16[1,128,512]{2,1,0:T(8,128)(2,1)S(1)}, bf16[1,128,512]{2,1,0:T(8,128)(2,1)S(1)}, u32[]{:S(2)}, u32[]{:S(2)}) %collective-permute-start.14) | collective-permute-done | bytes 131104 | tf_op jit(solution)/shard_map/ppermute | solution.py:407
  78.0 2.3 %collective-permute-done.12.refs_2_ = bf16[1,128,512]{2,1,0:T(8,128)(2,1)S(1)} collective-permute-done((bf16[1,128,512]{2,1,0:T(8,128)(2,1)S(1)}, bf16[1,128,512]{2,1,0:T(8,128)(2,1)S(1)}, u32[]{:S(2)}, u32[]{:S(2)}) %collective-permute-start.12) | collective-permute-done | bytes 131104 | tf_op jit(solution)/shard_map/ppermute | solution.py:407
  80.3 1.0 %shard_map.87 = bf16[128,2048]{1,0:T(8,128)(2,1)} custom-call(f32[1,128,512]{2,1,0:T(8,128)S(1)} %get-tuple-element.45.refs_0_, bf16[1,128,512]{2,1,0:T(8,128)(2,1)S(1)} %slice.32.refs_1_, bf16[1,128,512]{2,1,0:T(8,128)(2,1)S(1)} %collective-permute-done.12.refs_2_, f32[1,128,512]{2,1,0:T(8,128)S(1)} %get-tuple-element.48.refs_3_, ...), custom_call_target="tpu_custom_call" | custom-call | tf_op jit(solution)/shard_map/pallas_call | solution.py:445
  (11 shorter events, 0.3 us)
Async XLA Ops:
  0.0 19.0 %collective-permute-start.3 = (bf16[128,2048]{1,0:T(8,128)(2,1)}, bf16[128,2048]{1,0:T(8,128)(2,1)S(1)}, u32[]{:S(2)}, u32[]{:S(2)}) collective-permute-start(bf16[128,2048]{1,0:T(8,128)(2,1)} %refs_0_.3), channel_id=1, source_target_pairs={{0,1},{1,0},{2,3},{3,2},{4,5},{5,4},{6,7},{7,6},{8,9},{9,8},{10,11... | collective-permute-start | bytes 1572872 | tf_op jit(solution)/shard_map/ppermute | solution.py:407
  2.9 16.0 %collective-permute-start.4 = (bf16[128,2048]{1,0:T(8,128)(2,1)}, bf16[128,2048]{1,0:T(8,128)(2,1)S(1)}, u32[]{:S(2)}, u32[]{:S(2)}) collective-permute-start(bf16[128,2048]{1,0:T(8,128)(2,1)} %refs_0_.3), channel_id=1, source_target_pairs={{0,2},{1,3},{2,0},{3,1},{4,6},{5,7},{6,4},{7,5},{8,10},{9,11},{10,... | collective-permute-start | bytes 1572872 | tf_op jit(solution)/shard_map/ppermute | solution.py:407
  5.9 13.7 %copy-start = (bf16[128,2048]{1,0:T(8,128)(2,1)S(1)}, bf16[128,2048]{1,0:T(8,128)(2,1)}, u32[]{:S(2)}) copy-start(bf16[128,2048]{1,0:T(8,128)(2,1)} %array_ref.1) | copy-start | bytes 1572868
  5.9 12.5 %collective-permute-start.2 = (bf16[32,128]{1,0:T(8,128)(2,1)}, bf16[32,128]{1,0:T(8,128)(2,1)S(1)}, u32[]{:S(2)}, u32[]{:S(2)}) collective-permute-start(bf16[32,128]{1,0:T(8,128)(2,1)} %shard_map.73.refs_0_.refs_2_), channel_id=1, source_target_pairs={{0,3},{1,2},{2,1},{3,0},{4,7},{5,6},{6,5},{7,4},{8,11},{9,10},{10,... | collective-permute-start | bytes 24584 | tf_op jit(solution)/shard_map/ppermute | solution.py:407
  6.0 12.6 %collective-permute-start.1 = (bf16[32,128]{1,0:T(8,128)(2,1)}, bf16[32,128]{1,0:T(8,128)(2,1)S(1)}, u32[]{:S(2)}, u32[]{:S(2)}) collective-permute-start(bf16[32,128]{1,0:T(8,128)(2,1)} %shard_map.73.refs_0_.refs_2_), channel_id=1, source_target_pairs={{0,2},{1,3},{2,0},{3,1},{4,6},{5,7},{6,4},{7,5},{8,10},{9,11},{10,... | collective-permute-start | bytes 24584 | tf_op jit(solution)/shard_map/ppermute | solution.py:407
  7.9 10.6 %collective-permute-start = (bf16[32,128]{1,0:T(8,128)(2,1)}, bf16[32,128]{1,0:T(8,128)(2,1)S(1)}, u32[]{:S(2)}, u32[]{:S(2)}) collective-permute-start(bf16[32,128]{1,0:T(8,128)(2,1)} %shard_map.73.refs_0_.refs_2_), channel_id=1, source_target_pairs={{0,1},{1,0},{2,3},{3,2},{4,5},{5,4},{6,7},{7,6},{8,9},{9,8},{10,11... | collective-permute-start | bytes 24584 | tf_op jit(solution)/shard_map/ppermute | solution.py:407
  9.4 0.7 copy-start.2
  18.5 4.8 %copy-start.1 = (bf16[128,2048]{1,0:T(8,128)(2,1)S(1)}, bf16[128,2048]{1,0:T(8,128)(2,1)}, u32[]{:S(2)}) copy-start(bf16[128,2048]{1,0:T(8,128)(2,1)} %refs_0_.3) | copy-start | bytes 1572868
  19.0 9.3 %collective-permute-start.8 = (bf16[64,2048]{1,0:T(8,128)(2,1)S(1)}, bf16[64,2048]{1,0:T(8,128)(2,1)S(1)}, u32[]{:S(2)}, u32[]{:S(2)}) collective-permute-start(bf16[64,2048]{1,0:T(8,128)(2,1)S(1)} %get-tuple-element.36), channel_id=1, source_target_pairs={{0,1},{1,0},{2,3},{3,2},{4,5},{5,4},{6,7},{7,6},{8,9},{9,8},{10,11... | collective-permute-start | bytes 786440 | tf_op jit(solution)/shard_map/ppermute | solution.py:407
  19.6 9.2 %collective-permute-start.7 = (bf16[64,2048]{1,0:T(8,128)(2,1)S(1)}, bf16[64,2048]{1,0:T(8,128)(2,1)S(1)}, u32[]{:S(2)}, u32[]{:S(2)}) collective-permute-start(bf16[64,2048]{1,0:T(8,128)(2,1)S(1)} %get-tuple-element.33._), channel_id=1, source_target_pairs={{0,2},{1,3},{2,0},{3,1},{4,6},{5,7},{6,4},{7,5},{8,10},{9,11},{10,... | collective-permute-start | bytes 786440 | tf_op jit(solution)/shard_map/ppermute | solution.py:407
  19.7 18.9 %collective-permute-start.6 = (bf16[128,2048]{1,0:T(8,128)(2,1)S(1)}, bf16[128,2048]{1,0:T(8,128)(2,1)S(1)}, u32[]{:S(2)}, u32[]{:S(2)}) collective-permute-start(bf16[128,2048]{1,0:T(8,128)(2,1)S(1)} %shard_map.77.refs_2_.refs_0_), channel_id=1, source_target_pairs={{0,2},{1,3},{2,0},{3,1},{4,6},{5,7},{6,4},{7,5},{8,10},{9,11},{10,... | collective-permute-start | bytes 1572872 | tf_op jit(solution)/shard_map/ppermute | solution.py:407
  21.8 16.9 %collective-permute-start.5 = (bf16[128,2048]{1,0:T(8,128)(2,1)S(1)}, bf16[128,2048]{1,0:T(8,128)(2,1)S(1)}, u32[]{:S(2)}, u32[]{:S(2)}) collective-permute-start(bf16[128,2048]{1,0:T(8,128)(2,1)S(1)} %shard_map.77.refs_2_.refs_0_), channel_id=1, source_target_pairs={{0,1},{1,0},{2,3},{3,2},{4,5},{5,4},{6,7},{7,6},{8,9},{9,8},{10,11... | collective-permute-start | bytes 1572872 | tf_op jit(solution)/shard_map/ppermute | solution.py:407
  38.7 6.4 %collective-permute-start.10 = (bf16[64,2048]{1,0:T(8,128)(2,1)S(1)}, bf16[64,2048]{1,0:T(8,128)(2,1)S(1)}, u32[]{:S(2)}, u32[]{:S(2)}) collective-permute-start(bf16[64,2048]{1,0:T(8,128)(2,1)S(1)} %get-tuple-element.41), channel_id=1, source_target_pairs={{0,1},{1,0},{2,3},{3,2},{4,5},{5,4},{6,7},{7,6},{8,9},{9,8},{10,11... | collective-permute-start | bytes 786440 | tf_op jit(solution)/shard_map/ppermute | solution.py:407
  40.3 6.4 %collective-permute-start.9 = (bf16[64,2048]{1,0:T(8,128)(2,1)S(1)}, bf16[64,2048]{1,0:T(8,128)(2,1)S(1)}, u32[]{:S(2)}, u32[]{:S(2)}) collective-permute-start(bf16[64,2048]{1,0:T(8,128)(2,1)S(1)} %get-tuple-element.40.refs_2_), channel_id=1, source_target_pairs={{0,2},{1,3},{2,0},{3,1},{4,6},{5,7},{6,4},{7,5},{8,10},{9,11},{10,... | collective-permute-start | bytes 786440 | tf_op jit(solution)/shard_map/ppermute | solution.py:407
  58.6 10.8 %collective-permute-start.17 = (bf16[2,128,512]{2,1,0:T(8,128)(2,1)S(1)}, bf16[2,128,512]{2,1,0:T(8,128)(2,1)S(1)}, u32[]{:S(2)}, u32[]{:S(2)}) collective-permute-start(bf16[2,128,512]{2,1,0:T(8,128)(2,1)S(1)} %get-tuple-element.55), channel_id=1, source_target_pairs={{0,2},{1,3},{2,0},{3,1},{4,6},{5,7},{6,4},{7,5},{8,10},{9,11},{10,... | collective-permute-start | bytes 786440 | tf_op jit(solution)/shard_map/ppermute | solution.py:407
  61.3 9.2 %collective-permute-start.15 = (bf16[2,128,512]{2,1,0:T(8,128)(2,1)S(1)}, bf16[2,128,512]{2,1,0:T(8,128)(2,1)S(1)}, u32[]{:S(2)}, u32[]{:S(2)}) collective-permute-start(bf16[2,128,512]{2,1,0:T(8,128)(2,1)S(1)} %get-tuple-element.52), channel_id=1, source_target_pairs={{0,1},{1,0},{2,3},{3,2},{4,5},{5,4},{6,7},{7,6},{8,9},{9,8},{10,11... | collective-permute-start | bytes 786440 | tf_op jit(solution)/shard_map/ppermute | solution.py:407
  63.6 8.6 %collective-permute-start.13 = (bf16[2,128,512]{2,1,0:T(8,128)(2,1)S(1)}, bf16[2,128,512]{2,1,0:T(8,128)(2,1)S(1)}, u32[]{:S(2)}, u32[]{:S(2)}) collective-permute-start(bf16[2,128,512]{2,1,0:T(8,128)(2,1)S(1)} %get-tuple-element.49), channel_id=1, source_target_pairs={{0,2},{1,3},{2,0},{3,1},{4,6},{5,7},{6,4},{7,5},{8,10},{9,11},{10,... | collective-permute-start | bytes 786440 | tf_op jit(solution)/shard_map/ppermute | solution.py:407
  67.8 7.4 %collective-permute-start.11 = (bf16[2,128,512]{2,1,0:T(8,128)(2,1)S(1)}, bf16[2,128,512]{2,1,0:T(8,128)(2,1)S(1)}, u32[]{:S(2)}, u32[]{:S(2)}) collective-permute-start(bf16[2,128,512]{2,1,0:T(8,128)(2,1)S(1)} %get-tuple-element.46), channel_id=1, source_target_pairs={{0,1},{1,0},{2,3},{3,2},{4,5},{5,4},{6,7},{7,6},{8,9},{9,8},{10,11... | collective-permute-start | bytes 786440 | tf_op jit(solution)/shard_map/ppermute | solution.py:407
  69.4 7.2 %collective-permute-start.18 = (bf16[1,128,512]{2,1,0:T(8,128)(2,1)S(1)}, bf16[1,128,512]{2,1,0:T(8,128)(2,1)S(1)}, u32[]{:S(2)}, u32[]{:S(2)}) collective-permute-start(bf16[1,128,512]{2,1,0:T(8,128)(2,1)S(1)} %add_convert_fusion), channel_id=1, source_target_pairs={{0,1},{1,0},{2,3},{3,2},{4,5},{5,4},{6,7},{7,6},{8,9},{9,8},{10,11... | collective-permute-start | bytes 393224 | tf_op jit(solution)/shard_map/ppermute | solution.py:407
  70.6 6.0 %collective-permute-start.16 = (bf16[1,128,512]{2,1,0:T(8,128)(2,1)S(1)}, bf16[1,128,512]{2,1,0:T(8,128)(2,1)S(1)}, u32[]{:S(2)}, u32[]{:S(2)}) collective-permute-start(bf16[1,128,512]{2,1,0:T(8,128)(2,1)S(1)} %add_convert_fusion.1), channel_id=1, source_target_pairs={{0,2},{1,3},{2,0},{3,1},{4,6},{5,7},{6,4},{7,5},{8,10},{9,11},{10,... | collective-permute-start | bytes 393224 | tf_op jit(solution)/shard_map/ppermute | solution.py:407
  72.3 5.7 %collective-permute-start.14 = (bf16[1,128,512]{2,1,0:T(8,128)(2,1)S(1)}, bf16[1,128,512]{2,1,0:T(8,128)(2,1)S(1)}, u32[]{:S(2)}, u32[]{:S(2)}) collective-permute-start(bf16[1,128,512]{2,1,0:T(8,128)(2,1)S(1)} %add_convert_fusion.2), channel_id=1, source_target_pairs={{0,1},{1,0},{2,3},{3,2},{4,5},{5,4},{6,7},{7,6},{8,9},{9,8},{10,11... | collective-permute-start | bytes 393224 | tf_op jit(solution)/shard_map/ppermute | solution.py:407
  75.2 5.0 %collective-permute-start.12 = (bf16[1,128,512]{2,1,0:T(8,128)(2,1)S(1)}, bf16[1,128,512]{2,1,0:T(8,128)(2,1)S(1)}, u32[]{:S(2)}, u32[]{:S(2)}) collective-permute-start(bf16[1,128,512]{2,1,0:T(8,128)(2,1)S(1)} %add_convert_fusion.3), channel_id=1, source_target_pairs={{0,2},{1,3},{2,0},{3,1},{4,6},{5,7},{6,4},{7,5},{8,10},{9,11},{10,... | collective-permute-start | bytes 393224 | tf_op jit(solution)/shard_map/ppermute | solution.py:407

commit v13 on v12

--- a/solution.py
+++ b/solution.py
@@ -300,7 +300,7 @@
 
     def fetch(e, i):
         part = pl.ds(i * cols, cols)
-        slot = lax.rem(e, held)
+        slot = e % held
         return pltpu.make_async_copy(wd_ref.at[e, part], weight.at[slot, part], sems.at[slot, i])
 
     for e in range(held):
@@ -308,18 +308,16 @@
             fetch(e, i).start()
     gather_columns(local, place_ref, token_refs, 1, gs)
 
-    @pl.loop(0, local)
-    def _(e):
+    for e in range(local):
         rows = jnp.concatenate([first_ref[e], gs[e]], axis=1)
         for i in range(2):
             part = slice(i * cols, (i + 1) * cols)
             fetch(e, i).wait()
-            back = dot(weight[lax.rem(e, held), part, :], rows)
+            back = dot(weight[e % held, part, :], rows)
             hg_ref[e, part, :] = (back * a_ref[e, part, :]).astype(jnp.bfloat16)
             hu_ref[e, part, :] = (back * b_ref[e, part, :]).astype(jnp.bfloat16)
 
-            @pl.when(e + held < local)
-            def _():
+            if e + held < local:
                 fetch(e + held, i).start()
 
 

time: 81.5 us -> 81.5 us (level)
  no operation moved by 1% of the time
where the time goes in v13:
time: 81.5 us; the launch traced here: 81.2 us
  Pallas kernels  41.1 us (50%)
  starting transfers between devices  21.9 us (27%)
  waiting for transfers between devices  17.1 us (21%)
    ppermute x19, starting transfers between devices, swap(): return lax.ppermute(array, axis, [(i, i ^ k) for i in range(n)])  21.9 us
    ppermute x19, waiting for transfers between devices, swap(): return lax.ppermute(array, axis, [(i, i ^ k) for i in range(n)])  17.1 us
    pallas_call x1, Pallas kernels, pre(): pl.pallas_call(functools.partial(pre_kernel, local, sizes(tokens)), in_sp...  9.77 us
    pallas_call x1, Pallas kernels, back(): pl.pallas_call(functools.partial(back_kernel, local, sizes(tokens)), in_s...  9.77 us
    pallas_call x4, Pallas kernels, partial_sums(): pl.pallas_call(functools.partial(out_kernel, n, local, orders, chunk), ou...  8.58 us
    pallas_call x1, Pallas kernels, load(): pl.pallas_call(functools.partial(load_kernel, count), in_specs=[OUTSIDE]...  8.3 us
  transfers between devices with their start and end apart: 19, of which 9 were waited for; matrix products, arithmetic and copies ran while one was open for 0% of the time, Pallas kernels for 35%

profile of v13, /device:TPU:0, one launch (start us, length us, event | category | flops | bytes accessed | tf_op | source)
XLA Modules:
  0.0 81.2 jit_solution(6442261636211216691)
XLA Ops:
  0.0 2.9 %collective-permute-start.3 = (bf16[128,2048]{1,0:T(8,128)(2,1)}, bf16[128,2048]{1,0:T(8,128)(2,1)S(1)}, u32[]{:S(2)}, u32[]{:S(2)}) collective-permute-start(bf16[128,2048]{1,0:T(8,128)(2,1)} %refs_0_.3), channel_id=1, source_target_pairs={{0,1},{1,0},{2,3},{3,2},{4,5},{5,4},{6,7},{7,6},{8,9},{9,8},{10,11... | collective-permute-start | bytes 1572872 | tf_op jit(solution)/shard_map/ppermute | solution.py:405
  2.9 1.5 %collective-permute-start.4 = (bf16[128,2048]{1,0:T(8,128)(2,1)}, bf16[128,2048]{1,0:T(8,128)(2,1)S(1)}, u32[]{:S(2)}, u32[]{:S(2)}) collective-permute-start(bf16[128,2048]{1,0:T(8,128)(2,1)} %refs_0_.3), channel_id=1, source_target_pairs={{0,2},{1,3},{2,0},{3,1},{4,6},{5,7},{6,4},{7,5},{8,10},{9,11},{10,... | collective-permute-start | bytes 1572872 | tf_op jit(solution)/shard_map/ppermute | solution.py:405
  4.5 1.5 %shard_map.73.refs_0_.refs_2_ = bf16[32,128]{1,0:T(8,128)(2,1)} custom-call(s32[8,128]{1,0:T(8,128)} %bitcast.2, bf16[8,128]{1,0:T(8,128)(2,1)} %bitcast.3), custom_call_target="tpu_custom_call" | custom-call | tf_op jit(solution)/shard_map/pallas_call | solution.py:56
  5.9 0.0 copy-start
  5.9 0.0 collective-permute-start.2
  6.0 2.0 %collective-permute-start.1 = (bf16[32,128]{1,0:T(8,128)(2,1)}, bf16[32,128]{1,0:T(8,128)(2,1)S(1)}, u32[]{:S(2)}, u32[]{:S(2)}) collective-permute-start(bf16[32,128]{1,0:T(8,128)(2,1)} %shard_map.73.refs_0_.refs_2_), channel_id=1, source_target_pairs={{0,2},{1,3},{2,0},{3,1},{4,6},{5,7},{6,4},{7,5},{8,10},{9,11},{10,... | collective-permute-start | bytes 24584 | tf_op jit(solution)/shard_map/ppermute | solution.py:405
  7.9 1.5 %collective-permute-start = (bf16[32,128]{1,0:T(8,128)(2,1)}, bf16[32,128]{1,0:T(8,128)(2,1)S(1)}, u32[]{:S(2)}, u32[]{:S(2)}) collective-permute-start(bf16[32,128]{1,0:T(8,128)(2,1)} %shard_map.73.refs_0_.refs_2_), channel_id=1, source_target_pairs={{0,1},{1,0},{2,3},{3,2},{4,5},{5,4},{6,7},{7,6},{8,9},{9,8},{10,11... | collective-permute-start | bytes 24584 | tf_op jit(solution)/shard_map/ppermute | solution.py:405
  9.4 0.0 copy-start.2
  9.4 0.7 copy-done.2
  10.2 8.3 %shard_map.75 = (bf16[4,2048,768]{2,1,0:T(8,128)(2,1)S(1)}, bf16[4,2048,768]{2,1,0:T(8,128)(2,1)S(1)}, f32[8,128]{1,0:T(8,128)S(1)}) custom-call(bf16[4,2048,768]{2,1,0:T(8,128)(2,1)} %refs_0_.2, bf16[4,2048,768]{2,1,0:T(8,128)(2,1)} %refs_1_.1, bf16[32,128]{1,0:T(8,128)(2,1)S(1)} %copy-done.2), custom_call_target="tpu_custom_call" | custom-call | bytes 50331648 | tf_op jit(solution)/shard_map/pallas_call | solution.py:179
  18.5 0.0 copy-start.1
  18.5 0.0 collective-permute-done.2.refs_3_
  18.5 0.0 collective-permute-done.1.refs_2_
  18.5 0.0 collective-permute-done.refs_1_
  18.5 0.4 shard_map.74
  19.0 0.0 collective-permute-done.3.x_ref.refs_1_
  19.0 0.0 collective-permute-done.4.y_ref.refs_0_
  19.0 0.6 collective-permute-start.8
  19.6 0.1 collective-permute-start.7
  19.7 0.0 copy-done
  19.7 2.0 %collective-permute-start.6 = (bf16[128,2048]{1,0:T(8,128)(2,1)S(1)}, bf16[128,2048]{1,0:T(8,128)(2,1)S(1)}, u32[]{:S(2)}, u32[]{:S(2)}) collective-permute-start(bf16[128,2048]{1,0:T(8,128)(2,1)S(1)} %shard_map.77.refs_2_.refs_0_), channel_id=1, source_target_pairs={{0,2},{1,3},{2,0},{3,1},{4,6},{5,7},{6,4},{7,5},{8,10},{9,11},{10,... | collective-permute-start | bytes 1572872 | tf_op jit(solution)/shard_map/ppermute | solution.py:405
  21.8 1.5 %collective-permute-start.5 = (bf16[128,2048]{1,0:T(8,128)(2,1)S(1)}, bf16[128,2048]{1,0:T(8,128)(2,1)S(1)}, u32[]{:S(2)}, u32[]{:S(2)}) collective-permute-start(bf16[128,2048]{1,0:T(8,128)(2,1)S(1)} %shard_map.77.refs_2_.refs_0_), channel_id=1, source_target_pairs={{0,1},{1,0},{2,3},{3,2},{4,5},{5,4},{6,7},{7,6},{8,9},{9,8},{10,11... | collective-permute-start | bytes 1572872 | tf_op jit(solution)/shard_map/ppermute | solution.py:405
  23.2 0.0 copy-done.1
  23.2 0.7 shard_map.78.first_ref
  24.0 4.4 %collective-permute-done.8.refs_2_ = bf16[64,2048]{1,0:T(8,128)(2,1)S(1)} collective-permute-done((bf16[64,2048]{1,0:T(8,128)(2,1)S(1)}, bf16[64,2048]{1,0:T(8,128)(2,1)S(1)}, u32[]{:S(2)}, u32[]{:S(2)}) %collective-permute-start.8) | collective-permute-done | bytes 262176 | tf_op jit(solution)/shard_map/ppermute | solution.py:405
  28.3 0.5 collective-permute-done.7.refs_1_
  28.9 9.8 %shard_map.79 = (f32[4,768,256]{2,1,0:T(8,128)S(1)}, f32[4,768,256]{2,1,0:T(8,128)S(1)}) custom-call(bf16[2,512,256]{2,1,0:T(8,128)(2,1)S(1)} %get-tuple-element.34.pick_ref, f32[4,8,256]{2,1,0:T(8,128)S(1)} %get-tuple-element.35.gate_ref, bf16[4,128,2048]{2,1,0:T(8,128)(2,1)S(1)} %shard_map.78.first_ref, ...), custom_call_target="tpu_custom_call" | custom-call | flops 6442450944 | bytes 25165824 | tf_op jit(solution)/shard_map/pallas_call | solution.py:277
  38.6 0.0 collective-permute-done.6.y_ref.refs_0_
  38.7 0.0 collective-permute-done.5.x_ref.refs_1_
  38.7 1.6 %collective-permute-start.10 = (bf16[64,2048]{1,0:T(8,128)(2,1)S(1)}, bf16[64,2048]{1,0:T(8,128)(2,1)S(1)}, u32[]{:S(2)}, u32[]{:S(2)}) collective-permute-start(bf16[64,2048]{1,0:T(8,128)(2,1)S(1)} %get-tuple-element.41), channel_id=1, source_target_pairs={{0,1},{1,0},{2,3},{3,2},{4,5},{5,4},{6,7},{7,6},{8,9},{9,8},{10,11... | collective-permute-start | bytes 786440 | tf_op jit(solution)/shard_map/ppermute | solution.py:405
  40.3 0.5 collective-permute-start.9
  40.8 0.9 %shard_map.81.first_ref = bf16[4,2048,128]{2,1,0:T(8,128)(2,1)S(1)} custom-call(bf16[2,256,512]{2,1,0:T(8,128)(2,1)S(1)} %get-tuple-element.31.refs_1_.place_ref, bf16[128,2048]{1,0:T(8,128)(2,1)S(1)} %shard_map.77.refs_2_.refs_0_, bf16[128,2048]{1,0:T(8,128)(2,1)S(1)} %collective-permute-done.5.x_ref.refs_1_, bf16[64,2048]{1,0:T(8,128)(2,1)S(1)} %get-tuple-element.40.refs_2_), custom_call_target="tpu_custom_call" | custom-call | tf_op jit(solution)/shard_map/pallas_call | solution.py:215
  41.7 3.4 %collective-permute-done.10.refs_2_ = bf16[64,2048]{1,0:T(8,128)(2,1)S(1)} collective-permute-done((bf16[64,2048]{1,0:T(8,128)(2,1)S(1)}, bf16[64,2048]{1,0:T(8,128)(2,1)S(1)}, u32[]{:S(2)}, u32[]{:S(2)}) %collective-permute-start.10) | collective-permute-done | bytes 262176 | tf_op jit(solution)/shard_map/ppermute | solution.py:405
  45.1 1.5 %collective-permute-done.9.refs_1_ = bf16[64,2048]{1,0:T(8,128)(2,1)S(1)} collective-permute-done((bf16[64,2048]{1,0:T(8,128)(2,1)S(1)}, bf16[64,2048]{1,0:T(8,128)(2,1)S(1)}, u32[]{:S(2)}, u32[]{:S(2)}) %collective-permute-start.9) | collective-permute-done | bytes 262176 | tf_op jit(solution)/shard_map/ppermute | solution.py:405
  46.6 9.8 %shard_map.82 = (bf16[4,768,256]{2,1,0:T(8,128)(2,1)S(1)}, bf16[4,768,256]{2,1,0:T(8,128)(2,1)S(1)}) custom-call(bf16[2,256,512]{2,1,0:T(8,128)(2,1)S(1)} %get-tuple-element.31.refs_1_.place_ref, bf16[4,2048,128]{2,1,0:T(8,128)(2,1)S(1)} %shard_map.81.first_ref, bf16[128,2048]{1,0:T(8,128)(2,1)S(1)} %collective-permute-done.6.y_ref.refs_0_, ...), custom_call_target="tpu_custom_call" | custom-call | flops 3221225472 | bytes 12582912 | tf_op jit(solution)/shard_map/pallas_call | solution.py:328
  56.4 2.1 %shard_map.86 = (f32[1,128,512]{2,1,0:T(8,128)S(1)}, bf16[2,128,512]{2,1,0:T(8,128)(2,1)S(1)}, bf16[1,128,512]{2,1,0:T(8,128)(2,1)S(1)}) custom-call(bf16[2,256,512]{2,1,0:T(8,128)(2,1)S(1)} %get-tuple-element.31.refs_1_.place_ref, bf16[4,768,256]{2,1,0:T(8,128)(2,1)S(1)} %get-tuple-element.43.hg_ref, bf16[4,768,256]{2,1,0:T(8,128)(2,1)S(1)} %get-tuple-element.44.hu_ref, ...), custom_call_target="tpu_custom_call" | custom-call | flops 402653184 | bytes 1572864 | tf_op jit(solution)/shard_map/pallas_call | solution.py:373
  58.6 0.6 collective-permute-start.17
  59.1 2.1 %shard_map.85 = (f32[1,128,512]{2,1,0:T(8,128)S(1)}, bf16[2,128,512]{2,1,0:T(8,128)(2,1)S(1)}, bf16[1,128,512]{2,1,0:T(8,128)(2,1)S(1)}) custom-call(bf16[2,256,512]{2,1,0:T(8,128)(2,1)S(1)} %get-tuple-element.31.refs_1_.place_ref, bf16[4,768,256]{2,1,0:T(8,128)(2,1)S(1)} %get-tuple-element.43.hg_ref, bf16[4,768,256]{2,1,0:T(8,128)(2,1)S(1)} %get-tuple-element.44.hu_ref, ...), custom_call_target="tpu_custom_call" | custom-call | flops 402653184 | bytes 1572864 | tf_op jit(solution)/shard_map/pallas_call | solution.py:373
  61.3 0.1 collective-permute-start.15
  61.4 2.1 %shard_map.84 = (f32[1,128,512]{2,1,0:T(8,128)S(1)}, bf16[2,128,512]{2,1,0:T(8,128)(2,1)S(1)}, bf16[1,128,512]{2,1,0:T(8,128)(2,1)S(1)}) custom-call(bf16[2,256,512]{2,1,0:T(8,128)(2,1)S(1)} %get-tuple-element.31.refs_1_.place_ref, bf16[4,768,256]{2,1,0:T(8,128)(2,1)S(1)} %get-tuple-element.43.hg_ref, bf16[4,768,256]{2,1,0:T(8,128)(2,1)S(1)} %get-tuple-element.44.hu_ref, ...), custom_call_target="tpu_custom_call" | custom-call | flops 402653184 | bytes 1572864 | tf_op jit(solution)/shard_map/pallas_call | solution.py:373
  63.6 2.0 %collective-permute-start.13 = (bf16[2,128,512]{2,1,0:T(8,128)(2,1)S(1)}, bf16[2,128,512]{2,1,0:T(8,128)(2,1)S(1)}, u32[]{:S(2)}, u32[]{:S(2)}) collective-permute-start(bf16[2,128,512]{2,1,0:T(8,128)(2,1)S(1)} %get-tuple-element.49), channel_id=1, source_target_pairs={{0,2},{1,3},{2,0},{3,1},{4,6},{5,7},{6,4},{7,5},{8,10},{9,11},{10,... | collective-permute-start | bytes 786440 | tf_op jit(solution)/shard_map/ppermute | solution.py:405
  65.6 2.1 %shard_map.83 = (f32[1,128,512]{2,1,0:T(8,128)S(1)}, bf16[2,128,512]{2,1,0:T(8,128)(2,1)S(1)}, bf16[1,128,512]{2,1,0:T(8,128)(2,1)S(1)}) custom-call(bf16[2,256,512]{2,1,0:T(8,128)(2,1)S(1)} %get-tuple-element.31.refs_1_.place_ref, bf16[4,768,256]{2,1,0:T(8,128)(2,1)S(1)} %get-tuple-element.43.hg_ref, bf16[4,768,256]{2,1,0:T(8,128)(2,1)S(1)} %get-tuple-element.44.hu_ref, ...), custom_call_target="tpu_custom_call" | custom-call | flops 402653184 | bytes 1572864 | tf_op jit(solution)/shard_map/pallas_call | solution.py:373
  67.8 1.6 %collective-permute-start.11 = (bf16[2,128,512]{2,1,0:T(8,128)(2,1)S(1)}, bf16[2,128,512]{2,1,0:T(8,128)(2,1)S(1)}, u32[]{:S(2)}, u32[]{:S(2)}) collective-permute-start(bf16[2,128,512]{2,1,0:T(8,128)(2,1)S(1)} %get-tuple-element.46), channel_id=1, source_target_pairs={{0,1},{1,0},{2,3},{3,2},{4,5},{5,4},{6,7},{7,6},{8,9},{9,8},{10,11... | collective-permute-start | bytes 786440 | tf_op jit(solution)/shard_map/ppermute | solution.py:405
  69.3 0.0 collective-permute-done.17
  69.4 0.6 collective-permute-start.18
  70.0 0.6 collective-permute-done.15
  70.6 1.7 %collective-permute-start.16 = (bf16[1,128,512]{2,1,0:T(8,128)(2,1)S(1)}, bf16[1,128,512]{2,1,0:T(8,128)(2,1)S(1)}, u32[]{:S(2)}, u32[]{:S(2)}) collective-permute-start(bf16[1,128,512]{2,1,0:T(8,128)(2,1)S(1)} %add_convert_fusion.1), channel_id=1, source_target_pairs={{0,2},{1,3},{2,0},{3,1},{4,6},{5,7},{6,4},{7,5},{8,10},{9,11},{10,... | collective-permute-start | bytes 393224 | tf_op jit(solution)/shard_map/ppermute | solution.py:405
  72.2 0.0 collective-permute-done.13
  72.3 0.5 collective-permute-start.14
  72.8 2.4 %collective-permute-done.11 = bf16[2,128,512]{2,1,0:T(8,128)(2,1)S(1)} collective-permute-done((bf16[2,128,512]{2,1,0:T(8,128)(2,1)S(1)}, bf16[2,128,512]{2,1,0:T(8,128)(2,1)S(1)}, u32[]{:S(2)}, u32[]{:S(2)}) %collective-permute-start.11) | collective-permute-done | bytes 262176 | tf_op jit(solution)/shard_map/ppermute | solution.py:405
  75.2 0.6 collective-permute-start.12
  76.0 0.7 collective-permute-done.18.refs_11_
  76.6 0.0 collective-permute-done.16.refs_8_
  76.6 1.4 %collective-permute-done.14.refs_5_ = bf16[1,128,512]{2,1,0:T(8,128)(2,1)S(1)} collective-permute-done((bf16[1,128,512]{2,1,0:T(8,128)(2,1)S(1)}, bf16[1,128,512]{2,1,0:T(8,128)(2,1)S(1)}, u32[]{:S(2)}, u32[]{:S(2)}) %collective-permute-start.14) | collective-permute-done | bytes 131104 | tf_op jit(solution)/shard_map/ppermute | solution.py:405
  78.0 2.3 %collective-permute-done.12.refs_2_ = bf16[1,128,512]{2,1,0:T(8,128)(2,1)S(1)} collective-permute-done((bf16[1,128,512]{2,1,0:T(8,128)(2,1)S(1)}, bf16[1,128,512]{2,1,0:T(8,128)(2,1)S(1)}, u32[]{:S(2)}, u32[]{:S(2)}) %collective-permute-start.12) | collective-permute-done | bytes 131104 | tf_op jit(solution)/shard_map/ppermute | solution.py:405
  80.3 1.0 %shard_map.87 = bf16[128,2048]{1,0:T(8,128)(2,1)} custom-call(f32[1,128,512]{2,1,0:T(8,128)S(1)} %get-tuple-element.45.refs_0_, bf16[1,128,512]{2,1,0:T(8,128)(2,1)S(1)} %slice.32.refs_1_, bf16[1,128,512]{2,1,0:T(8,128)(2,1)S(1)} %collective-permute-done.12.refs_2_, f32[1,128,512]{2,1,0:T(8,128)S(1)} %get-tuple-element.48.refs_3_, ...), custom_call_target="tpu_custom_call" | custom-call | tf_op jit(solution)/shard_map/pallas_call | solution.py:443
  (11 shorter events, 0.3 us)
Async XLA Ops:
  0.0 19.0 %collective-permute-start.3 = (bf16[128,2048]{1,0:T(8,128)(2,1)}, bf16[128,2048]{1,0:T(8,128)(2,1)S(1)}, u32[]{:S(2)}, u32[]{:S(2)}) collective-permute-start(bf16[128,2048]{1,0:T(8,128)(2,1)} %refs_0_.3), channel_id=1, source_target_pairs={{0,1},{1,0},{2,3},{3,2},{4,5},{5,4},{6,7},{7,6},{8,9},{9,8},{10,11... | collective-permute-start | bytes 1572872 | tf_op jit(solution)/shard_map/ppermute | solution.py:405
  2.9 16.0 %collective-permute-start.4 = (bf16[128,2048]{1,0:T(8,128)(2,1)}, bf16[128,2048]{1,0:T(8,128)(2,1)S(1)}, u32[]{:S(2)}, u32[]{:S(2)}) collective-permute-start(bf16[128,2048]{1,0:T(8,128)(2,1)} %refs_0_.3), channel_id=1, source_target_pairs={{0,2},{1,3},{2,0},{3,1},{4,6},{5,7},{6,4},{7,5},{8,10},{9,11},{10,... | collective-permute-start | bytes 1572872 | tf_op jit(solution)/shard_map/ppermute | solution.py:405
  5.9 13.7 %copy-start = (bf16[128,2048]{1,0:T(8,128)(2,1)S(1)}, bf16[128,2048]{1,0:T(8,128)(2,1)}, u32[]{:S(2)}) copy-start(bf16[128,2048]{1,0:T(8,128)(2,1)} %array_ref.1) | copy-start | bytes 1572868
  5.9 12.5 %collective-permute-start.2 = (bf16[32,128]{1,0:T(8,128)(2,1)}, bf16[32,128]{1,0:T(8,128)(2,1)S(1)}, u32[]{:S(2)}, u32[]{:S(2)}) collective-permute-start(bf16[32,128]{1,0:T(8,128)(2,1)} %shard_map.73.refs_0_.refs_2_), channel_id=1, source_target_pairs={{0,3},{1,2},{2,1},{3,0},{4,7},{5,6},{6,5},{7,4},{8,11},{9,10},{10,... | collective-permute-start | bytes 24584 | tf_op jit(solution)/shard_map/ppermute | solution.py:405
  6.0 12.6 %collective-permute-start.1 = (bf16[32,128]{1,0:T(8,128)(2,1)}, bf16[32,128]{1,0:T(8,128)(2,1)S(1)}, u32[]{:S(2)}, u32[]{:S(2)}) collective-permute-start(bf16[32,128]{1,0:T(8,128)(2,1)} %shard_map.73.refs_0_.refs_2_), channel_id=1, source_target_pairs={{0,2},{1,3},{2,0},{3,1},{4,6},{5,7},{6,4},{7,5},{8,10},{9,11},{10,... | collective-permute-start | bytes 24584 | tf_op jit(solution)/shard_map/ppermute | solution.py:405
  7.9 10.6 %collective-permute-start = (bf16[32,128]{1,0:T(8,128)(2,1)}, bf16[32,128]{1,0:T(8,128)(2,1)S(1)}, u32[]{:S(2)}, u32[]{:S(2)}) collective-permute-start(bf16[32,128]{1,0:T(8,128)(2,1)} %shard_map.73.refs_0_.refs_2_), channel_id=1, source_target_pairs={{0,1},{1,0},{2,3},{3,2},{4,5},{5,4},{6,7},{7,6},{8,9},{9,8},{10,11... | collective-permute-start | bytes 24584 | tf_op jit(solution)/shard_map/ppermute | solution.py:405
  9.4 0.7 copy-start.2
  18.5 4.8 %copy-start.1 = (bf16[128,2048]{1,0:T(8,128)(2,1)S(1)}, bf16[128,2048]{1,0:T(8,128)(2,1)}, u32[]{:S(2)}) copy-start(bf16[128,2048]{1,0:T(8,128)(2,1)} %refs_0_.3) | copy-start | bytes 1572868
  19.0 9.3 %collective-permute-start.8 = (bf16[64,2048]{1,0:T(8,128)(2,1)S(1)}, bf16[64,2048]{1,0:T(8,128)(2,1)S(1)}, u32[]{:S(2)}, u32[]{:S(2)}) collective-permute-start(bf16[64,2048]{1,0:T(8,128)(2,1)S(1)} %get-tuple-element.36), channel_id=1, source_target_pairs={{0,1},{1,0},{2,3},{3,2},{4,5},{5,4},{6,7},{7,6},{8,9},{9,8},{10,11... | collective-permute-start | bytes 786440 | tf_op jit(solution)/shard_map/ppermute | solution.py:405
  19.6 9.2 %collective-permute-start.7 = (bf16[64,2048]{1,0:T(8,128)(2,1)S(1)}, bf16[64,2048]{1,0:T(8,128)(2,1)S(1)}, u32[]{:S(2)}, u32[]{:S(2)}) collective-permute-start(bf16[64,2048]{1,0:T(8,128)(2,1)S(1)} %get-tuple-element.33._), channel_id=1, source_target_pairs={{0,2},{1,3},{2,0},{3,1},{4,6},{5,7},{6,4},{7,5},{8,10},{9,11},{10,... | collective-permute-start | bytes 786440 | tf_op jit(solution)/shard_map/ppermute | solution.py:405
  19.7 18.9 %collective-permute-start.6 = (bf16[128,2048]{1,0:T(8,128)(2,1)S(1)}, bf16[128,2048]{1,0:T(8,128)(2,1)S(1)}, u32[]{:S(2)}, u32[]{:S(2)}) collective-permute-start(bf16[128,2048]{1,0:T(8,128)(2,1)S(1)} %shard_map.77.refs_2_.refs_0_), channel_id=1, source_target_pairs={{0,2},{1,3},{2,0},{3,1},{4,6},{5,7},{6,4},{7,5},{8,10},{9,11},{10,... | collective-permute-start | bytes 1572872 | tf_op jit(solution)/shard_map/ppermute | solution.py:405
  21.8 16.9 %collective-permute-start.5 = (bf16[128,2048]{1,0:T(8,128)(2,1)S(1)}, bf16[128,2048]{1,0:T(8,128)(2,1)S(1)}, u32[]{:S(2)}, u32[]{:S(2)}) collective-permute-start(bf16[128,2048]{1,0:T(8,128)(2,1)S(1)} %shard_map.77.refs_2_.refs_0_), channel_id=1, source_target_pairs={{0,1},{1,0},{2,3},{3,2},{4,5},{5,4},{6,7},{7,6},{8,9},{9,8},{10,11... | collective-permute-start | bytes 1572872 | tf_op jit(solution)/shard_map/ppermute | solution.py:405
  38.7 6.4 %collective-permute-start.10 = (bf16[64,2048]{1,0:T(8,128)(2,1)S(1)}, bf16[64,2048]{1,0:T(8,128)(2,1)S(1)}, u32[]{:S(2)}, u32[]{:S(2)}) collective-permute-start(bf16[64,2048]{1,0:T(8,128)(2,1)S(1)} %get-tuple-element.41), channel_id=1, source_target_pairs={{0,1},{1,0},{2,3},{3,2},{4,5},{5,4},{6,7},{7,6},{8,9},{9,8},{10,11... | collective-permute-start | bytes 786440 | tf_op jit(solution)/shard_map/ppermute | solution.py:405
  40.3 6.4 %collective-permute-start.9 = (bf16[64,2048]{1,0:T(8,128)(2,1)S(1)}, bf16[64,2048]{1,0:T(8,128)(2,1)S(1)}, u32[]{:S(2)}, u32[]{:S(2)}) collective-permute-start(bf16[64,2048]{1,0:T(8,128)(2,1)S(1)} %get-tuple-element.40.refs_2_), channel_id=1, source_target_pairs={{0,2},{1,3},{2,0},{3,1},{4,6},{5,7},{6,4},{7,5},{8,10},{9,11},{10,... | collective-permute-start | bytes 786440 | tf_op jit(solution)/shard_map/ppermute | solution.py:405
  58.6 10.8 %collective-permute-start.17 = (bf16[2,128,512]{2,1,0:T(8,128)(2,1)S(1)}, bf16[2,128,512]{2,1,0:T(8,128)(2,1)S(1)}, u32[]{:S(2)}, u32[]{:S(2)}) collective-permute-start(bf16[2,128,512]{2,1,0:T(8,128)(2,1)S(1)} %get-tuple-element.55), channel_id=1, source_target_pairs={{0,2},{1,3},{2,0},{3,1},{4,6},{5,7},{6,4},{7,5},{8,10},{9,11},{10,... | collective-permute-start | bytes 786440 | tf_op jit(solution)/shard_map/ppermute | solution.py:405
  61.3 9.2 %collective-permute-start.15 = (bf16[2,128,512]{2,1,0:T(8,128)(2,1)S(1)}, bf16[2,128,512]{2,1,0:T(8,128)(2,1)S(1)}, u32[]{:S(2)}, u32[]{:S(2)}) collective-permute-start(bf16[2,128,512]{2,1,0:T(8,128)(2,1)S(1)} %get-tuple-element.52), channel_id=1, source_target_pairs={{0,1},{1,0},{2,3},{3,2},{4,5},{5,4},{6,7},{7,6},{8,9},{9,8},{10,11... | collective-permute-start | bytes 786440 | tf_op jit(solution)/shard_map/ppermute | solution.py:405
  63.6 8.6 %collective-permute-start.13 = (bf16[2,128,512]{2,1,0:T(8,128)(2,1)S(1)}, bf16[2,128,512]{2,1,0:T(8,128)(2,1)S(1)}, u32[]{:S(2)}, u32[]{:S(2)}) collective-permute-start(bf16[2,128,512]{2,1,0:T(8,128)(2,1)S(1)} %get-tuple-element.49), channel_id=1, source_target_pairs={{0,2},{1,3},{2,0},{3,1},{4,6},{5,7},{6,4},{7,5},{8,10},{9,11},{10,... | collective-permute-start | bytes 786440 | tf_op jit(solution)/shard_map/ppermute | solution.py:405
  67.8 7.4 %collective-permute-start.11 = (bf16[2,128,512]{2,1,0:T(8,128)(2,1)S(1)}, bf16[2,128,512]{2,1,0:T(8,128)(2,1)S(1)}, u32[]{:S(2)}, u32[]{:S(2)}) collective-permute-start(bf16[2,128,512]{2,1,0:T(8,128)(2,1)S(1)} %get-tuple-element.46), channel_id=1, source_target_pairs={{0,1},{1,0},{2,3},{3,2},{4,5},{5,4},{6,7},{7,6},{8,9},{9,8},{10,11... | collective-permute-start | bytes 786440 | tf_op jit(solution)/shard_map/ppermute | solution.py:405
  69.4 7.2 %collective-permute-start.18 = (bf16[1,128,512]{2,1,0:T(8,128)(2,1)S(1)}, bf16[1,128,512]{2,1,0:T(8,128)(2,1)S(1)}, u32[]{:S(2)}, u32[]{:S(2)}) collective-permute-start(bf16[1,128,512]{2,1,0:T(8,128)(2,1)S(1)} %add_convert_fusion), channel_id=1, source_target_pairs={{0,1},{1,0},{2,3},{3,2},{4,5},{5,4},{6,7},{7,6},{8,9},{9,8},{10,11... | collective-permute-start | bytes 393224 | tf_op jit(solution)/shard_map/ppermute | solution.py:405
  70.6 6.0 %collective-permute-start.16 = (bf16[1,128,512]{2,1,0:T(8,128)(2,1)S(1)}, bf16[1,128,512]{2,1,0:T(8,128)(2,1)S(1)}, u32[]{:S(2)}, u32[]{:S(2)}) collective-permute-start(bf16[1,128,512]{2,1,0:T(8,128)(2,1)S(1)} %add_convert_fusion.1), channel_id=1, source_target_pairs={{0,2},{1,3},{2,0},{3,1},{4,6},{5,7},{6,4},{7,5},{8,10},{9,11},{10,... | collective-permute-start | bytes 393224 | tf_op jit(solution)/shard_map/ppermute | solution.py:405
  72.3 5.8 %collective-permute-start.14 = (bf16[1,128,512]{2,1,0:T(8,128)(2,1)S(1)}, bf16[1,128,512]{2,1,0:T(8,128)(2,1)S(1)}, u32[]{:S(2)}, u32[]{:S(2)}) collective-permute-start(bf16[1,128,512]{2,1,0:T(8,128)(2,1)S(1)} %add_convert_fusion.2), channel_id=1, source_target_pairs={{0,1},{1,0},{2,3},{3,2},{4,5},{5,4},{6,7},{7,6},{8,9},{9,8},{10,11... | collective-permute-start | bytes 393224 | tf_op jit(solution)/shard_map/ppermute | solution.py:405
  75.2 5.0 %collective-permute-start.12 = (bf16[1,128,512]{2,1,0:T(8,128)(2,1)S(1)}, bf16[1,128,512]{2,1,0:T(8,128)(2,1)S(1)}, u32[]{:S(2)}, u32[]{:S(2)}) collective-permute-start(bf16[1,128,512]{2,1,0:T(8,128)(2,1)S(1)} %add_convert_fusion.3), channel_id=1, source_target_pairs={{0,2},{1,3},{2,0},{3,1},{4,6},{5,7},{6,4},{7,5},{8,10},{9,11},{10,... | collective-permute-start | bytes 393224 | tf_op jit(solution)/shard_map/ppermute | solution.py:405
